TPU v7x, 512 devices: a whole 4x4x16 slice. The times are simulated.
512 devices in a mesh: slab: 32 (over y, x, core), tile: 16 (over z).
Axes of the slice: x: 4, y: 4, z: 16, core: 2. Of those that a mesh axis runs over, the one named last changes fastest.
Arguments:
- history: bfloat16 [32, 2048, 8, 128], P('slab', 'tile'), may hold values from -15 to 15
- positions: bfloat16 [32, 2048, 3, 128], P('slab', 'tile'), may hold values from 0 to 1
- kappa_old: float32 [32, 2048, 128], P('slab', 'tile'), may hold values from 0.2 to 2
- threshold: float32 [32, 2048, 128], P('slab', 'tile'), may hold values from 0.3 to 1.5
- pair_ids: int32 [32, 2048, 8], P('slab', 'tile'), may hold values from 0 to 2047, as said below
- reader_counts: int32 [32, 2048], P('slab', 'tile'), may hold values from 1 to 8, as said below
- brick_map: int32 [32, 2048], P('slab', 'tile'), may hold values from 0 to 511, as said below
- strain_disp: bfloat16 [1024, 128], replicated, may hold values from -0.1875 to 0.1875
- couple: float32 [128, 128], replicated, may hold values from -0.5 to 0.5
Outputs:
- damage: float32 [32, 2048, 128], P('slab', 'tile')
- residual: float32 [1024, 16, 128], P('slab', 'tile')
Inputs may be any that keep to these rules, and one draw needn't show every extreme that they name: pair_ids[s, r, 0] = r; the other sources may be any clusters of the same depth layer. Only the first reader_counts[s, r] entries of pair_ids[s, r] are used. `brick_map`: a cluster among clusters t * 128 to (t + 1) * 128 - 1 lies in a brick among bricks (t - 1) * 32 to (t + 2) * 32 - 1.
All inputs are finite; a program needn't handle non-finite values.
Results may differ from a plain program's by a relative error of at most 0.0054.
Values may be sent and summed in bfloat16 or wider, within the bound.
No kernel may reach another device: no remote copies, remote signals or barrier semaphores. Data moves between devices by JAX's collectives and lax.ppermute only.
A program may use at most 64 MiB of HBM per device.

v0:
```python
import jax
import jax.numpy as jnp
from jax import lax
from jax.sharding import PartitionSpec as P

PAIRS = 8
BR_DEV = 32


SHARP = 12.0
SOFTEN = 2.0


def passed_along(block, axis, distance):
    devices = range(lax.axis_size(axis))
    route = [(i - distance, i) for i in devices if i - distance in devices]
    return lax.ppermute(block, axis, route)


def padded_2(array, sides, width):
    for axis, dim in sides:
        peers, length = (lax.axis_size(axis), array.shape[dim])
        up = [(i, (i + 1) % peers) for i in range(peers - 1)]
        down = [(j, i) for i, j in up]
        last = lax.slice_in_dim(array, length - width, length, axis=dim)
        leading = lax.slice_in_dim(array, 0, width, axis=dim)
        before = lax.ppermute(last, axis, up)
        after = lax.ppermute(leading, axis, down)
        array = jnp.concatenate([before, array, after], axis=dim)
    return array


def local(
    history,
    positions,
    kappa_old,
    threshold,
    pair_ids,
    reader_counts,
    brick_map,
    strain_disp,
    couple,
):
    hist = history[0]
    clusters = hist.shape[0]
    columns = hist.shape[1]
    points = hist.shape[2]
    packed = jnp.concatenate([hist, positions[0]], axis=1)
    tile_at = lax.axis_index("tile")
    ids = pair_ids[0]
    source = lax.all_gather(packed, "tile", axis=0, tiled=True)
    blocks = jnp.take(source, ids, axis=0)
    here = positions[0].astype(jnp.float32)
    counts = reader_counts[0]
    numer = jnp.zeros((clusters, columns, points), jnp.float32)
    denom = jnp.zeros((clusters, points), jnp.float32)
    for entry in range(PAIRS):
        src_hist = blocks[:, entry, :columns, :]
        src_pos = blocks[:, entry, columns:, :].astype(jnp.float32)
        dist = jnp.zeros((clusters, points, points), jnp.float32)
        for axis_k in range(3):
            delta = here[:, axis_k, :, None] - src_pos[:, axis_k, None, :]
            dist = dist + delta * delta
        live = (entry < counts).astype(jnp.float32)[:, None, None]
        weight = (jnp.exp(-SHARP * dist) * live).astype(jnp.bfloat16)
        numer = numer + jnp.einsum(
            "rcj,rij->rci", src_hist, weight, preferred_element_type=jnp.float32
        )
        denom = denom + jnp.sum(weight.astype(jnp.float32), axis=2)
    averaged = numer / denom[:, None, :]
    kappa = jnp.maximum(jnp.maximum(kappa_old[0], averaged[:, 0, :]), threshold[0])
    damage_here = 1.0 - threshold[0] / kappa * jnp.exp(-(kappa - threshold[0]) / SOFTEN)
    effective = ((1.0 - damage_here)[:, None, :] * averaged).astype(jnp.bfloat16)
    term = jnp.dot(
        effective.reshape(clusters, columns * points),
        strain_disp,
        preferred_element_type=jnp.float32,
    )
    bricks = BR_DEV
    owner = brick_map[0]
    local_brick = owner - (tile_at - 1) * bricks
    rows_near = lax.iota(jnp.int32, 3 * bricks)
    onehot = (local_brick[None, :] == rows_near[:, None]).astype(jnp.float32)
    shares = jnp.dot(
        onehot, term, precision=lax.Precision.HIGHEST, preferred_element_type=jnp.float32
    )
    shares = shares.reshape(3, bricks, term.shape[1])
    from_lower = passed_along(shares[2], "tile", 1)
    from_upper = passed_along(shares[0], "tile", -1)
    force = shares[1] + from_lower + from_upper
    padded = padded_2(force, (("slab", 0),), 1)
    beside = padded[:-2] + padded[2:]
    residual_here = force + jnp.dot(
        beside, couple, precision=lax.Precision.HIGHEST, preferred_element_type=jnp.float32
    )
    return (damage_here[None, :, :], residual_here[:, None, :])


def solution(mesh):
    placed = (
        P("slab", "tile", None, None),
        P("slab", "tile", None, None),
        P("slab", "tile", None),
        P("slab", "tile", None),
        P("slab", "tile", None),
        P("slab", "tile"),
        P("slab", "tile"),
        P(),
        P(),
    )
    return jax.shard_map(
        local,
        mesh=mesh,
        in_specs=placed,
        out_specs=(P("slab", "tile", None), P("slab", "tile", None)),
        check_vma=False,
    )
```

profile of v0, /device:TPU:7, one launch (start us, length us, event | category | flops | bytes accessed | tf_op | source)
XLA Modules:
  0.0 307.6 jit_solution(755815150721862255)
XLA Ops:
  7.2 0.0 copy-start
  7.2 0.0 all-gather.2.cloned.1.call-start
  7.2 1.0 copy.83
  8.2 1.7 pad_maximum_fusion
  9.9 0.0 all-gather.2.cloned.1.call-update
  9.9 0.7 compare_select_fusion
  10.6 0.1 copy.43
  10.7 0.1 reshape.192
  10.8 0.7 subtract_bitcast_fusion
  11.5 0.7 fusion.36
  12.1 0.7 compare_and_fusion
  12.8 0.9 bitcast_convert_fusion
  13.8 79.4 %all-gather.2.cloned.1.call-done = bf16[2048,11,128]{2,0,1:T(8,128)(2,1)} async-done(((bf16[128,11,128]{2,0,1:T(8,128)(2,1)}), bf16[2048,11,128]{2,0,1:T(8,128)(2,1)}) %all-gather.2.cloned.1.call-update) | async-done | bytes 5767184 | tf_op jit(solution)/shard_map/all_gather | solution.py:51
  93.2 9.0 %copy.44 = bf16[2048,11,128]{2,1,0:T(8,128)(2,1)} copy(bf16[2048,11,128]{2,0,1:T(8,128)(2,1)} %all-gather.2.cloned.1.call-done) | data formatting | bytes 11534336 | tf_op jit(solution)/shard_map/all_gather | solution.py:51
  102.2 11.9 %gather_fusion = bf16[1024,11,128]{2,1,0:T(8,128)(2,1)} fusion(bf16[2048,11,128]{2,1,0:T(8,128)(2,1)} %copy.44, s32[1024]{0:T(1024)S(1)} %broadcast_clamp_fusion), kind=kCustom, calls=%fused_computation | custom fusion | bytes 5771264 | tf_op jit(solution)/shard_map/jit(_take)/gather | solution.py:52
  114.1 3.6 %copy_select_fusion = bf16[128,8,11,128]{3,2,0,1:T(8,128)(2,1)S(1)} fusion(bf16[128,8,11,128]{3,2,1,0:T(8,128)(2,1)} %bitcast.146, pred[128,8]{0,1:T(8,128)(4,1)S(1)} %compare_and_fusion), kind=kLoop, calls=%fused_computation.17 | loop fusion | flops 1441792 | bytes 5768192 | tf_op jit(solution)/shard_map/jit(_take)/select_n | solution.py:52
  117.7 0.3 fusion.16
  118.1 0.3 fusion.53
  118.4 0.3 fusion.55
  118.6 0.3 fusion.57
  118.9 13.0 %fusion = f32[128,8,128]{2,1,0:T(8,128)S(1)} fusion(f32[128]{0:T(128)S(1)} %get-tuple-element.61, f32[128,128]{1,0:T(8,128)S(1)} %bitcast.164, f32[128,128]{1,0:T(8,128)S(1)} %get-tuple-element.55, f32[128,128]{1,0:T(8,128)S(1)} %bitcast.166, f32[128,128]{1,0:T(8,128)S(1)} %get-tuple-element.56, f32[128,128]{1,0:T(8,128)S(1)} %bitcast.162, ...), kind=kOutput, calls=%fused_computation.18 | convolution fusion | flops 56623104 | bytes 1180160 | tf_op jit(solution)/shard_map/rcj,rij->rci/dot_general | solution.py:66
  131.9 13.0 %fusion.2 = f32[128,8,128]{2,1,0:T(8,128)S(1)} fusion(f32[128]{0:T(128)S(1)} %get-tuple-element.65, f32[128,128]{1,0:T(8,128)S(1)} %bitcast.176, f32[128,128]{1,0:T(8,128)S(1)} %bitcast.178, f32[128,128]{1,0:T(8,128)S(1)} %bitcast.174, f32[128,128]{1,0:T(8,128)S(1)} %get-tuple-element.55, f32[128,128]{1,0:T(8,128)S(1)} %get-tuple-element.56, ...), kind=kOutput, calls=%fused_computation.20 | convolution fusion | flops 56623104 | bytes 1180160 | tf_op jit(solution)/shard_map/rcj,rij->rci/dot_general | solution.py:66
  144.9 13.0 %fusion.3 = f32[128,8,128]{2,1,0:T(8,128)S(1)} fusion(f32[128]{0:T(128)S(1)} %get-tuple-element.64, f32[128,128]{1,0:T(8,128)S(1)} %bitcast.182, f32[128,128]{1,0:T(8,128)S(1)} %bitcast.180, f32[128,128]{1,0:T(8,128)S(1)} %bitcast.184, f32[128,128]{1,0:T(8,128)S(1)} %get-tuple-element.55, f32[128,128]{1,0:T(8,128)S(1)} %get-tuple-element.56, ...), kind=kOutput, calls=%fused_computation.21 | convolution fusion | flops 56623104 | bytes 1180160 | tf_op jit(solution)/shard_map/rcj,rij->rci/dot_general | solution.py:66
  157.9 25.4 %convert_reduce_fusion.7 = (f32[128,128]{1,0:T(8,128)S(1)}, f32[128,128]{1,0:T(8,128)S(1)}, f32[128,128]{1,0:T(8,128)S(1)}, f32[128,128]{1,0:T(8,128)S(1)}) fusion(f32[128]{0:T(128)S(1)} %get-tuple-element.61, f32[128,128]{1,0:T(8,128)S(1)} %bitcast.165, f32[128,128]{1,0:T(8,128)S(1)} %get-tuple-element.55, f32[128,128]{1,0:T(8,128)S(1)} %bitcast.167, ...), kind=kLoop, calls=%fused_computation.8 | loop fusion | flops 108986368 | bytes 1247232 | tf_op jit(solution)/shard_map/reduce_sum | solution.py:69
  183.3 13.0 %fusion.4 = f32[128,8,128]{2,1,0:T(8,128)S(1)} fusion(f32[128]{0:T(128)S(1)} %get-tuple-element.63, f32[128,128]{1,0:T(8,128)S(1)} %bitcast.189, f32[128,128]{1,0:T(8,128)S(1)} %bitcast.191, f32[128,128]{1,0:T(8,128)S(1)} %bitcast.187, f32[128,128]{1,0:T(8,128)S(1)} %get-tuple-element.55, f32[128,128]{1,0:T(8,128)S(1)} %get-tuple-element.56, ...), kind=kOutput, calls=%fused_computation.22 | convolution fusion | flops 56623104 | bytes 1180160 | tf_op jit(solution)/shard_map/rcj,rij->rci/dot_general | solution.py:66
  196.3 0.3 fusion.59
  196.6 13.0 %fusion.1 = f32[128,8,128]{2,1,0:T(8,128)S(1)} fusion(f32[128]{0:T(128)S(1)} %get-tuple-element.66, f32[128,128]{1,0:T(8,128)S(1)} %bitcast.152, f32[128,128]{1,0:T(8,128)S(1)} %bitcast.150, f32[128,128]{1,0:T(8,128)S(1)} %bitcast.154, f32[128,128]{1,0:T(8,128)S(1)} %get-tuple-element.55, f32[128,128]{1,0:T(8,128)S(1)} %get-tuple-element.56, ...), kind=kOutput, calls=%fused_computation.19 | convolution fusion | flops 56623104 | bytes 1180160 | tf_op jit(solution)/shard_map/rcj,rij->rci/dot_general | solution.py:66
  209.5 13.0 %fusion.5 = f32[128,8,128]{2,1,0:T(8,128)S(1)} fusion(f32[128]{0:T(128)S(1)} %get-tuple-element.62, f32[128,128]{1,0:T(8,128)S(1)} %bitcast.158, f32[128,128]{1,0:T(8,128)S(1)} %bitcast.156, f32[128,128]{1,0:T(8,128)S(1)} %bitcast.160, f32[128,128]{1,0:T(8,128)S(1)} %get-tuple-element.55, f32[128,128]{1,0:T(8,128)S(1)} %get-tuple-element.56, ...), kind=kOutput, calls=%fused_computation.23 | convolution fusion | flops 56623104 | bytes 1180160 | tf_op jit(solution)/shard_map/rcj,rij->rci/dot_general | solution.py:66
  222.5 13.0 %fusion.6 = f32[128,8,128]{2,1,0:T(8,128)S(1)} fusion(f32[128]{0:T(128)S(1)} %get-tuple-element.68, f32[128,128]{1,0:T(8,128)S(1)} %bitcast.194, f32[128,128]{1,0:T(8,128)S(1)} %bitcast.196, f32[128,128]{1,0:T(8,128)S(1)} %bitcast.192, f32[128,128]{1,0:T(8,128)S(1)} %get-tuple-element.55, f32[128,128]{1,0:T(8,128)S(1)} %get-tuple-element.56, ...), kind=kOutput, calls=%fused_computation.24 | convolution fusion | flops 56623104 | bytes 1180160 | tf_op jit(solution)/shard_map/rcj,rij->rci/dot_general | solution.py:66
  235.5 25.4 %convert_reduce_fusion.6 = (f32[128,128]{1,0:T(8,128)S(1)}, f32[128,128]{1,0:T(8,128)S(1)}, f32[128,128]{1,0:T(8,128)S(1)}, f32[128,128]{1,0:T(8,128)S(1)}) fusion(f32[128]{0:T(128)S(1)} %get-tuple-element.66, f32[128,128]{1,0:T(8,128)S(1)} %bitcast.153, f32[128,128]{1,0:T(8,128)S(1)} %get-tuple-element.55, f32[128,128]{1,0:T(8,128)S(1)} %bitcast.151, ...), kind=kLoop, calls=%fused_computation.7 | loop fusion | flops 108986368 | bytes 1247232 | tf_op jit(solution)/shard_map/reduce_sum | solution.py:69
  260.9 0.0 copy-start.1
  260.9 0.0 copy-start.2
  260.9 0.0 copy-start.3
  261.0 13.0 %fusion.7 = f32[128,8,128]{2,1,0:T(8,128)S(1)} fusion(f32[128]{0:T(128)S(1)} %get-tuple-element.67, f32[128,128]{1,0:T(8,128)S(1)} %bitcast.171, f32[128,128]{1,0:T(8,128)S(1)} %bitcast.169, f32[128,128]{1,0:T(8,128)S(1)} %bitcast.173, f32[128,128]{1,0:T(8,128)S(1)} %get-tuple-element.55, f32[128,128]{1,0:T(8,128)S(1)} %get-tuple-element.56, ...), kind=kOutput, calls=%fused_computation.25 | convolution fusion | flops 56623104 | bytes 1180160 | tf_op jit(solution)/shard_map/rcj,rij->rci/dot_general | solution.py:66
  274.0 0.6 fusion.8
  274.6 0.0 copy-done.1
  274.6 0.0 copy-done.2
  274.7 0.2 copy.55
  274.9 0.0 copy-done
  274.9 0.3 fusion.63
  275.2 0.2 fusion.29
  275.4 3.0 collective-permute-start
  278.3 1.3 collective-permute-start.1
  279.6 0.0 collective-permute-done
  279.6 3.2 %collective-permute-done.1 = f32[32,128]{1,0:T(8,128)S(1)} collective-permute-done((f32[32,128]{1,0:T(8,128)S(1)}, f32[32,128]{1,0:T(8,128)S(1)}, u32[]{:S(2)}, u32[]{:S(2)}) %collective-permute-start.1) | collective-permute-done | bytes 16416 | tf_op jit(solution)/shard_map/ppermute | solution.py:17
  282.8 10.2 %collective-permute-start.2 = (f32[1,128]{1,0:T(1,128)S(1)}, f32[1,128]{1,0:T(1,128)S(1)}, u32[]{:S(2)}, u32[]{:S(2)}) collective-permute-start(f32[1,128]{1,0:T(1,128)S(1)} %get-tuple-element.59), channel_id=1, source_target_pairs={{0,16},{16,32},{32,48},{48,64},{64,80},{80,96},{96,112},{112,128},... | collective-permute-start | bytes 1544 | tf_op jit(solution)/shard_map/ppermute | solution.py:27
  293.0 1.9 collective-permute-start.3
  294.9 0.7 fusion.18
  295.6 0.0 collective-permute-done.2
  295.6 4.4 %collective-permute-done.3 = f32[1,128]{1,0:T(1,128)S(1)} collective-permute-done((f32[1,128]{1,0:T(1,128)S(1)}, f32[1,128]{1,0:T(1,128)S(1)}, u32[]{:S(2)}, u32[]{:S(2)}) %collective-permute-start.3) | collective-permute-done | bytes 544 | tf_op jit(solution)/shard_map/ppermute | solution.py:28
  300.0 0.0 copy-done.3
  300.0 0.8 convolution_add_fusion
  (8 shorter events, 0.2 us)
Async XLA Ops:
  7.2 267.7 %copy-start = (bf16[1024,128]{1,0:T(8,128)(2,1)S(1)}, bf16[1024,128]{1,0:T(8,128)(2,1)}, u32[]{:S(2)}) copy-start(bf16[1024,128]{1,0:T(8,128)(2,1)} %param.16) | copy-start | bytes 786436
  7.2 86.0 %all-gather.2.cloned.1.call-start = ((), (), s32[]{:S(2)}) async-start(), calls=%async_computation | async-start | bytes 6127616 | tf_op jit(solution)/shard_map/all_gather | solution.py:51
  260.9 13.7 %copy-start.1 = (f32[1,128,128]{2,1,0:T(8,128)S(1)}, f32[1,128,128]{2,1,0:T(8,128)}, u32[]{:S(2)}) copy-start(f32[1,128,128]{2,1,0:T(8,128)} %param.12) | copy-start | bytes 196612
  260.9 13.7 %copy-start.2 = (f32[1,128,128]{2,1,0:T(8,128)S(1)}, f32[1,128,128]{2,1,0:T(8,128)}, u32[]{:S(2)}) copy-start(f32[1,128,128]{2,1,0:T(8,128)} %param.11) | copy-start | bytes 196612
  260.9 39.0 %copy-start.3 = (f32[128,128]{1,0:T(8,128)S(1)}, f32[128,128]{1,0:T(8,128)}, u32[]{:S(2)}) copy-start(f32[128,128]{1,0:T(8,128)} %param.17) | copy-start | bytes 196612
  275.4 4.3 %collective-permute-start = (f32[32,128]{1,0:T(8,128)S(1)}, f32[32,128]{1,0:T(8,128)S(1)}, u32[]{:S(2)}, u32[]{:S(2)}) collective-permute-start(f32[32,128]{1,0:T(8,128)S(1)} %get-tuple-element.57), channel_id=1, source_target_pairs={{0,1},{1,2},{2,3},{3,4},{4,5},{5,6},{6,7},{7,8},{8,9},{9,10},{10,1... | collective-permute-start | bytes 49160 | tf_op jit(solution)/shard_map/ppermute | solution.py:17
  278.3 4.5 %collective-permute-start.1 = (f32[32,128]{1,0:T(8,128)S(1)}, f32[32,128]{1,0:T(8,128)S(1)}, u32[]{:S(2)}, u32[]{:S(2)}) collective-permute-start(f32[32,128]{1,0:T(8,128)S(1)} %get-tuple-element.58), channel_id=1, source_target_pairs={{1,0},{2,1},{3,2},{4,3},{5,4},{6,5},{7,6},{8,7},{9,8},{10,9},{11,1... | collective-permute-start | bytes 49160 | tf_op jit(solution)/shard_map/ppermute | solution.py:17
  282.8 12.8 %collective-permute-start.2 = (f32[1,128]{1,0:T(1,128)S(1)}, f32[1,128]{1,0:T(1,128)S(1)}, u32[]{:S(2)}, u32[]{:S(2)}) collective-permute-start(f32[1,128]{1,0:T(1,128)S(1)} %get-tuple-element.59), channel_id=1, source_target_pairs={{0,16},{16,32},{32,48},{48,64},{64,80},{80,96},{96,112},{112,128},... | collective-permute-start | bytes 1544 | tf_op jit(solution)/shard_map/ppermute | solution.py:27
  293.0 7.0 %collective-permute-start.3 = (f32[1,128]{1,0:T(1,128)S(1)}, f32[1,128]{1,0:T(1,128)S(1)}, u32[]{:S(2)}, u32[]{:S(2)}) collective-permute-start(f32[1,128]{1,0:T(1,128)S(1)} %get-tuple-element.60), channel_id=1, source_target_pairs={{16,0},{32,16},{48,32},{64,48},{80,64},{96,80},{112,96},{128,112},... | collective-permute-start | bytes 1544 | tf_op jit(solution)/shard_map/ppermute | solution.py:28
Sparse Core Ops, SparseCore 0:
  10.1 83.0 all-gather.1
where the time goes:
time: 308 us
  matrix products  105 us (34%)
  waiting for transfers between devices  87 us (28%)
  other arithmetic  61.5 us (20%)
  local copies, waits for them, and re-layouts  23.4 us (8%)
  starting transfers between devices  16.4 us (5%)
  between operations  14.3 us (5%)
    dot_general x8, matrix products, local(): jnp.einsum('rcj,rij->rci', src_hist, weight, preferred_element_type=jnp.f...  104 us
    all_gather x1, waiting for transfers between devices, local(): source = lax.all_gather(packed, 'tile', axis=0, tiled=True)  79.4 us
    reduce_sum x2, other arithmetic, local(): denom = denom + jnp.sum(weight.astype(jnp.float32), axis=2)  50.8 us
    gather x1, local copies, waits for them, and re-layouts, local(): blocks = jnp.take(source, ids, axis=0)  11.9 us
    ppermute x1, starting transfers between devices, padded_2(): before = lax.ppermute(last, axis, up)  10.2 us
    all_gather x1, local copies, waits for them, and re-layouts, local(): source = lax.all_gather(packed, 'tile', axis=0, tiled=True)  9.01 us
  transfers between devices with their start and end apart: 5, of which 3 were waited for; matrix products, arithmetic and copies ran while one was open for 1% of the time, Pallas kernels for 0%

commit v1 on v0

v1 whole, which is shorter than its diff:
```python
import functools
import math

import jax
import jax.numpy as jnp
from jax import lax
from jax.experimental import pallas as pl
from jax.experimental.pallas import tpu as pltpu
from jax.sharding import PartitionSpec as P

PTS = 128
COLS = 8
PAIRS = 8
CL = 128
BR_DEV = 32
N_TILE = 16
SHARP = 12.0
SOFTEN = 2.0
SCALE = SHARP * math.log2(math.e)

UNITS = 4
STEP = 2 * UNITS
KDIM = 16
MAX_STEPS = (CL * PAIRS + N_TILE * (STEP - 1)) // STEP
LISTED = MAX_STEPS * STEP
HIST_ROWS = CL * COLS
ACC_ROWS = (CL + 1) * 2 * COLS


def list_kernel(ids_ref, cnt_ref, tile_ref, here_ref, r_ref, q_ref, meta_ref, x_ref, cur_ref, rows_ref):
    reader_rows(here_ref, rows_ref, x_ref)
    tile = tile_ref[0]
    for c in range(N_TILE):
        cur_ref[c] = 0

    def count_reader(r, carry):
        def count_entry(p, carry):
            c = ((ids_ref[p, r] >> 7) - tile) & (N_TILE - 1)
            cur_ref[c] = cur_ref[c] + 1
            return carry

        return lax.fori_loop(0, cnt_ref[0, r], count_entry, carry)

    lax.fori_loop(0, CL, count_reader, 0)
    start = jnp.int32(0)
    ends = []
    for c in range(N_TILE):
        meta_ref[c] = start
        at = start * STEP
        start = start + ((cur_ref[c] + (STEP - 1)) >> 3)
        cur_ref[c] = at
        ends.append(start * STEP)
    meta_ref[N_TILE] = start
    meta_ref[N_TILE + 1] = tile

    def fill_reader(r, carry):
        def fill_entry(p, carry):
            q = ids_ref[p, r]
            c = ((q >> 7) - tile) & (N_TILE - 1)
            at = cur_ref[c]
            r_ref[at] = r
            q_ref[at] = q & (CL - 1)
            cur_ref[c] = at + 1
            return carry

        return lax.fori_loop(0, cnt_ref[0, r], fill_entry, carry)

    lax.fori_loop(0, CL, fill_reader, 0)
    for c in range(N_TILE):

        def pad(at, carry):
            r_ref[at] = CL
            q_ref[at] = 0
            return carry

        lax.fori_loop(cur_ref[c], ends[c], pad, 0)


def reader_rows(here_ref, rows_ref, x_ref):
    here = [here_ref[k].astype(jnp.float32) for k in range(3)]
    twice = [split3((2.0 * SCALE) * h) for h in here]
    norm = split3(-SCALE * (here[0] * here[0] + here[1] * here[1] + here[2] * here[2]))
    rows = [twice[k][t] for t in range(3) for k in range(3)] + list(norm)
    rows_ref[...] = jnp.ones_like(rows_ref)
    for k, row in enumerate(rows):
        rows_ref[pl.ds(k, CL, stride=KDIM), :] = row
    rows_ref[pl.ds(KDIM - 1, CL, stride=KDIM), :] = jnp.zeros((CL, PTS), jnp.float32)

    def turn(r, carry):
        rows = rows_ref[pl.ds(pl.multiple_of(r * KDIM, KDIM), KDIM), :]
        x_ref[r] = jnp.concatenate([rows, rows], axis=0).T.astype(jnp.bfloat16)
        return carry

    lax.fori_loop(0, CL, turn, 0)


SMEM = pl.BlockSpec(memory_space=pltpu.SMEM)
VMEM = pl.BlockSpec(memory_space=pltpu.VMEM)


def make_lists(ids, counts, tile, here):
    return pl.pallas_call(
        list_kernel,
        out_shape=[
            jax.ShapeDtypeStruct((LISTED,), jnp.int32),
            jax.ShapeDtypeStruct((LISTED,), jnp.int32),
            jax.ShapeDtypeStruct((N_TILE + 2,), jnp.int32),
            jax.ShapeDtypeStruct((CL, PTS, 2 * KDIM), jnp.bfloat16),
        ],
        in_specs=[SMEM] * 3 + [VMEM],
        out_specs=[SMEM] * 3 + [VMEM],
        scratch_shapes=[
            pltpu.SMEM((N_TILE,), jnp.int32),
            pltpu.VMEM((CL * KDIM, PTS), jnp.float32),
        ],
        compiler_params=pltpu.CompilerParams(vmem_limit_bytes=16 * 2**20),
        cost_estimate=pl.CostEstimate(flops=10**6, bytes_accessed=5 * 10**6, transcendentals=0),
    )(ids, counts, tile, here)


def split3(x):
    hi = x.astype(jnp.bfloat16).astype(jnp.float32)
    mid = (x - hi).astype(jnp.bfloat16).astype(jnp.float32)
    return hi, mid, x - hi - mid


def prepare(source, d, hist_ref, y_ref):
    hist_ref[...] = source[d, :HIST_ROWS].astype(jnp.float32)
    at = HIST_ROWS
    spots = [source[d, at + k * CL : at + (k + 1) * CL].astype(jnp.float32) for k in range(3)]
    norm = spots[0] * spots[0] + spots[1] * spots[1] + spots[2] * spots[2]
    rows = spots * 3 + [None] * 3 + list(split3(-SCALE * norm))
    for k, row in enumerate(rows):
        if row is not None:
            y_ref[pl.ds(k, CL, stride=KDIM), :] = row


def constant_rows(y_ref):
    y_ref[...] = jnp.ones_like(y_ref)
    y_ref[pl.ds(KDIM - 1, CL, stride=KDIM), :] = jnp.zeros((CL, PTS), jnp.float32)


def pairs(begin, end, r_s, q_s, x_ref, hist_ref, y_ref, acc_ref):
    first = lax.broadcasted_iota(jnp.int32, (PTS, 2 * KDIM), 1) < KDIM
    zero_y = jnp.zeros((KDIM, PTS), jnp.float32)
    zero_h = jnp.zeros((COLS, PTS), jnp.float32)
    row = lax.broadcasted_iota(jnp.int32, (2 * COLS, 2 * PTS), 0) >> 3
    side = lax.broadcasted_iota(jnp.int32, (2 * COLS, 2 * PTS), 1) >> 7
    ones = (row == side).astype(jnp.float32).astype(jnp.bfloat16)

    def beside(one, other, zero):
        top = jnp.concatenate([one, zero], axis=1)
        bottom = jnp.concatenate([zero, other], axis=1)
        return jnp.concatenate([top, bottom], axis=0).astype(jnp.bfloat16)

    def step(i, carry):
        outs = []
        for u in range(UNITS):
            r = [r_s[i * STEP + 2 * u + k] for k in range(2)]
            q = [q_s[i * STEP + 2 * u + k] for k in range(2)]
            lhs = jnp.where(first, x_ref[r[0] & (CL - 1)], x_ref[r[1] & (CL - 1)])
            ys = [y_ref[pl.ds(pl.multiple_of(k * KDIM, KDIM), KDIM), :] for k in q]
            power = jnp.dot(lhs, beside(*ys, zero_y), preferred_element_type=jnp.float32)
            weight = jnp.exp2(power).astype(jnp.bfloat16)
            hs = [hist_ref[pl.ds(pl.multiple_of(k * COLS, COLS), COLS), :] for k in q]
            both = jnp.concatenate([beside(*hs, zero_h), ones], axis=0)
            out = lax.dot_general(
                both, weight, (((1,), (1,)), ((), ())), preferred_element_type=jnp.float32
            )
            outs.append((r, out))
        for r, out in outs:
            for half in range(2):
                at = pl.multiple_of(r[half] * (2 * COLS), 2 * COLS)
                acc_ref[pl.ds(at, COLS), :] += out[half * COLS : (half + 1) * COLS]
                acc_ref[pl.ds(at + COLS, COLS), :] += out[(2 + half) * COLS : (3 + half) * COLS]
        return carry

    lax.fori_loop(begin, end, step, 0)


def finish(acc_ref, kappa_ref, threshold_ref, disp_ref, brick_ref, damage_ref, shares_ref):
    inverse = 1.0 / acc_ref[pl.ds(COLS, CL, stride=2 * COLS), :]
    threshold = threshold_ref[...]
    strain = acc_ref[pl.ds(0, CL, stride=2 * COLS), :] * inverse
    kappa = jnp.maximum(jnp.maximum(kappa_ref[...], strain), threshold)
    damage = 1.0 - (threshold / kappa) * jnp.exp(-(kappa - threshold) / SOFTEN)
    damage_ref[...] = damage
    left = 1.0 - damage
    term = jnp.zeros((CL, PTS), jnp.float32)
    for c in range(COLS):
        mean = acc_ref[pl.ds(c, CL, stride=2 * COLS), :] * inverse
        term = term + jnp.dot(
            (left * mean).astype(jnp.bfloat16),
            disp_ref[c * PTS : (c + 1) * PTS, :],
            preferred_element_type=jnp.float32,
        )
    rows = lax.broadcasted_iota(jnp.int32, (3 * BR_DEV, CL), 0)
    onehot = (rows == brick_ref[...]).astype(jnp.float32)
    shares_ref[...] = jnp.dot(
        onehot, term, precision=lax.Precision.HIGHEST, preferred_element_type=jnp.float32
    )


def gather_kernel(
    meta,
    r_s,
    q_s,
    x_ref,
    source,
    kappa_ref,
    threshold_ref,
    disp_ref,
    brick_ref,
    damage_ref,
    shares_ref,
    acc_ref,
    hist_ref,
    y_ref,
):
    acc_ref[...] = jnp.zeros_like(acc_ref)
    constant_rows(y_ref)

    def block(rel, carry):
        prepare(source, (meta[N_TILE + 1] + rel) & (N_TILE - 1), hist_ref, y_ref)
        pairs(meta[rel], meta[rel + 1], r_s, q_s, x_ref, hist_ref, y_ref, acc_ref)
        return carry

    lax.fori_loop(0, N_TILE, block, 0)
    finish(acc_ref, kappa_ref, threshold_ref, disp_ref, brick_ref, damage_ref, shares_ref)


def consume(lists, source, final):
    r_list, q_list, meta, x_rows = lists
    return pl.pallas_call(
        gather_kernel,
        out_shape=[
            jax.ShapeDtypeStruct((CL, PTS), jnp.float32),
            jax.ShapeDtypeStruct((3 * BR_DEV, PTS), jnp.float32),
        ],
        in_specs=[SMEM] * 3 + [VMEM] * 6,
        out_specs=[VMEM] * 2,
        scratch_shapes=[
            pltpu.VMEM((ACC_ROWS, PTS), jnp.float32),
            pltpu.VMEM((HIST_ROWS, PTS), jnp.float32),
            pltpu.VMEM((CL * KDIM, PTS), jnp.float32),
        ],
        compiler_params=pltpu.CompilerParams(vmem_limit_bytes=32 * 2**20),
        cost_estimate=pl.CostEstimate(
            flops=2 * 320 * PTS * 256 * 256, bytes_accessed=12 * 2**20, transcendentals=10**7
        ),
    )(meta, r_list, q_list, x_rows, source, *final)


def shifted(block, axis, distance):
    devices = range(lax.axis_size(axis))
    route = [(i - distance, i) for i in devices if i - distance in devices]
    return lax.ppermute(block, axis, route)


def local(
    history,
    positions,
    kappa_old,
    threshold,
    pair_ids,
    reader_counts,
    brick_map,
    strain_disp,
    couple,
):
    points = positions[0].transpose(1, 0, 2)
    own = jnp.concatenate(
        [history[0].reshape(HIST_ROWS, PTS), points.reshape(3 * CL, PTS)], axis=0
    )
    tile = lax.axis_index("tile")
    lists = make_lists(pair_ids[0].T, reader_counts, tile.astype(jnp.int32).reshape(1), points)
    source = lax.all_gather(own, "tile", axis=0, tiled=False)
    brick = brick_map - (tile - 1) * BR_DEV
    damage_here, shares = consume(
        lists, source, (kappa_old[0], threshold[0], strain_disp, brick)
    )
    low, mid, top = shares[:BR_DEV], shares[BR_DEV : 2 * BR_DEV], shares[2 * BR_DEV :]
    force = mid + shifted(top, "tile", 1) + shifted(low, "tile", -1)
    before = shifted(force[-1:], "slab", 1)
    after = shifted(force[:1], "slab", -1)
    padded = jnp.concatenate([before, force, after], axis=0)
    residual_here = force + jnp.dot(
        padded[:-2] + padded[2:],
        couple,
        precision=lax.Precision.HIGHEST,
        preferred_element_type=jnp.float32,
    )
    return (damage_here[None], residual_here[:, None, :])


def solution(mesh):
    placed = (
        P("slab", "tile", None, None),
        P("slab", "tile", None, None),
        P("slab", "tile", None),
        P("slab", "tile", None),
        P("slab", "tile", None),
        P("slab", "tile"),
        P("slab", "tile"),
        P(),
        P(),
    )
    return jax.shard_map(
        local,
        mesh=mesh,
        in_specs=placed,
        out_specs=(P("slab", "tile", None), P("slab", "tile", None)),
        check_vma=False,
    )
```

time: 308 us -> 169 us (0.55)
  the two profiles are of different devices: /device:TPU:7 before, /device:TPU:1 now
where the time goes in v1:
time: 169 us
  Pallas kernels  67.3 us (40%)
  waiting for transfers between devices  56.9 us (34%)
  starting transfers between devices  15.7 us (9%)
  between operations  14.1 us (8%)
  local copies, waits for them, and re-layouts  11.7 us (7%)
  other arithmetic  2.44 us (1%)
    all_gather x1, waiting for transfers between devices, local(): source = lax.all_gather(own, 'tile', axis=0, tiled=False)  49 us
    pallas_call x1, Pallas kernels, consume(): pl.pallas_call(gather_kernel, out_shape=[jax.ShapeDtypeStruct((CL, PTS),...  36 us
    pallas_call x1, Pallas kernels, make_lists(): pl.pallas_call(list_kernel, out_shape=[jax.ShapeDtypeStruct((LISTED,), jn...  31.3 us
    ppermute x4, starting transfers between devices, shifted(): return lax.ppermute(block, axis, route)  15.7 us
    unnamed x20, local copies, waits for them, and re-layouts  11.7 us
    ppermute x4, waiting for transfers between devices, shifted(): return lax.ppermute(block, axis, route)  7.89 us
  transfers between devices with their start and end apart: 5, of which 3 were waited for; matrix products, arithmetic and copies ran while one was open for 0% of the time, Pallas kernels for 19%

profile of v1, /device:TPU:1, one launch (start us, length us, event | category | flops | bytes accessed | tf_op | source)
XLA Modules:
  0.0 169.0 jit_solution(4652595076384181933)
XLA Ops:
  7.2 0.0 copy-start
  7.2 0.0 all-gather.3.cloned.1.call-start
  7.2 1.8 %pad_maximum_fusion = bf16[1408,128]{1,0:T(8,128)(2,1)} fusion(bf16[384,128]{1,0:T(8,128)(2,1)} %bitcast.18, bf16[1024,128]{1,0:T(8,128)(2,1)} %bitcast.24), kind=kLoop, calls=%fused_computation.1 | loop fusion | flops 720896 | bytes 720896 | tf_op jit(solution)/shard_map/concatenate | solution.py:272
  9.0 0.0 all-gather.3.cloned.1.call-update
  9.0 0.0 copy-start.1
  9.0 0.9 copy-done.1
  9.9 0.0 copy-start.2
  9.9 0.7 copy-done.2
  10.6 0.0 copy-start.3
  10.6 0.7 copy-done.3
  11.3 31.3 %shard_map.104 = (s32[1136]{0:T(1024)S(1)}, s32[1136]{0:T(1024)S(1)}, s32[18]{0:T(128)S(1)}, bf16[128,128,32]{2,1,0:T(8,128)(2,1)S(1)}) custom-call(s32[8,128]{1,0:T(8,128)S(1)} %bitcast.20, s32[1,128]{1,0:T(1,128)S(1)} %copy-done.3, s32[1]{0:T(128)} %bitcast.2.tile_ref, bf16[3,128,128]{2,1,0:T(8,128)(2,1)S(1)} %bitcast.19), custom_call_target="tpu_custom_call" | custom-call | flops 1000000 | bytes 5000000 | tf_op jit(solution)/shard_map/pallas_call | solution.py:102
  42.6 0.0 copy-start.5
  42.6 2.0 %copy-done.5 = bf16[128,128,32]{2,1,0:T(8,128)(2,1)} copy-done((bf16[128,128,32]{2,1,0:T(8,128)(2,1)}, bf16[128,128,32]{2,1,0:T(8,128)(2,1)S(1)}, u32[]{:S(2)}) %copy-start.5) | copy-done | bytes 1048600
  44.6 0.7 broadcast_subtract_fusion.brick_ref
  45.3 49.0 %all-gather.3.cloned.1.call-done = bf16[22528,128]{1,0:T(8,128)(2,1)} async-done(((bf16[1408,128]{1,0:T(8,128)(2,1)}), bf16[22528,128]{1,0:T(8,128)(2,1)}) %all-gather.3.cloned.1.call-update) | async-done | bytes 5767184 | tf_op jit(solution)/shard_map/all_gather | solution.py:277
  94.3 0.0 copy-start.4
  94.3 2.6 %copy-done.4 = bf16[22528,128]{1,0:T(8,128)(2,1)S(1)} copy-done((bf16[22528,128]{1,0:T(8,128)(2,1)S(1)}, bf16[22528,128]{1,0:T(8,128)(2,1)}, u32[]{:S(2)}) %copy-start.4) | copy-done | bytes 5767192
  96.9 0.0 copy-start.6
  96.9 2.2 %copy-done.6 = bf16[128,128,32]{2,1,0:T(8,128)(2,1)S(1)} copy-done((bf16[128,128,32]{2,1,0:T(8,128)(2,1)S(1)}, bf16[128,128,32]{2,1,0:T(8,128)(2,1)}, u32[]{:S(2)}) %copy-start.6) | copy-done | bytes 1048600
  99.1 0.0 copy-start.7
  99.1 0.9 copy-done.7
  100.0 0.0 copy-start.8
  100.0 0.8 copy-done.8
  100.9 0.0 copy-start.9
  100.9 0.8 copy-done.9
  101.7 36.0 %shard_map.105 = (f32[128,128]{1,0:T(8,128)}, f32[96,128]{1,0:T(8,128)S(1)}) custom-call(s32[18]{0:T(128)S(1)} %get-tuple-element.8.meta, s32[1136]{0:T(1024)S(1)} %get-tuple-element.9.r_s, s32[1136]{0:T(1024)S(1)} %get-tuple-element.10.q_s, bf16[128,128,32]{2,1,0:T(8,128)(2,1)S(1)} %copy-done.6, bf16[16,1408,128]{2,1,0:T(8,128)(2,1)S(1)} %bitcast.21, ...), custom_call_target="tpu_custom_call" | custom-call | flops 5368709120 | bytes 12582912 | tf_op jit(solution)/shard_map/pallas_call | solution.py:234
  137.7 3.0 %collective-permute-start = (f32[32,128]{1,0:T(8,128)S(1)}, f32[32,128]{1,0:T(8,128)S(1)}, u32[]{:S(2)}, u32[]{:S(2)}) collective-permute-start(f32[32,128]{1,0:T(8,128)S(1)} %get-tuple-element.16), channel_id=1, source_target_pairs={{0,1},{1,2},{2,3},{3,4},{4,5},{5,6},{6,7},{7,8},{8,9},{9,10},{10,1... | collective-permute-start | bytes 49160 | tf_op jit(solution)/shard_map/ppermute | solution.py:257
  140.7 1.3 collective-permute-start.1
  142.0 0.0 collective-permute-done
  142.0 5.0 %collective-permute-done.1 = f32[32,128]{1,0:T(8,128)S(1)} collective-permute-done((f32[32,128]{1,0:T(8,128)S(1)}, f32[32,128]{1,0:T(8,128)S(1)}, u32[]{:S(2)}, u32[]{:S(2)}) %collective-permute-start.1) | collective-permute-done | bytes 16416 | tf_op jit(solution)/shard_map/ppermute | solution.py:257
  147.0 9.5 %collective-permute-start.2 = (f32[1,128]{1,0:T(1,128)S(1)}, f32[1,128]{1,0:T(1,128)S(1)}, u32[]{:S(2)}, u32[]{:S(2)}) collective-permute-start(f32[1,128]{1,0:T(1,128)S(1)} %get-tuple-element.18), channel_id=1, source_target_pairs={{0,16},{16,32},{32,48},{48,64},{64,80},{80,96},{96,112},{112,128},... | collective-permute-start | bytes 1544 | tf_op jit(solution)/shard_map/ppermute | solution.py:257
  156.5 1.9 %collective-permute-start.3 = (f32[1,128]{1,0:T(1,128)S(1)}, f32[1,128]{1,0:T(1,128)S(1)}, u32[]{:S(2)}, u32[]{:S(2)}) collective-permute-start(f32[1,128]{1,0:T(1,128)S(1)} %get-tuple-element.19), channel_id=1, source_target_pairs={{16,0},{32,16},{48,32},{64,48},{80,64},{96,80},{112,96},{128,112},... | collective-permute-start | bytes 1544 | tf_op jit(solution)/shard_map/ppermute | solution.py:257
  158.4 0.0 collective-permute-done.2
  158.5 2.9 %collective-permute-done.3 = f32[1,128]{1,0:T(1,128)S(1)} collective-permute-done((f32[1,128]{1,0:T(1,128)S(1)}, f32[1,128]{1,0:T(1,128)S(1)}, u32[]{:S(2)}, u32[]{:S(2)}) %collective-permute-start.3) | collective-permute-done | bytes 544 | tf_op jit(solution)/shard_map/ppermute | solution.py:257
  161.4 0.0 copy-done
  161.4 0.8 convolution_add_fusion
  (3 shorter events, 0.0 us)
Async XLA Ops:
  7.2 154.2 %copy-start = (f32[128,128]{1,0:T(8,128)S(1)}, f32[128,128]{1,0:T(8,128)}, u32[]{:S(2)}) copy-start(f32[128,128]{1,0:T(8,128)} %param.17) | copy-start | bytes 196612
  7.2 87.1 %all-gather.3.cloned.1.call-start = ((), (), s32[]{:S(2)}) async-start(), calls=%async_computation | async-start | bytes 6127616 | tf_op jit(solution)/shard_map/all_gather | solution.py:277
  9.0 0.9 copy-start.1
  9.9 0.7 copy-start.2
  10.6 0.7 copy-start.3
  42.6 2.0 %copy-start.5 = (bf16[128,128,32]{2,1,0:T(8,128)(2,1)}, bf16[128,128,32]{2,1,0:T(8,128)(2,1)S(1)}, u32[]{:S(2)}) copy-start(bf16[128,128,32]{2,1,0:T(8,128)(2,1)S(1)} %get-tuple-element.11.x_ref) | copy-start | bytes 3145732
  94.3 2.6 %copy-start.4 = (bf16[22528,128]{1,0:T(8,128)(2,1)S(1)}, bf16[22528,128]{1,0:T(8,128)(2,1)}, u32[]{:S(2)}) copy-start(bf16[22528,128]{1,0:T(8,128)(2,1)} %all-gather.3.cloned.1.call-done) | copy-start | bytes 17301508
  96.9 2.2 %copy-start.6 = (bf16[128,128,32]{2,1,0:T(8,128)(2,1)S(1)}, bf16[128,128,32]{2,1,0:T(8,128)(2,1)}, u32[]{:S(2)}) copy-start(bf16[128,128,32]{2,1,0:T(8,128)(2,1)} %copy-done.5) | copy-start | bytes 3145732
  99.1 0.9 copy-start.7
  100.0 0.8 copy-start.8
  100.9 0.8 copy-start.9
  137.7 4.3 %collective-permute-start = (f32[32,128]{1,0:T(8,128)S(1)}, f32[32,128]{1,0:T(8,128)S(1)}, u32[]{:S(2)}, u32[]{:S(2)}) collective-permute-start(f32[32,128]{1,0:T(8,128)S(1)} %get-tuple-element.16), channel_id=1, source_target_pairs={{0,1},{1,2},{2,3},{3,4},{4,5},{5,6},{6,7},{7,8},{8,9},{9,10},{10,1... | collective-permute-start | bytes 49160 | tf_op jit(solution)/shard_map/ppermute | solution.py:257
  140.7 6.3 %collective-permute-start.1 = (f32[32,128]{1,0:T(8,128)S(1)}, f32[32,128]{1,0:T(8,128)S(1)}, u32[]{:S(2)}, u32[]{:S(2)}) collective-permute-start(f32[32,128]{1,0:T(8,128)S(1)} %get-tuple-element.17), channel_id=1, source_target_pairs={{1,0},{2,1},{3,2},{4,3},{5,4},{6,5},{7,6},{8,7},{9,8},{10,9},{11,1... | collective-permute-start | bytes 49160 | tf_op jit(solution)/shard_map/ppermute | solution.py:257
  147.0 11.5 %collective-permute-start.2 = (f32[1,128]{1,0:T(1,128)S(1)}, f32[1,128]{1,0:T(1,128)S(1)}, u32[]{:S(2)}, u32[]{:S(2)}) collective-permute-start(f32[1,128]{1,0:T(1,128)S(1)} %get-tuple-element.18), channel_id=1, source_target_pairs={{0,16},{16,32},{32,48},{48,64},{64,80},{80,96},{96,112},{112,128},... | collective-permute-start | bytes 1544 | tf_op jit(solution)/shard_map/ppermute | solution.py:257
  156.5 4.9 %collective-permute-start.3 = (f32[1,128]{1,0:T(1,128)S(1)}, f32[1,128]{1,0:T(1,128)S(1)}, u32[]{:S(2)}, u32[]{:S(2)}) collective-permute-start(f32[1,128]{1,0:T(1,128)S(1)} %get-tuple-element.19), channel_id=1, source_target_pairs={{16,0},{32,16},{48,32},{64,48},{80,64},{96,80},{112,96},{128,112},... | collective-permute-start | bytes 1544 | tf_op jit(solution)/shard_map/ppermute | solution.py:257
Sparse Core Ops, SparseCore 0:
  10.1 84.1 all-gather.2

commit v2 on v1

v2 whole, which is shorter than its diff:
```python
import functools
import math

import jax
import jax.numpy as jnp
from jax import lax
from jax.experimental import pallas as pl
from jax.experimental.pallas import tpu as pltpu
from jax.sharding import PartitionSpec as P

PTS = 128
COLS = 8
PAIRS = 8
CL = 128
BR_DEV = 32
N_TILE = 16
SHARP = 12.0
SOFTEN = 2.0
SCALE = SHARP * math.log2(math.e)

UNITS = 8
STEP = 2 * UNITS
ROUNDS = N_TILE // 2 + 1
REGION = CL * PAIRS
YDIM = 8
KDIM = 2 * YDIM
HIST_ROWS = CL * COLS
ACC_ROWS = (CL + 1) * 2 * COLS
SMEM = pl.BlockSpec(memory_space=pltpu.SMEM)
VMEM = pl.BlockSpec(memory_space=pltpu.VMEM)


def split2(x):
    hi = x.astype(jnp.bfloat16).astype(jnp.float32)
    return hi, x - hi


def split3(x):
    hi, rest = split2(x)
    return (hi,) + split2(rest)


def reader_rows(here_ref, rows_ref, x_ref):
    here = [here_ref[k].astype(jnp.float32) for k in range(3)]
    twice = [split2((2.0 * SCALE) * h) for h in here]
    norm = split2(-SCALE * (here[0] * here[0] + here[1] * here[1] + here[2] * here[2]))
    one = jnp.ones((CL, PTS), jnp.float32)
    none = jnp.zeros((CL, PTS), jnp.float32)
    rows = [twice[k][0] for k in range(3)] + [one] * 3 + [norm[0], none]
    rows += [twice[k][1] for k in range(3)] + [none] * 3 + [norm[1], none]
    for k, row in enumerate(rows):
        rows_ref[pl.ds(k, CL, stride=KDIM), :] = row

    def turn(g, carry):
        four = [
            rows_ref[pl.ds(pl.multiple_of((g * 4 + m) * KDIM, KDIM), KDIM), :] for m in range(4)
        ]
        turned = jnp.concatenate([f for f in four for _ in range(2)], axis=0).T
        turned = turned.astype(jnp.bfloat16)
        for m in range(4):
            x_ref[g * 4 + m] = turned[:, m * 2 * KDIM : (m + 1) * 2 * KDIM]
        return carry

    lax.fori_loop(0, CL // 4, turn, 0)


def setup_kernel(ids_ref, cnt_ref, tile_ref, here_ref, list_ref, steps_ref, x_ref, cur_ref, rows_ref):
    reader_rows(here_ref, rows_ref, x_ref)
    tile = tile_ref[0]
    for k in range(ROUNDS + 1):
        cur_ref[k] = k * REGION

    def reader(r, carry):
        count = cnt_ref[0, r]
        for p in range(PAIRS):
            q = ids_ref[p, r]
            d = ((q >> 7) - tile) & (N_TILE - 1)
            near = jnp.minimum(d, N_TILE - d)
            k = jnp.where(p < count, near, ROUNDS)
            slot = jnp.where(d == near, CL, 0)
            at = cur_ref[k]
            list_ref[at] = (r << 8) | slot | (q & (CL - 1))
            cur_ref[k] = at + 1
        return carry

    lax.fori_loop(0, CL, reader, 0)
    for k in range(ROUNDS):
        used = cur_ref[k]
        steps = (used - k * REGION + (STEP - 1)) >> 4
        steps_ref[k] = steps

        def pad(at, carry):
            list_ref[at] = (CL << 8) | CL
            return carry

        lax.fori_loop(used, k * REGION + steps * STEP, pad, 0)


def setup(ids, counts, tile, here):
    return pl.pallas_call(
        setup_kernel,
        out_shape=[
            jax.ShapeDtypeStruct(((ROUNDS + 1) * REGION,), jnp.int32),
            jax.ShapeDtypeStruct((ROUNDS,), jnp.int32),
            jax.ShapeDtypeStruct((CL, PTS, 2 * KDIM), jnp.bfloat16),
        ],
        in_specs=[SMEM] * 3 + [VMEM],
        out_specs=[SMEM] * 2 + [VMEM],
        scratch_shapes=[
            pltpu.SMEM((ROUNDS + 1,), jnp.int32),
            pltpu.VMEM((CL * KDIM, PTS), jnp.float32),
        ],
        compiler_params=pltpu.CompilerParams(vmem_limit_bytes=16 * 2**20),
        cost_estimate=pl.CostEstimate(flops=10**6, bytes_accessed=10**7, transcendentals=0),
    )(ids, counts, tile, here)


def prepare(slot, parts, hist_ref, y_ref):
    base = slot * HIST_ROWS
    at = 0
    spots = []
    for part in parts:
        rows = part.shape[0]
        take = min(rows, HIST_ROWS - at)
        if take > 0:
            hist_ref[base + at : base + at + take] = part[:take].astype(jnp.float32)
            at += take
        for k in range(max(take, 0), rows, CL):
            spots.append(part[k : k + CL].astype(jnp.float32))
    norm = spots[0] * spots[0] + spots[1] * spots[1] + spots[2] * spots[2]
    one = jnp.ones((CL, PTS), jnp.float32)
    rows = spots + list(split3(-SCALE * norm)) + [one, 0.0 * one]
    for k, row in enumerate(rows):
        y_ref[pl.ds(base + k, CL, stride=YDIM), :] = row


def pairs(base, steps, list_s, x_ref, hist_ref, y_ref, acc_ref):
    first = lax.broadcasted_iota(jnp.int32, (PTS, 2 * KDIM), 1) < KDIM
    zero_y = jnp.zeros((KDIM, PTS), jnp.float32)
    zero_h = jnp.zeros((COLS, PTS), jnp.float32)
    row = lax.broadcasted_iota(jnp.int32, (2 * COLS, 2 * PTS), 0) >> 3
    side = lax.broadcasted_iota(jnp.int32, (2 * COLS, 2 * PTS), 1) >> 7
    ones = (row == side).astype(jnp.float32).astype(jnp.bfloat16)

    def beside(one, other, zero):
        top = jnp.concatenate([one, zero], axis=1)
        bottom = jnp.concatenate([zero, other], axis=1)
        return jnp.concatenate([top, bottom], axis=0).astype(jnp.bfloat16)

    def eight(ref, k):
        return ref[pl.ds(pl.multiple_of(k * 8, 8), 8), :]

    def step(i, carry):
        entries = [list_s[base + i * STEP + k] for k in range(STEP)]
        readers = [e >> 8 for e in entries]
        sources = [e & (2 * CL - 1) for e in entries]
        units = [(2 * u, 2 * u + 1) for u in range(UNITS)]
        weights = []
        for a, b in units:
            lhs = jnp.where(first, x_ref[readers[a] & (CL - 1)], x_ref[readers[b] & (CL - 1)])
            ys = [eight(y_ref, sources[k]) for k in (a, b)]
            rhs = beside(*[jnp.concatenate([y, y], axis=0) for y in ys], zero_y)
            power = jnp.dot(lhs, rhs, preferred_element_type=jnp.float32)
            weights.append(jnp.exp2(power).astype(jnp.bfloat16))
        outs = []
        for (a, b), weight in zip(units, weights):
            hs = [eight(hist_ref, sources[k]) for k in (a, b)]
            both = jnp.concatenate([beside(*hs, zero_h), ones], axis=0)
            outs.append(
                lax.dot_general(
                    both, weight, (((1,), (1,)), ((), ())), preferred_element_type=jnp.float32
                )
            )
        for unit, out in zip(units, outs):
            for half in range(2):
                at = pl.multiple_of(readers[unit[half]] * (2 * COLS), 2 * COLS)
                acc_ref[pl.ds(at, COLS), :] += out[half * COLS : (half + 1) * COLS]
                acc_ref[pl.ds(at + COLS, COLS), :] += out[(2 + half) * COLS : (3 + half) * COLS]
        return carry

    lax.fori_loop(0, steps, step, 0)


def finish(acc_ref, kappa_ref, threshold_ref, disp_ref, brick_ref, damage_ref, shares_ref):
    inverse = 1.0 / acc_ref[pl.ds(COLS, CL, stride=2 * COLS), :]
    threshold = threshold_ref[...]
    strain = acc_ref[pl.ds(0, CL, stride=2 * COLS), :] * inverse
    kappa = jnp.maximum(jnp.maximum(kappa_ref[...], strain), threshold)
    damage = 1.0 - (threshold / kappa) * jnp.exp(-(kappa - threshold) / SOFTEN)
    damage_ref[...] = damage
    left = 1.0 - damage
    term = jnp.zeros((CL, PTS), jnp.float32)
    for c in range(COLS):
        mean = acc_ref[pl.ds(c, CL, stride=2 * COLS), :] * inverse
        term = term + jnp.dot(
            (left * mean).astype(jnp.bfloat16),
            disp_ref[c * PTS : (c + 1) * PTS, :],
            preferred_element_type=jnp.float32,
        )
    rows = lax.broadcasted_iota(jnp.int32, (3 * BR_DEV, CL), 0)
    onehot = (rows == brick_ref[...]).astype(jnp.float32)
    shares_ref[...] = jnp.dot(
        onehot, term, precision=lax.Precision.HIGHEST, preferred_element_type=jnp.float32
    )


def ring_kernel(round_, sizes, has_acc, final, *refs):
    refs = list(refs)
    take = lambda n: [refs.pop(0) for _ in range(n)]
    steps_s, list_s, x_ref = take(3)
    blocks = [take(n) for n in sizes]
    acc_in = take(1)[0] if has_acc else None
    final_in = take(4) if final else None
    final_out = take(2) if final else None
    acc_ref, hist_ref, y_ref = take(3)
    acc_ref[...] = acc_in[...] if has_acc else jnp.zeros_like(acc_ref)
    for slot, parts in enumerate(blocks):
        prepare(slot if len(blocks) == 2 else 1, parts, hist_ref, y_ref)
    pairs(round_ * REGION, steps_s[round_], list_s, x_ref, hist_ref, y_ref, acc_ref)
    if final:
        finish(acc_ref, *final_in, *final_out)


def consume(prepared, round_, blocks, acc, final=None):
    lists, steps, x_rows = prepared
    args = [steps, lists, x_rows] + [part for parts in blocks for part in parts]
    if acc is not None:
        args.append(acc)
    acc_shape = (ACC_ROWS, PTS)
    scratch = [
        pltpu.VMEM((2 * HIST_ROWS, PTS), jnp.float32),
        pltpu.VMEM((2 * CL * YDIM, PTS), jnp.float32),
    ]
    if final is None:
        out_shape = jax.ShapeDtypeStruct(acc_shape, jnp.float32)
        out_specs = VMEM
    else:
        args += list(final)
        out_shape = [
            jax.ShapeDtypeStruct((CL, PTS), jnp.float32),
            jax.ShapeDtypeStruct((3 * BR_DEV, PTS), jnp.float32),
        ]
        out_specs = [VMEM] * 2
        scratch = [pltpu.VMEM(acc_shape, jnp.float32)] + scratch
    sizes = tuple(len(parts) for parts in blocks)
    return pl.pallas_call(
        functools.partial(ring_kernel, round_, sizes, acc is not None, final is not None),
        out_shape=out_shape,
        in_specs=[SMEM] * 2 + [VMEM] * (len(args) - 2),
        out_specs=out_specs,
        scratch_shapes=scratch,
        compiler_params=pltpu.CompilerParams(vmem_limit_bytes=16 * 2**20),
        cost_estimate=pl.CostEstimate(
            flops=2 * 40 * PTS * 256 * 256, bytes_accessed=8 * 2**20, transcendentals=10**6
        ),
    )(*args)


def hop(block, distance):
    peers = lax.axis_size("tile")
    return lax.ppermute(block, "tile", [(i, (i + distance) % peers) for i in range(peers)])


def shifted(block, axis, distance):
    devices = range(lax.axis_size(axis))
    route = [(i - distance, i) for i in devices if i - distance in devices]
    return lax.ppermute(block, axis, route)


def local(
    history,
    positions,
    kappa_old,
    threshold,
    pair_ids,
    reader_counts,
    brick_map,
    strain_disp,
    couple,
):
    points = positions[0].transpose(1, 0, 2)
    own = jnp.concatenate(
        [history[0].reshape(HIST_ROWS, PTS), points.reshape(3 * CL, PTS)], axis=0
    )
    tile = lax.axis_index("tile")
    half = own.shape[0] // 2
    up, down = hop(own, 1), hop(own, -1)
    prepared = setup(pair_ids[0].T, reader_counts, tile.astype(jnp.int32).reshape(1), points)
    acc = consume(prepared, 0, [[own]], None)
    for s in range(1, N_TILE // 2):
        up, down, acc = lax.optimization_barrier((up, down, acc))
        block = [[up], [down]]
        if s + 1 < N_TILE // 2:
            up, down = hop(up, 1), hop(down, -1)
        else:
            far = [hop(up[:half], 1), hop(down[half:], -1)]
        acc = consume(prepared, s, block, acc)
    brick = brick_map - (tile - 1) * BR_DEV
    damage_here, shares = consume(
        prepared, N_TILE // 2, [far], acc, (kappa_old[0], threshold[0], strain_disp, brick)
    )
    low, mid, top = shares[:BR_DEV], shares[BR_DEV : 2 * BR_DEV], shares[2 * BR_DEV :]
    force = mid + shifted(top, "tile", 1) + shifted(low, "tile", -1)
    before = shifted(force[-1:], "slab", 1)
    after = shifted(force[:1], "slab", -1)
    padded = jnp.concatenate([before, force, after], axis=0)
    residual_here = force + jnp.dot(
        padded[:-2] + padded[2:],
        couple,
        precision=lax.Precision.HIGHEST,
        preferred_element_type=jnp.float32,
    )
    return (damage_here[None], residual_here[:, None, :])


def solution(mesh):
    placed = (
        P("slab", "tile", None, None),
        P("slab", "tile", None, None),
        P("slab", "tile", None),
        P("slab", "tile", None),
        P("slab", "tile", None),
        P("slab", "tile"),
        P("slab", "tile"),
        P(),
        P(),
    )
    return jax.shard_map(
        local,
        mesh=mesh,
        in_specs=placed,
        out_specs=(P("slab", "tile", None), P("slab", "tile", None)),
        check_vma=False,
    )
```

time: 169 us -> 155 us (0.917)
  the two profiles are of different devices: /device:TPU:1 before, /device:TPU:7 now
where the time goes in v2:
time: 155 us; the launch traced here: 154 us
  starting transfers between devices  81.8 us (53%)
  Pallas kernels  46.6 us (30%)
  waiting for transfers between devices  18.3 us (12%)
  local copies, waits for them, and re-layouts  4.48 us (3%)
    ppermute x16, starting transfers between devices, hop(): lax.ppermute(block, 'tile', [(i, (i + distance) % peers) for i in range(p...  61.3 us
    pallas_call x9, Pallas kernels, consume(): pl.pallas_call(functools.partial(ring_kernel, round_, sizes, acc is not N...  30 us
    ppermute x4, starting transfers between devices, shifted(): return lax.ppermute(block, axis, route)  20.5 us
    pallas_call x1, Pallas kernels, setup(): pl.pallas_call(setup_kernel, out_shape=[jax.ShapeDtypeStruct(((ROUNDS + 1...  16.7 us
    ppermute x16, waiting for transfers between devices, hop(): lax.ppermute(block, 'tile', [(i, (i + distance) % peers) for i in range(p...  10.1 us
    ppermute x4, waiting for transfers between devices, shifted(): return lax.ppermute(block, axis, route)  8.22 us
    unnamed x20, local copies, waits for them, and re-layouts  4.45 us
  transfers between devices with their start and end apart: 20, of which 12 were waited for; matrix products, arithmetic and copies ran while one was open for 0% of the time, Pallas kernels for 28%

profile of v2, /device:TPU:7, one launch (start us, length us, event | category | flops | bytes accessed | tf_op | source)
XLA Modules:
  0.0 154.1 jit_solution(16324291227533012513)
XLA Ops:
  0.6 0.0 copy-start
  0.6 1.1 pad_maximum_fusion.refs_3_
  1.7 11.1 %collective-permute-start.1 = (bf16[1408,128]{1,0:T(8,128)(2,1)S(1)}, bf16[1408,128]{1,0:T(8,128)(2,1)S(1)}, u32[]{:S(2)}, u32[]{:S(2)}) collective-permute-start(bf16[1408,128]{1,0:T(8,128)(2,1)S(1)} %pad_maximum_fusion.refs_3_), channel_id=1, source_target_pairs={{0,15},{1,0},{2,1},{3,2},{4,3},{5,4},{6,5},{7,6},{8,7},{9,8},{10,9... | collective-permute-start | bytes 1081352 | tf_op jit(solution)/shard_map/ppermute | solution.py:261
  12.8 1.9 %collective-permute-start = (bf16[1408,128]{1,0:T(8,128)(2,1)S(1)}, bf16[1408,128]{1,0:T(8,128)(2,1)S(1)}, u32[]{:S(2)}, u32[]{:S(2)}) collective-permute-start(bf16[1408,128]{1,0:T(8,128)(2,1)S(1)} %pad_maximum_fusion.refs_3_), channel_id=1, source_target_pairs={{0,1},{1,2},{2,3},{3,4},{4,5},{5,6},{6,7},{7,8},{8,9},{9,10},{10,1... | collective-permute-start | bytes 1081352 | tf_op jit(solution)/shard_map/ppermute | solution.py:261
  14.8 0.0 copy-start.3
  14.8 0.9 copy-done.3
  15.7 0.7 copy-done.7
  16.4 0.7 copy-done.8
  17.0 16.7 %shard_map.104 = (s32[10240]{0:T(1024)S(1)}, s32[9]{0:T(128)S(1)}, bf16[128,128,32]{2,1,0:T(8,128)(2,1)S(1)}) custom-call(s32[8,128]{1,0:T(8,128)S(1)} %bitcast.21, s32[1,128]{1,0:T(1,128)S(1)} %copy-done.8, s32[1]{0:T(128)} %bitcast.2.tile_ref, bf16[3,128,128]{2,1,0:T(8,128)(2,1)S(1)} %bitcast.18), custom_call_target="tpu_custom_call" | custom-call | flops 1000000 | bytes 10000000 | tf_op jit(solution)/shard_map/pallas_call | solution.py:100
  33.7 5.8 %shard_map.105.refs_5_ = f32[2064,128]{1,0:T(8,128)S(1)} custom-call(s32[9]{0:T(128)S(1)} %get-tuple-element.28.refs_0_, s32[10240]{0:T(1024)S(1)} %get-tuple-element.29.refs_1_, bf16[128,128,32]{2,1,0:T(8,128)(2,1)S(1)} %get-tuple-element.30.refs_2_, bf16[1408,128]{1,0:T(8,128)(2,1)S(1)} %pad_maximum_fusion.refs_3_), custom_call_target="tpu_custom_call" | custom-call | flops 671088640 | bytes 8388608 | tf_op jit(solution)/shard_map/pallas_call | solution.py:246
  39.5 0.0 collective-permute-done.1.refs_4_
  39.5 0.0 collective-permute-done.refs_3_
  39.5 1.9 %collective-permute-start.2 = (bf16[1408,128]{1,0:T(8,128)(2,1)S(1)}, bf16[1408,128]{1,0:T(8,128)(2,1)S(1)}, u32[]{:S(2)}, u32[]{:S(2)}) collective-permute-start(bf16[1408,128]{1,0:T(8,128)(2,1)S(1)} %collective-permute-done.refs_3_), channel_id=1, source_target_pairs={{0,1},{1,2},{2,3},{3,4},{4,5},{5,6},{6,7},{7,8},{8,9},{9,10},{10,1... | collective-permute-start | bytes 1081352 | tf_op jit(solution)/shard_map/ppermute | solution.py:261
  41.4 4.7 %collective-permute-start.3 = (bf16[1408,128]{1,0:T(8,128)(2,1)S(1)}, bf16[1408,128]{1,0:T(8,128)(2,1)S(1)}, u32[]{:S(2)}, u32[]{:S(2)}) collective-permute-start(bf16[1408,128]{1,0:T(8,128)(2,1)S(1)} %collective-permute-done.1.refs_4_), channel_id=1, source_target_pairs={{0,15},{1,0},{2,1},{3,2},{4,3},{5,4},{6,5},{7,6},{8,7},{9,8},{10,9... | collective-permute-start | bytes 1081352 | tf_op jit(solution)/shard_map/ppermute | solution.py:261
  46.2 2.9 %shard_map.106.refs_5_ = f32[2064,128]{1,0:T(8,128)S(1)} custom-call(s32[9]{0:T(128)S(1)} %get-tuple-element.28.refs_0_, s32[10240]{0:T(1024)S(1)} %get-tuple-element.29.refs_1_, bf16[128,128,32]{2,1,0:T(8,128)(2,1)S(1)} %get-tuple-element.30.refs_2_, bf16[1408,128]{1,0:T(8,128)(2,1)S(1)} %collective-permute-done.refs_3_, ...), custom_call_target="tpu_custom_call" | custom-call | flops 671088640 | bytes 8388608 | tf_op jit(solution)/shard_map/pallas_call | solution.py:246
  49.1 2.2 %collective-permute-done.2.refs_3_ = bf16[1408,128]{1,0:T(8,128)(2,1)S(1)} collective-permute-done((bf16[1408,128]{1,0:T(8,128)(2,1)S(1)}, bf16[1408,128]{1,0:T(8,128)(2,1)S(1)}, u32[]{:S(2)}, u32[]{:S(2)}) %collective-permute-start.2) | collective-permute-done | bytes 360480 | tf_op jit(solution)/shard_map/ppermute | solution.py:261
  51.2 0.9 collective-permute-done.3.refs_4_
  52.1 1.9 %collective-permute-start.4 = (bf16[1408,128]{1,0:T(8,128)(2,1)S(1)}, bf16[1408,128]{1,0:T(8,128)(2,1)S(1)}, u32[]{:S(2)}, u32[]{:S(2)}) collective-permute-start(bf16[1408,128]{1,0:T(8,128)(2,1)S(1)} %collective-permute-done.2.refs_3_), channel_id=1, source_target_pairs={{0,1},{1,2},{2,3},{3,4},{4,5},{5,6},{6,7},{7,8},{8,9},{9,10},{10,1... | collective-permute-start | bytes 1081352 | tf_op jit(solution)/shard_map/ppermute | solution.py:261
  54.1 5.3 %collective-permute-start.5 = (bf16[1408,128]{1,0:T(8,128)(2,1)S(1)}, bf16[1408,128]{1,0:T(8,128)(2,1)S(1)}, u32[]{:S(2)}, u32[]{:S(2)}) collective-permute-start(bf16[1408,128]{1,0:T(8,128)(2,1)S(1)} %collective-permute-done.3.refs_4_), channel_id=1, source_target_pairs={{0,15},{1,0},{2,1},{3,2},{4,3},{5,4},{6,5},{7,6},{8,7},{9,8},{10,9... | collective-permute-start | bytes 1081352 | tf_op jit(solution)/shard_map/ppermute | solution.py:261
  59.4 3.3 %shard_map.107.refs_5_ = f32[2064,128]{1,0:T(8,128)S(1)} custom-call(s32[9]{0:T(128)S(1)} %get-tuple-element.28.refs_0_, s32[10240]{0:T(1024)S(1)} %get-tuple-element.29.refs_1_, bf16[128,128,32]{2,1,0:T(8,128)(2,1)S(1)} %get-tuple-element.30.refs_2_, bf16[1408,128]{1,0:T(8,128)(2,1)S(1)} %collective-permute-done.2.refs_3_, ...), custom_call_target="tpu_custom_call" | custom-call | flops 671088640 | bytes 8388608 | tf_op jit(solution)/shard_map/pallas_call | solution.py:246
  62.7 0.8 collective-permute-done.4.refs_3_
  63.5 0.9 collective-permute-done.5.refs_4_
  64.4 1.9 %collective-permute-start.6 = (bf16[1408,128]{1,0:T(8,128)(2,1)S(1)}, bf16[1408,128]{1,0:T(8,128)(2,1)S(1)}, u32[]{:S(2)}, u32[]{:S(2)}) collective-permute-start(bf16[1408,128]{1,0:T(8,128)(2,1)S(1)} %collective-permute-done.4.refs_3_), channel_id=1, source_target_pairs={{0,1},{1,2},{2,3},{3,4},{4,5},{5,6},{6,7},{7,8},{8,9},{9,10},{10,1... | collective-permute-start | bytes 1081352 | tf_op jit(solution)/shard_map/ppermute | solution.py:261
  66.3 5.3 %collective-permute-start.7 = (bf16[1408,128]{1,0:T(8,128)(2,1)S(1)}, bf16[1408,128]{1,0:T(8,128)(2,1)S(1)}, u32[]{:S(2)}, u32[]{:S(2)}) collective-permute-start(bf16[1408,128]{1,0:T(8,128)(2,1)S(1)} %collective-permute-done.5.refs_4_), channel_id=1, source_target_pairs={{0,15},{1,0},{2,1},{3,2},{4,3},{5,4},{6,5},{7,6},{8,7},{9,8},{10,9... | collective-permute-start | bytes 1081352 | tf_op jit(solution)/shard_map/ppermute | solution.py:261
  71.7 2.9 %shard_map.108.refs_5_ = f32[2064,128]{1,0:T(8,128)S(1)} custom-call(s32[9]{0:T(128)S(1)} %get-tuple-element.28.refs_0_, s32[10240]{0:T(1024)S(1)} %get-tuple-element.29.refs_1_, bf16[128,128,32]{2,1,0:T(8,128)(2,1)S(1)} %get-tuple-element.30.refs_2_, bf16[1408,128]{1,0:T(8,128)(2,1)S(1)} %collective-permute-done.4.refs_3_, ...), custom_call_target="tpu_custom_call" | custom-call | flops 671088640 | bytes 8388608 | tf_op jit(solution)/shard_map/pallas_call | solution.py:246
  74.6 0.3 collective-permute-done.6.refs_3_
  74.9 1.1 collective-permute-done.7.refs_4_
  76.0 2.2 %collective-permute-start.8 = (bf16[1408,128]{1,0:T(8,128)(2,1)S(1)}, bf16[1408,128]{1,0:T(8,128)(2,1)S(1)}, u32[]{:S(2)}, u32[]{:S(2)}) collective-permute-start(bf16[1408,128]{1,0:T(8,128)(2,1)S(1)} %collective-permute-done.6.refs_3_), channel_id=1, source_target_pairs={{0,1},{1,2},{2,3},{3,4},{4,5},{5,6},{6,7},{7,8},{8,9},{9,10},{10,1... | collective-permute-start | bytes 1081352 | tf_op jit(solution)/shard_map/ppermute | solution.py:261
  78.3 4.7 %collective-permute-start.9 = (bf16[1408,128]{1,0:T(8,128)(2,1)S(1)}, bf16[1408,128]{1,0:T(8,128)(2,1)S(1)}, u32[]{:S(2)}, u32[]{:S(2)}) collective-permute-start(bf16[1408,128]{1,0:T(8,128)(2,1)S(1)} %collective-permute-done.7.refs_4_), channel_id=1, source_target_pairs={{0,15},{1,0},{2,1},{3,2},{4,3},{5,4},{6,5},{7,6},{8,7},{9,8},{10,9... | collective-permute-start | bytes 1081352 | tf_op jit(solution)/shard_map/ppermute | solution.py:261
  83.0 3.3 %shard_map.109.refs_5_ = f32[2064,128]{1,0:T(8,128)S(1)} custom-call(s32[9]{0:T(128)S(1)} %get-tuple-element.28.refs_0_, s32[10240]{0:T(1024)S(1)} %get-tuple-element.29.refs_1_, bf16[128,128,32]{2,1,0:T(8,128)(2,1)S(1)} %get-tuple-element.30.refs_2_, bf16[1408,128]{1,0:T(8,128)(2,1)S(1)} %collective-permute-done.6.refs_3_, ...), custom_call_target="tpu_custom_call" | custom-call | flops 671088640 | bytes 8388608 | tf_op jit(solution)/shard_map/pallas_call | solution.py:246
  86.3 0.0 collective-permute-done.8.refs_3_
  86.3 1.0 collective-permute-done.9.refs_4_
  87.3 3.3 %collective-permute-start.10 = (bf16[1408,128]{1,0:T(8,128)(2,1)S(1)}, bf16[1408,128]{1,0:T(8,128)(2,1)S(1)}, u32[]{:S(2)}, u32[]{:S(2)}) collective-permute-start(bf16[1408,128]{1,0:T(8,128)(2,1)S(1)} %collective-permute-done.8.refs_3_), channel_id=1, source_target_pairs={{0,1},{1,2},{2,3},{3,4},{4,5},{5,6},{6,7},{7,8},{8,9},{9,10},{10,1... | collective-permute-start | bytes 1081352 | tf_op jit(solution)/shard_map/ppermute | solution.py:261
  90.6 3.7 %collective-permute-start.11 = (bf16[1408,128]{1,0:T(8,128)(2,1)S(1)}, bf16[1408,128]{1,0:T(8,128)(2,1)S(1)}, u32[]{:S(2)}, u32[]{:S(2)}) collective-permute-start(bf16[1408,128]{1,0:T(8,128)(2,1)S(1)} %collective-permute-done.9.refs_4_), channel_id=1, source_target_pairs={{0,15},{1,0},{2,1},{3,2},{4,3},{5,4},{6,5},{7,6},{8,7},{9,8},{10,9... | collective-permute-start | bytes 1081352 | tf_op jit(solution)/shard_map/ppermute | solution.py:261
  94.3 2.9 %shard_map.110.refs_5_ = f32[2064,128]{1,0:T(8,128)S(1)} custom-call(s32[9]{0:T(128)S(1)} %get-tuple-element.28.refs_0_, s32[10240]{0:T(1024)S(1)} %get-tuple-element.29.refs_1_, bf16[128,128,32]{2,1,0:T(8,128)(2,1)S(1)} %get-tuple-element.30.refs_2_, bf16[1408,128]{1,0:T(8,128)(2,1)S(1)} %collective-permute-done.8.refs_3_, ...), custom_call_target="tpu_custom_call" | custom-call | flops 671088640 | bytes 8388608 | tf_op jit(solution)/shard_map/pallas_call | solution.py:246
  97.2 0.0 collective-permute-done.10.refs_3_
  97.2 1.6 %collective-permute-done.11.refs_4_ = bf16[1408,128]{1,0:T(8,128)(2,1)S(1)} collective-permute-done((bf16[1408,128]{1,0:T(8,128)(2,1)S(1)}, bf16[1408,128]{1,0:T(8,128)(2,1)S(1)}, u32[]{:S(2)}, u32[]{:S(2)}) %collective-permute-start.11) | collective-permute-done | bytes 360480 | tf_op jit(solution)/shard_map/ppermute | solution.py:261
  98.8 4.6 %collective-permute-start.12 = (bf16[1408,128]{1,0:T(8,128)(2,1)S(1)}, bf16[1408,128]{1,0:T(8,128)(2,1)S(1)}, u32[]{:S(2)}, u32[]{:S(2)}) collective-permute-start(bf16[1408,128]{1,0:T(8,128)(2,1)S(1)} %collective-permute-done.10.refs_3_), channel_id=1, source_target_pairs={{0,1},{1,2},{2,3},{3,4},{4,5},{5,6},{6,7},{7,8},{8,9},{9,10},{10,1... | collective-permute-start | bytes 1081352 | tf_op jit(solution)/shard_map/ppermute | solution.py:261
  103.3 2.2 %collective-permute-start.13 = (bf16[1408,128]{1,0:T(8,128)(2,1)S(1)}, bf16[1408,128]{1,0:T(8,128)(2,1)S(1)}, u32[]{:S(2)}, u32[]{:S(2)}) collective-permute-start(bf16[1408,128]{1,0:T(8,128)(2,1)S(1)} %collective-permute-done.11.refs_4_), channel_id=1, source_target_pairs={{0,15},{1,0},{2,1},{3,2},{4,3},{5,4},{6,5},{7,6},{8,7},{9,8},{10,9... | collective-permute-start | bytes 1081352 | tf_op jit(solution)/shard_map/ppermute | solution.py:261
  105.6 0.0 copy-start.2
  105.6 2.2 %copy-done.2 = bf16[128,128,32]{2,1,0:T(8,128)(2,1)S(1)} copy-done((bf16[128,128,32]{2,1,0:T(8,128)(2,1)S(1)}, bf16[128,128,32]{2,1,0:T(8,128)(2,1)}, u32[]{:S(2)}) %copy-start.2) | copy-done | bytes 1048600
  107.8 2.9 %shard_map.111.refs_5_ = f32[2064,128]{1,0:T(8,128)S(1)} custom-call(s32[9]{0:T(128)S(1)} %get-tuple-element.28.refs_0_, s32[10240]{0:T(1024)S(1)} %get-tuple-element.29.refs_1_, bf16[128,128,32]{2,1,0:T(8,128)(2,1)S(1)} %copy-done.2, bf16[1408,128]{1,0:T(8,128)(2,1)S(1)} %collective-permute-done.10.refs_3_, ...), custom_call_target="tpu_custom_call" | custom-call | flops 671088640 | bytes 8388608 | tf_op jit(solution)/shard_map/pallas_call | solution.py:246
  110.7 0.0 collective-permute-done.12.refs_3_
  110.7 0.8 collective-permute-done.13.refs_4_
  111.6 3.7 %collective-permute-start.14 = (bf16[704,128]{1,0:T(8,128)(2,1)S(1)}, bf16[704,128]{1,0:T(8,128)(2,1)S(1)}, u32[]{:S(2)}, u32[]{:S(2)}) collective-permute-start(bf16[704,128]{1,0:T(8,128)(2,1)S(1)} %slice.29), channel_id=1, source_target_pairs={{0,1},{1,2},{2,3},{3,4},{4,5},{5,6},{6,7},{7,8},{8,9},{9,10},{10,1... | collective-permute-start | bytes 540680 | tf_op jit(solution)/shard_map/ppermute | solution.py:261
  115.2 2.8 %collective-permute-start.15 = (bf16[704,128]{1,0:T(8,128)(2,1)S(1)}, bf16[704,128]{1,0:T(8,128)(2,1)S(1)}, u32[]{:S(2)}, u32[]{:S(2)}) collective-permute-start(bf16[704,128]{1,0:T(8,128)(2,1)S(1)} %slice.30), channel_id=1, source_target_pairs={{0,15},{1,0},{2,1},{3,2},{4,3},{5,4},{6,5},{7,6},{8,7},{9,8},{10,9... | collective-permute-start | bytes 540680 | tf_op jit(solution)/shard_map/ppermute | solution.py:261
  118.1 0.0 copy-start.4
  118.1 0.0 copy-start.5
  118.1 0.0 copy-start.6
  118.1 2.9 %shard_map.112.refs_5_ = f32[2064,128]{1,0:T(8,128)S(1)} custom-call(s32[9]{0:T(128)S(1)} %get-tuple-element.28.refs_0_, s32[10240]{0:T(1024)S(1)} %get-tuple-element.29.refs_1_, bf16[128,128,32]{2,1,0:T(8,128)(2,1)S(1)} %copy-done.2, bf16[1408,128]{1,0:T(8,128)(2,1)S(1)} %collective-permute-done.12.refs_3_, ...), custom_call_target="tpu_custom_call" | custom-call | flops 671088640 | bytes 8388608 | tf_op jit(solution)/shard_map/pallas_call | solution.py:246
  121.0 0.0 collective-permute-done.14.refs_3_
  121.0 0.4 collective-permute-done.15.refs_4_
  121.5 0.0 copy-done.4
  121.5 0.0 copy-done.6
  121.5 3.0 %shard_map.113 = (f32[128,128]{1,0:T(8,128)}, f32[96,128]{1,0:T(8,128)S(1)}) custom-call(s32[9]{0:T(128)S(1)} %get-tuple-element.28.refs_0_, s32[10240]{0:T(1024)S(1)} %get-tuple-element.29.refs_1_, bf16[128,128,32]{2,1,0:T(8,128)(2,1)S(1)} %copy-done.2, bf16[704,128]{1,0:T(8,128)(2,1)S(1)} %collective-permute-done.14.refs_3_, ...), custom_call_target="tpu_custom_call" | custom-call | flops 671088640 | bytes 8388608 | tf_op jit(solution)/shard_map/pallas_call | solution.py:246
  124.5 3.0 %collective-permute-start.16 = (f32[32,128]{1,0:T(8,128)S(1)}, f32[32,128]{1,0:T(8,128)S(1)}, u32[]{:S(2)}, u32[]{:S(2)}) collective-permute-start(f32[32,128]{1,0:T(8,128)S(1)} %get-tuple-element.56), channel_id=1, source_target_pairs={{0,1},{1,2},{2,3},{3,4},{4,5},{5,6},{6,7},{7,8},{8,9},{9,10},{10,1... | collective-permute-start | bytes 49160 | tf_op jit(solution)/shard_map/ppermute | solution.py:267
  127.6 1.3 collective-permute-start.17
  128.9 0.0 collective-permute-done.16
  128.9 3.2 %collective-permute-done.17 = f32[32,128]{1,0:T(8,128)S(1)} collective-permute-done((f32[32,128]{1,0:T(8,128)S(1)}, f32[32,128]{1,0:T(8,128)S(1)}, u32[]{:S(2)}, u32[]{:S(2)}) %collective-permute-start.17) | collective-permute-done | bytes 16416 | tf_op jit(solution)/shard_map/ppermute | solution.py:267
  132.1 14.3 %collective-permute-start.18 = (f32[1,128]{1,0:T(1,128)S(1)}, f32[1,128]{1,0:T(1,128)S(1)}, u32[]{:S(2)}, u32[]{:S(2)}) collective-permute-start(f32[1,128]{1,0:T(1,128)S(1)} %get-tuple-element.58), channel_id=1, source_target_pairs={{0,16},{16,32},{32,48},{48,64},{64,80},{80,96},{96,112},{112,128},... | collective-permute-start | bytes 1544 | tf_op jit(solution)/shard_map/ppermute | solution.py:267
  146.3 1.9 %collective-permute-start.19 = (f32[1,128]{1,0:T(1,128)S(1)}, f32[1,128]{1,0:T(1,128)S(1)}, u32[]{:S(2)}, u32[]{:S(2)}) collective-permute-start(f32[1,128]{1,0:T(1,128)S(1)} %get-tuple-element.59), channel_id=1, source_target_pairs={{16,0},{32,16},{48,32},{64,48},{80,64},{96,80},{112,96},{128,112},... | collective-permute-start | bytes 1544 | tf_op jit(solution)/shard_map/ppermute | solution.py:267
  148.3 0.0 collective-permute-done.18
  148.3 5.0 %collective-permute-done.19 = f32[1,128]{1,0:T(1,128)S(1)} collective-permute-done((f32[1,128]{1,0:T(1,128)S(1)}, f32[1,128]{1,0:T(1,128)S(1)}, u32[]{:S(2)}, u32[]{:S(2)}) %collective-permute-start.19) | collective-permute-done | bytes 544 | tf_op jit(solution)/shard_map/ppermute | solution.py:267
  153.3 0.8 convolution_add_fusion
  (14 shorter events, 0.1 us)
Async XLA Ops:
  0.6 152.7 %copy-start = (f32[128,128]{1,0:T(8,128)S(1)}, f32[128,128]{1,0:T(8,128)}, u32[]{:S(2)}) copy-start(f32[128,128]{1,0:T(8,128)} %param.17) | copy-start | bytes 196612
  1.7 37.8 %collective-permute-start.1 = (bf16[1408,128]{1,0:T(8,128)(2,1)S(1)}, bf16[1408,128]{1,0:T(8,128)(2,1)S(1)}, u32[]{:S(2)}, u32[]{:S(2)}) collective-permute-start(bf16[1408,128]{1,0:T(8,128)(2,1)S(1)} %pad_maximum_fusion.refs_3_), channel_id=1, source_target_pairs={{0,15},{1,0},{2,1},{3,2},{4,3},{5,4},{6,5},{7,6},{8,7},{9,8},{10,9... | collective-permute-start | bytes 1081352 | tf_op jit(solution)/shard_map/ppermute | solution.py:261
  12.8 26.7 %collective-permute-start = (bf16[1408,128]{1,0:T(8,128)(2,1)S(1)}, bf16[1408,128]{1,0:T(8,128)(2,1)S(1)}, u32[]{:S(2)}, u32[]{:S(2)}) collective-permute-start(bf16[1408,128]{1,0:T(8,128)(2,1)S(1)} %pad_maximum_fusion.refs_3_), channel_id=1, source_target_pairs={{0,1},{1,2},{2,3},{3,4},{4,5},{5,6},{6,7},{7,8},{8,9},{9,10},{10,1... | collective-permute-start | bytes 1081352 | tf_op jit(solution)/shard_map/ppermute | solution.py:261
  14.8 0.9 copy-start.3
  15.7 0.7 copy-start.7
  16.3 0.7 copy-start.8
  33.7 60.6 %copy-start.1 = (bf16[128,128,32]{2,1,0:T(8,128)(2,1)}, bf16[128,128,32]{2,1,0:T(8,128)(2,1)S(1)}, u32[]{:S(2)}) copy-start(bf16[128,128,32]{2,1,0:T(8,128)(2,1)S(1)} %get-tuple-element.30.refs_2_) | copy-start | bytes 3145732
  39.5 11.7 %collective-permute-start.2 = (bf16[1408,128]{1,0:T(8,128)(2,1)S(1)}, bf16[1408,128]{1,0:T(8,128)(2,1)S(1)}, u32[]{:S(2)}, u32[]{:S(2)}) collective-permute-start(bf16[1408,128]{1,0:T(8,128)(2,1)S(1)} %collective-permute-done.refs_3_), channel_id=1, source_target_pairs={{0,1},{1,2},{2,3},{3,4},{4,5},{5,6},{6,7},{7,8},{8,9},{9,10},{10,1... | collective-permute-start | bytes 1081352 | tf_op jit(solution)/shard_map/ppermute | solution.py:261
  41.4 10.7 %collective-permute-start.3 = (bf16[1408,128]{1,0:T(8,128)(2,1)S(1)}, bf16[1408,128]{1,0:T(8,128)(2,1)S(1)}, u32[]{:S(2)}, u32[]{:S(2)}) collective-permute-start(bf16[1408,128]{1,0:T(8,128)(2,1)S(1)} %collective-permute-done.1.refs_4_), channel_id=1, source_target_pairs={{0,15},{1,0},{2,1},{3,2},{4,3},{5,4},{6,5},{7,6},{8,7},{9,8},{10,9... | collective-permute-start | bytes 1081352 | tf_op jit(solution)/shard_map/ppermute | solution.py:261
  52.1 11.4 %collective-permute-start.4 = (bf16[1408,128]{1,0:T(8,128)(2,1)S(1)}, bf16[1408,128]{1,0:T(8,128)(2,1)S(1)}, u32[]{:S(2)}, u32[]{:S(2)}) collective-permute-start(bf16[1408,128]{1,0:T(8,128)(2,1)S(1)} %collective-permute-done.2.refs_3_), channel_id=1, source_target_pairs={{0,1},{1,2},{2,3},{3,4},{4,5},{5,6},{6,7},{7,8},{8,9},{9,10},{10,1... | collective-permute-start | bytes 1081352 | tf_op jit(solution)/shard_map/ppermute | solution.py:261
  54.1 10.4 %collective-permute-start.5 = (bf16[1408,128]{1,0:T(8,128)(2,1)S(1)}, bf16[1408,128]{1,0:T(8,128)(2,1)S(1)}, u32[]{:S(2)}, u32[]{:S(2)}) collective-permute-start(bf16[1408,128]{1,0:T(8,128)(2,1)S(1)} %collective-permute-done.3.refs_4_), channel_id=1, source_target_pairs={{0,15},{1,0},{2,1},{3,2},{4,3},{5,4},{6,5},{7,6},{8,7},{9,8},{10,9... | collective-permute-start | bytes 1081352 | tf_op jit(solution)/shard_map/ppermute | solution.py:261
  64.4 10.5 %collective-permute-start.6 = (bf16[1408,128]{1,0:T(8,128)(2,1)S(1)}, bf16[1408,128]{1,0:T(8,128)(2,1)S(1)}, u32[]{:S(2)}, u32[]{:S(2)}) collective-permute-start(bf16[1408,128]{1,0:T(8,128)(2,1)S(1)} %collective-permute-done.4.refs_3_), channel_id=1, source_target_pairs={{0,1},{1,2},{2,3},{3,4},{4,5},{5,6},{6,7},{7,8},{8,9},{9,10},{10,1... | collective-permute-start | bytes 1081352 | tf_op jit(solution)/shard_map/ppermute | solution.py:261
  66.3 9.7 %collective-permute-start.7 = (bf16[1408,128]{1,0:T(8,128)(2,1)S(1)}, bf16[1408,128]{1,0:T(8,128)(2,1)S(1)}, u32[]{:S(2)}, u32[]{:S(2)}) collective-permute-start(bf16[1408,128]{1,0:T(8,128)(2,1)S(1)} %collective-permute-done.5.refs_4_), channel_id=1, source_target_pairs={{0,15},{1,0},{2,1},{3,2},{4,3},{5,4},{6,5},{7,6},{8,7},{9,8},{10,9... | collective-permute-start | bytes 1081352 | tf_op jit(solution)/shard_map/ppermute | solution.py:261
  76.0 10.3 %collective-permute-start.8 = (bf16[1408,128]{1,0:T(8,128)(2,1)S(1)}, bf16[1408,128]{1,0:T(8,128)(2,1)S(1)}, u32[]{:S(2)}, u32[]{:S(2)}) collective-permute-start(bf16[1408,128]{1,0:T(8,128)(2,1)S(1)} %collective-permute-done.6.refs_3_), channel_id=1, source_target_pairs={{0,1},{1,2},{2,3},{3,4},{4,5},{5,6},{6,7},{7,8},{8,9},{9,10},{10,1... | collective-permute-start | bytes 1081352 | tf_op jit(solution)/shard_map/ppermute | solution.py:261
  78.3 9.1 %collective-permute-start.9 = (bf16[1408,128]{1,0:T(8,128)(2,1)S(1)}, bf16[1408,128]{1,0:T(8,128)(2,1)S(1)}, u32[]{:S(2)}, u32[]{:S(2)}) collective-permute-start(bf16[1408,128]{1,0:T(8,128)(2,1)S(1)} %collective-permute-done.7.refs_4_), channel_id=1, source_target_pairs={{0,15},{1,0},{2,1},{3,2},{4,3},{5,4},{6,5},{7,6},{8,7},{9,8},{10,9... | collective-permute-start | bytes 1081352 | tf_op jit(solution)/shard_map/ppermute | solution.py:261
  87.3 9.9 %collective-permute-start.10 = (bf16[1408,128]{1,0:T(8,128)(2,1)S(1)}, bf16[1408,128]{1,0:T(8,128)(2,1)S(1)}, u32[]{:S(2)}, u32[]{:S(2)}) collective-permute-start(bf16[1408,128]{1,0:T(8,128)(2,1)S(1)} %collective-permute-done.8.refs_3_), channel_id=1, source_target_pairs={{0,1},{1,2},{2,3},{3,4},{4,5},{5,6},{6,7},{7,8},{8,9},{9,10},{10,1... | collective-permute-start | bytes 1081352 | tf_op jit(solution)/shard_map/ppermute | solution.py:261
  90.6 8.2 %collective-permute-start.11 = (bf16[1408,128]{1,0:T(8,128)(2,1)S(1)}, bf16[1408,128]{1,0:T(8,128)(2,1)S(1)}, u32[]{:S(2)}, u32[]{:S(2)}) collective-permute-start(bf16[1408,128]{1,0:T(8,128)(2,1)S(1)} %collective-permute-done.9.refs_4_), channel_id=1, source_target_pairs={{0,15},{1,0},{2,1},{3,2},{4,3},{5,4},{6,5},{7,6},{8,7},{9,8},{10,9... | collective-permute-start | bytes 1081352 | tf_op jit(solution)/shard_map/ppermute | solution.py:261
  98.8 11.9 %collective-permute-start.12 = (bf16[1408,128]{1,0:T(8,128)(2,1)S(1)}, bf16[1408,128]{1,0:T(8,128)(2,1)S(1)}, u32[]{:S(2)}, u32[]{:S(2)}) collective-permute-start(bf16[1408,128]{1,0:T(8,128)(2,1)S(1)} %collective-permute-done.10.refs_3_), channel_id=1, source_target_pairs={{0,1},{1,2},{2,3},{3,4},{4,5},{5,6},{6,7},{7,8},{8,9},{9,10},{10,1... | collective-permute-start | bytes 1081352 | tf_op jit(solution)/shard_map/ppermute | solution.py:261
  103.3 8.2 %collective-permute-start.13 = (bf16[1408,128]{1,0:T(8,128)(2,1)S(1)}, bf16[1408,128]{1,0:T(8,128)(2,1)S(1)}, u32[]{:S(2)}, u32[]{:S(2)}) collective-permute-start(bf16[1408,128]{1,0:T(8,128)(2,1)S(1)} %collective-permute-done.11.refs_4_), channel_id=1, source_target_pairs={{0,15},{1,0},{2,1},{3,2},{4,3},{5,4},{6,5},{7,6},{8,7},{9,8},{10,9... | collective-permute-start | bytes 1081352 | tf_op jit(solution)/shard_map/ppermute | solution.py:261
  105.6 2.2 %copy-start.2 = (bf16[128,128,32]{2,1,0:T(8,128)(2,1)S(1)}, bf16[128,128,32]{2,1,0:T(8,128)(2,1)}, u32[]{:S(2)}) copy-start(bf16[128,128,32]{2,1,0:T(8,128)(2,1)} %copy-done.1) | copy-start | bytes 3145732
  107.8 10.3 %copy-start.9 = (s32[1,128]{1,0:T(1,128)S(1)}, s32[1,128]{1,0:T(1,128)}, u32[]{:S(2)}) copy-start(s32[1,128]{1,0:T(1,128)} %param.15) | copy-start | bytes 1540
  111.6 9.5 %collective-permute-start.14 = (bf16[704,128]{1,0:T(8,128)(2,1)S(1)}, bf16[704,128]{1,0:T(8,128)(2,1)S(1)}, u32[]{:S(2)}, u32[]{:S(2)}) collective-permute-start(bf16[704,128]{1,0:T(8,128)(2,1)S(1)} %slice.29), channel_id=1, source_target_pairs={{0,1},{1,2},{2,3},{3,4},{4,5},{5,6},{6,7},{7,8},{8,9},{9,10},{10,1... | collective-permute-start | bytes 540680 | tf_op jit(solution)/shard_map/ppermute | solution.py:261
  115.2 6.2 %collective-permute-start.15 = (bf16[704,128]{1,0:T(8,128)(2,1)S(1)}, bf16[704,128]{1,0:T(8,128)(2,1)S(1)}, u32[]{:S(2)}, u32[]{:S(2)}) collective-permute-start(bf16[704,128]{1,0:T(8,128)(2,1)S(1)} %slice.30), channel_id=1, source_target_pairs={{0,15},{1,0},{2,1},{3,2},{4,3},{5,4},{6,5},{7,6},{8,7},{9,8},{10,9... | collective-permute-start | bytes 540680 | tf_op jit(solution)/shard_map/ppermute | solution.py:261
  118.1 3.4 %copy-start.4 = (bf16[1024,128]{1,0:T(8,128)(2,1)S(1)}, bf16[1024,128]{1,0:T(8,128)(2,1)}, u32[]{:S(2)}) copy-start(bf16[1024,128]{1,0:T(8,128)(2,1)} %refs_8_.1) | copy-start | bytes 786436
  118.1 3.4 %copy-start.5 = (f32[1,128,128]{2,1,0:T(8,128)S(1)}, f32[1,128,128]{2,1,0:T(8,128)}, u32[]{:S(2)}) copy-start(f32[1,128,128]{2,1,0:T(8,128)} %param.11) | copy-start | bytes 196612
  118.1 3.4 %copy-start.6 = (f32[1,128,128]{2,1,0:T(8,128)S(1)}, f32[1,128,128]{2,1,0:T(8,128)}, u32[]{:S(2)}) copy-start(f32[1,128,128]{2,1,0:T(8,128)} %param.12) | copy-start | bytes 196612
  124.5 4.3 %collective-permute-start.16 = (f32[32,128]{1,0:T(8,128)S(1)}, f32[32,128]{1,0:T(8,128)S(1)}, u32[]{:S(2)}, u32[]{:S(2)}) collective-permute-start(f32[32,128]{1,0:T(8,128)S(1)} %get-tuple-element.56), channel_id=1, source_target_pairs={{0,1},{1,2},{2,3},{3,4},{4,5},{5,6},{6,7},{7,8},{8,9},{9,10},{10,1... | collective-permute-start | bytes 49160 | tf_op jit(solution)/shard_map/ppermute | solution.py:267
  127.6 4.5 %collective-permute-start.17 = (f32[32,128]{1,0:T(8,128)S(1)}, f32[32,128]{1,0:T(8,128)S(1)}, u32[]{:S(2)}, u32[]{:S(2)}) collective-permute-start(f32[32,128]{1,0:T(8,128)S(1)} %get-tuple-element.57), channel_id=1, source_target_pairs={{1,0},{2,1},{3,2},{4,3},{5,4},{6,5},{7,6},{8,7},{9,8},{10,9},{11,1... | collective-permute-start | bytes 49160 | tf_op jit(solution)/shard_map/ppermute | solution.py:267
  132.1 16.2 %collective-permute-start.18 = (f32[1,128]{1,0:T(1,128)S(1)}, f32[1,128]{1,0:T(1,128)S(1)}, u32[]{:S(2)}, u32[]{:S(2)}) collective-permute-start(f32[1,128]{1,0:T(1,128)S(1)} %get-tuple-element.58), channel_id=1, source_target_pairs={{0,16},{16,32},{32,48},{48,64},{64,80},{80,96},{96,112},{112,128},... | collective-permute-start | bytes 1544 | tf_op jit(solution)/shard_map/ppermute | solution.py:267
  146.3 7.0 %collective-permute-start.19 = (f32[1,128]{1,0:T(1,128)S(1)}, f32[1,128]{1,0:T(1,128)S(1)}, u32[]{:S(2)}, u32[]{:S(2)}) collective-permute-start(f32[1,128]{1,0:T(1,128)S(1)} %get-tuple-element.59), channel_id=1, source_target_pairs={{16,0},{32,16},{48,32},{64,48},{80,64},{96,80},{112,96},{128,112},... | collective-permute-start | bytes 1544 | tf_op jit(solution)/shard_map/ppermute | solution.py:267

commit v3 on v2

v3 whole, which is shorter than its diff:
```python
import functools
import math

import jax
import jax.numpy as jnp
from jax import lax
from jax.experimental import pallas as pl
from jax.experimental.pallas import tpu as pltpu
from jax.sharding import PartitionSpec as P

PTS = 128
COLS = 8
PAIRS = 8
CL = 128
BR_DEV = 32
N_TILE = 16
SHARP = 12.0
SOFTEN = 2.0
SCALE = SHARP * math.log2(math.e)

OWN_UNITS = 8
UNITS = 16
LISTED = CL * PAIRS + 2 * UNITS
YDIM = 8
KDIM = 2 * YDIM
HIST_ROWS = CL * COLS
ROWS = HIST_ROWS + 3 * CL
ACC_ROWS = (CL + 1) * 2 * COLS
SMEM = pl.BlockSpec(memory_space=pltpu.SMEM)
VMEM = pl.BlockSpec(memory_space=pltpu.VMEM)
ANY = pl.BlockSpec(memory_space=pl.ANY)


def split2(x):
    hi = x.astype(jnp.bfloat16).astype(jnp.float32)
    return hi, x - hi


def split3(x):
    hi, rest = split2(x)
    return (hi,) + split2(rest)


def reader_rows(here_ref, rows_ref, x_ref):
    here = [here_ref[k].astype(jnp.float32) for k in range(3)]
    twice = [split2((2.0 * SCALE) * h) for h in here]
    norm = split2(-SCALE * (here[0] * here[0] + here[1] * here[1] + here[2] * here[2]))
    one = jnp.ones((CL, PTS), jnp.float32)
    none = jnp.zeros((CL, PTS), jnp.float32)
    rows = [twice[k][0] for k in range(3)] + [one] * 3 + [norm[0], none]
    rows += [twice[k][1] for k in range(3)] + [none] * 3 + [norm[1], none]
    for k, row in enumerate(rows):
        rows_ref[pl.ds(k, CL, stride=KDIM), :] = row

    def turn(g, carry):
        four = [
            rows_ref[pl.ds(pl.multiple_of((g * 4 + m) * KDIM, KDIM), KDIM), :] for m in range(4)
        ]
        turned = jnp.concatenate([f for f in four for _ in range(2)], axis=0).T
        turned = turned.astype(jnp.bfloat16)
        for m in range(4):
            x_ref[g * 4 + m] = turned[:, m * 2 * KDIM : (m + 1) * 2 * KDIM]
        return carry

    lax.fori_loop(0, CL // 4, turn, 0)


def list_pairs(ids_ref, cnt_ref, tile, list_ref, steps_ref, cur_ref):
    for k in range(3):
        cur_ref[k] = k * LISTED

    def reader(r, carry):
        count = cnt_ref[0, r]
        for p in range(PAIRS):
            q = ids_ref[p, r]
            far = jnp.where((q >> 7) == tile, 0, 1)
            k = jnp.where(p < count, far, 2)
            at = cur_ref[k]
            list_ref[at] = (r << 11) | q
            cur_ref[k] = at + 1
        return carry

    lax.fori_loop(0, CL, reader, 0)
    for k, units in ((0, OWN_UNITS), (1, UNITS)):
        used = cur_ref[k] - k * LISTED
        steps = lax.div(used + (2 * units - 1), 2 * units)
        steps_ref[k] = steps

        def pad(at, carry):
            list_ref[at] = CL << 11
            return carry

        lax.fori_loop(k * LISTED + used, k * LISTED + steps * (2 * units), pad, 0)


def source_rows(block, spots, y_ref):
    norm = spots[0] * spots[0] + spots[1] * spots[1] + spots[2] * spots[2]
    one = jnp.ones((CL, PTS), jnp.float32)
    rows = spots + list(split3(-SCALE * norm)) + [one, 0.0 * one]
    for k, row in enumerate(rows):
        y_ref[pl.ds(block * (CL * YDIM) + k, CL, stride=YDIM), :] = row


def pairs(units, base, steps, mask, row_of, list_s, x_ref, hist_ref, y_ref, acc_ref):
    first = lax.broadcasted_iota(jnp.int32, (PTS, 2 * KDIM), 1) < KDIM
    zero_y = jnp.zeros((KDIM, PTS), jnp.float32)
    zero_h = jnp.zeros((COLS, PTS), jnp.float32)
    row = lax.broadcasted_iota(jnp.int32, (2 * COLS, 2 * PTS), 0) >> 3
    side = lax.broadcasted_iota(jnp.int32, (2 * COLS, 2 * PTS), 1) >> 7
    ones = (row == side).astype(jnp.float32).astype(jnp.bfloat16)

    def beside(one, other, zero):
        top = jnp.concatenate([one, zero], axis=1)
        bottom = jnp.concatenate([zero, other], axis=1)
        return jnp.concatenate([top, bottom], axis=0).astype(jnp.bfloat16)

    def source_points(q):
        y = y_ref[pl.ds(pl.multiple_of(q * YDIM, YDIM), YDIM), :]
        return jnp.concatenate([y, y], axis=0)

    def source_hist(q):
        at = pl.multiple_of(row_of(q), 2 * COLS)
        two = hist_ref[pl.ds(at, 2 * COLS), :].astype(jnp.float32)
        return jnp.where((q & 1) == 1, two[COLS:], two[:COLS])

    def step(i, carry):
        entries = [list_s[base + i * (2 * units) + k] for k in range(2 * units)]
        readers = [e >> 11 for e in entries]
        sources = [e & mask for e in entries]
        both = [(2 * u, 2 * u + 1) for u in range(units)]
        weights = []
        for a, b in both:
            lhs = jnp.where(first, x_ref[readers[a] & (CL - 1)], x_ref[readers[b] & (CL - 1)])
            rhs = beside(source_points(sources[a]), source_points(sources[b]), zero_y)
            power = jnp.dot(lhs, rhs, preferred_element_type=jnp.float32)
            weights.append(jnp.exp2(power).astype(jnp.bfloat16))
        outs = []
        for (a, b), weight in zip(both, weights):
            hist = beside(source_hist(sources[a]), source_hist(sources[b]), zero_h)
            outs.append(
                lax.dot_general(
                    jnp.concatenate([hist, ones], axis=0),
                    weight,
                    (((1,), (1,)), ((), ())),
                    preferred_element_type=jnp.float32,
                )
            )
        for unit, out in zip(both, outs):
            for half in range(2):
                at = pl.multiple_of(readers[unit[half]] * (2 * COLS), 2 * COLS)
                acc_ref[pl.ds(at, COLS), :] += out[half * COLS : (half + 1) * COLS]
                acc_ref[pl.ds(at + COLS, COLS), :] += out[(2 + half) * COLS : (3 + half) * COLS]
        return carry

    lax.fori_loop(0, steps, step, 0)


def own_kernel(
    ids_ref,
    cnt_ref,
    tile_ref,
    here_ref,
    hist_ref,
    list_ref,
    steps_ref,
    x_ref,
    acc_ref,
    cur_ref,
    rows_ref,
    y_ref,
):
    reader_rows(here_ref, rows_ref, x_ref)
    list_pairs(ids_ref, cnt_ref, tile_ref[0], list_ref, steps_ref, cur_ref)
    source_rows(0, [here_ref[k].astype(jnp.float32) for k in range(3)], y_ref)
    acc_ref[...] = jnp.zeros_like(acc_ref)
    row_of = lambda q: (q >> 1) * (2 * COLS)
    pairs(
        OWN_UNITS, 0, steps_ref[0], CL - 1, row_of, list_ref, x_ref, hist_ref, y_ref, acc_ref
    )


def own_pairs(ids, counts, tile, here, hist):
    return pl.pallas_call(
        own_kernel,
        out_shape=[
            jax.ShapeDtypeStruct((3 * LISTED,), jnp.int32),
            jax.ShapeDtypeStruct((2,), jnp.int32),
            jax.ShapeDtypeStruct((CL, PTS, 2 * KDIM), jnp.bfloat16),
            jax.ShapeDtypeStruct((ACC_ROWS, PTS), jnp.float32),
        ],
        in_specs=[SMEM] * 3 + [VMEM] * 2,
        out_specs=[SMEM] * 2 + [VMEM] * 2,
        scratch_shapes=[
            pltpu.SMEM((3,), jnp.int32),
            pltpu.VMEM((CL * KDIM, PTS), jnp.float32),
            pltpu.VMEM((CL * YDIM, PTS), jnp.float32),
        ],
        compiler_params=pltpu.CompilerParams(vmem_limit_bytes=16 * 2**20),
        cost_estimate=pl.CostEstimate(
            flops=2 * 80 * PTS * 256 * 256, bytes_accessed=10**7, transcendentals=10**6
        ),
    )(ids, counts, tile, here, hist)


def finish(acc_ref, kappa_ref, threshold_ref, disp_ref, brick_ref, damage_ref, shares_ref):
    inverse = 1.0 / acc_ref[pl.ds(COLS, CL, stride=2 * COLS), :]
    threshold = threshold_ref[...]
    strain = acc_ref[pl.ds(0, CL, stride=2 * COLS), :] * inverse
    kappa = jnp.maximum(jnp.maximum(kappa_ref[...], strain), threshold)
    damage = 1.0 - (threshold / kappa) * jnp.exp(-(kappa - threshold) / SOFTEN)
    damage_ref[...] = damage
    left = 1.0 - damage
    term = jnp.zeros((CL, PTS), jnp.float32)
    for c in range(COLS):
        mean = acc_ref[pl.ds(c, CL, stride=2 * COLS), :] * inverse
        term = term + jnp.dot(
            (left * mean).astype(jnp.bfloat16),
            disp_ref[c * PTS : (c + 1) * PTS, :],
            preferred_element_type=jnp.float32,
        )
    rows = lax.broadcasted_iota(jnp.int32, (3 * BR_DEV, CL), 0)
    onehot = (rows == brick_ref[...]).astype(jnp.float32)
    shares_ref[...] = jnp.dot(
        onehot, term, precision=lax.Precision.HIGHEST, preferred_element_type=jnp.float32
    )


def far_kernel(
    steps_s,
    list_s,
    x_hbm,
    acc_hbm,
    source_hbm,
    kappa_hbm,
    threshold_hbm,
    disp_hbm,
    brick_hbm,
    damage_ref,
    shares_ref,
    x_ref,
    acc_ref,
    source_ref,
    kappa_ref,
    threshold_ref,
    disp_ref,
    brick_ref,
    y_ref,
    sems,
):
    def block_copy(d):
        rows = pl.ds(pl.multiple_of(d * ROWS, ROWS), ROWS)
        return pltpu.make_async_copy(source_hbm.at[d], source_ref.at[rows], sems.at[d])

    others = [
        pltpu.make_async_copy(src, dst, sems.at[N_TILE + k])
        for k, (src, dst) in enumerate(
            (
                (x_hbm, x_ref),
                (acc_hbm, acc_ref),
                (kappa_hbm, kappa_ref),
                (threshold_hbm, threshold_ref),
                (disp_hbm, disp_ref),
                (brick_hbm, brick_ref),
            )
        )
    ]
    for d in range(N_TILE):
        block_copy(d).start()
    for copy in others:
        copy.start()

    def block(d, carry):
        block_copy(d).wait()
        spots = []
        for k in range(3):
            at = pl.multiple_of(d * ROWS + (HIST_ROWS + k * CL), CL)
            spots.append(source_ref[pl.ds(at, CL), :].astype(jnp.float32))
        source_rows(d, spots, y_ref)
        return carry

    lax.fori_loop(0, N_TILE, block, 0)
    for copy in others:
        copy.wait()
    row_of = lambda q: (q >> 7) * ROWS + ((q & (CL - 1)) >> 1) * (2 * COLS)
    pairs(
        UNITS,
        LISTED,
        steps_s[1],
        N_TILE * CL - 1,
        row_of,
        list_s,
        x_ref,
        source_ref,
        y_ref,
        acc_ref,
    )
    finish(acc_ref, kappa_ref, threshold_ref, disp_ref, brick_ref, damage_ref, shares_ref)


def far_pairs(prepared, source, final):
    lists, steps, x_rows, acc = prepared
    held = [x_rows, acc, source.reshape(N_TILE * ROWS, PTS)] + list(final)
    return pl.pallas_call(
        far_kernel,
        out_shape=[
            jax.ShapeDtypeStruct((CL, PTS), jnp.float32),
            jax.ShapeDtypeStruct((3 * BR_DEV, PTS), jnp.float32),
        ],
        in_specs=[SMEM] * 2 + [ANY] * 7,
        out_specs=[VMEM] * 2,
        scratch_shapes=[pltpu.VMEM(h.shape, h.dtype) for h in held]
        + [
            pltpu.VMEM((N_TILE * CL * YDIM, PTS), jnp.float32),
            pltpu.SemaphoreType.DMA((N_TILE + 6,)),
        ],
        compiler_params=pltpu.CompilerParams(vmem_limit_bytes=60 * 2**20),
        cost_estimate=pl.CostEstimate(
            flops=2 * 320 * PTS * 256 * 256, bytes_accessed=12 * 2**20, transcendentals=10**7
        ),
    )(steps, lists, x_rows, acc, source, *final)


def shifted(block, axis, distance):
    devices = range(lax.axis_size(axis))
    route = [(i - distance, i) for i in devices if i - distance in devices]
    return lax.ppermute(block, axis, route)


def local(
    history,
    positions,
    kappa_old,
    threshold,
    pair_ids,
    reader_counts,
    brick_map,
    strain_disp,
    couple,
):
    points = positions[0].transpose(1, 0, 2)
    own = jnp.concatenate(
        [history[0].reshape(HIST_ROWS, PTS), points.reshape(3 * CL, PTS)], axis=0
    )
    tile = lax.axis_index("tile")
    source = lax.all_gather(own, "tile", axis=0, tiled=False)
    prepared = own_pairs(
        pair_ids[0].T,
        reader_counts,
        tile.astype(jnp.int32).reshape(1),
        points,
        history[0].reshape(HIST_ROWS, PTS),
    )
    brick = brick_map - (tile - 1) * BR_DEV
    damage_here, shares = far_pairs(
        prepared, source, (kappa_old[0], threshold[0], strain_disp, brick)
    )
    low, mid, top = shares[:BR_DEV], shares[BR_DEV : 2 * BR_DEV], shares[2 * BR_DEV :]
    force = mid + shifted(top, "tile", 1) + shifted(low, "tile", -1)
    before = shifted(force[-1:], "slab", 1)
    after = shifted(force[:1], "slab", -1)
    padded = jnp.concatenate([before, force, after], axis=0)
    residual_here = force + jnp.dot(
        padded[:-2] + padded[2:],
        couple,
        precision=lax.Precision.HIGHEST,
        preferred_element_type=jnp.float32,
    )
    return (damage_here[None], residual_here[:, None, :])


def solution(mesh):
    placed = (
        P("slab", "tile", None, None),
        P("slab", "tile", None, None),
        P("slab", "tile", None),
        P("slab", "tile", None),
        P("slab", "tile", None),
        P("slab", "tile"),
        P("slab", "tile"),
        P(),
        P(),
    )
    return jax.shard_map(
        local,
        mesh=mesh,
        in_specs=placed,
        out_specs=(P("slab", "tile", None), P("slab", "tile", None)),
        check_vma=False,
    )
```

time: 155 us -> 144 us (0.929)
  starting transfers between devices: 81.8 us -> 17.1 us
  waiting for transfers between devices: 18.3 us -> 65.4 us
  between operations: 1.02 us -> 14.1 us
  Pallas kernels: 46.6 us -> 34 us
  local copies, waits for them, and re-layouts: 4.48 us -> 8.12 us
  other arithmetic: 1.06 us -> 3.05 us
    ppermute x16 -> x0, starting transfers between devices: 61.3 us -> none  [hop(): lax.ppermute(block, 'tile', [(i, (i + distance) % peers) for i in range(p...]
    all_gather x0 -> x1, waiting for transfers between devices: none -> 57.2 us  [local(): source = lax.all_gather(own, 'tile', axis=0, tiled=False)]
    pallas_call x10 -> x2, Pallas kernels: 46.6 us -> 34 us  [the longest x1 19.1 us: own_pairs(): pl.pallas_call(own_kernel, out_shape=[jax.ShapeDtypeStruct((3 * LISTED,),...]
    ppermute x16 -> x0, waiting for transfers between devices: 10.1 us -> none  [hop(): lax.ppermute(block, 'tile', [(i, (i + distance) % peers) for i in range(p...]
    ppermute x4, starting transfers between devices: 20.5 us -> 17.1 us  [shifted(): return lax.ppermute(block, axis, route)]
    unnamed x20, local copies, waits for them, and re-layouts: 4.45 us -> 7.38 us
  transfers between devices with their start and end apart: 20 -> 5, of which waited for: 12 -> 3; matrix products, arithmetic and copies ran while one was open for 0% -> 0% of each run, Pallas kernels for 28% -> 13%
where the time goes in v3:
time: 144 us; the launch traced here: 143 us
  waiting for transfers between devices  65.4 us (45%)
  Pallas kernels  34 us (24%)
  starting transfers between devices  17.1 us (12%)
  between operations  14.1 us (10%)
  local copies, waits for them, and re-layouts  8.12 us (6%)
  other arithmetic  3.05 us (2%)
    all_gather x1, waiting for transfers between devices, local(): source = lax.all_gather(own, 'tile', axis=0, tiled=False)  57.2 us
    pallas_call x1, Pallas kernels, own_pairs(): pl.pallas_call(own_kernel, out_shape=[jax.ShapeDtypeStruct((3 * LISTED,),...  19.1 us
    ppermute x4, starting transfers between devices, shifted(): return lax.ppermute(block, axis, route)  17.1 us
    pallas_call x1, Pallas kernels, far_pairs(): pl.pallas_call(far_kernel, out_shape=[jax.ShapeDtypeStruct((CL, PTS), jnp...  14.9 us
    ppermute x4, waiting for transfers between devices, shifted(): return lax.ppermute(block, axis, route)  8.21 us
    unnamed x20, local copies, waits for them, and re-layouts  7.38 us
  transfers between devices with their start and end apart: 5, of which 3 were waited for; matrix products, arithmetic and copies ran while one was open for 0% of the time, Pallas kernels for 13%

profile of v3, /device:TPU:7, one launch (start us, length us, event | category | flops | bytes accessed | tf_op | source)
XLA Modules:
  0.0 142.5 jit_solution(18259557930247575794)
XLA Ops:
  7.2 0.0 copy-start
  7.2 0.0 copy-start.9
  7.2 0.0 all-gather.3.cloned.1.call-start
  7.2 1.8 %pad_maximum_fusion = bf16[1408,128]{1,0:T(8,128)(2,1)} fusion(bf16[384,128]{1,0:T(8,128)(2,1)} %bitcast.20, bf16[1024,128]{1,0:T(8,128)(2,1)} %bitcast.18), kind=kLoop, calls=%fused_computation.1 | loop fusion | flops 720896 | bytes 720896 | tf_op jit(solution)/shard_map/concatenate | solution.py:341
  9.0 0.0 all-gather.3.cloned.1.call-update
  9.0 0.0 copy-start.1
  9.0 0.9 copy-done.1
  10.0 0.0 copy-start.2
  10.0 0.9 copy-done.2
  10.9 0.0 copy-start.3
  10.9 0.7 copy-done.3
  11.6 0.0 copy-start.4
  11.6 0.7 copy-done.4
  12.2 19.1 %shard_map.104 = (s32[3168]{0:T(1024)S(1)}, s32[2]{0:T(128)S(1)}, bf16[128,128,32]{2,1,0:T(8,128)(2,1)S(1)}, f32[2064,128]{1,0:T(8,128)S(1)}) custom-call(s32[8,128]{1,0:T(8,128)S(1)} %bitcast.22, s32[1,128]{1,0:T(1,128)S(1)} %copy-done.4, s32[1]{0:T(128)} %bitcast.2.tile_ref, bf16[3,128,128]{2,1,0:T(8,128)(2,1)S(1)} %bitcast.21, bf16[1024,128]{1,0:T(8,128)(2,1)S(1)} %bitcast.19), custom_call_target="tpu_custom_call" | custom-call | flops 1342177280 | bytes 10000000 | tf_op jit(solution)/shard_map/pallas_call | solution.py:183
  31.3 0.0 copy-start.5
  31.3 2.0 %copy-done.5 = bf16[128,128,32]{2,1,0:T(8,128)(2,1)} copy-done((bf16[128,128,32]{2,1,0:T(8,128)(2,1)}, bf16[128,128,32]{2,1,0:T(8,128)(2,1)S(1)}, u32[]{:S(2)}) %copy-start.5) | copy-done | bytes 1048600
  33.3 0.0 copy-start.6
  33.3 1.0 copy-done.6
  34.3 0.0 copy-start.7
  34.3 0.6 copy-done.7
  34.9 0.0 copy-start.8
  34.9 0.6 copy-done.8
  35.5 0.0 copy-done.9
  35.5 0.6 broadcast_subtract_fusion.brick_hbm
  36.1 57.2 %all-gather.3.cloned.1.call-done = bf16[22528,128]{1,0:T(8,128)(2,1)} async-done(((bf16[1408,128]{1,0:T(8,128)(2,1)}), bf16[22528,128]{1,0:T(8,128)(2,1)}) %all-gather.3.cloned.1.call-update) | async-done | bytes 5767184 | tf_op jit(solution)/shard_map/all_gather | solution.py:345
  93.2 14.9 %shard_map.105 = (f32[128,128]{1,0:T(8,128)}, f32[96,128]{1,0:T(8,128)}) custom-call(s32[2]{0:T(128)} %copy-done.8, s32[3168]{0:T(1024)} %copy-done.7, bf16[128,128,32]{2,1,0:T(8,128)(2,1)} %copy-done.5, f32[2064,128]{1,0:T(8,128)} %copy-done.6, bf16[16,1408,128]{2,1,0:T(8,128)(2,1)} %bitcast.24, f32[128,128]{1,0:T(8,128)} %bitcast.25, f32[128,128]{1,0:T(8,128)} %bitcast.26, ...), custom_call_target="tpu_custom_call" | custom-call | flops 5368709120 | bytes 12582912 | tf_op jit(solution)/shard_map/pallas_call | solution.py:303
  108.1 0.7 fusion.5
  108.9 3.9 %collective-permute-start = (f32[32,128]{1,0:T(8,128)S(1)}, f32[32,128]{1,0:T(8,128)S(1)}, u32[]{:S(2)}, u32[]{:S(2)}) collective-permute-start(f32[32,128]{1,0:T(8,128)S(1)} %get-tuple-element.16), channel_id=1, source_target_pairs={{0,1},{1,2},{2,3},{3,4},{4,5},{5,6},{6,7},{7,8},{8,9},{9,10},{10,1... | collective-permute-start | bytes 49160 | tf_op jit(solution)/shard_map/ppermute | solution.py:326
  112.7 1.3 collective-permute-start.1
  114.0 0.0 collective-permute-done
  114.0 3.2 %collective-permute-done.1 = f32[32,128]{1,0:T(8,128)S(1)} collective-permute-done((f32[32,128]{1,0:T(8,128)S(1)}, f32[32,128]{1,0:T(8,128)S(1)}, u32[]{:S(2)}, u32[]{:S(2)}) %collective-permute-start.1) | collective-permute-done | bytes 16416 | tf_op jit(solution)/shard_map/ppermute | solution.py:326
  117.2 0.7 add_add_fusion
  117.9 10.0 %collective-permute-start.2 = (f32[1,128]{1,0:T(1,128)S(1)}, f32[1,128]{1,0:T(1,128)S(1)}, u32[]{:S(2)}, u32[]{:S(2)}) collective-permute-start(f32[1,128]{1,0:T(1,128)S(1)} %get-tuple-element.18), channel_id=1, source_target_pairs={{0,16},{16,32},{32,48},{48,64},{64,80},{80,96},{96,112},{112,128},... | collective-permute-start | bytes 1544 | tf_op jit(solution)/shard_map/ppermute | solution.py:326
  127.9 1.9 %collective-permute-start.3 = (f32[1,128]{1,0:T(1,128)S(1)}, f32[1,128]{1,0:T(1,128)S(1)}, u32[]{:S(2)}, u32[]{:S(2)}) collective-permute-start(f32[1,128]{1,0:T(1,128)S(1)} %get-tuple-element.19), channel_id=1, source_target_pairs={{16,0},{32,16},{48,32},{64,48},{80,64},{96,80},{112,96},{128,112},... | collective-permute-start | bytes 1544 | tf_op jit(solution)/shard_map/ppermute | solution.py:326
  129.9 0.0 collective-permute-done.2
  129.9 5.0 %collective-permute-done.3 = f32[1,128]{1,0:T(1,128)S(1)} collective-permute-done((f32[1,128]{1,0:T(1,128)S(1)}, f32[1,128]{1,0:T(1,128)S(1)}, u32[]{:S(2)}, u32[]{:S(2)}) %collective-permute-start.3) | collective-permute-done | bytes 544 | tf_op jit(solution)/shard_map/ppermute | solution.py:326
  134.9 0.0 copy-done
  134.9 0.8 convolution_add_fusion
  (1 shorter events, 0.0 us)
Async XLA Ops:
  7.2 127.8 %copy-start = (f32[128,128]{1,0:T(8,128)S(1)}, f32[128,128]{1,0:T(8,128)}, u32[]{:S(2)}) copy-start(f32[128,128]{1,0:T(8,128)} %param.17) | copy-start | bytes 196612
  7.2 28.3 %copy-start.9 = (s32[1,128]{1,0:T(1,128)S(1)}, s32[1,128]{1,0:T(1,128)}, u32[]{:S(2)}) copy-start(s32[1,128]{1,0:T(1,128)} %param.15) | copy-start | bytes 1540
  7.2 86.0 %all-gather.3.cloned.1.call-start = ((), (), s32[]{:S(2)}) async-start(), calls=%async_computation | async-start | bytes 6127616 | tf_op jit(solution)/shard_map/all_gather | solution.py:345
  9.0 1.0 copy-start.1
  10.0 0.9 copy-start.2
  10.9 0.7 copy-start.3
  11.6 0.7 copy-start.4
  31.3 2.0 %copy-start.5 = (bf16[128,128,32]{2,1,0:T(8,128)(2,1)}, bf16[128,128,32]{2,1,0:T(8,128)(2,1)S(1)}, u32[]{:S(2)}) copy-start(bf16[128,128,32]{2,1,0:T(8,128)(2,1)S(1)} %get-tuple-element.10.x_hbm) | copy-start | bytes 3145732
  33.3 1.0 copy-start.6
  34.3 0.6 copy-start.7
  34.9 0.6 copy-start.8
  108.9 5.2 %collective-permute-start = (f32[32,128]{1,0:T(8,128)S(1)}, f32[32,128]{1,0:T(8,128)S(1)}, u32[]{:S(2)}, u32[]{:S(2)}) collective-permute-start(f32[32,128]{1,0:T(8,128)S(1)} %get-tuple-element.16), channel_id=1, source_target_pairs={{0,1},{1,2},{2,3},{3,4},{4,5},{5,6},{6,7},{7,8},{8,9},{9,10},{10,1... | collective-permute-start | bytes 49160 | tf_op jit(solution)/shard_map/ppermute | solution.py:326
  112.7 4.5 %collective-permute-start.1 = (f32[32,128]{1,0:T(8,128)S(1)}, f32[32,128]{1,0:T(8,128)S(1)}, u32[]{:S(2)}, u32[]{:S(2)}) collective-permute-start(f32[32,128]{1,0:T(8,128)S(1)} %get-tuple-element.17), channel_id=1, source_target_pairs={{1,0},{2,1},{3,2},{4,3},{5,4},{6,5},{7,6},{8,7},{9,8},{10,9},{11,1... | collective-permute-start | bytes 49160 | tf_op jit(solution)/shard_map/ppermute | solution.py:326
  117.9 11.9 %collective-permute-start.2 = (f32[1,128]{1,0:T(1,128)S(1)}, f32[1,128]{1,0:T(1,128)S(1)}, u32[]{:S(2)}, u32[]{:S(2)}) collective-permute-start(f32[1,128]{1,0:T(1,128)S(1)} %get-tuple-element.18), channel_id=1, source_target_pairs={{0,16},{16,32},{32,48},{48,64},{64,80},{80,96},{96,112},{112,128},... | collective-permute-start | bytes 1544 | tf_op jit(solution)/shard_map/ppermute | solution.py:326
  127.9 7.0 %collective-permute-start.3 = (f32[1,128]{1,0:T(1,128)S(1)}, f32[1,128]{1,0:T(1,128)S(1)}, u32[]{:S(2)}, u32[]{:S(2)}) collective-permute-start(f32[1,128]{1,0:T(1,128)S(1)} %get-tuple-element.19), channel_id=1, source_target_pairs={{16,0},{32,16},{48,32},{64,48},{80,64},{96,80},{112,96},{128,112},... | collective-permute-start | bytes 1544 | tf_op jit(solution)/shard_map/ppermute | solution.py:326
Sparse Core Ops, SparseCore 0:
  10.1 83.0 all-gather.2

commit v4 on v2

--- a/solution.py
+++ b/solution.py
@@ -18,10 +18,11 @@
 SOFTEN = 2.0
 SCALE = SHARP * math.log2(math.e)
 
-UNITS = 8
+UNITS = 16
 STEP = 2 * UNITS
 ROUNDS = N_TILE // 2 + 1
 REGION = CL * PAIRS
+KEY_SHIFT = 20
 YDIM = 8
 KDIM = 2 * YDIM
 HIST_ROWS = CL * COLS
@@ -51,87 +52,90 @@
     for k, row in enumerate(rows):
         rows_ref[pl.ds(k, CL, stride=KDIM), :] = row
 
-    def turn(g, carry):
-        four = [
-            rows_ref[pl.ds(pl.multiple_of((g * 4 + m) * KDIM, KDIM), KDIM), :] for m in range(4)
-        ]
-        turned = jnp.concatenate([f for f in four for _ in range(2)], axis=0).T
-        turned = turned.astype(jnp.bfloat16)
-        for m in range(4):
-            x_ref[g * 4 + m] = turned[:, m * 2 * KDIM : (m + 1) * 2 * KDIM]
+    def turn(i, carry):
+        for u in range(4):
+            g = i * 4 + u
+            four = [
+                rows_ref[pl.ds(pl.multiple_of((g * 4 + m) * KDIM, KDIM), KDIM), :]
+                for m in range(4)
+            ]
+            turned = jnp.concatenate([f for f in four for _ in range(2)], axis=0).T
+            turned = turned.astype(jnp.bfloat16)
+            for m in range(4):
+                x_ref[g * 4 + m] = turned[:, m * 2 * KDIM : (m + 1) * 2 * KDIM]
         return carry
 
-    lax.fori_loop(0, CL // 4, turn, 0)
-
-
-def setup_kernel(ids_ref, cnt_ref, tile_ref, here_ref, list_ref, steps_ref, x_ref, cur_ref, rows_ref):
+    lax.fori_loop(0, CL // 16, turn, 0)
+
+
+def setup_kernel(key_ref, here_ref, list_ref, steps_ref, x_ref, cur_ref, rows_ref):
     reader_rows(here_ref, rows_ref, x_ref)
-    tile = tile_ref[0]
-    for k in range(ROUNDS + 1):
+    for k in range(ROUNDS):
         cur_ref[k] = k * REGION
 
     def reader(r, carry):
-        count = cnt_ref[0, r]
         for p in range(PAIRS):
-            q = ids_ref[p, r]
-            d = ((q >> 7) - tile) & (N_TILE - 1)
-            near = jnp.minimum(d, N_TILE - d)
-            k = jnp.where(p < count, near, ROUNDS)
-            slot = jnp.where(d == near, CL, 0)
-            at = cur_ref[k]
-            list_ref[at] = (r << 8) | slot | (q & (CL - 1))
-            cur_ref[k] = at + 1
+            key = key_ref[p, r]
+            k = key >> KEY_SHIFT
+
+            @pl.when(k < ROUNDS)
+            def _():
+                at = cur_ref[k]
+                list_ref[at] = key & ((1 << KEY_SHIFT) - 1)
+                cur_ref[k] = at + 1
+
         return carry
 
     lax.fori_loop(0, CL, reader, 0)
     for k in range(ROUNDS):
-        used = cur_ref[k]
-        steps = (used - k * REGION + (STEP - 1)) >> 4
+        used = cur_ref[k] - k * REGION
+        steps = (used + (STEP - 1)) >> 5
         steps_ref[k] = steps
 
         def pad(at, carry):
-            list_ref[at] = (CL << 8) | CL
+            list_ref[at] = (CL << 9) | CL
             return carry
 
-        lax.fori_loop(used, k * REGION + steps * STEP, pad, 0)
-
-
-def setup(ids, counts, tile, here):
+        lax.fori_loop(k * REGION + used, k * REGION + steps * STEP, pad, 0)
+
+
+def setup(keys, here):
     return pl.pallas_call(
         setup_kernel,
         out_shape=[
-            jax.ShapeDtypeStruct(((ROUNDS + 1) * REGION,), jnp.int32),
+            jax.ShapeDtypeStruct((ROUNDS * REGION,), jnp.int32),
             jax.ShapeDtypeStruct((ROUNDS,), jnp.int32),
             jax.ShapeDtypeStruct((CL, PTS, 2 * KDIM), jnp.bfloat16),
         ],
-        in_specs=[SMEM] * 3 + [VMEM],
+        in_specs=[SMEM, VMEM],
         out_specs=[SMEM] * 2 + [VMEM],
         scratch_shapes=[
-            pltpu.SMEM((ROUNDS + 1,), jnp.int32),
+            pltpu.SMEM((ROUNDS,), jnp.int32),
             pltpu.VMEM((CL * KDIM, PTS), jnp.float32),
         ],
         compiler_params=pltpu.CompilerParams(vmem_limit_bytes=16 * 2**20),
         cost_estimate=pl.CostEstimate(flops=10**6, bytes_accessed=10**7, transcendentals=0),
-    )(ids, counts, tile, here)
-
-
-def prepare(slot, parts, hist_ref, y_ref):
-    base = slot * HIST_ROWS
-    at = 0
-    spots = []
-    for part in parts:
-        rows = part.shape[0]
-        take = min(rows, HIST_ROWS - at)
-        if take > 0:
-            hist_ref[base + at : base + at + take] = part[:take].astype(jnp.float32)
-            at += take
-        for k in range(max(take, 0), rows, CL):
-            spots.append(part[k : k + CL].astype(jnp.float32))
+    )(keys, here)
+
+
+def pair_keys(ids, counts, tile):
+    reader = lax.broadcasted_iota(jnp.int32, ids.shape, 1)
+    entry = lax.broadcasted_iota(jnp.int32, ids.shape, 0)
+    ahead = ((ids >> 7) - tile) & (N_TILE - 1)
+    near = jnp.minimum(ahead, N_TILE - ahead)
+    own = ahead == 0
+    slot = jnp.where(own, 2, jnp.where(ahead == near, 1, 0))
+    turn = jnp.where(own, 1 + lax.rem(reader, ROUNDS - 2), near)
+    turn = jnp.where(entry < counts, turn, ROUNDS)
+    return (turn << KEY_SHIFT) | (reader << 9) | (slot << 7) | (ids & (CL - 1))
+
+
+def source_rows(block, spots, y_ref):
     norm = spots[0] * spots[0] + spots[1] * spots[1] + spots[2] * spots[2]
     one = jnp.ones((CL, PTS), jnp.float32)
     rows = spots + list(split3(-SCALE * norm)) + [one, 0.0 * one]
     for k, row in enumerate(rows):
-        y_ref[pl.ds(base + k, CL, stride=YDIM), :] = row
+        y_ref[pl.ds(block * (CL * YDIM) + k, CL, stride=YDIM), :] = row
 
 
 def pairs(base, steps, list_s, x_ref, hist_ref, y_ref, acc_ref):
@@ -147,31 +151,38 @@
         bottom = jnp.concatenate([zero, other], axis=1)
         return jnp.concatenate([top, bottom], axis=0).astype(jnp.bfloat16)
 
-    def eight(ref, k):
-        return ref[pl.ds(pl.multiple_of(k * 8, 8), 8), :]
+    def source_points(q):
+        y = y_ref[pl.ds(pl.multiple_of(q * YDIM, YDIM), YDIM), :]
+        return jnp.concatenate([y, y], axis=0)
+
+    def source_hist(q):
+        at = pl.multiple_of((q >> 1) * (2 * COLS), 2 * COLS)
+        two = hist_ref[pl.ds(at, 2 * COLS), :].astype(jnp.float32)
+        return jnp.where((q & 1) == 1, two[COLS:], two[:COLS])
 
     def step(i, carry):
         entries = [list_s[base + i * STEP + k] for k in range(STEP)]
-        readers = [e >> 8 for e in entries]
-        sources = [e & (2 * CL - 1) for e in entries]
-        units = [(2 * u, 2 * u + 1) for u in range(UNITS)]
+        readers = [e >> 9 for e in entries]
+        sources = [e & (4 * CL - 1) for e in entries]
+        both = [(2 * u, 2 * u + 1) for u in range(UNITS)]
         weights = []
-        for a, b in units:
+        for a, b in both:
             lhs = jnp.where(first, x_ref[readers[a] & (CL - 1)], x_ref[readers[b] & (CL - 1)])
-            ys = [eight(y_ref, sources[k]) for k in (a, b)]
-            rhs = beside(*[jnp.concatenate([y, y], axis=0) for y in ys], zero_y)
+            rhs = beside(source_points(sources[a]), source_points(sources[b]), zero_y)
             power = jnp.dot(lhs, rhs, preferred_element_type=jnp.float32)
             weights.append(jnp.exp2(power).astype(jnp.bfloat16))
         outs = []
-        for (a, b), weight in zip(units, weights):
-            hs = [eight(hist_ref, sources[k]) for k in (a, b)]
-            both = jnp.concatenate([beside(*hs, zero_h), ones], axis=0)
+        for (a, b), weight in zip(both, weights):
+            hist = beside(source_hist(sources[a]), source_hist(sources[b]), zero_h)
             outs.append(
                 lax.dot_general(
-                    both, weight, (((1,), (1,)), ((), ())), preferred_element_type=jnp.float32
+                    jnp.concatenate([hist, ones], axis=0),
+                    weight,
+                    (((1,), (1,)), ((), ())),
+                    preferred_element_type=jnp.float32,
                 )
             )
-        for unit, out in zip(units, outs):
+        for unit, out in zip(both, outs):
             for half in range(2):
                 at = pl.multiple_of(readers[unit[half]] * (2 * COLS), 2 * COLS)
                 acc_ref[pl.ds(at, COLS), :] += out[half * COLS : (half + 1) * COLS]
@@ -179,6 +190,21 @@
         return carry
 
     lax.fori_loop(0, steps, step, 0)
+
+
+def prepare(slot, parts, hist_ref, y_ref):
+    at = 0
+    spots = []
+    for part in parts:
+        rows = part.shape[0]
+        take = min(rows, HIST_ROWS - at)
+        if take > 0:
+            base = slot * HIST_ROWS + at
+            hist_ref[base : base + take] = part[:take]
+            at += take
+        for k in range(max(take, 0), rows, CL):
+            spots.append(part[k : k + CL].astype(jnp.float32))
+    source_rows(slot, spots, y_ref)
 
 
 def finish(acc_ref, kappa_ref, threshold_ref, disp_ref, brick_ref, damage_ref, shares_ref):
@@ -204,32 +230,32 @@
     )
 
 
-def ring_kernel(round_, sizes, has_acc, final, *refs):
+def ring_kernel(turn, shape, has_acc, final, *refs):
     refs = list(refs)
     take = lambda n: [refs.pop(0) for _ in range(n)]
     steps_s, list_s, x_ref = take(3)
-    blocks = [take(n) for n in sizes]
+    blocks = [(slot, take(n)) for slot, n in shape]
     acc_in = take(1)[0] if has_acc else None
     final_in = take(4) if final else None
     final_out = take(2) if final else None
     acc_ref, hist_ref, y_ref = take(3)
     acc_ref[...] = acc_in[...] if has_acc else jnp.zeros_like(acc_ref)
-    for slot, parts in enumerate(blocks):
-        prepare(slot if len(blocks) == 2 else 1, parts, hist_ref, y_ref)
-    pairs(round_ * REGION, steps_s[round_], list_s, x_ref, hist_ref, y_ref, acc_ref)
+    for slot, parts in blocks:
+        prepare(slot, parts, hist_ref, y_ref)
+    pairs(turn * REGION, steps_s[turn], list_s, x_ref, hist_ref, y_ref, acc_ref)
     if final:
         finish(acc_ref, *final_in, *final_out)
 
 
-def consume(prepared, round_, blocks, acc, final=None):
+def consume(prepared, turn, blocks, acc, final=None):
     lists, steps, x_rows = prepared
-    args = [steps, lists, x_rows] + [part for parts in blocks for part in parts]
+    args = [steps, lists, x_rows] + [part for _, parts in blocks for part in parts]
     if acc is not None:
         args.append(acc)
     acc_shape = (ACC_ROWS, PTS)
     scratch = [
-        pltpu.VMEM((2 * HIST_ROWS, PTS), jnp.float32),
-        pltpu.VMEM((2 * CL * YDIM, PTS), jnp.float32),
+        pltpu.VMEM((3 * HIST_ROWS, PTS), jnp.bfloat16),
+        pltpu.VMEM((3 * CL * YDIM, PTS), jnp.float32),
     ]
     if final is None:
         out_shape = jax.ShapeDtypeStruct(acc_shape, jnp.float32)
@@ -242,9 +268,9 @@
         ]
         out_specs = [VMEM] * 2
         scratch = [pltpu.VMEM(acc_shape, jnp.float32)] + scratch
-    sizes = tuple(len(parts) for parts in blocks)
+    shape = tuple((slot, len(parts)) for slot, parts in blocks)
     return pl.pallas_call(
-        functools.partial(ring_kernel, round_, sizes, acc is not None, final is not None),
+        functools.partial(ring_kernel, turn, shape, acc is not None, final is not None),
         out_shape=out_shape,
         in_specs=[SMEM] * 2 + [VMEM] * (len(args) - 2),
         out_specs=out_specs,
@@ -284,20 +310,25 @@
     )
     tile = lax.axis_index("tile")
     half = own.shape[0] // 2
+    last = N_TILE // 2 - 1
     up, down = hop(own, 1), hop(own, -1)
-    prepared = setup(pair_ids[0].T, reader_counts, tile.astype(jnp.int32).reshape(1), points)
-    acc = consume(prepared, 0, [[own]], None)
-    for s in range(1, N_TILE // 2):
-        up, down, acc = lax.optimization_barrier((up, down, acc))
-        block = [[up], [down]]
-        if s + 1 < N_TILE // 2:
+    keys = pair_keys(pair_ids[0].T, reader_counts, tile)
+    prepared = setup(keys, points)
+    acc = None
+    for s in range(1, last + 1):
+        block = [(0, [up]), (1, [down]), (2, [own])]
+        if acc is None:
+            up, prepared = lax.optimization_barrier((up, prepared))
+        else:
+            up, acc = lax.optimization_barrier((up, acc))
+        if s < last:
             up, down = hop(up, 1), hop(down, -1)
         else:
             far = [hop(up[:half], 1), hop(down[half:], -1)]
         acc = consume(prepared, s, block, acc)
     brick = brick_map - (tile - 1) * BR_DEV
     damage_here, shares = consume(
-        prepared, N_TILE // 2, [far], acc, (kappa_old[0], threshold[0], strain_disp, brick)
+        prepared, last + 1, [(1, far)], acc, (kappa_old[0], threshold[0], strain_disp, brick)
     )
     low, mid, top = shares[:BR_DEV], shares[BR_DEV : 2 * BR_DEV], shares[2 * BR_DEV :]
     force = mid + shifted(top, "tile", 1) + shifted(low, "tile", -1)

time: 155 us -> 133 us (0.86)
  starting transfers between devices: 81.8 us -> 73.2 us
  waiting for transfers between devices: 18.3 us -> 10.9 us
  Pallas kernels: 46.6 us -> 41.3 us
    ppermute x16, waiting for transfers between devices: 10.1 us -> 2.68 us  [hop(): lax.ppermute(block, 'tile', [(i, (i + distance) % peers) for i in range(p...]
    ppermute x4, starting transfers between devices: 20.5 us -> 14.7 us  [shifted(): return lax.ppermute(block, axis, route)]
    pallas_call x10 -> x9, Pallas kernels: 46.6 us -> 41.3 us  [the longest x8 29.2 us: consume(): pl.pallas_call(functools.partial(ring_kernel, turn, shape, acc is not Non...]
    ppermute x16, starting transfers between devices: 61.3 us -> 58.5 us  [hop(): lax.ppermute(block, 'tile', [(i, (i + distance) % peers) for i in range(p...]
    unnamed x20 -> x16, local copies, waits for them, and re-layouts: 4.45 us -> 3.11 us
  transfers between devices with their start and end apart: 20 -> 20, of which waited for: 12 -> 4; matrix products, arithmetic and copies ran while one was open for 0% -> 1% of each run, Pallas kernels for 28% -> 29%
where the time goes in v4:
time: 133 us; the launch traced here: 132 us
  starting transfers between devices  73.2 us (55%)
  Pallas kernels  41.3 us (31%)
  waiting for transfers between devices  10.9 us (8%)
  local copies, waits for them, and re-layouts  3.14 us (2%)
  other arithmetic  1.78 us (1%)
    ppermute x16, starting transfers between devices, hop(): lax.ppermute(block, 'tile', [(i, (i + distance) % peers) for i in range(p...  58.5 us
    pallas_call x8, Pallas kernels, consume(): pl.pallas_call(functools.partial(ring_kernel, turn, shape, acc is not Non...  29.2 us
    ppermute x4, starting transfers between devices, shifted(): return lax.ppermute(block, axis, route)  14.7 us
    pallas_call x1, Pallas kernels, setup(): pl.pallas_call(setup_kernel, out_shape=[jax.ShapeDtypeStruct((ROUNDS * RE...  12.2 us
    ppermute x4, waiting for transfers between devices, shifted(): return lax.ppermute(block, axis, route)  8.21 us
    unnamed x16, local copies, waits for them, and re-layouts  3.11 us
    ppermute x16, waiting for transfers between devices, hop(): lax.ppermute(block, 'tile', [(i, (i + distance) % peers) for i in range(p...  2.68 us
  transfers between devices with their start and end apart: 20, of which 4 were waited for; matrix products, arithmetic and copies ran while one was open for 1% of the time, Pallas kernels for 29%

profile of v4, /device:TPU:7, one launch (start us, length us, event | category | flops | bytes accessed | tf_op | source)
XLA Modules:
  0.0 132.2 jit_solution(4142367507907813574)
XLA Ops:
  0.6 0.0 copy-start
  0.6 1.1 pad_maximum_fusion.refs_5_
  1.7 3.5 %collective-permute-start = (bf16[1408,128]{1,0:T(8,128)(2,1)S(1)}, bf16[1408,128]{1,0:T(8,128)(2,1)S(1)}, u32[]{:S(2)}, u32[]{:S(2)}) collective-permute-start(bf16[1408,128]{1,0:T(8,128)(2,1)S(1)} %pad_maximum_fusion.refs_5_), channel_id=1, source_target_pairs={{0,1},{1,2},{2,3},{3,4},{4,5},{5,6},{6,7},{7,8},{8,9},{9,10},{10,1... | collective-permute-start | bytes 1081352 | tf_op jit(solution)/shard_map/ppermute | solution.py:287
  5.3 9.5 %collective-permute-start.2 = (bf16[1408,128]{1,0:T(8,128)(2,1)S(1)}, bf16[1408,128]{1,0:T(8,128)(2,1)S(1)}, u32[]{:S(2)}, u32[]{:S(2)}) collective-permute-start(bf16[1408,128]{1,0:T(8,128)(2,1)S(1)} %pad_maximum_fusion.refs_5_), channel_id=1, source_target_pairs={{0,15},{1,0},{2,1},{3,2},{4,3},{5,4},{6,5},{7,6},{8,7},{9,8},{10,9... | collective-permute-start | bytes 1081352 | tf_op jit(solution)/shard_map/ppermute | solution.py:287
  14.8 0.7 fusion.10.key_ref
  15.5 0.0 copy-start.3
  15.5 0.9 copy-done.3
  16.4 12.2 %shard_map.104 = (s32[9216]{0:T(1024)S(1)}, s32[9]{0:T(128)S(1)}, bf16[128,128,32]{2,1,0:T(8,128)(2,1)S(1)}) custom-call(s32[8,128]{1,0:T(8,128)S(1)} %fusion.10.key_ref, bf16[3,128,128]{2,1,0:T(8,128)(2,1)S(1)} %bitcast.35), custom_call_target="tpu_custom_call" | custom-call | flops 1000000 | bytes 10000000 | tf_op jit(solution)/shard_map/pallas_call | solution.py:103
  28.6 0.0 copy-start.1
  28.6 0.0 collective-permute-done.refs_3_
  28.6 1.9 %collective-permute-start.1 = (bf16[1408,128]{1,0:T(8,128)(2,1)S(1)}, bf16[1408,128]{1,0:T(8,128)(2,1)S(1)}, u32[]{:S(2)}, u32[]{:S(2)}) collective-permute-start(bf16[1408,128]{1,0:T(8,128)(2,1)S(1)} %collective-permute-done.refs_3_), channel_id=1, source_target_pairs={{0,1},{1,2},{2,3},{3,4},{4,5},{5,6},{6,7},{7,8},{8,9},{9,10},{10,1... | collective-permute-start | bytes 1081352 | tf_op jit(solution)/shard_map/ppermute | solution.py:287
  30.5 0.0 collective-permute-done.2.refs_4_
  30.5 4.6 %collective-permute-start.4 = (bf16[1408,128]{1,0:T(8,128)(2,1)S(1)}, bf16[1408,128]{1,0:T(8,128)(2,1)S(1)}, u32[]{:S(2)}, u32[]{:S(2)}) collective-permute-start(bf16[1408,128]{1,0:T(8,128)(2,1)S(1)} %collective-permute-done.2.refs_4_), channel_id=1, source_target_pairs={{0,15},{1,0},{2,1},{3,2},{4,3},{5,4},{6,5},{7,6},{8,7},{9,8},{10,9... | collective-permute-start | bytes 1081352 | tf_op jit(solution)/shard_map/ppermute | solution.py:287
  35.1 3.9 %shard_map.105.refs_6_ = f32[2064,128]{1,0:T(8,128)S(1)} custom-call(s32[9]{0:T(128)S(1)} %get-tuple-element.26.refs_0_, s32[9216]{0:T(1024)S(1)} %get-tuple-element.27.refs_1_, bf16[128,128,32]{2,1,0:T(8,128)(2,1)S(1)} %get-tuple-element.28.refs_2_, bf16[1408,128]{1,0:T(8,128)(2,1)S(1)} %collective-permute-done.refs_3_, ...), custom_call_target="tpu_custom_call" | custom-call | flops 671088640 | bytes 8388608 | tf_op jit(solution)/shard_map/pallas_call | solution.py:272
  39.0 1.8 %collective-permute-done.1.refs_3_ = bf16[1408,128]{1,0:T(8,128)(2,1)S(1)} collective-permute-done((bf16[1408,128]{1,0:T(8,128)(2,1)S(1)}, bf16[1408,128]{1,0:T(8,128)(2,1)S(1)}, u32[]{:S(2)}, u32[]{:S(2)}) %collective-permute-start.1) | collective-permute-done | bytes 360480 | tf_op jit(solution)/shard_map/ppermute | solution.py:287
  40.8 1.9 %collective-permute-start.3 = (bf16[1408,128]{1,0:T(8,128)(2,1)S(1)}, bf16[1408,128]{1,0:T(8,128)(2,1)S(1)}, u32[]{:S(2)}, u32[]{:S(2)}) collective-permute-start(bf16[1408,128]{1,0:T(8,128)(2,1)S(1)} %collective-permute-done.1.refs_3_), channel_id=1, source_target_pairs={{0,1},{1,2},{2,3},{3,4},{4,5},{5,6},{6,7},{7,8},{8,9},{9,10},{10,1... | collective-permute-start | bytes 1081352 | tf_op jit(solution)/shard_map/ppermute | solution.py:287
  42.7 0.0 collective-permute-done.4.refs_4_
  42.7 4.6 %collective-permute-start.6 = (bf16[1408,128]{1,0:T(8,128)(2,1)S(1)}, bf16[1408,128]{1,0:T(8,128)(2,1)S(1)}, u32[]{:S(2)}, u32[]{:S(2)}) collective-permute-start(bf16[1408,128]{1,0:T(8,128)(2,1)S(1)} %collective-permute-done.4.refs_4_), channel_id=1, source_target_pairs={{0,15},{1,0},{2,1},{3,2},{4,3},{5,4},{6,5},{7,6},{8,7},{9,8},{10,9... | collective-permute-start | bytes 1081352 | tf_op jit(solution)/shard_map/ppermute | solution.py:287
  47.3 3.9 %shard_map.106.refs_6_ = f32[2064,128]{1,0:T(8,128)S(1)} custom-call(s32[9]{0:T(128)S(1)} %get-tuple-element.26.refs_0_, s32[9216]{0:T(1024)S(1)} %get-tuple-element.27.refs_1_, bf16[128,128,32]{2,1,0:T(8,128)(2,1)S(1)} %get-tuple-element.28.refs_2_, bf16[1408,128]{1,0:T(8,128)(2,1)S(1)} %collective-permute-done.1.refs_3_, ...), custom_call_target="tpu_custom_call" | custom-call | flops 671088640 | bytes 8388608 | tf_op jit(solution)/shard_map/pallas_call | solution.py:272
  51.1 0.9 collective-permute-done.3.refs_3_
  52.0 1.9 %collective-permute-start.5 = (bf16[1408,128]{1,0:T(8,128)(2,1)S(1)}, bf16[1408,128]{1,0:T(8,128)(2,1)S(1)}, u32[]{:S(2)}, u32[]{:S(2)}) collective-permute-start(bf16[1408,128]{1,0:T(8,128)(2,1)S(1)} %collective-permute-done.3.refs_3_), channel_id=1, source_target_pairs={{0,1},{1,2},{2,3},{3,4},{4,5},{5,6},{6,7},{7,8},{8,9},{9,10},{10,1... | collective-permute-start | bytes 1081352 | tf_op jit(solution)/shard_map/ppermute | solution.py:287
  53.9 0.0 collective-permute-done.6.refs_4_
  53.9 4.6 %collective-permute-start.8 = (bf16[1408,128]{1,0:T(8,128)(2,1)S(1)}, bf16[1408,128]{1,0:T(8,128)(2,1)S(1)}, u32[]{:S(2)}, u32[]{:S(2)}) collective-permute-start(bf16[1408,128]{1,0:T(8,128)(2,1)S(1)} %collective-permute-done.6.refs_4_), channel_id=1, source_target_pairs={{0,15},{1,0},{2,1},{3,2},{4,3},{5,4},{6,5},{7,6},{8,7},{9,8},{10,9... | collective-permute-start | bytes 1081352 | tf_op jit(solution)/shard_map/ppermute | solution.py:287
  58.5 3.9 %shard_map.107.refs_6_ = f32[2064,128]{1,0:T(8,128)S(1)} custom-call(s32[9]{0:T(128)S(1)} %get-tuple-element.26.refs_0_, s32[9216]{0:T(1024)S(1)} %get-tuple-element.27.refs_1_, bf16[128,128,32]{2,1,0:T(8,128)(2,1)S(1)} %get-tuple-element.28.refs_2_, bf16[1408,128]{1,0:T(8,128)(2,1)S(1)} %collective-permute-done.3.refs_3_, ...), custom_call_target="tpu_custom_call" | custom-call | flops 671088640 | bytes 8388608 | tf_op jit(solution)/shard_map/pallas_call | solution.py:272
  62.4 0.0 collective-permute-done.5.refs_3_
  62.4 1.9 %collective-permute-start.7 = (bf16[1408,128]{1,0:T(8,128)(2,1)S(1)}, bf16[1408,128]{1,0:T(8,128)(2,1)S(1)}, u32[]{:S(2)}, u32[]{:S(2)}) collective-permute-start(bf16[1408,128]{1,0:T(8,128)(2,1)S(1)} %collective-permute-done.5.refs_3_), channel_id=1, source_target_pairs={{0,1},{1,2},{2,3},{3,4},{4,5},{5,6},{6,7},{7,8},{8,9},{9,10},{10,1... | collective-permute-start | bytes 1081352 | tf_op jit(solution)/shard_map/ppermute | solution.py:287
  64.3 0.0 collective-permute-done.8.refs_4_
  64.3 4.6 %collective-permute-start.10 = (bf16[1408,128]{1,0:T(8,128)(2,1)S(1)}, bf16[1408,128]{1,0:T(8,128)(2,1)S(1)}, u32[]{:S(2)}, u32[]{:S(2)}) collective-permute-start(bf16[1408,128]{1,0:T(8,128)(2,1)S(1)} %collective-permute-done.8.refs_4_), channel_id=1, source_target_pairs={{0,15},{1,0},{2,1},{3,2},{4,3},{5,4},{6,5},{7,6},{8,7},{9,8},{10,9... | collective-permute-start | bytes 1081352 | tf_op jit(solution)/shard_map/ppermute | solution.py:287
  68.9 3.9 %shard_map.108.refs_6_ = f32[2064,128]{1,0:T(8,128)S(1)} custom-call(s32[9]{0:T(128)S(1)} %get-tuple-element.26.refs_0_, s32[9216]{0:T(1024)S(1)} %get-tuple-element.27.refs_1_, bf16[128,128,32]{2,1,0:T(8,128)(2,1)S(1)} %get-tuple-element.28.refs_2_, bf16[1408,128]{1,0:T(8,128)(2,1)S(1)} %collective-permute-done.5.refs_3_, ...), custom_call_target="tpu_custom_call" | custom-call | flops 671088640 | bytes 8388608 | tf_op jit(solution)/shard_map/pallas_call | solution.py:272
  72.8 0.0 collective-permute-done.7.refs_3_
  72.8 1.9 %collective-permute-start.9 = (bf16[1408,128]{1,0:T(8,128)(2,1)S(1)}, bf16[1408,128]{1,0:T(8,128)(2,1)S(1)}, u32[]{:S(2)}, u32[]{:S(2)}) collective-permute-start(bf16[1408,128]{1,0:T(8,128)(2,1)S(1)} %collective-permute-done.7.refs_3_), channel_id=1, source_target_pairs={{0,1},{1,2},{2,3},{3,4},{4,5},{5,6},{6,7},{7,8},{8,9},{9,10},{10,1... | collective-permute-start | bytes 1081352 | tf_op jit(solution)/shard_map/ppermute | solution.py:287
  74.7 0.0 collective-permute-done.10.refs_4_
  74.7 4.6 %collective-permute-start.12 = (bf16[1408,128]{1,0:T(8,128)(2,1)S(1)}, bf16[1408,128]{1,0:T(8,128)(2,1)S(1)}, u32[]{:S(2)}, u32[]{:S(2)}) collective-permute-start(bf16[1408,128]{1,0:T(8,128)(2,1)S(1)} %collective-permute-done.10.refs_4_), channel_id=1, source_target_pairs={{0,15},{1,0},{2,1},{3,2},{4,3},{5,4},{6,5},{7,6},{8,7},{9,8},{10,9... | collective-permute-start | bytes 1081352 | tf_op jit(solution)/shard_map/ppermute | solution.py:287
  79.3 0.0 copy-done.1
  79.3 3.1 %shard_map.109.refs_6_ = f32[2064,128]{1,0:T(8,128)S(1)} custom-call(s32[9]{0:T(128)S(1)} %get-tuple-element.26.refs_0_, s32[9216]{0:T(1024)S(1)} %get-tuple-element.27.refs_1_, bf16[128,128,32]{2,1,0:T(8,128)(2,1)S(1)} %get-tuple-element.28.refs_2_, bf16[1408,128]{1,0:T(8,128)(2,1)S(1)} %collective-permute-done.7.refs_3_, ...), custom_call_target="tpu_custom_call" | custom-call | flops 671088640 | bytes 8388608 | tf_op jit(solution)/shard_map/pallas_call | solution.py:272
  82.5 0.0 collective-permute-done.9.refs_3_
  82.5 1.9 %collective-permute-start.11 = (bf16[1408,128]{1,0:T(8,128)(2,1)S(1)}, bf16[1408,128]{1,0:T(8,128)(2,1)S(1)}, u32[]{:S(2)}, u32[]{:S(2)}) collective-permute-start(bf16[1408,128]{1,0:T(8,128)(2,1)S(1)} %collective-permute-done.9.refs_3_), channel_id=1, source_target_pairs={{0,1},{1,2},{2,3},{3,4},{4,5},{5,6},{6,7},{7,8},{8,9},{9,10},{10,1... | collective-permute-start | bytes 1081352 | tf_op jit(solution)/shard_map/ppermute | solution.py:287
  84.4 0.0 collective-permute-done.12.refs_4_
  84.4 4.6 %collective-permute-start.14 = (bf16[1408,128]{1,0:T(8,128)(2,1)S(1)}, bf16[1408,128]{1,0:T(8,128)(2,1)S(1)}, u32[]{:S(2)}, u32[]{:S(2)}) collective-permute-start(bf16[1408,128]{1,0:T(8,128)(2,1)S(1)} %collective-permute-done.12.refs_4_), channel_id=1, source_target_pairs={{0,15},{1,0},{2,1},{3,2},{4,3},{5,4},{6,5},{7,6},{8,7},{9,8},{10,9... | collective-permute-start | bytes 1081352 | tf_op jit(solution)/shard_map/ppermute | solution.py:287
  89.0 0.0 copy-start.2
  89.0 2.2 %copy-done.2 = bf16[128,128,32]{2,1,0:T(8,128)(2,1)S(1)} copy-done((bf16[128,128,32]{2,1,0:T(8,128)(2,1)S(1)}, bf16[128,128,32]{2,1,0:T(8,128)(2,1)}, u32[]{:S(2)}) %copy-start.2) | copy-done | bytes 1048600
  91.2 3.9 %shard_map.110.refs_6_ = f32[2064,128]{1,0:T(8,128)S(1)} custom-call(s32[9]{0:T(128)S(1)} %get-tuple-element.26.refs_0_, s32[9216]{0:T(1024)S(1)} %get-tuple-element.27.refs_1_, bf16[128,128,32]{2,1,0:T(8,128)(2,1)S(1)} %copy-done.2, bf16[1408,128]{1,0:T(8,128)(2,1)S(1)} %collective-permute-done.9.refs_3_, ...), custom_call_target="tpu_custom_call" | custom-call | flops 671088640 | bytes 8388608 | tf_op jit(solution)/shard_map/pallas_call | solution.py:272
  95.1 0.0 collective-permute-done.11.refs_3_
  95.1 1.9 %collective-permute-start.13 = (bf16[704,128]{1,0:T(8,128)(2,1)S(1)}, bf16[704,128]{1,0:T(8,128)(2,1)S(1)}, u32[]{:S(2)}, u32[]{:S(2)}) collective-permute-start(bf16[704,128]{1,0:T(8,128)(2,1)S(1)} %slice.29), channel_id=1, source_target_pairs={{0,1},{1,2},{2,3},{3,4},{4,5},{5,6},{6,7},{7,8},{8,9},{9,10},{10,1... | collective-permute-start | bytes 540680 | tf_op jit(solution)/shard_map/ppermute | solution.py:287
  97.0 0.0 collective-permute-done.14.refs_4_
  97.1 4.6 %collective-permute-start.15 = (bf16[704,128]{1,0:T(8,128)(2,1)S(1)}, bf16[704,128]{1,0:T(8,128)(2,1)S(1)}, u32[]{:S(2)}, u32[]{:S(2)}) collective-permute-start(bf16[704,128]{1,0:T(8,128)(2,1)S(1)} %slice.38), channel_id=1, source_target_pairs={{0,15},{1,0},{2,1},{3,2},{4,3},{5,4},{6,5},{7,6},{8,7},{9,8},{10,9... | collective-permute-start | bytes 540680 | tf_op jit(solution)/shard_map/ppermute | solution.py:287
  101.6 0.0 copy-done.7
  101.7 0.0 copy-start.4
  101.7 0.0 copy-start.5
  101.7 0.0 copy-start.6
  101.7 3.9 %shard_map.111.refs_5_ = f32[2064,128]{1,0:T(8,128)S(1)} custom-call(s32[9]{0:T(128)S(1)} %get-tuple-element.26.refs_0_, s32[9216]{0:T(1024)S(1)} %get-tuple-element.27.refs_1_, bf16[128,128,32]{2,1,0:T(8,128)(2,1)S(1)} %copy-done.2, bf16[1408,128]{1,0:T(8,128)(2,1)S(1)} %collective-permute-done.11.refs_3_, ...), custom_call_target="tpu_custom_call" | custom-call | flops 671088640 | bytes 8388608 | tf_op jit(solution)/shard_map/pallas_call | solution.py:272
  105.6 0.0 collective-permute-done.13.refs_3_
  105.6 0.0 collective-permute-done.15.refs_4_
  105.6 0.0 copy-done.4
  105.6 2.8 %shard_map.112 = (f32[128,128]{1,0:T(8,128)}, f32[96,128]{1,0:T(8,128)S(1)}) custom-call(s32[9]{0:T(128)S(1)} %get-tuple-element.26.refs_0_, s32[9216]{0:T(1024)S(1)} %get-tuple-element.27.refs_1_, bf16[128,128,32]{2,1,0:T(8,128)(2,1)S(1)} %copy-done.2, bf16[704,128]{1,0:T(8,128)(2,1)S(1)} %collective-permute-done.13.refs_3_, ...), custom_call_target="tpu_custom_call" | custom-call | flops 671088640 | bytes 8388608 | tf_op jit(solution)/shard_map/pallas_call | solution.py:272
  108.4 1.3 collective-permute-start.16
  109.7 1.3 collective-permute-start.17
  111.0 0.0 collective-permute-done.16
  111.0 3.2 %collective-permute-done.17 = f32[32,128]{1,0:T(8,128)S(1)} collective-permute-done((f32[32,128]{1,0:T(8,128)S(1)}, f32[32,128]{1,0:T(8,128)S(1)}, u32[]{:S(2)}, u32[]{:S(2)}) %collective-permute-start.17) | collective-permute-done | bytes 16416 | tf_op jit(solution)/shard_map/ppermute | solution.py:293
  114.2 10.2 %collective-permute-start.18 = (f32[1,128]{1,0:T(1,128)S(1)}, f32[1,128]{1,0:T(1,128)S(1)}, u32[]{:S(2)}, u32[]{:S(2)}) collective-permute-start(f32[1,128]{1,0:T(1,128)S(1)} %get-tuple-element.48), channel_id=1, source_target_pairs={{0,16},{16,32},{32,48},{48,64},{64,80},{80,96},{96,112},{112,128},... | collective-permute-start | bytes 1544 | tf_op jit(solution)/shard_map/ppermute | solution.py:293
  124.4 1.9 %collective-permute-start.19 = (f32[1,128]{1,0:T(1,128)S(1)}, f32[1,128]{1,0:T(1,128)S(1)}, u32[]{:S(2)}, u32[]{:S(2)}) collective-permute-start(f32[1,128]{1,0:T(1,128)S(1)} %get-tuple-element.49), channel_id=1, source_target_pairs={{16,0},{32,16},{48,32},{64,48},{80,64},{96,80},{112,96},{128,112},... | collective-permute-start | bytes 1544 | tf_op jit(solution)/shard_map/ppermute | solution.py:293
  126.4 0.0 collective-permute-done.18
  126.4 5.0 %collective-permute-done.19 = f32[1,128]{1,0:T(1,128)S(1)} collective-permute-done((f32[1,128]{1,0:T(1,128)S(1)}, f32[1,128]{1,0:T(1,128)S(1)}, u32[]{:S(2)}, u32[]{:S(2)}) %collective-permute-start.19) | collective-permute-done | bytes 544 | tf_op jit(solution)/shard_map/ppermute | solution.py:293
  131.4 0.8 convolution_add_fusion
  (11 shorter events, 0.1 us)
Async XLA Ops:
  0.6 130.8 %copy-start = (f32[128,128]{1,0:T(8,128)S(1)}, f32[128,128]{1,0:T(8,128)}, u32[]{:S(2)}) copy-start(f32[128,128]{1,0:T(8,128)} %param.17) | copy-start | bytes 196612
  1.7 26.9 %collective-permute-start = (bf16[1408,128]{1,0:T(8,128)(2,1)S(1)}, bf16[1408,128]{1,0:T(8,128)(2,1)S(1)}, u32[]{:S(2)}, u32[]{:S(2)}) collective-permute-start(bf16[1408,128]{1,0:T(8,128)(2,1)S(1)} %pad_maximum_fusion.refs_5_), channel_id=1, source_target_pairs={{0,1},{1,2},{2,3},{3,4},{4,5},{5,6},{6,7},{7,8},{8,9},{9,10},{10,1... | collective-permute-start | bytes 1081352 | tf_op jit(solution)/shard_map/ppermute | solution.py:287
  5.3 25.2 %collective-permute-start.2 = (bf16[1408,128]{1,0:T(8,128)(2,1)S(1)}, bf16[1408,128]{1,0:T(8,128)(2,1)S(1)}, u32[]{:S(2)}, u32[]{:S(2)}) collective-permute-start(bf16[1408,128]{1,0:T(8,128)(2,1)S(1)} %pad_maximum_fusion.refs_5_), channel_id=1, source_target_pairs={{0,15},{1,0},{2,1},{3,2},{4,3},{5,4},{6,5},{7,6},{8,7},{9,8},{10,9... | collective-permute-start | bytes 1081352 | tf_op jit(solution)/shard_map/ppermute | solution.py:287
  15.5 0.9 copy-start.3
  28.6 50.8 %copy-start.1 = (bf16[128,128,32]{2,1,0:T(8,128)(2,1)}, bf16[128,128,32]{2,1,0:T(8,128)(2,1)S(1)}, u32[]{:S(2)}) copy-start(bf16[128,128,32]{2,1,0:T(8,128)(2,1)S(1)} %get-tuple-element.28.refs_2_) | copy-start | bytes 3145732
  28.6 12.2 %collective-permute-start.1 = (bf16[1408,128]{1,0:T(8,128)(2,1)S(1)}, bf16[1408,128]{1,0:T(8,128)(2,1)S(1)}, u32[]{:S(2)}, u32[]{:S(2)}) collective-permute-start(bf16[1408,128]{1,0:T(8,128)(2,1)S(1)} %collective-permute-done.refs_3_), channel_id=1, source_target_pairs={{0,1},{1,2},{2,3},{3,4},{4,5},{5,6},{6,7},{7,8},{8,9},{9,10},{10,1... | collective-permute-start | bytes 1081352 | tf_op jit(solution)/shard_map/ppermute | solution.py:287
  30.5 12.2 %collective-permute-start.4 = (bf16[1408,128]{1,0:T(8,128)(2,1)S(1)}, bf16[1408,128]{1,0:T(8,128)(2,1)S(1)}, u32[]{:S(2)}, u32[]{:S(2)}) collective-permute-start(bf16[1408,128]{1,0:T(8,128)(2,1)S(1)} %collective-permute-done.2.refs_4_), channel_id=1, source_target_pairs={{0,15},{1,0},{2,1},{3,2},{4,3},{5,4},{6,5},{7,6},{8,7},{9,8},{10,9... | collective-permute-start | bytes 1081352 | tf_op jit(solution)/shard_map/ppermute | solution.py:287
  40.8 11.2 %collective-permute-start.3 = (bf16[1408,128]{1,0:T(8,128)(2,1)S(1)}, bf16[1408,128]{1,0:T(8,128)(2,1)S(1)}, u32[]{:S(2)}, u32[]{:S(2)}) collective-permute-start(bf16[1408,128]{1,0:T(8,128)(2,1)S(1)} %collective-permute-done.1.refs_3_), channel_id=1, source_target_pairs={{0,1},{1,2},{2,3},{3,4},{4,5},{5,6},{6,7},{7,8},{8,9},{9,10},{10,1... | collective-permute-start | bytes 1081352 | tf_op jit(solution)/shard_map/ppermute | solution.py:287
  42.7 11.2 %collective-permute-start.6 = (bf16[1408,128]{1,0:T(8,128)(2,1)S(1)}, bf16[1408,128]{1,0:T(8,128)(2,1)S(1)}, u32[]{:S(2)}, u32[]{:S(2)}) collective-permute-start(bf16[1408,128]{1,0:T(8,128)(2,1)S(1)} %collective-permute-done.4.refs_4_), channel_id=1, source_target_pairs={{0,15},{1,0},{2,1},{3,2},{4,3},{5,4},{6,5},{7,6},{8,7},{9,8},{10,9... | collective-permute-start | bytes 1081352 | tf_op jit(solution)/shard_map/ppermute | solution.py:287
  52.0 10.4 %collective-permute-start.5 = (bf16[1408,128]{1,0:T(8,128)(2,1)S(1)}, bf16[1408,128]{1,0:T(8,128)(2,1)S(1)}, u32[]{:S(2)}, u32[]{:S(2)}) collective-permute-start(bf16[1408,128]{1,0:T(8,128)(2,1)S(1)} %collective-permute-done.3.refs_3_), channel_id=1, source_target_pairs={{0,1},{1,2},{2,3},{3,4},{4,5},{5,6},{6,7},{7,8},{8,9},{9,10},{10,1... | collective-permute-start | bytes 1081352 | tf_op jit(solution)/shard_map/ppermute | solution.py:287
  53.9 10.4 %collective-permute-start.8 = (bf16[1408,128]{1,0:T(8,128)(2,1)S(1)}, bf16[1408,128]{1,0:T(8,128)(2,1)S(1)}, u32[]{:S(2)}, u32[]{:S(2)}) collective-permute-start(bf16[1408,128]{1,0:T(8,128)(2,1)S(1)} %collective-permute-done.6.refs_4_), channel_id=1, source_target_pairs={{0,15},{1,0},{2,1},{3,2},{4,3},{5,4},{6,5},{7,6},{8,7},{9,8},{10,9... | collective-permute-start | bytes 1081352 | tf_op jit(solution)/shard_map/ppermute | solution.py:287
  62.4 10.4 %collective-permute-start.7 = (bf16[1408,128]{1,0:T(8,128)(2,1)S(1)}, bf16[1408,128]{1,0:T(8,128)(2,1)S(1)}, u32[]{:S(2)}, u32[]{:S(2)}) collective-permute-start(bf16[1408,128]{1,0:T(8,128)(2,1)S(1)} %collective-permute-done.5.refs_3_), channel_id=1, source_target_pairs={{0,1},{1,2},{2,3},{3,4},{4,5},{5,6},{6,7},{7,8},{8,9},{9,10},{10,1... | collective-permute-start | bytes 1081352 | tf_op jit(solution)/shard_map/ppermute | solution.py:287
  64.3 10.4 %collective-permute-start.10 = (bf16[1408,128]{1,0:T(8,128)(2,1)S(1)}, bf16[1408,128]{1,0:T(8,128)(2,1)S(1)}, u32[]{:S(2)}, u32[]{:S(2)}) collective-permute-start(bf16[1408,128]{1,0:T(8,128)(2,1)S(1)} %collective-permute-done.8.refs_4_), channel_id=1, source_target_pairs={{0,15},{1,0},{2,1},{3,2},{4,3},{5,4},{6,5},{7,6},{8,7},{9,8},{10,9... | collective-permute-start | bytes 1081352 | tf_op jit(solution)/shard_map/ppermute | solution.py:287
  72.8 9.7 %collective-permute-start.9 = (bf16[1408,128]{1,0:T(8,128)(2,1)S(1)}, bf16[1408,128]{1,0:T(8,128)(2,1)S(1)}, u32[]{:S(2)}, u32[]{:S(2)}) collective-permute-start(bf16[1408,128]{1,0:T(8,128)(2,1)S(1)} %collective-permute-done.7.refs_3_), channel_id=1, source_target_pairs={{0,1},{1,2},{2,3},{3,4},{4,5},{5,6},{6,7},{7,8},{8,9},{9,10},{10,1... | collective-permute-start | bytes 1081352 | tf_op jit(solution)/shard_map/ppermute | solution.py:287
  74.7 9.7 %collective-permute-start.12 = (bf16[1408,128]{1,0:T(8,128)(2,1)S(1)}, bf16[1408,128]{1,0:T(8,128)(2,1)S(1)}, u32[]{:S(2)}, u32[]{:S(2)}) collective-permute-start(bf16[1408,128]{1,0:T(8,128)(2,1)S(1)} %collective-permute-done.10.refs_4_), channel_id=1, source_target_pairs={{0,15},{1,0},{2,1},{3,2},{4,3},{5,4},{6,5},{7,6},{8,7},{9,8},{10,9... | collective-permute-start | bytes 1081352 | tf_op jit(solution)/shard_map/ppermute | solution.py:287
  82.5 12.6 %collective-permute-start.11 = (bf16[1408,128]{1,0:T(8,128)(2,1)S(1)}, bf16[1408,128]{1,0:T(8,128)(2,1)S(1)}, u32[]{:S(2)}, u32[]{:S(2)}) collective-permute-start(bf16[1408,128]{1,0:T(8,128)(2,1)S(1)} %collective-permute-done.9.refs_3_), channel_id=1, source_target_pairs={{0,1},{1,2},{2,3},{3,4},{4,5},{5,6},{6,7},{7,8},{8,9},{9,10},{10,1... | collective-permute-start | bytes 1081352 | tf_op jit(solution)/shard_map/ppermute | solution.py:287
  84.4 12.6 %collective-permute-start.14 = (bf16[1408,128]{1,0:T(8,128)(2,1)S(1)}, bf16[1408,128]{1,0:T(8,128)(2,1)S(1)}, u32[]{:S(2)}, u32[]{:S(2)}) collective-permute-start(bf16[1408,128]{1,0:T(8,128)(2,1)S(1)} %collective-permute-done.12.refs_4_), channel_id=1, source_target_pairs={{0,15},{1,0},{2,1},{3,2},{4,3},{5,4},{6,5},{7,6},{8,7},{9,8},{10,9... | collective-permute-start | bytes 1081352 | tf_op jit(solution)/shard_map/ppermute | solution.py:287
  89.0 2.2 %copy-start.2 = (bf16[128,128,32]{2,1,0:T(8,128)(2,1)S(1)}, bf16[128,128,32]{2,1,0:T(8,128)(2,1)}, u32[]{:S(2)}) copy-start(bf16[128,128,32]{2,1,0:T(8,128)(2,1)} %copy-done.1) | copy-start | bytes 3145732
  91.2 10.5 %copy-start.7 = (s32[1,128]{1,0:T(1,128)S(1)}, s32[1,128]{1,0:T(1,128)}, u32[]{:S(2)}) copy-start(s32[1,128]{1,0:T(1,128)} %param.15) | copy-start | bytes 1540
  95.1 10.5 %collective-permute-start.13 = (bf16[704,128]{1,0:T(8,128)(2,1)S(1)}, bf16[704,128]{1,0:T(8,128)(2,1)S(1)}, u32[]{:S(2)}, u32[]{:S(2)}) collective-permute-start(bf16[704,128]{1,0:T(8,128)(2,1)S(1)} %slice.29), channel_id=1, source_target_pairs={{0,1},{1,2},{2,3},{3,4},{4,5},{5,6},{6,7},{7,8},{8,9},{9,10},{10,1... | collective-permute-start | bytes 540680 | tf_op jit(solution)/shard_map/ppermute | solution.py:287
  97.1 8.5 %collective-permute-start.15 = (bf16[704,128]{1,0:T(8,128)(2,1)S(1)}, bf16[704,128]{1,0:T(8,128)(2,1)S(1)}, u32[]{:S(2)}, u32[]{:S(2)}) collective-permute-start(bf16[704,128]{1,0:T(8,128)(2,1)S(1)} %slice.38), channel_id=1, source_target_pairs={{0,15},{1,0},{2,1},{3,2},{4,3},{5,4},{6,5},{7,6},{8,7},{9,8},{10,9... | collective-permute-start | bytes 540680 | tf_op jit(solution)/shard_map/ppermute | solution.py:287
  101.7 3.9 %copy-start.4 = (bf16[1024,128]{1,0:T(8,128)(2,1)S(1)}, bf16[1024,128]{1,0:T(8,128)(2,1)}, u32[]{:S(2)}) copy-start(bf16[1024,128]{1,0:T(8,128)(2,1)} %refs_8_.1) | copy-start | bytes 786436
  101.7 3.9 %copy-start.5 = (f32[1,128,128]{2,1,0:T(8,128)S(1)}, f32[1,128,128]{2,1,0:T(8,128)}, u32[]{:S(2)}) copy-start(f32[1,128,128]{2,1,0:T(8,128)} %param.11) | copy-start | bytes 196612
  101.7 3.9 %copy-start.6 = (f32[1,128,128]{2,1,0:T(8,128)S(1)}, f32[1,128,128]{2,1,0:T(8,128)}, u32[]{:S(2)}) copy-start(f32[1,128,128]{2,1,0:T(8,128)} %param.12) | copy-start | bytes 196612
  108.4 2.6 %collective-permute-start.16 = (f32[32,128]{1,0:T(8,128)S(1)}, f32[32,128]{1,0:T(8,128)S(1)}, u32[]{:S(2)}, u32[]{:S(2)}) collective-permute-start(f32[32,128]{1,0:T(8,128)S(1)} %get-tuple-element.46), channel_id=1, source_target_pairs={{0,1},{1,2},{2,3},{3,4},{4,5},{5,6},{6,7},{7,8},{8,9},{9,10},{10,1... | collective-permute-start | bytes 49160 | tf_op jit(solution)/shard_map/ppermute | solution.py:293
  109.7 4.5 %collective-permute-start.17 = (f32[32,128]{1,0:T(8,128)S(1)}, f32[32,128]{1,0:T(8,128)S(1)}, u32[]{:S(2)}, u32[]{:S(2)}) collective-permute-start(f32[32,128]{1,0:T(8,128)S(1)} %get-tuple-element.47), channel_id=1, source_target_pairs={{1,0},{2,1},{3,2},{4,3},{5,4},{6,5},{7,6},{8,7},{9,8},{10,9},{11,1... | collective-permute-start | bytes 49160 | tf_op jit(solution)/shard_map/ppermute | solution.py:293
  114.2 12.1 %collective-permute-start.18 = (f32[1,128]{1,0:T(1,128)S(1)}, f32[1,128]{1,0:T(1,128)S(1)}, u32[]{:S(2)}, u32[]{:S(2)}) collective-permute-start(f32[1,128]{1,0:T(1,128)S(1)} %get-tuple-element.48), channel_id=1, source_target_pairs={{0,16},{16,32},{32,48},{48,64},{64,80},{80,96},{96,112},{112,128},... | collective-permute-start | bytes 1544 | tf_op jit(solution)/shard_map/ppermute | solution.py:293
  124.4 7.0 %collective-permute-start.19 = (f32[1,128]{1,0:T(1,128)S(1)}, f32[1,128]{1,0:T(1,128)S(1)}, u32[]{:S(2)}, u32[]{:S(2)}) collective-permute-start(f32[1,128]{1,0:T(1,128)S(1)} %get-tuple-element.49), channel_id=1, source_target_pairs={{16,0},{32,16},{48,32},{64,48},{80,64},{96,80},{112,96},{128,112},... | collective-permute-start | bytes 1544 | tf_op jit(solution)/shard_map/ppermute | solution.py:293

commit v5 on v4

--- a/solution.py
+++ b/solution.py
@@ -41,7 +41,7 @@
     return (hi,) + split2(rest)
 
 
-def reader_rows(here_ref, rows_ref, x_ref):
+def reader_rows(here_ref, rows_ref):
     here = [here_ref[k].astype(jnp.float32) for k in range(3)]
     twice = [split2((2.0 * SCALE) * h) for h in here]
     norm = split2(-SCALE * (here[0] * here[0] + here[1] * here[1] + here[2] * here[2]))
@@ -52,42 +52,34 @@
     for k, row in enumerate(rows):
         rows_ref[pl.ds(k, CL, stride=KDIM), :] = row
 
-    def turn(i, carry):
-        for u in range(4):
-            g = i * 4 + u
-            four = [
-                rows_ref[pl.ds(pl.multiple_of((g * 4 + m) * KDIM, KDIM), KDIM), :]
-                for m in range(4)
-            ]
-            turned = jnp.concatenate([f for f in four for _ in range(2)], axis=0).T
-            turned = turned.astype(jnp.bfloat16)
-            for m in range(4):
-                x_ref[g * 4 + m] = turned[:, m * 2 * KDIM : (m + 1) * 2 * KDIM]
-        return carry
-
-    lax.fori_loop(0, CL // 16, turn, 0)
+
+def turn_rows(g, rows_ref, x_ref):
+    four = [rows_ref[pl.ds(pl.multiple_of((g * 4 + m) * KDIM, KDIM), KDIM), :] for m in range(4)]
+    turned = jnp.concatenate([f for f in four for _ in range(2)], axis=0).T
+    turned = turned.astype(jnp.bfloat16)
+    for m in range(4):
+        x_ref[g * 4 + m] = turned[:, m * 2 * KDIM : (m + 1) * 2 * KDIM]
 
 
 def setup_kernel(key_ref, here_ref, list_ref, steps_ref, x_ref, cur_ref, rows_ref):
-    reader_rows(here_ref, rows_ref, x_ref)
+    reader_rows(here_ref, rows_ref)
     for k in range(ROUNDS):
         cur_ref[k] = k * REGION
 
-    def reader(r, carry):
-        for p in range(PAIRS):
-            key = key_ref[p, r]
-            k = key >> KEY_SHIFT
-
-            @pl.when(k < ROUNDS)
-            def _():
+    def sixteen(i, carry):
+        for u in range(4):
+            turn_rows(i * 4 + u, rows_ref, x_ref)
+        for u in range(16):
+            for p in range(PAIRS):
+                key = key_ref[p, i * 16 + u]
+                k = key >> KEY_SHIFT
                 at = cur_ref[k]
                 list_ref[at] = key & ((1 << KEY_SHIFT) - 1)
                 cur_ref[k] = at + 1
-
         return carry
 
-    lax.fori_loop(0, CL, reader, 0)
-    for k in range(ROUNDS):
+    lax.fori_loop(0, CL // 16, sixteen, 0)
+    for k in range(1, ROUNDS):
         used = cur_ref[k] - k * REGION
         steps = (used + (STEP - 1)) >> 5
         steps_ref[k] = steps
@@ -126,7 +118,7 @@
     own = ahead == 0
     slot = jnp.where(own, 2, jnp.where(ahead == near, 1, 0))
     turn = jnp.where(own, 1 + lax.rem(reader, ROUNDS - 2), near)
-    turn = jnp.where(entry < counts, turn, ROUNDS)
+    turn = jnp.where(entry < counts, turn, 0)
     return (turn << KEY_SHIFT) | (reader << 9) | (slot << 7) | (ids & (CL - 1))
 
 
@@ -309,7 +301,6 @@
         [history[0].reshape(HIST_ROWS, PTS), points.reshape(3 * CL, PTS)], axis=0
     )
     tile = lax.axis_index("tile")
-    half = own.shape[0] // 2
     last = N_TILE // 2 - 1
     up, down = hop(own, 1), hop(own, -1)
     keys = pair_keys(pair_ids[0].T, reader_counts, tile)
@@ -324,11 +315,11 @@
         if s < last:
             up, down = hop(up, 1), hop(down, -1)
         else:
-            far = [hop(up[:half], 1), hop(down[half:], -1)]
+            far = hop(up, 1)
         acc = consume(prepared, s, block, acc)
     brick = brick_map - (tile - 1) * BR_DEV
     damage_here, shares = consume(
-        prepared, last + 1, [(1, far)], acc, (kappa_old[0], threshold[0], strain_disp, brick)
+        prepared, last + 1, [(1, [far])], acc, (kappa_old[0], threshold[0], strain_disp, brick)
     )
     low, mid, top = shares[:BR_DEV], shares[BR_DEV : 2 * BR_DEV], shares[2 * BR_DEV :]
     force = mid + shifted(top, "tile", 1) + shifted(low, "tile", -1)

time: 133 us -> 126 us (0.947)
  starting transfers between devices: 73.2 us -> 67.7 us
  Pallas kernels: 41.3 us -> 38 us
  waiting for transfers between devices: 10.9 us -> 13.1 us
    ppermute x16 -> x15, starting transfers between devices: 58.5 us -> 53.9 us  [hop(): lax.ppermute(block, 'tile', [(i, (i + distance) % peers) for i in range(p...]
    pallas_call x1, Pallas kernels: 12.2 us -> 8.79 us  [setup(): pl.pallas_call(setup_kernel, out_shape=[jax.ShapeDtypeStruct((ROUNDS * RE...]
    ppermute x16 -> x15, waiting for transfers between devices: 2.68 us -> 4.87 us  [hop(): lax.ppermute(block, 'tile', [(i, (i + distance) % peers) for i in range(p...]
  transfers between devices with their start and end apart: 20 -> 19, of which waited for: 4 -> 5; matrix products, arithmetic and copies ran while one was open for 1% -> 1% of each run, Pallas kernels for 29% -> 28%
where the time goes in v5:
time: 126 us
  starting transfers between devices  67.7 us (54%)
  Pallas kernels  38 us (30%)
  waiting for transfers between devices  13.1 us (10%)
  local copies, waits for them, and re-layouts  3.11 us (2%)
  other arithmetic  1.78 us (1%)
    ppermute x15, starting transfers between devices, hop(): lax.ppermute(block, 'tile', [(i, (i + distance) % peers) for i in range(p...  53.9 us
    pallas_call x8, Pallas kernels, consume(): pl.pallas_call(functools.partial(ring_kernel, turn, shape, acc is not Non...  29.2 us
    ppermute x4, starting transfers between devices, shifted(): return lax.ppermute(block, axis, route)  13.8 us
    pallas_call x1, Pallas kernels, setup(): pl.pallas_call(setup_kernel, out_shape=[jax.ShapeDtypeStruct((ROUNDS * RE...  8.79 us
    ppermute x4, waiting for transfers between devices, shifted(): return lax.ppermute(block, axis, route)  8.21 us
    ppermute x15, waiting for transfers between devices, hop(): lax.ppermute(block, 'tile', [(i, (i + distance) % peers) for i in range(p...  4.87 us
    unnamed x16, local copies, waits for them, and re-layouts  3.1 us
  transfers between devices with their start and end apart: 19, of which 5 were waited for; matrix products, arithmetic and copies ran while one was open for 1% of the time, Pallas kernels for 28%

profile of v5, /device:TPU:7, one launch (start us, length us, event | category | flops | bytes accessed | tf_op | source)
XLA Modules:
  0.0 125.5 jit_solution(5295957620063371034)
XLA Ops:
  0.6 0.0 copy-start
  0.6 1.1 pad_maximum_fusion.refs_5_
  1.7 3.5 %collective-permute-start = (bf16[1408,128]{1,0:T(8,128)(2,1)S(1)}, bf16[1408,128]{1,0:T(8,128)(2,1)S(1)}, u32[]{:S(2)}, u32[]{:S(2)}) collective-permute-start(bf16[1408,128]{1,0:T(8,128)(2,1)S(1)} %pad_maximum_fusion.refs_5_), channel_id=1, source_target_pairs={{0,1},{1,2},{2,3},{3,4},{4,5},{5,6},{6,7},{7,8},{8,9},{9,10},{10,1... | collective-permute-start | bytes 1081352 | tf_op jit(solution)/shard_map/ppermute | solution.py:279
  5.3 9.5 %collective-permute-start.2 = (bf16[1408,128]{1,0:T(8,128)(2,1)S(1)}, bf16[1408,128]{1,0:T(8,128)(2,1)S(1)}, u32[]{:S(2)}, u32[]{:S(2)}) collective-permute-start(bf16[1408,128]{1,0:T(8,128)(2,1)S(1)} %pad_maximum_fusion.refs_5_), channel_id=1, source_target_pairs={{0,15},{1,0},{2,1},{3,2},{4,3},{5,4},{6,5},{7,6},{8,7},{9,8},{10,9... | collective-permute-start | bytes 1081352 | tf_op jit(solution)/shard_map/ppermute | solution.py:279
  14.8 0.7 fusion.10.key_ref
  15.5 0.0 copy-start.3
  15.5 0.9 copy-done.3
  16.4 8.8 %shard_map.104 = (s32[9216]{0:T(1024)S(1)}, s32[9]{0:T(128)S(1)}, bf16[128,128,32]{2,1,0:T(8,128)(2,1)S(1)}) custom-call(s32[8,128]{1,0:T(8,128)S(1)} %fusion.10.key_ref, bf16[3,128,128]{2,1,0:T(8,128)(2,1)S(1)} %bitcast.35), custom_call_target="tpu_custom_call" | custom-call | flops 1000000 | bytes 10000000 | tf_op jit(solution)/shard_map/pallas_call | solution.py:95
  25.2 0.0 copy-start.1
  25.2 0.0 collective-permute-done.refs_3_
  25.2 1.9 %collective-permute-start.1 = (bf16[1408,128]{1,0:T(8,128)(2,1)S(1)}, bf16[1408,128]{1,0:T(8,128)(2,1)S(1)}, u32[]{:S(2)}, u32[]{:S(2)}) collective-permute-start(bf16[1408,128]{1,0:T(8,128)(2,1)S(1)} %collective-permute-done.refs_3_), channel_id=1, source_target_pairs={{0,1},{1,2},{2,3},{3,4},{4,5},{5,6},{6,7},{7,8},{8,9},{9,10},{10,1... | collective-permute-start | bytes 1081352 | tf_op jit(solution)/shard_map/ppermute | solution.py:279
  27.1 0.0 collective-permute-done.2.refs_4_
  27.1 4.6 %collective-permute-start.4 = (bf16[1408,128]{1,0:T(8,128)(2,1)S(1)}, bf16[1408,128]{1,0:T(8,128)(2,1)S(1)}, u32[]{:S(2)}, u32[]{:S(2)}) collective-permute-start(bf16[1408,128]{1,0:T(8,128)(2,1)S(1)} %collective-permute-done.2.refs_4_), channel_id=1, source_target_pairs={{0,15},{1,0},{2,1},{3,2},{4,3},{5,4},{6,5},{7,6},{8,7},{9,8},{10,9... | collective-permute-start | bytes 1081352 | tf_op jit(solution)/shard_map/ppermute | solution.py:279
  31.7 3.9 %shard_map.105.refs_6_ = f32[2064,128]{1,0:T(8,128)S(1)} custom-call(s32[9]{0:T(128)S(1)} %get-tuple-element.26.refs_0_, s32[9216]{0:T(1024)S(1)} %get-tuple-element.27.refs_1_, bf16[128,128,32]{2,1,0:T(8,128)(2,1)S(1)} %get-tuple-element.28.refs_2_, bf16[1408,128]{1,0:T(8,128)(2,1)S(1)} %collective-permute-done.refs_3_, ...), custom_call_target="tpu_custom_call" | custom-call | flops 671088640 | bytes 8388608 | tf_op jit(solution)/shard_map/pallas_call | solution.py:264
  35.6 1.9 %collective-permute-done.1.refs_3_ = bf16[1408,128]{1,0:T(8,128)(2,1)S(1)} collective-permute-done((bf16[1408,128]{1,0:T(8,128)(2,1)S(1)}, bf16[1408,128]{1,0:T(8,128)(2,1)S(1)}, u32[]{:S(2)}, u32[]{:S(2)}) %collective-permute-start.1) | collective-permute-done | bytes 360480 | tf_op jit(solution)/shard_map/ppermute | solution.py:279
  37.4 1.9 %collective-permute-start.3 = (bf16[1408,128]{1,0:T(8,128)(2,1)S(1)}, bf16[1408,128]{1,0:T(8,128)(2,1)S(1)}, u32[]{:S(2)}, u32[]{:S(2)}) collective-permute-start(bf16[1408,128]{1,0:T(8,128)(2,1)S(1)} %collective-permute-done.1.refs_3_), channel_id=1, source_target_pairs={{0,1},{1,2},{2,3},{3,4},{4,5},{5,6},{6,7},{7,8},{8,9},{9,10},{10,1... | collective-permute-start | bytes 1081352 | tf_op jit(solution)/shard_map/ppermute | solution.py:279
  39.4 0.0 collective-permute-done.4.refs_4_
  39.4 4.6 %collective-permute-start.6 = (bf16[1408,128]{1,0:T(8,128)(2,1)S(1)}, bf16[1408,128]{1,0:T(8,128)(2,1)S(1)}, u32[]{:S(2)}, u32[]{:S(2)}) collective-permute-start(bf16[1408,128]{1,0:T(8,128)(2,1)S(1)} %collective-permute-done.4.refs_4_), channel_id=1, source_target_pairs={{0,15},{1,0},{2,1},{3,2},{4,3},{5,4},{6,5},{7,6},{8,7},{9,8},{10,9... | collective-permute-start | bytes 1081352 | tf_op jit(solution)/shard_map/ppermute | solution.py:279
  44.0 3.1 %shard_map.106.refs_6_ = f32[2064,128]{1,0:T(8,128)S(1)} custom-call(s32[9]{0:T(128)S(1)} %get-tuple-element.26.refs_0_, s32[9216]{0:T(1024)S(1)} %get-tuple-element.27.refs_1_, bf16[128,128,32]{2,1,0:T(8,128)(2,1)S(1)} %get-tuple-element.28.refs_2_, bf16[1408,128]{1,0:T(8,128)(2,1)S(1)} %collective-permute-done.1.refs_3_, ...), custom_call_target="tpu_custom_call" | custom-call | flops 671088640 | bytes 8388608 | tf_op jit(solution)/shard_map/pallas_call | solution.py:264
  47.1 1.7 %collective-permute-done.3.refs_3_ = bf16[1408,128]{1,0:T(8,128)(2,1)S(1)} collective-permute-done((bf16[1408,128]{1,0:T(8,128)(2,1)S(1)}, bf16[1408,128]{1,0:T(8,128)(2,1)S(1)}, u32[]{:S(2)}, u32[]{:S(2)}) %collective-permute-start.3) | collective-permute-done | bytes 360480 | tf_op jit(solution)/shard_map/ppermute | solution.py:279
  48.8 1.9 %collective-permute-start.5 = (bf16[1408,128]{1,0:T(8,128)(2,1)S(1)}, bf16[1408,128]{1,0:T(8,128)(2,1)S(1)}, u32[]{:S(2)}, u32[]{:S(2)}) collective-permute-start(bf16[1408,128]{1,0:T(8,128)(2,1)S(1)} %collective-permute-done.3.refs_3_), channel_id=1, source_target_pairs={{0,1},{1,2},{2,3},{3,4},{4,5},{5,6},{6,7},{7,8},{8,9},{9,10},{10,1... | collective-permute-start | bytes 1081352 | tf_op jit(solution)/shard_map/ppermute | solution.py:279
  50.7 0.0 collective-permute-done.6.refs_4_
  50.7 4.6 %collective-permute-start.8 = (bf16[1408,128]{1,0:T(8,128)(2,1)S(1)}, bf16[1408,128]{1,0:T(8,128)(2,1)S(1)}, u32[]{:S(2)}, u32[]{:S(2)}) collective-permute-start(bf16[1408,128]{1,0:T(8,128)(2,1)S(1)} %collective-permute-done.6.refs_4_), channel_id=1, source_target_pairs={{0,15},{1,0},{2,1},{3,2},{4,3},{5,4},{6,5},{7,6},{8,7},{9,8},{10,9... | collective-permute-start | bytes 1081352 | tf_op jit(solution)/shard_map/ppermute | solution.py:279
  55.3 3.9 %shard_map.107.refs_6_ = f32[2064,128]{1,0:T(8,128)S(1)} custom-call(s32[9]{0:T(128)S(1)} %get-tuple-element.26.refs_0_, s32[9216]{0:T(1024)S(1)} %get-tuple-element.27.refs_1_, bf16[128,128,32]{2,1,0:T(8,128)(2,1)S(1)} %get-tuple-element.28.refs_2_, bf16[1408,128]{1,0:T(8,128)(2,1)S(1)} %collective-permute-done.3.refs_3_, ...), custom_call_target="tpu_custom_call" | custom-call | flops 671088640 | bytes 8388608 | tf_op jit(solution)/shard_map/pallas_call | solution.py:264
  59.1 0.0 collective-permute-done.5.refs_3_
  59.2 1.9 %collective-permute-start.7 = (bf16[1408,128]{1,0:T(8,128)(2,1)S(1)}, bf16[1408,128]{1,0:T(8,128)(2,1)S(1)}, u32[]{:S(2)}, u32[]{:S(2)}) collective-permute-start(bf16[1408,128]{1,0:T(8,128)(2,1)S(1)} %collective-permute-done.5.refs_3_), channel_id=1, source_target_pairs={{0,1},{1,2},{2,3},{3,4},{4,5},{5,6},{6,7},{7,8},{8,9},{9,10},{10,1... | collective-permute-start | bytes 1081352 | tf_op jit(solution)/shard_map/ppermute | solution.py:279
  61.1 0.0 collective-permute-done.8.refs_4_
  61.1 4.6 %collective-permute-start.10 = (bf16[1408,128]{1,0:T(8,128)(2,1)S(1)}, bf16[1408,128]{1,0:T(8,128)(2,1)S(1)}, u32[]{:S(2)}, u32[]{:S(2)}) collective-permute-start(bf16[1408,128]{1,0:T(8,128)(2,1)S(1)} %collective-permute-done.8.refs_4_), channel_id=1, source_target_pairs={{0,15},{1,0},{2,1},{3,2},{4,3},{5,4},{6,5},{7,6},{8,7},{9,8},{10,9... | collective-permute-start | bytes 1081352 | tf_op jit(solution)/shard_map/ppermute | solution.py:279
  65.7 3.9 %shard_map.108.refs_6_ = f32[2064,128]{1,0:T(8,128)S(1)} custom-call(s32[9]{0:T(128)S(1)} %get-tuple-element.26.refs_0_, s32[9216]{0:T(1024)S(1)} %get-tuple-element.27.refs_1_, bf16[128,128,32]{2,1,0:T(8,128)(2,1)S(1)} %get-tuple-element.28.refs_2_, bf16[1408,128]{1,0:T(8,128)(2,1)S(1)} %collective-permute-done.5.refs_3_, ...), custom_call_target="tpu_custom_call" | custom-call | flops 671088640 | bytes 8388608 | tf_op jit(solution)/shard_map/pallas_call | solution.py:264
  69.6 0.0 collective-permute-done.7.refs_3_
  69.6 1.9 %collective-permute-start.9 = (bf16[1408,128]{1,0:T(8,128)(2,1)S(1)}, bf16[1408,128]{1,0:T(8,128)(2,1)S(1)}, u32[]{:S(2)}, u32[]{:S(2)}) collective-permute-start(bf16[1408,128]{1,0:T(8,128)(2,1)S(1)} %collective-permute-done.7.refs_3_), channel_id=1, source_target_pairs={{0,1},{1,2},{2,3},{3,4},{4,5},{5,6},{6,7},{7,8},{8,9},{9,10},{10,1... | collective-permute-start | bytes 1081352 | tf_op jit(solution)/shard_map/ppermute | solution.py:279
  71.5 0.0 collective-permute-done.10.refs_4_
  71.5 4.6 %collective-permute-start.12 = (bf16[1408,128]{1,0:T(8,128)(2,1)S(1)}, bf16[1408,128]{1,0:T(8,128)(2,1)S(1)}, u32[]{:S(2)}, u32[]{:S(2)}) collective-permute-start(bf16[1408,128]{1,0:T(8,128)(2,1)S(1)} %collective-permute-done.10.refs_4_), channel_id=1, source_target_pairs={{0,15},{1,0},{2,1},{3,2},{4,3},{5,4},{6,5},{7,6},{8,7},{9,8},{10,9... | collective-permute-start | bytes 1081352 | tf_op jit(solution)/shard_map/ppermute | solution.py:279
  76.1 3.9 %shard_map.109.refs_6_ = f32[2064,128]{1,0:T(8,128)S(1)} custom-call(s32[9]{0:T(128)S(1)} %get-tuple-element.26.refs_0_, s32[9216]{0:T(1024)S(1)} %get-tuple-element.27.refs_1_, bf16[128,128,32]{2,1,0:T(8,128)(2,1)S(1)} %get-tuple-element.28.refs_2_, bf16[1408,128]{1,0:T(8,128)(2,1)S(1)} %collective-permute-done.7.refs_3_, ...), custom_call_target="tpu_custom_call" | custom-call | flops 671088640 | bytes 8388608 | tf_op jit(solution)/shard_map/pallas_call | solution.py:264
  80.0 0.0 copy-start.7
  80.0 0.0 collective-permute-done.9.refs_3_
  80.0 1.9 %collective-permute-start.11 = (bf16[1408,128]{1,0:T(8,128)(2,1)S(1)}, bf16[1408,128]{1,0:T(8,128)(2,1)S(1)}, u32[]{:S(2)}, u32[]{:S(2)}) collective-permute-start(bf16[1408,128]{1,0:T(8,128)(2,1)S(1)} %collective-permute-done.9.refs_3_), channel_id=1, source_target_pairs={{0,1},{1,2},{2,3},{3,4},{4,5},{5,6},{6,7},{7,8},{8,9},{9,10},{10,1... | collective-permute-start | bytes 1081352 | tf_op jit(solution)/shard_map/ppermute | solution.py:279
  81.9 0.0 collective-permute-done.12.refs_4_
  81.9 4.6 %collective-permute-start.14 = (bf16[1408,128]{1,0:T(8,128)(2,1)S(1)}, bf16[1408,128]{1,0:T(8,128)(2,1)S(1)}, u32[]{:S(2)}, u32[]{:S(2)}) collective-permute-start(bf16[1408,128]{1,0:T(8,128)(2,1)S(1)} %collective-permute-done.12.refs_4_), channel_id=1, source_target_pairs={{0,15},{1,0},{2,1},{3,2},{4,3},{5,4},{6,5},{7,6},{8,7},{9,8},{10,9... | collective-permute-start | bytes 1081352 | tf_op jit(solution)/shard_map/ppermute | solution.py:279
  86.5 0.0 copy-done.1
  86.5 3.9 %shard_map.110.refs_6_ = f32[2064,128]{1,0:T(8,128)S(1)} custom-call(s32[9]{0:T(128)S(1)} %get-tuple-element.26.refs_0_, s32[9216]{0:T(1024)S(1)} %get-tuple-element.27.refs_1_, bf16[128,128,32]{2,1,0:T(8,128)(2,1)S(1)} %get-tuple-element.28.refs_2_, bf16[1408,128]{1,0:T(8,128)(2,1)S(1)} %collective-permute-done.9.refs_3_, ...), custom_call_target="tpu_custom_call" | custom-call | flops 671088640 | bytes 8388608 | tf_op jit(solution)/shard_map/pallas_call | solution.py:264
  90.4 0.0 collective-permute-done.11.refs_3_
  90.4 1.9 %collective-permute-start.13 = (bf16[1408,128]{1,0:T(8,128)(2,1)S(1)}, bf16[1408,128]{1,0:T(8,128)(2,1)S(1)}, u32[]{:S(2)}, u32[]{:S(2)}) collective-permute-start(bf16[1408,128]{1,0:T(8,128)(2,1)S(1)} %collective-permute-done.11.refs_3_), channel_id=1, source_target_pairs={{0,1},{1,2},{2,3},{3,4},{4,5},{5,6},{6,7},{7,8},{8,9},{9,10},{10,1... | collective-permute-start | bytes 1081352 | tf_op jit(solution)/shard_map/ppermute | solution.py:279
  92.4 0.0 copy-done.7
  92.4 0.0 collective-permute-done.14.refs_4_
  92.4 0.0 copy-start.2
  92.4 2.2 %copy-done.2 = bf16[128,128,32]{2,1,0:T(8,128)(2,1)S(1)} copy-done((bf16[128,128,32]{2,1,0:T(8,128)(2,1)S(1)}, bf16[128,128,32]{2,1,0:T(8,128)(2,1)}, u32[]{:S(2)}) %copy-start.2) | copy-done | bytes 1048600
  94.6 0.0 copy-start.4
  94.6 3.9 %shard_map.111.refs_4_ = f32[2064,128]{1,0:T(8,128)S(1)} custom-call(s32[9]{0:T(128)S(1)} %get-tuple-element.26.refs_0_, s32[9216]{0:T(1024)S(1)} %get-tuple-element.27.refs_1_, bf16[128,128,32]{2,1,0:T(8,128)(2,1)S(1)} %copy-done.2, bf16[1408,128]{1,0:T(8,128)(2,1)S(1)} %collective-permute-done.11.refs_3_, ...), custom_call_target="tpu_custom_call" | custom-call | flops 671088640 | bytes 8388608 | tf_op jit(solution)/shard_map/pallas_call | solution.py:264
  98.5 1.3 %collective-permute-done.13.refs_3_ = bf16[1408,128]{1,0:T(8,128)(2,1)S(1)} collective-permute-done((bf16[1408,128]{1,0:T(8,128)(2,1)S(1)}, bf16[1408,128]{1,0:T(8,128)(2,1)S(1)}, u32[]{:S(2)}, u32[]{:S(2)}) %collective-permute-start.13) | collective-permute-done | bytes 360480 | tf_op jit(solution)/shard_map/ppermute | solution.py:279
  99.8 0.0 copy-done.4
  99.8 0.0 copy-done.5
  99.8 0.0 copy-done.6
  99.8 2.8 %shard_map.112 = (f32[128,128]{1,0:T(8,128)}, f32[96,128]{1,0:T(8,128)S(1)}) custom-call(s32[9]{0:T(128)S(1)} %get-tuple-element.26.refs_0_, s32[9216]{0:T(1024)S(1)} %get-tuple-element.27.refs_1_, bf16[128,128,32]{2,1,0:T(8,128)(2,1)S(1)} %copy-done.2, bf16[1408,128]{1,0:T(8,128)(2,1)S(1)} %collective-permute-done.13.refs_3_, ...), custom_call_target="tpu_custom_call" | custom-call | flops 671088640 | bytes 8388608 | tf_op jit(solution)/shard_map/pallas_call | solution.py:264
  102.6 1.3 %collective-permute-start.15 = (f32[32,128]{1,0:T(8,128)S(1)}, f32[32,128]{1,0:T(8,128)S(1)}, u32[]{:S(2)}, u32[]{:S(2)}) collective-permute-start(f32[32,128]{1,0:T(8,128)S(1)} %get-tuple-element.46), channel_id=1, source_target_pairs={{0,1},{1,2},{2,3},{3,4},{4,5},{5,6},{6,7},{7,8},{8,9},{9,10},{10,1... | collective-permute-start | bytes 49160 | tf_op jit(solution)/shard_map/ppermute | solution.py:285
  103.9 1.3 %collective-permute-start.16 = (f32[32,128]{1,0:T(8,128)S(1)}, f32[32,128]{1,0:T(8,128)S(1)}, u32[]{:S(2)}, u32[]{:S(2)}) collective-permute-start(f32[32,128]{1,0:T(8,128)S(1)} %get-tuple-element.47), channel_id=1, source_target_pairs={{1,0},{2,1},{3,2},{4,3},{5,4},{6,5},{7,6},{8,7},{9,8},{10,9},{11,1... | collective-permute-start | bytes 49160 | tf_op jit(solution)/shard_map/ppermute | solution.py:285
  105.2 0.0 collective-permute-done.15
  105.2 3.2 %collective-permute-done.16 = f32[32,128]{1,0:T(8,128)S(1)} collective-permute-done((f32[32,128]{1,0:T(8,128)S(1)}, f32[32,128]{1,0:T(8,128)S(1)}, u32[]{:S(2)}, u32[]{:S(2)}) %collective-permute-start.16) | collective-permute-done | bytes 16416 | tf_op jit(solution)/shard_map/ppermute | solution.py:285
  108.4 9.4 %collective-permute-start.17 = (f32[1,128]{1,0:T(1,128)S(1)}, f32[1,128]{1,0:T(1,128)S(1)}, u32[]{:S(2)}, u32[]{:S(2)}) collective-permute-start(f32[1,128]{1,0:T(1,128)S(1)} %get-tuple-element.48), channel_id=1, source_target_pairs={{0,16},{16,32},{32,48},{48,64},{64,80},{80,96},{96,112},{112,128},... | collective-permute-start | bytes 1544 | tf_op jit(solution)/shard_map/ppermute | solution.py:285
  117.8 1.9 %collective-permute-start.18 = (f32[1,128]{1,0:T(1,128)S(1)}, f32[1,128]{1,0:T(1,128)S(1)}, u32[]{:S(2)}, u32[]{:S(2)}) collective-permute-start(f32[1,128]{1,0:T(1,128)S(1)} %get-tuple-element.49), channel_id=1, source_target_pairs={{16,0},{32,16},{48,32},{64,48},{80,64},{96,80},{112,96},{128,112},... | collective-permute-start | bytes 1544 | tf_op jit(solution)/shard_map/ppermute | solution.py:285
  119.7 0.0 collective-permute-done.17
  119.7 5.0 %collective-permute-done.18 = f32[1,128]{1,0:T(1,128)S(1)} collective-permute-done((f32[1,128]{1,0:T(1,128)S(1)}, f32[1,128]{1,0:T(1,128)S(1)}, u32[]{:S(2)}, u32[]{:S(2)}) %collective-permute-start.18) | collective-permute-done | bytes 544 | tf_op jit(solution)/shard_map/ppermute | solution.py:285
  124.8 0.0 copy-done
  124.8 0.8 convolution_add_fusion
  (7 shorter events, 0.0 us)
Async XLA Ops:
  0.6 124.1 %copy-start = (f32[128,128]{1,0:T(8,128)S(1)}, f32[128,128]{1,0:T(8,128)}, u32[]{:S(2)}) copy-start(f32[128,128]{1,0:T(8,128)} %param.17) | copy-start | bytes 196612
  1.7 23.5 %collective-permute-start = (bf16[1408,128]{1,0:T(8,128)(2,1)S(1)}, bf16[1408,128]{1,0:T(8,128)(2,1)S(1)}, u32[]{:S(2)}, u32[]{:S(2)}) collective-permute-start(bf16[1408,128]{1,0:T(8,128)(2,1)S(1)} %pad_maximum_fusion.refs_5_), channel_id=1, source_target_pairs={{0,1},{1,2},{2,3},{3,4},{4,5},{5,6},{6,7},{7,8},{8,9},{9,10},{10,1... | collective-permute-start | bytes 1081352 | tf_op jit(solution)/shard_map/ppermute | solution.py:279
  5.3 21.9 %collective-permute-start.2 = (bf16[1408,128]{1,0:T(8,128)(2,1)S(1)}, bf16[1408,128]{1,0:T(8,128)(2,1)S(1)}, u32[]{:S(2)}, u32[]{:S(2)}) collective-permute-start(bf16[1408,128]{1,0:T(8,128)(2,1)S(1)} %pad_maximum_fusion.refs_5_), channel_id=1, source_target_pairs={{0,15},{1,0},{2,1},{3,2},{4,3},{5,4},{6,5},{7,6},{8,7},{9,8},{10,9... | collective-permute-start | bytes 1081352 | tf_op jit(solution)/shard_map/ppermute | solution.py:279
  15.5 0.9 copy-start.3
  25.2 61.3 %copy-start.1 = (bf16[128,128,32]{2,1,0:T(8,128)(2,1)}, bf16[128,128,32]{2,1,0:T(8,128)(2,1)S(1)}, u32[]{:S(2)}) copy-start(bf16[128,128,32]{2,1,0:T(8,128)(2,1)S(1)} %get-tuple-element.28.refs_2_) | copy-start | bytes 3145732
  25.2 12.2 %collective-permute-start.1 = (bf16[1408,128]{1,0:T(8,128)(2,1)S(1)}, bf16[1408,128]{1,0:T(8,128)(2,1)S(1)}, u32[]{:S(2)}, u32[]{:S(2)}) collective-permute-start(bf16[1408,128]{1,0:T(8,128)(2,1)S(1)} %collective-permute-done.refs_3_), channel_id=1, source_target_pairs={{0,1},{1,2},{2,3},{3,4},{4,5},{5,6},{6,7},{7,8},{8,9},{9,10},{10,1... | collective-permute-start | bytes 1081352 | tf_op jit(solution)/shard_map/ppermute | solution.py:279
  27.1 12.2 %collective-permute-start.4 = (bf16[1408,128]{1,0:T(8,128)(2,1)S(1)}, bf16[1408,128]{1,0:T(8,128)(2,1)S(1)}, u32[]{:S(2)}, u32[]{:S(2)}) collective-permute-start(bf16[1408,128]{1,0:T(8,128)(2,1)S(1)} %collective-permute-done.2.refs_4_), channel_id=1, source_target_pairs={{0,15},{1,0},{2,1},{3,2},{4,3},{5,4},{6,5},{7,6},{8,7},{9,8},{10,9... | collective-permute-start | bytes 1081352 | tf_op jit(solution)/shard_map/ppermute | solution.py:279
  37.4 11.3 %collective-permute-start.3 = (bf16[1408,128]{1,0:T(8,128)(2,1)S(1)}, bf16[1408,128]{1,0:T(8,128)(2,1)S(1)}, u32[]{:S(2)}, u32[]{:S(2)}) collective-permute-start(bf16[1408,128]{1,0:T(8,128)(2,1)S(1)} %collective-permute-done.1.refs_3_), channel_id=1, source_target_pairs={{0,1},{1,2},{2,3},{3,4},{4,5},{5,6},{6,7},{7,8},{8,9},{9,10},{10,1... | collective-permute-start | bytes 1081352 | tf_op jit(solution)/shard_map/ppermute | solution.py:279
  39.4 11.3 %collective-permute-start.6 = (bf16[1408,128]{1,0:T(8,128)(2,1)S(1)}, bf16[1408,128]{1,0:T(8,128)(2,1)S(1)}, u32[]{:S(2)}, u32[]{:S(2)}) collective-permute-start(bf16[1408,128]{1,0:T(8,128)(2,1)S(1)} %collective-permute-done.4.refs_4_), channel_id=1, source_target_pairs={{0,15},{1,0},{2,1},{3,2},{4,3},{5,4},{6,5},{7,6},{8,7},{9,8},{10,9... | collective-permute-start | bytes 1081352 | tf_op jit(solution)/shard_map/ppermute | solution.py:279
  48.8 10.4 %collective-permute-start.5 = (bf16[1408,128]{1,0:T(8,128)(2,1)S(1)}, bf16[1408,128]{1,0:T(8,128)(2,1)S(1)}, u32[]{:S(2)}, u32[]{:S(2)}) collective-permute-start(bf16[1408,128]{1,0:T(8,128)(2,1)S(1)} %collective-permute-done.3.refs_3_), channel_id=1, source_target_pairs={{0,1},{1,2},{2,3},{3,4},{4,5},{5,6},{6,7},{7,8},{8,9},{9,10},{10,1... | collective-permute-start | bytes 1081352 | tf_op jit(solution)/shard_map/ppermute | solution.py:279
  50.7 10.4 %collective-permute-start.8 = (bf16[1408,128]{1,0:T(8,128)(2,1)S(1)}, bf16[1408,128]{1,0:T(8,128)(2,1)S(1)}, u32[]{:S(2)}, u32[]{:S(2)}) collective-permute-start(bf16[1408,128]{1,0:T(8,128)(2,1)S(1)} %collective-permute-done.6.refs_4_), channel_id=1, source_target_pairs={{0,15},{1,0},{2,1},{3,2},{4,3},{5,4},{6,5},{7,6},{8,7},{9,8},{10,9... | collective-permute-start | bytes 1081352 | tf_op jit(solution)/shard_map/ppermute | solution.py:279
  59.2 10.4 %collective-permute-start.7 = (bf16[1408,128]{1,0:T(8,128)(2,1)S(1)}, bf16[1408,128]{1,0:T(8,128)(2,1)S(1)}, u32[]{:S(2)}, u32[]{:S(2)}) collective-permute-start(bf16[1408,128]{1,0:T(8,128)(2,1)S(1)} %collective-permute-done.5.refs_3_), channel_id=1, source_target_pairs={{0,1},{1,2},{2,3},{3,4},{4,5},{5,6},{6,7},{7,8},{8,9},{9,10},{10,1... | collective-permute-start | bytes 1081352 | tf_op jit(solution)/shard_map/ppermute | solution.py:279
  61.1 10.4 %collective-permute-start.10 = (bf16[1408,128]{1,0:T(8,128)(2,1)S(1)}, bf16[1408,128]{1,0:T(8,128)(2,1)S(1)}, u32[]{:S(2)}, u32[]{:S(2)}) collective-permute-start(bf16[1408,128]{1,0:T(8,128)(2,1)S(1)} %collective-permute-done.8.refs_4_), channel_id=1, source_target_pairs={{0,15},{1,0},{2,1},{3,2},{4,3},{5,4},{6,5},{7,6},{8,7},{9,8},{10,9... | collective-permute-start | bytes 1081352 | tf_op jit(solution)/shard_map/ppermute | solution.py:279
  69.6 10.4 %collective-permute-start.9 = (bf16[1408,128]{1,0:T(8,128)(2,1)S(1)}, bf16[1408,128]{1,0:T(8,128)(2,1)S(1)}, u32[]{:S(2)}, u32[]{:S(2)}) collective-permute-start(bf16[1408,128]{1,0:T(8,128)(2,1)S(1)} %collective-permute-done.7.refs_3_), channel_id=1, source_target_pairs={{0,1},{1,2},{2,3},{3,4},{4,5},{5,6},{6,7},{7,8},{8,9},{9,10},{10,1... | collective-permute-start | bytes 1081352 | tf_op jit(solution)/shard_map/ppermute | solution.py:279
  71.5 10.4 %collective-permute-start.12 = (bf16[1408,128]{1,0:T(8,128)(2,1)S(1)}, bf16[1408,128]{1,0:T(8,128)(2,1)S(1)}, u32[]{:S(2)}, u32[]{:S(2)}) collective-permute-start(bf16[1408,128]{1,0:T(8,128)(2,1)S(1)} %collective-permute-done.10.refs_4_), channel_id=1, source_target_pairs={{0,15},{1,0},{2,1},{3,2},{4,3},{5,4},{6,5},{7,6},{8,7},{9,8},{10,9... | collective-permute-start | bytes 1081352 | tf_op jit(solution)/shard_map/ppermute | solution.py:279
  80.0 12.4 %copy-start.7 = (s32[1,128]{1,0:T(1,128)S(1)}, s32[1,128]{1,0:T(1,128)}, u32[]{:S(2)}) copy-start(s32[1,128]{1,0:T(1,128)} %param.15) | copy-start | bytes 1540
  80.0 10.4 %collective-permute-start.11 = (bf16[1408,128]{1,0:T(8,128)(2,1)S(1)}, bf16[1408,128]{1,0:T(8,128)(2,1)S(1)}, u32[]{:S(2)}, u32[]{:S(2)}) collective-permute-start(bf16[1408,128]{1,0:T(8,128)(2,1)S(1)} %collective-permute-done.9.refs_3_), channel_id=1, source_target_pairs={{0,1},{1,2},{2,3},{3,4},{4,5},{5,6},{6,7},{7,8},{8,9},{9,10},{10,1... | collective-permute-start | bytes 1081352 | tf_op jit(solution)/shard_map/ppermute | solution.py:279
  81.9 10.4 %collective-permute-start.14 = (bf16[1408,128]{1,0:T(8,128)(2,1)S(1)}, bf16[1408,128]{1,0:T(8,128)(2,1)S(1)}, u32[]{:S(2)}, u32[]{:S(2)}) collective-permute-start(bf16[1408,128]{1,0:T(8,128)(2,1)S(1)} %collective-permute-done.12.refs_4_), channel_id=1, source_target_pairs={{0,15},{1,0},{2,1},{3,2},{4,3},{5,4},{6,5},{7,6},{8,7},{9,8},{10,9... | collective-permute-start | bytes 1081352 | tf_op jit(solution)/shard_map/ppermute | solution.py:279
  90.4 9.4 %collective-permute-start.13 = (bf16[1408,128]{1,0:T(8,128)(2,1)S(1)}, bf16[1408,128]{1,0:T(8,128)(2,1)S(1)}, u32[]{:S(2)}, u32[]{:S(2)}) collective-permute-start(bf16[1408,128]{1,0:T(8,128)(2,1)S(1)} %collective-permute-done.11.refs_3_), channel_id=1, source_target_pairs={{0,1},{1,2},{2,3},{3,4},{4,5},{5,6},{6,7},{7,8},{8,9},{9,10},{10,1... | collective-permute-start | bytes 1081352 | tf_op jit(solution)/shard_map/ppermute | solution.py:279
  92.4 2.2 %copy-start.2 = (bf16[128,128,32]{2,1,0:T(8,128)(2,1)S(1)}, bf16[128,128,32]{2,1,0:T(8,128)(2,1)}, u32[]{:S(2)}) copy-start(bf16[128,128,32]{2,1,0:T(8,128)(2,1)} %copy-done.1) | copy-start | bytes 3145732
  94.6 5.2 %copy-start.4 = (bf16[1024,128]{1,0:T(8,128)(2,1)S(1)}, bf16[1024,128]{1,0:T(8,128)(2,1)}, u32[]{:S(2)}) copy-start(bf16[1024,128]{1,0:T(8,128)(2,1)} %refs_7_.1) | copy-start | bytes 786436
  94.6 5.2 %copy-start.5 = (f32[1,128,128]{2,1,0:T(8,128)S(1)}, f32[1,128,128]{2,1,0:T(8,128)}, u32[]{:S(2)}) copy-start(f32[1,128,128]{2,1,0:T(8,128)} %param.11) | copy-start | bytes 196612
  94.6 5.2 %copy-start.6 = (f32[1,128,128]{2,1,0:T(8,128)S(1)}, f32[1,128,128]{2,1,0:T(8,128)}, u32[]{:S(2)}) copy-start(f32[1,128,128]{2,1,0:T(8,128)} %param.12) | copy-start | bytes 196612
  102.6 2.6 %collective-permute-start.15 = (f32[32,128]{1,0:T(8,128)S(1)}, f32[32,128]{1,0:T(8,128)S(1)}, u32[]{:S(2)}, u32[]{:S(2)}) collective-permute-start(f32[32,128]{1,0:T(8,128)S(1)} %get-tuple-element.46), channel_id=1, source_target_pairs={{0,1},{1,2},{2,3},{3,4},{4,5},{5,6},{6,7},{7,8},{8,9},{9,10},{10,1... | collective-permute-start | bytes 49160 | tf_op jit(solution)/shard_map/ppermute | solution.py:285
  103.9 4.5 %collective-permute-start.16 = (f32[32,128]{1,0:T(8,128)S(1)}, f32[32,128]{1,0:T(8,128)S(1)}, u32[]{:S(2)}, u32[]{:S(2)}) collective-permute-start(f32[32,128]{1,0:T(8,128)S(1)} %get-tuple-element.47), channel_id=1, source_target_pairs={{1,0},{2,1},{3,2},{4,3},{5,4},{6,5},{7,6},{8,7},{9,8},{10,9},{11,1... | collective-permute-start | bytes 49160 | tf_op jit(solution)/shard_map/ppermute | solution.py:285
  108.4 11.3 %collective-permute-start.17 = (f32[1,128]{1,0:T(1,128)S(1)}, f32[1,128]{1,0:T(1,128)S(1)}, u32[]{:S(2)}, u32[]{:S(2)}) collective-permute-start(f32[1,128]{1,0:T(1,128)S(1)} %get-tuple-element.48), channel_id=1, source_target_pairs={{0,16},{16,32},{32,48},{48,64},{64,80},{80,96},{96,112},{112,128},... | collective-permute-start | bytes 1544 | tf_op jit(solution)/shard_map/ppermute | solution.py:285
  117.8 7.0 %collective-permute-start.18 = (f32[1,128]{1,0:T(1,128)S(1)}, f32[1,128]{1,0:T(1,128)S(1)}, u32[]{:S(2)}, u32[]{:S(2)}) collective-permute-start(f32[1,128]{1,0:T(1,128)S(1)} %get-tuple-element.49), channel_id=1, source_target_pairs={{16,0},{32,16},{48,32},{64,48},{80,64},{96,80},{112,96},{128,112},... | collective-permute-start | bytes 1544 | tf_op jit(solution)/shard_map/ppermute | solution.py:285

commit v6 on v5

--- a/solution.py
+++ b/solution.py
@@ -23,6 +23,7 @@
 ROUNDS = N_TILE // 2 + 1
 REGION = CL * PAIRS
 KEY_SHIFT = 20
+OWN_ROUNDS = 3
 YDIM = 8
 KDIM = 2 * YDIM
 HIST_ROWS = CL * COLS
@@ -42,7 +43,10 @@
 
 
 def reader_rows(here_ref, rows_ref):
-    here = [here_ref[k].astype(jnp.float32) for k in range(3)]
+    here = [
+        here_ref[HIST_ROWS + k * CL : HIST_ROWS + (k + 1) * CL].astype(jnp.float32)
+        for k in range(3)
+    ]
     twice = [split2((2.0 * SCALE) * h) for h in here]
     norm = split2(-SCALE * (here[0] * here[0] + here[1] * here[1] + here[2] * here[2]))
     one = jnp.ones((CL, PTS), jnp.float32)
@@ -91,7 +95,7 @@
         lax.fori_loop(k * REGION + used, k * REGION + steps * STEP, pad, 0)
 
 
-def setup(keys, here):
+def setup(keys, own):
     return pl.pallas_call(
         setup_kernel,
         out_shape=[
@@ -107,7 +111,7 @@
         ],
         compiler_params=pltpu.CompilerParams(vmem_limit_bytes=16 * 2**20),
         cost_estimate=pl.CostEstimate(flops=10**6, bytes_accessed=10**7, transcendentals=0),
-    )(keys, here)
+    )(keys, own)
 
 
 def pair_keys(ids, counts, tile):
@@ -117,7 +121,7 @@
     near = jnp.minimum(ahead, N_TILE - ahead)
     own = ahead == 0
     slot = jnp.where(own, 2, jnp.where(ahead == near, 1, 0))
-    turn = jnp.where(own, 1 + lax.rem(reader, ROUNDS - 2), near)
+    turn = jnp.where(own, 1 + lax.rem(reader, OWN_ROUNDS), near)
     turn = jnp.where(entry < counts, turn, 0)
     return (turn << KEY_SHIFT) | (reader << 9) | (slot << 7) | (ids & (CL - 1))
 
@@ -234,13 +238,15 @@
     acc_ref[...] = acc_in[...] if has_acc else jnp.zeros_like(acc_ref)
     for slot, parts in blocks:
         prepare(slot, parts, hist_ref, y_ref)
-    pairs(turn * REGION, steps_s[turn], list_s, x_ref, hist_ref, y_ref, acc_ref)
+    pairs(0 if final else turn * REGION, steps_s[turn], list_s, x_ref, hist_ref, y_ref, acc_ref)
     if final:
         finish(acc_ref, *final_in, *final_out)
 
 
 def consume(prepared, turn, blocks, acc, final=None):
     lists, steps, x_rows = prepared
+    if final is not None:
+        lists = lists[turn * REGION : (turn + 1) * REGION]
     args = [steps, lists, x_rows] + [part for _, parts in blocks for part in parts]
     if acc is not None:
         args.append(acc)
@@ -304,10 +310,10 @@
     last = N_TILE // 2 - 1
     up, down = hop(own, 1), hop(own, -1)
     keys = pair_keys(pair_ids[0].T, reader_counts, tile)
-    prepared = setup(keys, points)
+    prepared = setup(keys, own)
     acc = None
     for s in range(1, last + 1):
-        block = [(0, [up]), (1, [down]), (2, [own])]
+        block = [(0, [up]), (1, [down])] + ([(2, [own])] if s <= OWN_ROUNDS else [])
         if acc is None:
             up, prepared = lax.optimization_barrier((up, prepared))
         else:

time: 126 us -> 125 us (level)
  Pallas kernels: 38 us -> 35.1 us
  starting transfers between devices: 67.7 us -> 70.2 us
    pallas_call x8, Pallas kernels: 29.2 us -> 26.5 us  [consume(): pl.pallas_call(functools.partial(ring_kernel, turn, shape, acc is not Non...]
    ppermute x4, starting transfers between devices: 13.8 us -> 16.3 us  [shifted(): return lax.ppermute(block, axis, route)]
  transfers between devices with their start and end apart: 19 -> 19, of which waited for: 5 -> 5; matrix products, arithmetic and copies ran while one was open for 1% -> 1% of each run, Pallas kernels for 28% -> 26%
where the time goes in v6:
time: 125 us; the launch traced here: 124 us
  starting transfers between devices  70.2 us (56%)
  Pallas kernels  35.1 us (28%)
  waiting for transfers between devices  13 us (10%)
  local copies, waits for them, and re-layouts  2.23 us (2%)
  other arithmetic  1.78 us (1%)
    ppermute x15, starting transfers between devices, hop(): lax.ppermute(block, 'tile', [(i, (i + distance) % peers) for i in range(p...  53.9 us
    pallas_call x8, Pallas kernels, consume(): pl.pallas_call(functools.partial(ring_kernel, turn, shape, acc is not Non...  26.5 us
    ppermute x4, starting transfers between devices, shifted(): return lax.ppermute(block, axis, route)  16.3 us
    pallas_call x1, Pallas kernels, setup(): pl.pallas_call(setup_kernel, out_shape=[jax.ShapeDtypeStruct((ROUNDS * RE...  8.55 us
    ppermute x4, waiting for transfers between devices, shifted(): return lax.ppermute(block, axis, route)  8.21 us
    ppermute x15, waiting for transfers between devices, hop(): lax.ppermute(block, 'tile', [(i, (i + distance) % peers) for i in range(p...  4.76 us
  transfers between devices with their start and end apart: 19, of which 5 were waited for; matrix products, arithmetic and copies ran while one was open for 1% of the time, Pallas kernels for 26%

profile of v6, /device:TPU:7, one launch (start us, length us, event | category | flops | bytes accessed | tf_op | source)
XLA Modules:
  0.0 124.1 jit_solution(9549587030118728201)
XLA Ops:
  0.6 0.0 copy-start
  0.6 1.1 pad_maximum_fusion.here_ref.refs_5_
  1.7 3.5 %collective-permute-start = (bf16[1408,128]{1,0:T(8,128)(2,1)S(1)}, bf16[1408,128]{1,0:T(8,128)(2,1)S(1)}, u32[]{:S(2)}, u32[]{:S(2)}) collective-permute-start(bf16[1408,128]{1,0:T(8,128)(2,1)S(1)} %pad_maximum_fusion.here_ref.refs_5_), channel_id=1, source_target_pairs={{0,1},{1,2},{2,3},{3,4},{4,5},{5,6},{6,7},{7,8},{8,9},{9,10},{10,1... | collective-permute-start | bytes 1081352 | tf_op jit(solution)/shard_map/ppermute | solution.py:285
  5.3 9.5 %collective-permute-start.2 = (bf16[1408,128]{1,0:T(8,128)(2,1)S(1)}, bf16[1408,128]{1,0:T(8,128)(2,1)S(1)}, u32[]{:S(2)}, u32[]{:S(2)}) collective-permute-start(bf16[1408,128]{1,0:T(8,128)(2,1)S(1)} %pad_maximum_fusion.here_ref.refs_5_), channel_id=1, source_target_pairs={{0,15},{1,0},{2,1},{3,2},{4,3},{5,4},{6,5},{7,6},{8,7},{9,8},{10,9... | collective-permute-start | bytes 1081352 | tf_op jit(solution)/shard_map/ppermute | solution.py:285
  14.8 0.7 fusion.10.key_ref
  15.5 8.6 %shard_map.104 = (s32[9216]{0:T(1024)S(1)}, s32[9]{0:T(128)S(1)}, bf16[128,128,32]{2,1,0:T(8,128)(2,1)S(1)}) custom-call(s32[8,128]{1,0:T(8,128)S(1)} %fusion.10.key_ref, bf16[1408,128]{1,0:T(8,128)(2,1)S(1)} %pad_maximum_fusion.here_ref.refs_5_), custom_call_target="tpu_custom_call" | custom-call | flops 1000000 | bytes 10000000 | tf_op jit(solution)/shard_map/pallas_call | solution.py:99
  24.0 0.0 copy-start.1
  24.1 0.0 collective-permute-done.refs_3_
  24.1 1.9 %collective-permute-start.1 = (bf16[1408,128]{1,0:T(8,128)(2,1)S(1)}, bf16[1408,128]{1,0:T(8,128)(2,1)S(1)}, u32[]{:S(2)}, u32[]{:S(2)}) collective-permute-start(bf16[1408,128]{1,0:T(8,128)(2,1)S(1)} %collective-permute-done.refs_3_), channel_id=1, source_target_pairs={{0,1},{1,2},{2,3},{3,4},{4,5},{5,6},{6,7},{7,8},{8,9},{9,10},{10,1... | collective-permute-start | bytes 1081352 | tf_op jit(solution)/shard_map/ppermute | solution.py:285
  26.0 0.0 collective-permute-done.2.refs_4_
  26.0 4.6 %collective-permute-start.4 = (bf16[1408,128]{1,0:T(8,128)(2,1)S(1)}, bf16[1408,128]{1,0:T(8,128)(2,1)S(1)}, u32[]{:S(2)}, u32[]{:S(2)}) collective-permute-start(bf16[1408,128]{1,0:T(8,128)(2,1)S(1)} %collective-permute-done.2.refs_4_), channel_id=1, source_target_pairs={{0,15},{1,0},{2,1},{3,2},{4,3},{5,4},{6,5},{7,6},{8,7},{9,8},{10,9... | collective-permute-start | bytes 1081352 | tf_op jit(solution)/shard_map/ppermute | solution.py:285
  30.6 4.6 %shard_map.105.refs_6_ = f32[2064,128]{1,0:T(8,128)S(1)} custom-call(s32[9]{0:T(128)S(1)} %get-tuple-element.26.refs_0_, s32[9216]{0:T(1024)S(1)} %get-tuple-element.27.refs_1_, bf16[128,128,32]{2,1,0:T(8,128)(2,1)S(1)} %get-tuple-element.28.refs_2_, bf16[1408,128]{1,0:T(8,128)(2,1)S(1)} %collective-permute-done.refs_3_, ...), custom_call_target="tpu_custom_call" | custom-call | flops 671088640 | bytes 8388608 | tf_op jit(solution)/shard_map/pallas_call | solution.py:270
  35.2 0.9 collective-permute-done.1.refs_3_
  36.1 1.9 %collective-permute-start.3 = (bf16[1408,128]{1,0:T(8,128)(2,1)S(1)}, bf16[1408,128]{1,0:T(8,128)(2,1)S(1)}, u32[]{:S(2)}, u32[]{:S(2)}) collective-permute-start(bf16[1408,128]{1,0:T(8,128)(2,1)S(1)} %collective-permute-done.1.refs_3_), channel_id=1, source_target_pairs={{0,1},{1,2},{2,3},{3,4},{4,5},{5,6},{6,7},{7,8},{8,9},{9,10},{10,1... | collective-permute-start | bytes 1081352 | tf_op jit(solution)/shard_map/ppermute | solution.py:285
  38.0 0.0 collective-permute-done.4.refs_4_
  38.0 4.6 %collective-permute-start.6 = (bf16[1408,128]{1,0:T(8,128)(2,1)S(1)}, bf16[1408,128]{1,0:T(8,128)(2,1)S(1)}, u32[]{:S(2)}, u32[]{:S(2)}) collective-permute-start(bf16[1408,128]{1,0:T(8,128)(2,1)S(1)} %collective-permute-done.4.refs_4_), channel_id=1, source_target_pairs={{0,15},{1,0},{2,1},{3,2},{4,3},{5,4},{6,5},{7,6},{8,7},{9,8},{10,9... | collective-permute-start | bytes 1081352 | tf_op jit(solution)/shard_map/ppermute | solution.py:285
  42.6 3.9 %shard_map.106.refs_6_ = f32[2064,128]{1,0:T(8,128)S(1)} custom-call(s32[9]{0:T(128)S(1)} %get-tuple-element.26.refs_0_, s32[9216]{0:T(1024)S(1)} %get-tuple-element.27.refs_1_, bf16[128,128,32]{2,1,0:T(8,128)(2,1)S(1)} %get-tuple-element.28.refs_2_, bf16[1408,128]{1,0:T(8,128)(2,1)S(1)} %collective-permute-done.1.refs_3_, ...), custom_call_target="tpu_custom_call" | custom-call | flops 671088640 | bytes 8388608 | tf_op jit(solution)/shard_map/pallas_call | solution.py:270
  46.4 0.7 collective-permute-done.3.refs_3_
  47.1 1.9 %collective-permute-start.5 = (bf16[1408,128]{1,0:T(8,128)(2,1)S(1)}, bf16[1408,128]{1,0:T(8,128)(2,1)S(1)}, u32[]{:S(2)}, u32[]{:S(2)}) collective-permute-start(bf16[1408,128]{1,0:T(8,128)(2,1)S(1)} %collective-permute-done.3.refs_3_), channel_id=1, source_target_pairs={{0,1},{1,2},{2,3},{3,4},{4,5},{5,6},{6,7},{7,8},{8,9},{9,10},{10,1... | collective-permute-start | bytes 1081352 | tf_op jit(solution)/shard_map/ppermute | solution.py:285
  49.0 0.0 collective-permute-done.6.refs_4_
  49.0 4.6 %collective-permute-start.8 = (bf16[1408,128]{1,0:T(8,128)(2,1)S(1)}, bf16[1408,128]{1,0:T(8,128)(2,1)S(1)}, u32[]{:S(2)}, u32[]{:S(2)}) collective-permute-start(bf16[1408,128]{1,0:T(8,128)(2,1)S(1)} %collective-permute-done.6.refs_4_), channel_id=1, source_target_pairs={{0,15},{1,0},{2,1},{3,2},{4,3},{5,4},{6,5},{7,6},{8,7},{9,8},{10,9... | collective-permute-start | bytes 1081352 | tf_op jit(solution)/shard_map/ppermute | solution.py:285
  53.6 3.9 %shard_map.107.refs_5_ = f32[2064,128]{1,0:T(8,128)S(1)} custom-call(s32[9]{0:T(128)S(1)} %get-tuple-element.26.refs_0_, s32[9216]{0:T(1024)S(1)} %get-tuple-element.27.refs_1_, bf16[128,128,32]{2,1,0:T(8,128)(2,1)S(1)} %get-tuple-element.28.refs_2_, bf16[1408,128]{1,0:T(8,128)(2,1)S(1)} %collective-permute-done.3.refs_3_, ...), custom_call_target="tpu_custom_call" | custom-call | flops 671088640 | bytes 8388608 | tf_op jit(solution)/shard_map/pallas_call | solution.py:270
  57.5 0.0 collective-permute-done.5.refs_3_
  57.5 1.9 %collective-permute-start.7 = (bf16[1408,128]{1,0:T(8,128)(2,1)S(1)}, bf16[1408,128]{1,0:T(8,128)(2,1)S(1)}, u32[]{:S(2)}, u32[]{:S(2)}) collective-permute-start(bf16[1408,128]{1,0:T(8,128)(2,1)S(1)} %collective-permute-done.5.refs_3_), channel_id=1, source_target_pairs={{0,1},{1,2},{2,3},{3,4},{4,5},{5,6},{6,7},{7,8},{8,9},{9,10},{10,1... | collective-permute-start | bytes 1081352 | tf_op jit(solution)/shard_map/ppermute | solution.py:285
  59.4 0.0 collective-permute-done.8.refs_4_
  59.4 4.6 %collective-permute-start.10 = (bf16[1408,128]{1,0:T(8,128)(2,1)S(1)}, bf16[1408,128]{1,0:T(8,128)(2,1)S(1)}, u32[]{:S(2)}, u32[]{:S(2)}) collective-permute-start(bf16[1408,128]{1,0:T(8,128)(2,1)S(1)} %collective-permute-done.8.refs_4_), channel_id=1, source_target_pairs={{0,15},{1,0},{2,1},{3,2},{4,3},{5,4},{6,5},{7,6},{8,7},{9,8},{10,9... | collective-permute-start | bytes 1081352 | tf_op jit(solution)/shard_map/ppermute | solution.py:285
  64.0 3.0 %shard_map.108.refs_5_ = f32[2064,128]{1,0:T(8,128)S(1)} custom-call(s32[9]{0:T(128)S(1)} %get-tuple-element.26.refs_0_, s32[9216]{0:T(1024)S(1)} %get-tuple-element.27.refs_1_, bf16[128,128,32]{2,1,0:T(8,128)(2,1)S(1)} %get-tuple-element.28.refs_2_, bf16[1408,128]{1,0:T(8,128)(2,1)S(1)} %collective-permute-done.5.refs_3_, ...), custom_call_target="tpu_custom_call" | custom-call | flops 671088640 | bytes 8388608 | tf_op jit(solution)/shard_map/pallas_call | solution.py:270
  67.0 0.0 collective-permute-done.7.refs_3_
  67.0 1.9 %collective-permute-start.9 = (bf16[1408,128]{1,0:T(8,128)(2,1)S(1)}, bf16[1408,128]{1,0:T(8,128)(2,1)S(1)}, u32[]{:S(2)}, u32[]{:S(2)}) collective-permute-start(bf16[1408,128]{1,0:T(8,128)(2,1)S(1)} %collective-permute-done.7.refs_3_), channel_id=1, source_target_pairs={{0,1},{1,2},{2,3},{3,4},{4,5},{5,6},{6,7},{7,8},{8,9},{9,10},{10,1... | collective-permute-start | bytes 1081352 | tf_op jit(solution)/shard_map/ppermute | solution.py:285
  68.9 0.0 collective-permute-done.10.refs_4_
  69.0 4.6 %collective-permute-start.12 = (bf16[1408,128]{1,0:T(8,128)(2,1)S(1)}, bf16[1408,128]{1,0:T(8,128)(2,1)S(1)}, u32[]{:S(2)}, u32[]{:S(2)}) collective-permute-start(bf16[1408,128]{1,0:T(8,128)(2,1)S(1)} %collective-permute-done.10.refs_4_), channel_id=1, source_target_pairs={{0,15},{1,0},{2,1},{3,2},{4,3},{5,4},{6,5},{7,6},{8,7},{9,8},{10,9... | collective-permute-start | bytes 1081352 | tf_op jit(solution)/shard_map/ppermute | solution.py:285
  73.5 3.0 %shard_map.109.refs_5_ = f32[2064,128]{1,0:T(8,128)S(1)} custom-call(s32[9]{0:T(128)S(1)} %get-tuple-element.26.refs_0_, s32[9216]{0:T(1024)S(1)} %get-tuple-element.27.refs_1_, bf16[128,128,32]{2,1,0:T(8,128)(2,1)S(1)} %get-tuple-element.28.refs_2_, bf16[1408,128]{1,0:T(8,128)(2,1)S(1)} %collective-permute-done.7.refs_3_, ...), custom_call_target="tpu_custom_call" | custom-call | flops 671088640 | bytes 8388608 | tf_op jit(solution)/shard_map/pallas_call | solution.py:270
  76.5 0.0 copy-start.7
  76.5 0.0 collective-permute-done.9.refs_3_
  76.5 1.9 %collective-permute-start.11 = (bf16[1408,128]{1,0:T(8,128)(2,1)S(1)}, bf16[1408,128]{1,0:T(8,128)(2,1)S(1)}, u32[]{:S(2)}, u32[]{:S(2)}) collective-permute-start(bf16[1408,128]{1,0:T(8,128)(2,1)S(1)} %collective-permute-done.9.refs_3_), channel_id=1, source_target_pairs={{0,1},{1,2},{2,3},{3,4},{4,5},{5,6},{6,7},{7,8},{8,9},{9,10},{10,1... | collective-permute-start | bytes 1081352 | tf_op jit(solution)/shard_map/ppermute | solution.py:285
  78.5 0.0 collective-permute-done.12.refs_4_
  78.5 4.6 %collective-permute-start.14 = (bf16[1408,128]{1,0:T(8,128)(2,1)S(1)}, bf16[1408,128]{1,0:T(8,128)(2,1)S(1)}, u32[]{:S(2)}, u32[]{:S(2)}) collective-permute-start(bf16[1408,128]{1,0:T(8,128)(2,1)S(1)} %collective-permute-done.12.refs_4_), channel_id=1, source_target_pairs={{0,15},{1,0},{2,1},{3,2},{4,3},{5,4},{6,5},{7,6},{8,7},{9,8},{10,9... | collective-permute-start | bytes 1081352 | tf_op jit(solution)/shard_map/ppermute | solution.py:285
  83.1 0.0 copy-done.1
  83.1 3.0 %shard_map.110.refs_5_ = f32[2064,128]{1,0:T(8,128)S(1)} custom-call(s32[9]{0:T(128)S(1)} %get-tuple-element.26.refs_0_, s32[9216]{0:T(1024)S(1)} %get-tuple-element.27.refs_1_, bf16[128,128,32]{2,1,0:T(8,128)(2,1)S(1)} %get-tuple-element.28.refs_2_, bf16[1408,128]{1,0:T(8,128)(2,1)S(1)} %collective-permute-done.9.refs_3_, ...), custom_call_target="tpu_custom_call" | custom-call | flops 671088640 | bytes 8388608 | tf_op jit(solution)/shard_map/pallas_call | solution.py:270
  86.1 0.0 collective-permute-done.11.refs_3_
  86.1 1.9 %collective-permute-start.13 = (bf16[1408,128]{1,0:T(8,128)(2,1)S(1)}, bf16[1408,128]{1,0:T(8,128)(2,1)S(1)}, u32[]{:S(2)}, u32[]{:S(2)}) collective-permute-start(bf16[1408,128]{1,0:T(8,128)(2,1)S(1)} %collective-permute-done.11.refs_3_), channel_id=1, source_target_pairs={{0,1},{1,2},{2,3},{3,4},{4,5},{5,6},{6,7},{7,8},{8,9},{9,10},{10,1... | collective-permute-start | bytes 1081352 | tf_op jit(solution)/shard_map/ppermute | solution.py:285
  88.0 0.0 copy-done.7
  88.0 0.0 collective-permute-done.14.refs_4_
  88.0 0.0 copy-start.2
  88.0 2.2 %copy-done.2 = bf16[128,128,32]{2,1,0:T(8,128)(2,1)S(1)} copy-done((bf16[128,128,32]{2,1,0:T(8,128)(2,1)S(1)}, bf16[128,128,32]{2,1,0:T(8,128)(2,1)}, u32[]{:S(2)}) %copy-start.2) | copy-done | bytes 1048600
  90.2 0.0 copy-start.3
  90.2 0.0 copy-start.4
  90.2 3.0 %shard_map.111.refs_4_ = f32[2064,128]{1,0:T(8,128)S(1)} custom-call(s32[9]{0:T(128)S(1)} %get-tuple-element.26.refs_0_, s32[9216]{0:T(1024)S(1)} %get-tuple-element.27.refs_1_, bf16[128,128,32]{2,1,0:T(8,128)(2,1)S(1)} %copy-done.2, bf16[1408,128]{1,0:T(8,128)(2,1)S(1)} %collective-permute-done.11.refs_3_, ...), custom_call_target="tpu_custom_call" | custom-call | flops 671088640 | bytes 8388608 | tf_op jit(solution)/shard_map/pallas_call | solution.py:270
  93.2 3.2 %collective-permute-done.13.refs_3_ = bf16[1408,128]{1,0:T(8,128)(2,1)S(1)} collective-permute-done((bf16[1408,128]{1,0:T(8,128)(2,1)S(1)}, bf16[1408,128]{1,0:T(8,128)(2,1)S(1)}, u32[]{:S(2)}, u32[]{:S(2)}) %collective-permute-start.13) | collective-permute-done | bytes 360480 | tf_op jit(solution)/shard_map/ppermute | solution.py:285
  96.4 0.0 copy-done.3
  96.4 0.0 copy-done.4
  96.4 0.0 copy-done.5
  96.4 0.0 copy-done.6
  96.4 2.3 %shard_map.112 = (f32[128,128]{1,0:T(8,128)}, f32[96,128]{1,0:T(8,128)S(1)}) custom-call(s32[9]{0:T(128)S(1)} %get-tuple-element.26.refs_0_, s32[1024]{0:T(1024)S(1)} %slice.26.refs_1_, bf16[128,128,32]{2,1,0:T(8,128)(2,1)S(1)} %copy-done.3, bf16[1408,128]{1,0:T(8,128)(2,1)S(1)} %collective-permute-done.13.refs_3_, f32[2064,128]{1,0:T(8,128)S(1)} %shard_map.111.refs_4_, ...), custom_call_target="tpu_custom_call" | custom-call | flops 671088640 | bytes 8388608 | tf_op jit(solution)/shard_map/pallas_call | solution.py:270
  98.7 1.3 %collective-permute-start.15 = (f32[32,128]{1,0:T(8,128)S(1)}, f32[32,128]{1,0:T(8,128)S(1)}, u32[]{:S(2)}, u32[]{:S(2)}) collective-permute-start(f32[32,128]{1,0:T(8,128)S(1)} %get-tuple-element.46), channel_id=1, source_target_pairs={{0,1},{1,2},{2,3},{3,4},{4,5},{5,6},{6,7},{7,8},{8,9},{9,10},{10,1... | collective-permute-start | bytes 49160 | tf_op jit(solution)/shard_map/ppermute | solution.py:291
  100.0 1.3 %collective-permute-start.16 = (f32[32,128]{1,0:T(8,128)S(1)}, f32[32,128]{1,0:T(8,128)S(1)}, u32[]{:S(2)}, u32[]{:S(2)}) collective-permute-start(f32[32,128]{1,0:T(8,128)S(1)} %get-tuple-element.47), channel_id=1, source_target_pairs={{1,0},{2,1},{3,2},{4,3},{5,4},{6,5},{7,6},{8,7},{9,8},{10,9},{11,1... | collective-permute-start | bytes 49160 | tf_op jit(solution)/shard_map/ppermute | solution.py:291
  101.3 0.0 collective-permute-done.15
  101.3 3.2 %collective-permute-done.16 = f32[32,128]{1,0:T(8,128)S(1)} collective-permute-done((f32[32,128]{1,0:T(8,128)S(1)}, f32[32,128]{1,0:T(8,128)S(1)}, u32[]{:S(2)}, u32[]{:S(2)}) %collective-permute-start.16) | collective-permute-done | bytes 16416 | tf_op jit(solution)/shard_map/ppermute | solution.py:291
  104.5 11.8 %collective-permute-start.17 = (f32[1,128]{1,0:T(1,128)S(1)}, f32[1,128]{1,0:T(1,128)S(1)}, u32[]{:S(2)}, u32[]{:S(2)}) collective-permute-start(f32[1,128]{1,0:T(1,128)S(1)} %get-tuple-element.48), channel_id=1, source_target_pairs={{0,16},{16,32},{32,48},{48,64},{64,80},{80,96},{96,112},{112,128},... | collective-permute-start | bytes 1544 | tf_op jit(solution)/shard_map/ppermute | solution.py:291
  116.3 1.9 %collective-permute-start.18 = (f32[1,128]{1,0:T(1,128)S(1)}, f32[1,128]{1,0:T(1,128)S(1)}, u32[]{:S(2)}, u32[]{:S(2)}) collective-permute-start(f32[1,128]{1,0:T(1,128)S(1)} %get-tuple-element.49), channel_id=1, source_target_pairs={{16,0},{32,16},{48,32},{64,48},{80,64},{96,80},{112,96},{128,112},... | collective-permute-start | bytes 1544 | tf_op jit(solution)/shard_map/ppermute | solution.py:291
  118.3 0.0 collective-permute-done.17
  118.3 5.0 %collective-permute-done.18 = f32[1,128]{1,0:T(1,128)S(1)} collective-permute-done((f32[1,128]{1,0:T(1,128)S(1)}, f32[1,128]{1,0:T(1,128)S(1)}, u32[]{:S(2)}, u32[]{:S(2)}) %collective-permute-start.18) | collective-permute-done | bytes 544 | tf_op jit(solution)/shard_map/ppermute | solution.py:291
  123.3 0.0 copy-done
  123.3 0.8 convolution_add_fusion
  (8 shorter events, 0.0 us)
Async XLA Ops:
  0.6 122.7 %copy-start = (f32[128,128]{1,0:T(8,128)S(1)}, f32[128,128]{1,0:T(8,128)}, u32[]{:S(2)}) copy-start(f32[128,128]{1,0:T(8,128)} %param.17) | copy-start | bytes 196612
  1.7 22.4 %collective-permute-start = (bf16[1408,128]{1,0:T(8,128)(2,1)S(1)}, bf16[1408,128]{1,0:T(8,128)(2,1)S(1)}, u32[]{:S(2)}, u32[]{:S(2)}) collective-permute-start(bf16[1408,128]{1,0:T(8,128)(2,1)S(1)} %pad_maximum_fusion.here_ref.refs_5_), channel_id=1, source_target_pairs={{0,1},{1,2},{2,3},{3,4},{4,5},{5,6},{6,7},{7,8},{8,9},{9,10},{10,1... | collective-permute-start | bytes 1081352 | tf_op jit(solution)/shard_map/ppermute | solution.py:285
  5.3 20.7 %collective-permute-start.2 = (bf16[1408,128]{1,0:T(8,128)(2,1)S(1)}, bf16[1408,128]{1,0:T(8,128)(2,1)S(1)}, u32[]{:S(2)}, u32[]{:S(2)}) collective-permute-start(bf16[1408,128]{1,0:T(8,128)(2,1)S(1)} %pad_maximum_fusion.here_ref.refs_5_), channel_id=1, source_target_pairs={{0,15},{1,0},{2,1},{3,2},{4,3},{5,4},{6,5},{7,6},{8,7},{9,8},{10,9... | collective-permute-start | bytes 1081352 | tf_op jit(solution)/shard_map/ppermute | solution.py:285
  24.0 59.0 %copy-start.1 = (bf16[128,128,32]{2,1,0:T(8,128)(2,1)}, bf16[128,128,32]{2,1,0:T(8,128)(2,1)S(1)}, u32[]{:S(2)}) copy-start(bf16[128,128,32]{2,1,0:T(8,128)(2,1)S(1)} %get-tuple-element.28.refs_2_) | copy-start | bytes 3145732
  24.1 12.0 %collective-permute-start.1 = (bf16[1408,128]{1,0:T(8,128)(2,1)S(1)}, bf16[1408,128]{1,0:T(8,128)(2,1)S(1)}, u32[]{:S(2)}, u32[]{:S(2)}) collective-permute-start(bf16[1408,128]{1,0:T(8,128)(2,1)S(1)} %collective-permute-done.refs_3_), channel_id=1, source_target_pairs={{0,1},{1,2},{2,3},{3,4},{4,5},{5,6},{6,7},{7,8},{8,9},{9,10},{10,1... | collective-permute-start | bytes 1081352 | tf_op jit(solution)/shard_map/ppermute | solution.py:285
  26.0 12.0 %collective-permute-start.4 = (bf16[1408,128]{1,0:T(8,128)(2,1)S(1)}, bf16[1408,128]{1,0:T(8,128)(2,1)S(1)}, u32[]{:S(2)}, u32[]{:S(2)}) collective-permute-start(bf16[1408,128]{1,0:T(8,128)(2,1)S(1)} %collective-permute-done.2.refs_4_), channel_id=1, source_target_pairs={{0,15},{1,0},{2,1},{3,2},{4,3},{5,4},{6,5},{7,6},{8,7},{9,8},{10,9... | collective-permute-start | bytes 1081352 | tf_op jit(solution)/shard_map/ppermute | solution.py:285
  36.1 11.1 %collective-permute-start.3 = (bf16[1408,128]{1,0:T(8,128)(2,1)S(1)}, bf16[1408,128]{1,0:T(8,128)(2,1)S(1)}, u32[]{:S(2)}, u32[]{:S(2)}) collective-permute-start(bf16[1408,128]{1,0:T(8,128)(2,1)S(1)} %collective-permute-done.1.refs_3_), channel_id=1, source_target_pairs={{0,1},{1,2},{2,3},{3,4},{4,5},{5,6},{6,7},{7,8},{8,9},{9,10},{10,1... | collective-permute-start | bytes 1081352 | tf_op jit(solution)/shard_map/ppermute | solution.py:285
  38.0 11.0 %collective-permute-start.6 = (bf16[1408,128]{1,0:T(8,128)(2,1)S(1)}, bf16[1408,128]{1,0:T(8,128)(2,1)S(1)}, u32[]{:S(2)}, u32[]{:S(2)}) collective-permute-start(bf16[1408,128]{1,0:T(8,128)(2,1)S(1)} %collective-permute-done.4.refs_4_), channel_id=1, source_target_pairs={{0,15},{1,0},{2,1},{3,2},{4,3},{5,4},{6,5},{7,6},{8,7},{9,8},{10,9... | collective-permute-start | bytes 1081352 | tf_op jit(solution)/shard_map/ppermute | solution.py:285
  47.1 10.4 %collective-permute-start.5 = (bf16[1408,128]{1,0:T(8,128)(2,1)S(1)}, bf16[1408,128]{1,0:T(8,128)(2,1)S(1)}, u32[]{:S(2)}, u32[]{:S(2)}) collective-permute-start(bf16[1408,128]{1,0:T(8,128)(2,1)S(1)} %collective-permute-done.3.refs_3_), channel_id=1, source_target_pairs={{0,1},{1,2},{2,3},{3,4},{4,5},{5,6},{6,7},{7,8},{8,9},{9,10},{10,1... | collective-permute-start | bytes 1081352 | tf_op jit(solution)/shard_map/ppermute | solution.py:285
  49.0 10.4 %collective-permute-start.8 = (bf16[1408,128]{1,0:T(8,128)(2,1)S(1)}, bf16[1408,128]{1,0:T(8,128)(2,1)S(1)}, u32[]{:S(2)}, u32[]{:S(2)}) collective-permute-start(bf16[1408,128]{1,0:T(8,128)(2,1)S(1)} %collective-permute-done.6.refs_4_), channel_id=1, source_target_pairs={{0,15},{1,0},{2,1},{3,2},{4,3},{5,4},{6,5},{7,6},{8,7},{9,8},{10,9... | collective-permute-start | bytes 1081352 | tf_op jit(solution)/shard_map/ppermute | solution.py:285
  57.5 9.5 %collective-permute-start.7 = (bf16[1408,128]{1,0:T(8,128)(2,1)S(1)}, bf16[1408,128]{1,0:T(8,128)(2,1)S(1)}, u32[]{:S(2)}, u32[]{:S(2)}) collective-permute-start(bf16[1408,128]{1,0:T(8,128)(2,1)S(1)} %collective-permute-done.5.refs_3_), channel_id=1, source_target_pairs={{0,1},{1,2},{2,3},{3,4},{4,5},{5,6},{6,7},{7,8},{8,9},{9,10},{10,1... | collective-permute-start | bytes 1081352 | tf_op jit(solution)/shard_map/ppermute | solution.py:285
  59.4 9.5 %collective-permute-start.10 = (bf16[1408,128]{1,0:T(8,128)(2,1)S(1)}, bf16[1408,128]{1,0:T(8,128)(2,1)S(1)}, u32[]{:S(2)}, u32[]{:S(2)}) collective-permute-start(bf16[1408,128]{1,0:T(8,128)(2,1)S(1)} %collective-permute-done.8.refs_4_), channel_id=1, source_target_pairs={{0,15},{1,0},{2,1},{3,2},{4,3},{5,4},{6,5},{7,6},{8,7},{9,8},{10,9... | collective-permute-start | bytes 1081352 | tf_op jit(solution)/shard_map/ppermute | solution.py:285
  67.0 9.5 %collective-permute-start.9 = (bf16[1408,128]{1,0:T(8,128)(2,1)S(1)}, bf16[1408,128]{1,0:T(8,128)(2,1)S(1)}, u32[]{:S(2)}, u32[]{:S(2)}) collective-permute-start(bf16[1408,128]{1,0:T(8,128)(2,1)S(1)} %collective-permute-done.7.refs_3_), channel_id=1, source_target_pairs={{0,1},{1,2},{2,3},{3,4},{4,5},{5,6},{6,7},{7,8},{8,9},{9,10},{10,1... | collective-permute-start | bytes 1081352 | tf_op jit(solution)/shard_map/ppermute | solution.py:285
  69.0 9.5 %collective-permute-start.12 = (bf16[1408,128]{1,0:T(8,128)(2,1)S(1)}, bf16[1408,128]{1,0:T(8,128)(2,1)S(1)}, u32[]{:S(2)}, u32[]{:S(2)}) collective-permute-start(bf16[1408,128]{1,0:T(8,128)(2,1)S(1)} %collective-permute-done.10.refs_4_), channel_id=1, source_target_pairs={{0,15},{1,0},{2,1},{3,2},{4,3},{5,4},{6,5},{7,6},{8,7},{9,8},{10,9... | collective-permute-start | bytes 1081352 | tf_op jit(solution)/shard_map/ppermute | solution.py:285
  76.5 11.5 %copy-start.7 = (s32[1,128]{1,0:T(1,128)S(1)}, s32[1,128]{1,0:T(1,128)}, u32[]{:S(2)}) copy-start(s32[1,128]{1,0:T(1,128)} %param.15) | copy-start | bytes 1540
  76.5 9.5 %collective-permute-start.11 = (bf16[1408,128]{1,0:T(8,128)(2,1)S(1)}, bf16[1408,128]{1,0:T(8,128)(2,1)S(1)}, u32[]{:S(2)}, u32[]{:S(2)}) collective-permute-start(bf16[1408,128]{1,0:T(8,128)(2,1)S(1)} %collective-permute-done.9.refs_3_), channel_id=1, source_target_pairs={{0,1},{1,2},{2,3},{3,4},{4,5},{5,6},{6,7},{7,8},{8,9},{9,10},{10,1... | collective-permute-start | bytes 1081352 | tf_op jit(solution)/shard_map/ppermute | solution.py:285
  78.5 9.5 %collective-permute-start.14 = (bf16[1408,128]{1,0:T(8,128)(2,1)S(1)}, bf16[1408,128]{1,0:T(8,128)(2,1)S(1)}, u32[]{:S(2)}, u32[]{:S(2)}) collective-permute-start(bf16[1408,128]{1,0:T(8,128)(2,1)S(1)} %collective-permute-done.12.refs_4_), channel_id=1, source_target_pairs={{0,15},{1,0},{2,1},{3,2},{4,3},{5,4},{6,5},{7,6},{8,7},{9,8},{10,9... | collective-permute-start | bytes 1081352 | tf_op jit(solution)/shard_map/ppermute | solution.py:285
  86.1 10.4 %collective-permute-start.13 = (bf16[1408,128]{1,0:T(8,128)(2,1)S(1)}, bf16[1408,128]{1,0:T(8,128)(2,1)S(1)}, u32[]{:S(2)}, u32[]{:S(2)}) collective-permute-start(bf16[1408,128]{1,0:T(8,128)(2,1)S(1)} %collective-permute-done.11.refs_3_), channel_id=1, source_target_pairs={{0,1},{1,2},{2,3},{3,4},{4,5},{5,6},{6,7},{7,8},{8,9},{9,10},{10,1... | collective-permute-start | bytes 1081352 | tf_op jit(solution)/shard_map/ppermute | solution.py:285
  88.0 2.2 %copy-start.2 = (bf16[128,128,32]{2,1,0:T(8,128)(2,1)S(1)}, bf16[128,128,32]{2,1,0:T(8,128)(2,1)}, u32[]{:S(2)}) copy-start(bf16[128,128,32]{2,1,0:T(8,128)(2,1)} %copy-done.1) | copy-start | bytes 3145732
  90.2 6.2 %copy-start.3 = (bf16[128,128,32]{2,1,0:T(8,128)(2,1)S(1)}, bf16[128,128,32]{2,1,0:T(8,128)(2,1)}, u32[]{:S(2)}) copy-start(bf16[128,128,32]{2,1,0:T(8,128)(2,1)} %copy-done.1) | copy-start | bytes 3145732
  90.2 6.2 %copy-start.4 = (bf16[1024,128]{1,0:T(8,128)(2,1)S(1)}, bf16[1024,128]{1,0:T(8,128)(2,1)}, u32[]{:S(2)}) copy-start(bf16[1024,128]{1,0:T(8,128)(2,1)} %refs_7_.1) | copy-start | bytes 786436
  90.2 6.2 %copy-start.5 = (f32[1,128,128]{2,1,0:T(8,128)S(1)}, f32[1,128,128]{2,1,0:T(8,128)}, u32[]{:S(2)}) copy-start(f32[1,128,128]{2,1,0:T(8,128)} %param.11) | copy-start | bytes 196612
  90.2 6.2 %copy-start.6 = (f32[1,128,128]{2,1,0:T(8,128)S(1)}, f32[1,128,128]{2,1,0:T(8,128)}, u32[]{:S(2)}) copy-start(f32[1,128,128]{2,1,0:T(8,128)} %param.12) | copy-start | bytes 196612
  98.7 2.6 %collective-permute-start.15 = (f32[32,128]{1,0:T(8,128)S(1)}, f32[32,128]{1,0:T(8,128)S(1)}, u32[]{:S(2)}, u32[]{:S(2)}) collective-permute-start(f32[32,128]{1,0:T(8,128)S(1)} %get-tuple-element.46), channel_id=1, source_target_pairs={{0,1},{1,2},{2,3},{3,4},{4,5},{5,6},{6,7},{7,8},{8,9},{9,10},{10,1... | collective-permute-start | bytes 49160 | tf_op jit(solution)/shard_map/ppermute | solution.py:291
  100.0 4.5 %collective-permute-start.16 = (f32[32,128]{1,0:T(8,128)S(1)}, f32[32,128]{1,0:T(8,128)S(1)}, u32[]{:S(2)}, u32[]{:S(2)}) collective-permute-start(f32[32,128]{1,0:T(8,128)S(1)} %get-tuple-element.47), channel_id=1, source_target_pairs={{1,0},{2,1},{3,2},{4,3},{5,4},{6,5},{7,6},{8,7},{9,8},{10,9},{11,1... | collective-permute-start | bytes 49160 | tf_op jit(solution)/shard_map/ppermute | solution.py:291
  104.5 13.8 %collective-permute-start.17 = (f32[1,128]{1,0:T(1,128)S(1)}, f32[1,128]{1,0:T(1,128)S(1)}, u32[]{:S(2)}, u32[]{:S(2)}) collective-permute-start(f32[1,128]{1,0:T(1,128)S(1)} %get-tuple-element.48), channel_id=1, source_target_pairs={{0,16},{16,32},{32,48},{48,64},{64,80},{80,96},{96,112},{112,128},... | collective-permute-start | bytes 1544 | tf_op jit(solution)/shard_map/ppermute | solution.py:291
  116.3 7.0 %collective-permute-start.18 = (f32[1,128]{1,0:T(1,128)S(1)}, f32[1,128]{1,0:T(1,128)S(1)}, u32[]{:S(2)}, u32[]{:S(2)}) collective-permute-start(f32[1,128]{1,0:T(1,128)S(1)} %get-tuple-element.49), channel_id=1, source_target_pairs={{16,0},{32,16},{48,32},{64,48},{80,64},{96,80},{112,96},{128,112},... | collective-permute-start | bytes 1544 | tf_op jit(solution)/shard_map/ppermute | solution.py:291

commit v7 on v6

--- a/solution.py
+++ b/solution.py
@@ -65,47 +65,49 @@
         x_ref[g * 4 + m] = turned[:, m * 2 * KDIM : (m + 1) * 2 * KDIM]
 
 
-def setup_kernel(key_ref, here_ref, list_ref, steps_ref, x_ref, cur_ref, rows_ref):
+def setup_kernel(
+    key_ref, here_ref, list_ref, bounds_ref, x_ref, low_ref, high_ref, rows_ref
+):
     reader_rows(here_ref, rows_ref)
     for k in range(ROUNDS):
-        cur_ref[k] = k * REGION
+        low_ref[k] = k * REGION + REGION // 2
+        high_ref[k] = k * REGION + REGION // 2
 
     def sixteen(i, carry):
         for u in range(4):
             turn_rows(i * 4 + u, rows_ref, x_ref)
-        for u in range(16):
+        for u in range(8):
             for p in range(PAIRS):
-                key = key_ref[p, i * 16 + u]
+                key = key_ref[p, i * 8 + u]
                 k = key >> KEY_SHIFT
-                at = cur_ref[k]
+                at = low_ref[k] - 1
                 list_ref[at] = key & ((1 << KEY_SHIFT) - 1)
-                cur_ref[k] = at + 1
+                low_ref[k] = at
+                key = key_ref[p, CL // 2 + i * 8 + u]
+                k = key >> KEY_SHIFT
+                at = high_ref[k]
+                list_ref[at] = key & ((1 << KEY_SHIFT) - 1)
+                high_ref[k] = at + 1
         return carry
 
     lax.fori_loop(0, CL // 16, sixteen, 0)
-    for k in range(1, ROUNDS):
-        used = cur_ref[k] - k * REGION
-        steps = (used + (STEP - 1)) >> 5
-        steps_ref[k] = steps
-
-        def pad(at, carry):
-            list_ref[at] = (CL << 9) | CL
-            return carry
-
-        lax.fori_loop(k * REGION + used, k * REGION + steps * STEP, pad, 0)
+    for k in range(ROUNDS):
+        bounds_ref[k] = low_ref[k]
+        bounds_ref[ROUNDS + k] = high_ref[k]
 
 
 def setup(keys, own):
     return pl.pallas_call(
         setup_kernel,
         out_shape=[
-            jax.ShapeDtypeStruct((ROUNDS * REGION,), jnp.int32),
-            jax.ShapeDtypeStruct((ROUNDS,), jnp.int32),
+            jax.ShapeDtypeStruct((ROUNDS * REGION + STEP,), jnp.int32),
+            jax.ShapeDtypeStruct((2 * ROUNDS,), jnp.int32),
             jax.ShapeDtypeStruct((CL, PTS, 2 * KDIM), jnp.bfloat16),
         ],
         in_specs=[SMEM, VMEM],
         out_specs=[SMEM] * 2 + [VMEM],
         scratch_shapes=[
+            pltpu.SMEM((ROUNDS,), jnp.int32),
             pltpu.SMEM((ROUNDS,), jnp.int32),
             pltpu.VMEM((CL * KDIM, PTS), jnp.float32),
         ],
@@ -134,7 +136,7 @@
         y_ref[pl.ds(block * (CL * YDIM) + k, CL, stride=YDIM), :] = row
 
 
-def pairs(base, steps, list_s, x_ref, hist_ref, y_ref, acc_ref):
+def pairs(start, end, list_s, x_ref, hist_ref, y_ref, acc_ref):
     first = lax.broadcasted_iota(jnp.int32, (PTS, 2 * KDIM), 1) < KDIM
     zero_y = jnp.zeros((KDIM, PTS), jnp.float32)
     zero_h = jnp.zeros((COLS, PTS), jnp.float32)
@@ -157,7 +159,9 @@
         return jnp.where((q & 1) == 1, two[COLS:], two[:COLS])
 
     def step(i, carry):
-        entries = [list_s[base + i * STEP + k] for k in range(STEP)]
+        at = start + i * STEP
+        unused = (CL << 9) | CL
+        entries = [jnp.where(at + k < end, list_s[at + k], unused) for k in range(STEP)]
         readers = [e >> 9 for e in entries]
         sources = [e & (4 * CL - 1) for e in entries]
         both = [(2 * u, 2 * u + 1) for u in range(UNITS)]
@@ -185,7 +189,7 @@
                 acc_ref[pl.ds(at + COLS, COLS), :] += out[(2 + half) * COLS : (3 + half) * COLS]
         return carry
 
-    lax.fori_loop(0, steps, step, 0)
+    lax.fori_loop(0, (end - start + (STEP - 1)) >> 5, step, 0)
 
 
 def prepare(slot, parts, hist_ref, y_ref):
@@ -229,7 +233,7 @@
 def ring_kernel(turn, shape, has_acc, final, *refs):
     refs = list(refs)
     take = lambda n: [refs.pop(0) for _ in range(n)]
-    steps_s, list_s, x_ref = take(3)
+    bounds_s, list_s, x_ref = take(3)
     blocks = [(slot, take(n)) for slot, n in shape]
     acc_in = take(1)[0] if has_acc else None
     final_in = take(4) if final else None
@@ -238,16 +242,17 @@
     acc_ref[...] = acc_in[...] if has_acc else jnp.zeros_like(acc_ref)
     for slot, parts in blocks:
         prepare(slot, parts, hist_ref, y_ref)
-    pairs(0 if final else turn * REGION, steps_s[turn], list_s, x_ref, hist_ref, y_ref, acc_ref)
+    skip = turn * REGION
+    start, end = bounds_s[turn] - skip, bounds_s[ROUNDS + turn] - skip
+    pairs(start, end, list_s, x_ref, hist_ref, y_ref, acc_ref)
     if final:
         finish(acc_ref, *final_in, *final_out)
 
 
 def consume(prepared, turn, blocks, acc, final=None):
-    lists, steps, x_rows = prepared
-    if final is not None:
-        lists = lists[turn * REGION : (turn + 1) * REGION]
-    args = [steps, lists, x_rows] + [part for _, parts in blocks for part in parts]
+    lists, bounds, x_rows = prepared
+    lists = lists[turn * REGION : (turn + 1) * REGION + STEP]
+    args = [bounds, lists, x_rows] + [part for _, parts in blocks for part in parts]
     if acc is not None:
         args.append(acc)
     acc_shape = (ACC_ROWS, PTS)

time: 125 us -> 124 us (level)
  Pallas kernels: 35.1 us -> 30.9 us
  waiting for transfers between devices: 13 us -> 15.9 us
    pallas_call x8, Pallas kernels: 26.5 us -> 23.1 us  [consume(): pl.pallas_call(functools.partial(ring_kernel, turn, shape, acc is not Non...]
    ppermute x15, waiting for transfers between devices: 4.76 us -> 7.71 us  [hop(): lax.ppermute(block, 'tile', [(i, (i + distance) % peers) for i in range(p...]
  transfers between devices with their start and end apart: 19 -> 19, of which waited for: 5 -> 8; matrix products, arithmetic and copies ran while one was open for 1% -> 1% of each run, Pallas kernels for 26% -> 23%
where the time goes in v7:
time: 124 us; the launch traced here: 123 us
  starting transfers between devices  70.4 us (57%)
  Pallas kernels  30.9 us (25%)
  waiting for transfers between devices  15.9 us (13%)
  local copies, waits for them, and re-layouts  2.23 us (2%)
  other arithmetic  1.78 us (1%)
    ppermute x15, starting transfers between devices, hop(): lax.ppermute(block, 'tile', [(i, (i + distance) % peers) for i in range(p...  53.9 us
    pallas_call x8, Pallas kernels, consume(): pl.pallas_call(functools.partial(ring_kernel, turn, shape, acc is not Non...  23.1 us
    ppermute x4, starting transfers between devices, shifted(): return lax.ppermute(block, axis, route)  16.6 us
    ppermute x4, waiting for transfers between devices, shifted(): return lax.ppermute(block, axis, route)  8.21 us
    pallas_call x1, Pallas kernels, setup(): pl.pallas_call(setup_kernel, out_shape=[jax.ShapeDtypeStruct((ROUNDS * RE...  7.75 us
    ppermute x15, waiting for transfers between devices, hop(): lax.ppermute(block, 'tile', [(i, (i + distance) % peers) for i in range(p...  7.71 us
  transfers between devices with their start and end apart: 19, of which 8 were waited for; matrix products, arithmetic and copies ran while one was open for 1% of the time, Pallas kernels for 23%

profile of v7, /device:TPU:7, one launch (start us, length us, event | category | flops | bytes accessed | tf_op | source)
XLA Modules:
  0.0 123.0 jit_solution(16895791094563192590)
XLA Ops:
  0.6 0.0 copy-start
  0.6 1.1 pad_maximum_fusion.here_ref.refs_5_
  1.7 3.5 %collective-permute-start = (bf16[1408,128]{1,0:T(8,128)(2,1)S(1)}, bf16[1408,128]{1,0:T(8,128)(2,1)S(1)}, u32[]{:S(2)}, u32[]{:S(2)}) collective-permute-start(bf16[1408,128]{1,0:T(8,128)(2,1)S(1)} %pad_maximum_fusion.here_ref.refs_5_), channel_id=1, source_target_pairs={{0,1},{1,2},{2,3},{3,4},{4,5},{5,6},{6,7},{7,8},{8,9},{9,10},{10,1... | collective-permute-start | bytes 1081352 | tf_op jit(solution)/shard_map/ppermute | solution.py:290
  5.3 9.5 %collective-permute-start.2 = (bf16[1408,128]{1,0:T(8,128)(2,1)S(1)}, bf16[1408,128]{1,0:T(8,128)(2,1)S(1)}, u32[]{:S(2)}, u32[]{:S(2)}) collective-permute-start(bf16[1408,128]{1,0:T(8,128)(2,1)S(1)} %pad_maximum_fusion.here_ref.refs_5_), channel_id=1, source_target_pairs={{0,15},{1,0},{2,1},{3,2},{4,3},{5,4},{6,5},{7,6},{8,7},{9,8},{10,9... | collective-permute-start | bytes 1081352 | tf_op jit(solution)/shard_map/ppermute | solution.py:290
  14.8 0.7 fusion.10.key_ref
  15.5 7.7 %shard_map.104 = (s32[9248]{0:T(1024)S(1)}, s32[18]{0:T(128)S(1)}, bf16[128,128,32]{2,1,0:T(8,128)(2,1)S(1)}) custom-call(s32[8,128]{1,0:T(8,128)S(1)} %fusion.10.key_ref, bf16[1408,128]{1,0:T(8,128)(2,1)S(1)} %pad_maximum_fusion.here_ref.refs_5_), custom_call_target="tpu_custom_call" | custom-call | flops 1000000 | bytes 10000000 | tf_op jit(solution)/shard_map/pallas_call | solution.py:100
  23.2 0.0 copy-start.1
  23.2 0.0 collective-permute-done.refs_3_
  23.3 1.9 %collective-permute-start.1 = (bf16[1408,128]{1,0:T(8,128)(2,1)S(1)}, bf16[1408,128]{1,0:T(8,128)(2,1)S(1)}, u32[]{:S(2)}, u32[]{:S(2)}) collective-permute-start(bf16[1408,128]{1,0:T(8,128)(2,1)S(1)} %collective-permute-done.refs_3_), channel_id=1, source_target_pairs={{0,1},{1,2},{2,3},{3,4},{4,5},{5,6},{6,7},{7,8},{8,9},{9,10},{10,1... | collective-permute-start | bytes 1081352 | tf_op jit(solution)/shard_map/ppermute | solution.py:290
  25.2 0.0 collective-permute-done.2.refs_4_
  25.2 4.6 %collective-permute-start.4 = (bf16[1408,128]{1,0:T(8,128)(2,1)S(1)}, bf16[1408,128]{1,0:T(8,128)(2,1)S(1)}, u32[]{:S(2)}, u32[]{:S(2)}) collective-permute-start(bf16[1408,128]{1,0:T(8,128)(2,1)S(1)} %collective-permute-done.2.refs_4_), channel_id=1, source_target_pairs={{0,15},{1,0},{2,1},{3,2},{4,3},{5,4},{6,5},{7,6},{8,7},{9,8},{10,9... | collective-permute-start | bytes 1081352 | tf_op jit(solution)/shard_map/ppermute | solution.py:290
  29.8 3.3 %shard_map.105.refs_6_ = f32[2064,128]{1,0:T(8,128)S(1)} custom-call(s32[18]{0:T(128)S(1)} %get-tuple-element.26.refs_0_, s32[1056]{0:T(1024)S(1)} %get-tuple-element.54.refs_1_, bf16[128,128,32]{2,1,0:T(8,128)(2,1)S(1)} %get-tuple-element.28.refs_2_, bf16[1408,128]{1,0:T(8,128)(2,1)S(1)} %collective-permute-done.refs_3_, ...), custom_call_target="tpu_custom_call" | custom-call | flops 671088640 | bytes 8388608 | tf_op jit(solution)/shard_map/pallas_call | solution.py:275
  33.1 2.3 %collective-permute-done.1.refs_3_ = bf16[1408,128]{1,0:T(8,128)(2,1)S(1)} collective-permute-done((bf16[1408,128]{1,0:T(8,128)(2,1)S(1)}, bf16[1408,128]{1,0:T(8,128)(2,1)S(1)}, u32[]{:S(2)}, u32[]{:S(2)}) %collective-permute-start.1) | collective-permute-done | bytes 360480 | tf_op jit(solution)/shard_map/ppermute | solution.py:290
  35.3 1.9 %collective-permute-start.3 = (bf16[1408,128]{1,0:T(8,128)(2,1)S(1)}, bf16[1408,128]{1,0:T(8,128)(2,1)S(1)}, u32[]{:S(2)}, u32[]{:S(2)}) collective-permute-start(bf16[1408,128]{1,0:T(8,128)(2,1)S(1)} %collective-permute-done.1.refs_3_), channel_id=1, source_target_pairs={{0,1},{1,2},{2,3},{3,4},{4,5},{5,6},{6,7},{7,8},{8,9},{9,10},{10,1... | collective-permute-start | bytes 1081352 | tf_op jit(solution)/shard_map/ppermute | solution.py:290
  37.2 0.0 collective-permute-done.4.refs_4_
  37.3 4.6 %collective-permute-start.6 = (bf16[1408,128]{1,0:T(8,128)(2,1)S(1)}, bf16[1408,128]{1,0:T(8,128)(2,1)S(1)}, u32[]{:S(2)}, u32[]{:S(2)}) collective-permute-start(bf16[1408,128]{1,0:T(8,128)(2,1)S(1)} %collective-permute-done.4.refs_4_), channel_id=1, source_target_pairs={{0,15},{1,0},{2,1},{3,2},{4,3},{5,4},{6,5},{7,6},{8,7},{9,8},{10,9... | collective-permute-start | bytes 1081352 | tf_op jit(solution)/shard_map/ppermute | solution.py:290
  41.8 4.0 %shard_map.106.refs_6_ = f32[2064,128]{1,0:T(8,128)S(1)} custom-call(s32[18]{0:T(128)S(1)} %get-tuple-element.26.refs_0_, s32[1056]{0:T(1024)S(1)} %get-tuple-element.53.refs_1_, bf16[128,128,32]{2,1,0:T(8,128)(2,1)S(1)} %get-tuple-element.28.refs_2_, bf16[1408,128]{1,0:T(8,128)(2,1)S(1)} %collective-permute-done.1.refs_3_, ...), custom_call_target="tpu_custom_call" | custom-call | flops 671088640 | bytes 8388608 | tf_op jit(solution)/shard_map/pallas_call | solution.py:275
  45.8 0.6 collective-permute-done.3.refs_3_
  46.5 1.9 %collective-permute-start.5 = (bf16[1408,128]{1,0:T(8,128)(2,1)S(1)}, bf16[1408,128]{1,0:T(8,128)(2,1)S(1)}, u32[]{:S(2)}, u32[]{:S(2)}) collective-permute-start(bf16[1408,128]{1,0:T(8,128)(2,1)S(1)} %collective-permute-done.3.refs_3_), channel_id=1, source_target_pairs={{0,1},{1,2},{2,3},{3,4},{4,5},{5,6},{6,7},{7,8},{8,9},{9,10},{10,1... | collective-permute-start | bytes 1081352 | tf_op jit(solution)/shard_map/ppermute | solution.py:290
  48.4 0.0 collective-permute-done.6.refs_4_
  48.4 4.6 %collective-permute-start.8 = (bf16[1408,128]{1,0:T(8,128)(2,1)S(1)}, bf16[1408,128]{1,0:T(8,128)(2,1)S(1)}, u32[]{:S(2)}, u32[]{:S(2)}) collective-permute-start(bf16[1408,128]{1,0:T(8,128)(2,1)S(1)} %collective-permute-done.6.refs_4_), channel_id=1, source_target_pairs={{0,15},{1,0},{2,1},{3,2},{4,3},{5,4},{6,5},{7,6},{8,7},{9,8},{10,9... | collective-permute-start | bytes 1081352 | tf_op jit(solution)/shard_map/ppermute | solution.py:290
  53.0 4.0 %shard_map.107.refs_5_ = f32[2064,128]{1,0:T(8,128)S(1)} custom-call(s32[18]{0:T(128)S(1)} %get-tuple-element.26.refs_0_, s32[1056]{0:T(1024)S(1)} %get-tuple-element.52.refs_1_, bf16[128,128,32]{2,1,0:T(8,128)(2,1)S(1)} %get-tuple-element.28.refs_2_, bf16[1408,128]{1,0:T(8,128)(2,1)S(1)} %collective-permute-done.3.refs_3_, ...), custom_call_target="tpu_custom_call" | custom-call | flops 671088640 | bytes 8388608 | tf_op jit(solution)/shard_map/pallas_call | solution.py:275
  57.0 0.0 collective-permute-done.5.refs_3_
  57.0 1.9 %collective-permute-start.7 = (bf16[1408,128]{1,0:T(8,128)(2,1)S(1)}, bf16[1408,128]{1,0:T(8,128)(2,1)S(1)}, u32[]{:S(2)}, u32[]{:S(2)}) collective-permute-start(bf16[1408,128]{1,0:T(8,128)(2,1)S(1)} %collective-permute-done.5.refs_3_), channel_id=1, source_target_pairs={{0,1},{1,2},{2,3},{3,4},{4,5},{5,6},{6,7},{7,8},{8,9},{9,10},{10,1... | collective-permute-start | bytes 1081352 | tf_op jit(solution)/shard_map/ppermute | solution.py:290
  58.9 0.0 collective-permute-done.8.refs_4_
  58.9 4.6 %collective-permute-start.10 = (bf16[1408,128]{1,0:T(8,128)(2,1)S(1)}, bf16[1408,128]{1,0:T(8,128)(2,1)S(1)}, u32[]{:S(2)}, u32[]{:S(2)}) collective-permute-start(bf16[1408,128]{1,0:T(8,128)(2,1)S(1)} %collective-permute-done.8.refs_4_), channel_id=1, source_target_pairs={{0,15},{1,0},{2,1},{3,2},{4,3},{5,4},{6,5},{7,6},{8,7},{9,8},{10,9... | collective-permute-start | bytes 1081352 | tf_op jit(solution)/shard_map/ppermute | solution.py:290
  63.5 2.4 %shard_map.108.refs_5_ = f32[2064,128]{1,0:T(8,128)S(1)} custom-call(s32[18]{0:T(128)S(1)} %get-tuple-element.26.refs_0_, s32[1056]{0:T(1024)S(1)} %get-tuple-element.51.refs_1_, bf16[128,128,32]{2,1,0:T(8,128)(2,1)S(1)} %get-tuple-element.28.refs_2_, bf16[1408,128]{1,0:T(8,128)(2,1)S(1)} %collective-permute-done.5.refs_3_, ...), custom_call_target="tpu_custom_call" | custom-call | flops 671088640 | bytes 8388608 | tf_op jit(solution)/shard_map/pallas_call | solution.py:275
  65.9 0.5 collective-permute-done.7.refs_3_
  66.4 1.9 %collective-permute-start.9 = (bf16[1408,128]{1,0:T(8,128)(2,1)S(1)}, bf16[1408,128]{1,0:T(8,128)(2,1)S(1)}, u32[]{:S(2)}, u32[]{:S(2)}) collective-permute-start(bf16[1408,128]{1,0:T(8,128)(2,1)S(1)} %collective-permute-done.7.refs_3_), channel_id=1, source_target_pairs={{0,1},{1,2},{2,3},{3,4},{4,5},{5,6},{6,7},{7,8},{8,9},{9,10},{10,1... | collective-permute-start | bytes 1081352 | tf_op jit(solution)/shard_map/ppermute | solution.py:290
  68.3 0.0 collective-permute-done.10.refs_4_
  68.3 4.6 %collective-permute-start.12 = (bf16[1408,128]{1,0:T(8,128)(2,1)S(1)}, bf16[1408,128]{1,0:T(8,128)(2,1)S(1)}, u32[]{:S(2)}, u32[]{:S(2)}) collective-permute-start(bf16[1408,128]{1,0:T(8,128)(2,1)S(1)} %collective-permute-done.10.refs_4_), channel_id=1, source_target_pairs={{0,15},{1,0},{2,1},{3,2},{4,3},{5,4},{6,5},{7,6},{8,7},{9,8},{10,9... | collective-permute-start | bytes 1081352 | tf_op jit(solution)/shard_map/ppermute | solution.py:290
  72.9 2.4 %shard_map.109.refs_5_ = f32[2064,128]{1,0:T(8,128)S(1)} custom-call(s32[18]{0:T(128)S(1)} %get-tuple-element.26.refs_0_, s32[1056]{0:T(1024)S(1)} %get-tuple-element.50.refs_1_, bf16[128,128,32]{2,1,0:T(8,128)(2,1)S(1)} %get-tuple-element.28.refs_2_, bf16[1408,128]{1,0:T(8,128)(2,1)S(1)} %collective-permute-done.7.refs_3_, ...), custom_call_target="tpu_custom_call" | custom-call | flops 671088640 | bytes 8388608 | tf_op jit(solution)/shard_map/pallas_call | solution.py:275
  75.3 0.4 collective-permute-done.9.refs_3_
  75.7 1.9 %collective-permute-start.11 = (bf16[1408,128]{1,0:T(8,128)(2,1)S(1)}, bf16[1408,128]{1,0:T(8,128)(2,1)S(1)}, u32[]{:S(2)}, u32[]{:S(2)}) collective-permute-start(bf16[1408,128]{1,0:T(8,128)(2,1)S(1)} %collective-permute-done.9.refs_3_), channel_id=1, source_target_pairs={{0,1},{1,2},{2,3},{3,4},{4,5},{5,6},{6,7},{7,8},{8,9},{9,10},{10,1... | collective-permute-start | bytes 1081352 | tf_op jit(solution)/shard_map/ppermute | solution.py:290
  77.7 0.0 collective-permute-done.12.refs_4_
  77.7 4.6 %collective-permute-start.14 = (bf16[1408,128]{1,0:T(8,128)(2,1)S(1)}, bf16[1408,128]{1,0:T(8,128)(2,1)S(1)}, u32[]{:S(2)}, u32[]{:S(2)}) collective-permute-start(bf16[1408,128]{1,0:T(8,128)(2,1)S(1)} %collective-permute-done.12.refs_4_), channel_id=1, source_target_pairs={{0,15},{1,0},{2,1},{3,2},{4,3},{5,4},{6,5},{7,6},{8,7},{9,8},{10,9... | collective-permute-start | bytes 1081352 | tf_op jit(solution)/shard_map/ppermute | solution.py:290
  82.2 0.0 copy-done.1
  82.3 0.0 copy-start.6
  82.3 2.4 %shard_map.110.refs_5_ = f32[2064,128]{1,0:T(8,128)S(1)} custom-call(s32[18]{0:T(128)S(1)} %get-tuple-element.26.refs_0_, s32[1056]{0:T(1024)S(1)} %get-tuple-element.49.refs_1_, bf16[128,128,32]{2,1,0:T(8,128)(2,1)S(1)} %get-tuple-element.28.refs_2_, bf16[1408,128]{1,0:T(8,128)(2,1)S(1)} %collective-permute-done.9.refs_3_, ...), custom_call_target="tpu_custom_call" | custom-call | flops 671088640 | bytes 8388608 | tf_op jit(solution)/shard_map/pallas_call | solution.py:275
  84.7 0.4 collective-permute-done.11.refs_3_
  85.1 1.9 %collective-permute-start.13 = (bf16[1408,128]{1,0:T(8,128)(2,1)S(1)}, bf16[1408,128]{1,0:T(8,128)(2,1)S(1)}, u32[]{:S(2)}, u32[]{:S(2)}) collective-permute-start(bf16[1408,128]{1,0:T(8,128)(2,1)S(1)} %collective-permute-done.11.refs_3_), channel_id=1, source_target_pairs={{0,1},{1,2},{2,3},{3,4},{4,5},{5,6},{6,7},{7,8},{8,9},{9,10},{10,1... | collective-permute-start | bytes 1081352 | tf_op jit(solution)/shard_map/ppermute | solution.py:290
  87.0 0.0 copy-done.6
  87.0 0.0 collective-permute-done.14.refs_4_
  87.1 0.0 copy-start.2
  87.1 2.2 %copy-done.2 = bf16[128,128,32]{2,1,0:T(8,128)(2,1)S(1)} copy-done((bf16[128,128,32]{2,1,0:T(8,128)(2,1)S(1)}, bf16[128,128,32]{2,1,0:T(8,128)(2,1)}, u32[]{:S(2)}) %copy-start.2) | copy-done | bytes 1048600
  89.2 0.0 copy-start.3
  89.3 0.0 copy-start.4
  89.3 0.0 copy-start.5
  89.3 2.4 %shard_map.111.refs_4_ = f32[2064,128]{1,0:T(8,128)S(1)} custom-call(s32[18]{0:T(128)S(1)} %get-tuple-element.26.refs_0_, s32[1056]{0:T(1024)S(1)} %get-tuple-element.48.refs_1_, bf16[128,128,32]{2,1,0:T(8,128)(2,1)S(1)} %copy-done.2, bf16[1408,128]{1,0:T(8,128)(2,1)S(1)} %collective-permute-done.11.refs_3_, ...), custom_call_target="tpu_custom_call" | custom-call | flops 671088640 | bytes 8388608 | tf_op jit(solution)/shard_map/pallas_call | solution.py:275
  91.7 3.5 %collective-permute-done.13.refs_3_ = bf16[1408,128]{1,0:T(8,128)(2,1)S(1)} collective-permute-done((bf16[1408,128]{1,0:T(8,128)(2,1)S(1)}, bf16[1408,128]{1,0:T(8,128)(2,1)S(1)}, u32[]{:S(2)}, u32[]{:S(2)}) %collective-permute-start.13) | collective-permute-done | bytes 360480 | tf_op jit(solution)/shard_map/ppermute | solution.py:290
  95.1 0.0 copy-done.3
  95.1 0.0 copy-done.4
  95.1 0.0 copy-done.5
  95.1 2.3 %shard_map.112 = (f32[128,128]{1,0:T(8,128)}, f32[96,128]{1,0:T(8,128)S(1)}) custom-call(s32[18]{0:T(128)S(1)} %get-tuple-element.26.refs_0_, s32[1056]{0:T(1024)S(1)} %get-tuple-element.55.refs_1_, bf16[128,128,32]{2,1,0:T(8,128)(2,1)S(1)} %copy-done.2, bf16[1408,128]{1,0:T(8,128)(2,1)S(1)} %collective-permute-done.13.refs_3_, ...), custom_call_target="tpu_custom_call" | custom-call | flops 671088640 | bytes 8388608 | tf_op jit(solution)/shard_map/pallas_call | solution.py:275
  97.4 1.3 %collective-permute-start.15 = (f32[32,128]{1,0:T(8,128)S(1)}, f32[32,128]{1,0:T(8,128)S(1)}, u32[]{:S(2)}, u32[]{:S(2)}) collective-permute-start(f32[32,128]{1,0:T(8,128)S(1)} %get-tuple-element.46), channel_id=1, source_target_pairs={{0,1},{1,2},{2,3},{3,4},{4,5},{5,6},{6,7},{7,8},{8,9},{9,10},{10,1... | collective-permute-start | bytes 49160 | tf_op jit(solution)/shard_map/ppermute | solution.py:296
  98.7 1.3 %collective-permute-start.16 = (f32[32,128]{1,0:T(8,128)S(1)}, f32[32,128]{1,0:T(8,128)S(1)}, u32[]{:S(2)}, u32[]{:S(2)}) collective-permute-start(f32[32,128]{1,0:T(8,128)S(1)} %get-tuple-element.47), channel_id=1, source_target_pairs={{1,0},{2,1},{3,2},{4,3},{5,4},{6,5},{7,6},{8,7},{9,8},{10,9},{11,1... | collective-permute-start | bytes 49160 | tf_op jit(solution)/shard_map/ppermute | solution.py:296
  100.0 0.0 collective-permute-done.15
  100.0 3.2 %collective-permute-done.16 = f32[32,128]{1,0:T(8,128)S(1)} collective-permute-done((f32[32,128]{1,0:T(8,128)S(1)}, f32[32,128]{1,0:T(8,128)S(1)}, u32[]{:S(2)}, u32[]{:S(2)}) %collective-permute-start.16) | collective-permute-done | bytes 16416 | tf_op jit(solution)/shard_map/ppermute | solution.py:296
  103.2 12.1 %collective-permute-start.17 = (f32[1,128]{1,0:T(1,128)S(1)}, f32[1,128]{1,0:T(1,128)S(1)}, u32[]{:S(2)}, u32[]{:S(2)}) collective-permute-start(f32[1,128]{1,0:T(1,128)S(1)} %get-tuple-element.56), channel_id=1, source_target_pairs={{0,16},{16,32},{32,48},{48,64},{64,80},{80,96},{96,112},{112,128},... | collective-permute-start | bytes 1544 | tf_op jit(solution)/shard_map/ppermute | solution.py:296
  115.3 1.9 %collective-permute-start.18 = (f32[1,128]{1,0:T(1,128)S(1)}, f32[1,128]{1,0:T(1,128)S(1)}, u32[]{:S(2)}, u32[]{:S(2)}) collective-permute-start(f32[1,128]{1,0:T(1,128)S(1)} %get-tuple-element.57), channel_id=1, source_target_pairs={{16,0},{32,16},{48,32},{64,48},{80,64},{96,80},{112,96},{128,112},... | collective-permute-start | bytes 1544 | tf_op jit(solution)/shard_map/ppermute | solution.py:296
  117.2 0.0 collective-permute-done.17
  117.2 5.0 %collective-permute-done.18 = f32[1,128]{1,0:T(1,128)S(1)} collective-permute-done((f32[1,128]{1,0:T(1,128)S(1)}, f32[1,128]{1,0:T(1,128)S(1)}, u32[]{:S(2)}, u32[]{:S(2)}) %collective-permute-start.18) | collective-permute-done | bytes 544 | tf_op jit(solution)/shard_map/ppermute | solution.py:296
  122.2 0.0 copy-done
  122.2 0.8 convolution_add_fusion
  (6 shorter events, 0.0 us)
Async XLA Ops:
  0.6 121.6 %copy-start = (f32[128,128]{1,0:T(8,128)S(1)}, f32[128,128]{1,0:T(8,128)}, u32[]{:S(2)}) copy-start(f32[128,128]{1,0:T(8,128)} %param.17) | copy-start | bytes 196612
  1.7 21.6 %collective-permute-start = (bf16[1408,128]{1,0:T(8,128)(2,1)S(1)}, bf16[1408,128]{1,0:T(8,128)(2,1)S(1)}, u32[]{:S(2)}, u32[]{:S(2)}) collective-permute-start(bf16[1408,128]{1,0:T(8,128)(2,1)S(1)} %pad_maximum_fusion.here_ref.refs_5_), channel_id=1, source_target_pairs={{0,1},{1,2},{2,3},{3,4},{4,5},{5,6},{6,7},{7,8},{8,9},{9,10},{10,1... | collective-permute-start | bytes 1081352 | tf_op jit(solution)/shard_map/ppermute | solution.py:290
  5.3 19.9 %collective-permute-start.2 = (bf16[1408,128]{1,0:T(8,128)(2,1)S(1)}, bf16[1408,128]{1,0:T(8,128)(2,1)S(1)}, u32[]{:S(2)}, u32[]{:S(2)}) collective-permute-start(bf16[1408,128]{1,0:T(8,128)(2,1)S(1)} %pad_maximum_fusion.here_ref.refs_5_), channel_id=1, source_target_pairs={{0,15},{1,0},{2,1},{3,2},{4,3},{5,4},{6,5},{7,6},{8,7},{9,8},{10,9... | collective-permute-start | bytes 1081352 | tf_op jit(solution)/shard_map/ppermute | solution.py:290
  23.2 59.0 %copy-start.1 = (bf16[128,128,32]{2,1,0:T(8,128)(2,1)}, bf16[128,128,32]{2,1,0:T(8,128)(2,1)S(1)}, u32[]{:S(2)}) copy-start(bf16[128,128,32]{2,1,0:T(8,128)(2,1)S(1)} %get-tuple-element.28.refs_2_) | copy-start | bytes 3145732
  23.3 12.1 %collective-permute-start.1 = (bf16[1408,128]{1,0:T(8,128)(2,1)S(1)}, bf16[1408,128]{1,0:T(8,128)(2,1)S(1)}, u32[]{:S(2)}, u32[]{:S(2)}) collective-permute-start(bf16[1408,128]{1,0:T(8,128)(2,1)S(1)} %collective-permute-done.refs_3_), channel_id=1, source_target_pairs={{0,1},{1,2},{2,3},{3,4},{4,5},{5,6},{6,7},{7,8},{8,9},{9,10},{10,1... | collective-permute-start | bytes 1081352 | tf_op jit(solution)/shard_map/ppermute | solution.py:290
  25.2 12.0 %collective-permute-start.4 = (bf16[1408,128]{1,0:T(8,128)(2,1)S(1)}, bf16[1408,128]{1,0:T(8,128)(2,1)S(1)}, u32[]{:S(2)}, u32[]{:S(2)}) collective-permute-start(bf16[1408,128]{1,0:T(8,128)(2,1)S(1)} %collective-permute-done.2.refs_4_), channel_id=1, source_target_pairs={{0,15},{1,0},{2,1},{3,2},{4,3},{5,4},{6,5},{7,6},{8,7},{9,8},{10,9... | collective-permute-start | bytes 1081352 | tf_op jit(solution)/shard_map/ppermute | solution.py:290
  35.3 11.1 %collective-permute-start.3 = (bf16[1408,128]{1,0:T(8,128)(2,1)S(1)}, bf16[1408,128]{1,0:T(8,128)(2,1)S(1)}, u32[]{:S(2)}, u32[]{:S(2)}) collective-permute-start(bf16[1408,128]{1,0:T(8,128)(2,1)S(1)} %collective-permute-done.1.refs_3_), channel_id=1, source_target_pairs={{0,1},{1,2},{2,3},{3,4},{4,5},{5,6},{6,7},{7,8},{8,9},{9,10},{10,1... | collective-permute-start | bytes 1081352 | tf_op jit(solution)/shard_map/ppermute | solution.py:290
  37.3 11.1 %collective-permute-start.6 = (bf16[1408,128]{1,0:T(8,128)(2,1)S(1)}, bf16[1408,128]{1,0:T(8,128)(2,1)S(1)}, u32[]{:S(2)}, u32[]{:S(2)}) collective-permute-start(bf16[1408,128]{1,0:T(8,128)(2,1)S(1)} %collective-permute-done.4.refs_4_), channel_id=1, source_target_pairs={{0,15},{1,0},{2,1},{3,2},{4,3},{5,4},{6,5},{7,6},{8,7},{9,8},{10,9... | collective-permute-start | bytes 1081352 | tf_op jit(solution)/shard_map/ppermute | solution.py:290
  46.5 10.5 %collective-permute-start.5 = (bf16[1408,128]{1,0:T(8,128)(2,1)S(1)}, bf16[1408,128]{1,0:T(8,128)(2,1)S(1)}, u32[]{:S(2)}, u32[]{:S(2)}) collective-permute-start(bf16[1408,128]{1,0:T(8,128)(2,1)S(1)} %collective-permute-done.3.refs_3_), channel_id=1, source_target_pairs={{0,1},{1,2},{2,3},{3,4},{4,5},{5,6},{6,7},{7,8},{8,9},{9,10},{10,1... | collective-permute-start | bytes 1081352 | tf_op jit(solution)/shard_map/ppermute | solution.py:290
  48.4 10.5 %collective-permute-start.8 = (bf16[1408,128]{1,0:T(8,128)(2,1)S(1)}, bf16[1408,128]{1,0:T(8,128)(2,1)S(1)}, u32[]{:S(2)}, u32[]{:S(2)}) collective-permute-start(bf16[1408,128]{1,0:T(8,128)(2,1)S(1)} %collective-permute-done.6.refs_4_), channel_id=1, source_target_pairs={{0,15},{1,0},{2,1},{3,2},{4,3},{5,4},{6,5},{7,6},{8,7},{9,8},{10,9... | collective-permute-start | bytes 1081352 | tf_op jit(solution)/shard_map/ppermute | solution.py:290
  57.0 9.4 %collective-permute-start.7 = (bf16[1408,128]{1,0:T(8,128)(2,1)S(1)}, bf16[1408,128]{1,0:T(8,128)(2,1)S(1)}, u32[]{:S(2)}, u32[]{:S(2)}) collective-permute-start(bf16[1408,128]{1,0:T(8,128)(2,1)S(1)} %collective-permute-done.5.refs_3_), channel_id=1, source_target_pairs={{0,1},{1,2},{2,3},{3,4},{4,5},{5,6},{6,7},{7,8},{8,9},{9,10},{10,1... | collective-permute-start | bytes 1081352 | tf_op jit(solution)/shard_map/ppermute | solution.py:290
  58.9 9.4 %collective-permute-start.10 = (bf16[1408,128]{1,0:T(8,128)(2,1)S(1)}, bf16[1408,128]{1,0:T(8,128)(2,1)S(1)}, u32[]{:S(2)}, u32[]{:S(2)}) collective-permute-start(bf16[1408,128]{1,0:T(8,128)(2,1)S(1)} %collective-permute-done.8.refs_4_), channel_id=1, source_target_pairs={{0,15},{1,0},{2,1},{3,2},{4,3},{5,4},{6,5},{7,6},{8,7},{9,8},{10,9... | collective-permute-start | bytes 1081352 | tf_op jit(solution)/shard_map/ppermute | solution.py:290
  66.4 9.4 %collective-permute-start.9 = (bf16[1408,128]{1,0:T(8,128)(2,1)S(1)}, bf16[1408,128]{1,0:T(8,128)(2,1)S(1)}, u32[]{:S(2)}, u32[]{:S(2)}) collective-permute-start(bf16[1408,128]{1,0:T(8,128)(2,1)S(1)} %collective-permute-done.7.refs_3_), channel_id=1, source_target_pairs={{0,1},{1,2},{2,3},{3,4},{4,5},{5,6},{6,7},{7,8},{8,9},{9,10},{10,1... | collective-permute-start | bytes 1081352 | tf_op jit(solution)/shard_map/ppermute | solution.py:290
  68.3 9.4 %collective-permute-start.12 = (bf16[1408,128]{1,0:T(8,128)(2,1)S(1)}, bf16[1408,128]{1,0:T(8,128)(2,1)S(1)}, u32[]{:S(2)}, u32[]{:S(2)}) collective-permute-start(bf16[1408,128]{1,0:T(8,128)(2,1)S(1)} %collective-permute-done.10.refs_4_), channel_id=1, source_target_pairs={{0,15},{1,0},{2,1},{3,2},{4,3},{5,4},{6,5},{7,6},{8,7},{9,8},{10,9... | collective-permute-start | bytes 1081352 | tf_op jit(solution)/shard_map/ppermute | solution.py:290
  75.7 9.4 %collective-permute-start.11 = (bf16[1408,128]{1,0:T(8,128)(2,1)S(1)}, bf16[1408,128]{1,0:T(8,128)(2,1)S(1)}, u32[]{:S(2)}, u32[]{:S(2)}) collective-permute-start(bf16[1408,128]{1,0:T(8,128)(2,1)S(1)} %collective-permute-done.9.refs_3_), channel_id=1, source_target_pairs={{0,1},{1,2},{2,3},{3,4},{4,5},{5,6},{6,7},{7,8},{8,9},{9,10},{10,1... | collective-permute-start | bytes 1081352 | tf_op jit(solution)/shard_map/ppermute | solution.py:290
  77.7 9.4 %collective-permute-start.14 = (bf16[1408,128]{1,0:T(8,128)(2,1)S(1)}, bf16[1408,128]{1,0:T(8,128)(2,1)S(1)}, u32[]{:S(2)}, u32[]{:S(2)}) collective-permute-start(bf16[1408,128]{1,0:T(8,128)(2,1)S(1)} %collective-permute-done.12.refs_4_), channel_id=1, source_target_pairs={{0,15},{1,0},{2,1},{3,2},{4,3},{5,4},{6,5},{7,6},{8,7},{9,8},{10,9... | collective-permute-start | bytes 1081352 | tf_op jit(solution)/shard_map/ppermute | solution.py:290
  82.3 4.8 %copy-start.6 = (s32[1,128]{1,0:T(1,128)S(1)}, s32[1,128]{1,0:T(1,128)}, u32[]{:S(2)}) copy-start(s32[1,128]{1,0:T(1,128)} %param.15) | copy-start | bytes 1540
  85.1 10.0 %collective-permute-start.13 = (bf16[1408,128]{1,0:T(8,128)(2,1)S(1)}, bf16[1408,128]{1,0:T(8,128)(2,1)S(1)}, u32[]{:S(2)}, u32[]{:S(2)}) collective-permute-start(bf16[1408,128]{1,0:T(8,128)(2,1)S(1)} %collective-permute-done.11.refs_3_), channel_id=1, source_target_pairs={{0,1},{1,2},{2,3},{3,4},{4,5},{5,6},{6,7},{7,8},{8,9},{9,10},{10,1... | collective-permute-start | bytes 1081352 | tf_op jit(solution)/shard_map/ppermute | solution.py:290
  87.1 2.2 %copy-start.2 = (bf16[128,128,32]{2,1,0:T(8,128)(2,1)S(1)}, bf16[128,128,32]{2,1,0:T(8,128)(2,1)}, u32[]{:S(2)}) copy-start(bf16[128,128,32]{2,1,0:T(8,128)(2,1)} %copy-done.1) | copy-start | bytes 3145732
  89.2 5.9 %copy-start.3 = (bf16[1024,128]{1,0:T(8,128)(2,1)S(1)}, bf16[1024,128]{1,0:T(8,128)(2,1)}, u32[]{:S(2)}) copy-start(bf16[1024,128]{1,0:T(8,128)(2,1)} %refs_7_.1) | copy-start | bytes 786436
  89.3 5.9 %copy-start.4 = (f32[1,128,128]{2,1,0:T(8,128)S(1)}, f32[1,128,128]{2,1,0:T(8,128)}, u32[]{:S(2)}) copy-start(f32[1,128,128]{2,1,0:T(8,128)} %param.11) | copy-start | bytes 196612
  89.3 5.9 %copy-start.5 = (f32[1,128,128]{2,1,0:T(8,128)S(1)}, f32[1,128,128]{2,1,0:T(8,128)}, u32[]{:S(2)}) copy-start(f32[1,128,128]{2,1,0:T(8,128)} %param.12) | copy-start | bytes 196612
  97.4 2.6 %collective-permute-start.15 = (f32[32,128]{1,0:T(8,128)S(1)}, f32[32,128]{1,0:T(8,128)S(1)}, u32[]{:S(2)}, u32[]{:S(2)}) collective-permute-start(f32[32,128]{1,0:T(8,128)S(1)} %get-tuple-element.46), channel_id=1, source_target_pairs={{0,1},{1,2},{2,3},{3,4},{4,5},{5,6},{6,7},{7,8},{8,9},{9,10},{10,1... | collective-permute-start | bytes 49160 | tf_op jit(solution)/shard_map/ppermute | solution.py:296
  98.7 4.5 %collective-permute-start.16 = (f32[32,128]{1,0:T(8,128)S(1)}, f32[32,128]{1,0:T(8,128)S(1)}, u32[]{:S(2)}, u32[]{:S(2)}) collective-permute-start(f32[32,128]{1,0:T(8,128)S(1)} %get-tuple-element.47), channel_id=1, source_target_pairs={{1,0},{2,1},{3,2},{4,3},{5,4},{6,5},{7,6},{8,7},{9,8},{10,9},{11,1... | collective-permute-start | bytes 49160 | tf_op jit(solution)/shard_map/ppermute | solution.py:296
  103.2 14.0 %collective-permute-start.17 = (f32[1,128]{1,0:T(1,128)S(1)}, f32[1,128]{1,0:T(1,128)S(1)}, u32[]{:S(2)}, u32[]{:S(2)}) collective-permute-start(f32[1,128]{1,0:T(1,128)S(1)} %get-tuple-element.56), channel_id=1, source_target_pairs={{0,16},{16,32},{32,48},{48,64},{64,80},{80,96},{96,112},{112,128},... | collective-permute-start | bytes 1544 | tf_op jit(solution)/shard_map/ppermute | solution.py:296
  115.3 7.0 %collective-permute-start.18 = (f32[1,128]{1,0:T(1,128)S(1)}, f32[1,128]{1,0:T(1,128)S(1)}, u32[]{:S(2)}, u32[]{:S(2)}) collective-permute-start(f32[1,128]{1,0:T(1,128)S(1)} %get-tuple-element.57), channel_id=1, source_target_pairs={{16,0},{32,16},{48,32},{64,48},{80,64},{96,80},{112,96},{128,112},... | collective-permute-start | bytes 1544 | tf_op jit(solution)/shard_map/ppermute | solution.py:296

commit v8 on v7

--- a/solution.py
+++ b/solution.py
@@ -65,17 +65,23 @@
         x_ref[g * 4 + m] = turned[:, m * 2 * KDIM : (m + 1) * 2 * KDIM]
 
 
-def setup_kernel(
-    key_ref, here_ref, list_ref, bounds_ref, x_ref, low_ref, high_ref, rows_ref
-):
+def turn_kernel(here_ref, x_ref, rows_ref):
     reader_rows(here_ref, rows_ref)
+
+    def sixteen(i, carry):
+        for u in range(4):
+            turn_rows(i * 4 + u, rows_ref, x_ref)
+        return carry
+
+    lax.fori_loop(0, CL // 16, sixteen, 0)
+
+
+def list_kernel(key_ref, list_ref, bounds_ref, low_ref, high_ref):
     for k in range(ROUNDS):
         low_ref[k] = k * REGION + REGION // 2
         high_ref[k] = k * REGION + REGION // 2
 
     def sixteen(i, carry):
-        for u in range(4):
-            turn_rows(i * 4 + u, rows_ref, x_ref)
         for u in range(8):
             for p in range(PAIRS):
                 key = key_ref[p, i * 8 + u]
@@ -96,24 +102,30 @@
         bounds_ref[ROUNDS + k] = high_ref[k]
 
 
-def setup(keys, own):
+def make_lists(keys):
     return pl.pallas_call(
-        setup_kernel,
+        list_kernel,
         out_shape=[
             jax.ShapeDtypeStruct((ROUNDS * REGION + STEP,), jnp.int32),
             jax.ShapeDtypeStruct((2 * ROUNDS,), jnp.int32),
-            jax.ShapeDtypeStruct((CL, PTS, 2 * KDIM), jnp.bfloat16),
         ],
-        in_specs=[SMEM, VMEM],
-        out_specs=[SMEM] * 2 + [VMEM],
-        scratch_shapes=[
-            pltpu.SMEM((ROUNDS,), jnp.int32),
-            pltpu.SMEM((ROUNDS,), jnp.int32),
-            pltpu.VMEM((CL * KDIM, PTS), jnp.float32),
-        ],
+        in_specs=[SMEM],
+        out_specs=[SMEM] * 2,
+        scratch_shapes=[pltpu.SMEM((ROUNDS,), jnp.int32), pltpu.SMEM((ROUNDS,), jnp.int32)],
+        cost_estimate=pl.CostEstimate(flops=10**6, bytes_accessed=10**7, transcendentals=0),
+    )(keys)
+
+
+def turned_rows(own):
+    return pl.pallas_call(
+        turn_kernel,
+        out_shape=jax.ShapeDtypeStruct((CL, PTS, 2 * KDIM), jnp.bfloat16),
+        in_specs=[VMEM],
+        out_specs=VMEM,
+        scratch_shapes=[pltpu.VMEM((CL * KDIM, PTS), jnp.float32)],
         compiler_params=pltpu.CompilerParams(vmem_limit_bytes=16 * 2**20),
         cost_estimate=pl.CostEstimate(flops=10**6, bytes_accessed=10**7, transcendentals=0),
-    )(keys, own)
+    )(own)
 
 
 def pair_keys(ids, counts, tile):
@@ -315,19 +327,26 @@
     last = N_TILE // 2 - 1
     up, down = hop(own, 1), hop(own, -1)
     keys = pair_keys(pair_ids[0].T, reader_counts, tile)
-    prepared = setup(keys, own)
+    lists = make_lists(keys)
     acc = None
+    blocks = {}
     for s in range(1, last + 1):
-        block = [(0, [up]), (1, [down])] + ([(2, [own])] if s <= OWN_ROUNDS else [])
-        if acc is None:
-            up, prepared = lax.optimization_barrier((up, prepared))
+        blocks[s] = [(0, [up]), (1, [down])] + ([(2, [own])] if s <= OWN_ROUNDS else [])
+        if s == 1:
+            up, lists, later = lax.optimization_barrier((up, lists, own))
+            x_rows = turned_rows(later)
+        elif s == 2:
+            up, x_rows = lax.optimization_barrier((up, x_rows))
         else:
+            acc = consume((*lists, x_rows), s - 2, blocks[s - 2], acc)
             up, acc = lax.optimization_barrier((up, acc))
         if s < last:
             up, down = hop(up, 1), hop(down, -1)
         else:
             far = hop(up, 1)
-        acc = consume(prepared, s, block, acc)
+    prepared = (*lists, x_rows)
+    for s in (last - 1, last):
+        acc = consume(prepared, s, blocks[s], acc)
     brick = brick_map - (tile - 1) * BR_DEV
     damage_here, shares = consume(
         prepared, last + 1, [(1, [far])], acc, (kappa_old[0], threshold[0], strain_disp, brick)

time: 124 us -> 123 us (level)
  waiting for transfers between devices: 15.9 us -> 12.5 us
  starting transfers between devices: 70.4 us -> 72.1 us
    ppermute x15, waiting for transfers between devices: 7.71 us -> 4.26 us  [hop(): lax.ppermute(block, 'tile', [(i, (i + distance) % peers) for i in range(p...]
    ppermute x4, starting transfers between devices: 16.6 us -> 18.2 us  [shifted(): return lax.ppermute(block, axis, route)]
    pallas_call x1 -> x2, Pallas kernels: 7.75 us -> 8.8 us  [the longest x1 5.07 us: make_lists(): pl.pallas_call(list_kernel, out_shape=[jax.ShapeDtypeStruct((ROUNDS * REG...]
  transfers between devices with their start and end apart: 19 -> 19, of which waited for: 8 -> 8; matrix products, arithmetic and copies ran while one was open for 1% -> 1% of each run, Pallas kernels for 23% -> 24%
where the time goes in v8:
time: 123 us; the launch traced here: 122 us
  starting transfers between devices  72.1 us (59%)
  Pallas kernels  31.2 us (25%)
  waiting for transfers between devices  12.5 us (10%)
  other arithmetic  2.37 us (2%)
  local copies, waits for them, and re-layouts  2.25 us (2%)
    ppermute x15, starting transfers between devices, hop(): lax.ppermute(block, 'tile', [(i, (i + distance) % peers) for i in range(p...  53.9 us
    pallas_call x8, Pallas kernels, consume(): pl.pallas_call(functools.partial(ring_kernel, turn, shape, acc is not Non...  22.4 us
    ppermute x4, starting transfers between devices, shifted(): return lax.ppermute(block, axis, route)  18.2 us
    ppermute x4, waiting for transfers between devices, shifted(): return lax.ppermute(block, axis, route)  8.21 us
    pallas_call x1, Pallas kernels, make_lists(): pl.pallas_call(list_kernel, out_shape=[jax.ShapeDtypeStruct((ROUNDS * REG...  5.07 us
    ppermute x15, waiting for transfers between devices, hop(): lax.ppermute(block, 'tile', [(i, (i + distance) % peers) for i in range(p...  4.26 us
    pallas_call x1, Pallas kernels, turned_rows(): pl.pallas_call(turn_kernel, out_shape=jax.ShapeDtypeStruct((CL, PTS, 2 *...  3.74 us
  transfers between devices with their start and end apart: 19, of which 8 were waited for; matrix products, arithmetic and copies ran while one was open for 1% of the time, Pallas kernels for 24%

profile of v8, /device:TPU:7, one launch (start us, length us, event | category | flops | bytes accessed | tf_op | source)
XLA Modules:
  0.0 122.3 jit_solution(5072283527545674006)
XLA Ops:
  0.6 0.0 copy-start
  0.6 1.1 pad_maximum_fusion.here_ref.refs_5_
  1.7 3.5 %collective-permute-start = (bf16[1408,128]{1,0:T(8,128)(2,1)S(1)}, bf16[1408,128]{1,0:T(8,128)(2,1)S(1)}, u32[]{:S(2)}, u32[]{:S(2)}) collective-permute-start(bf16[1408,128]{1,0:T(8,128)(2,1)S(1)} %pad_maximum_fusion.here_ref.refs_5_), channel_id=1, source_target_pairs={{0,1},{1,2},{2,3},{3,4},{4,5},{5,6},{6,7},{7,8},{8,9},{9,10},{10,1... | collective-permute-start | bytes 1081352 | tf_op jit(solution)/shard_map/ppermute | solution.py:302
  5.3 9.5 %collective-permute-start.3 = (bf16[1408,128]{1,0:T(8,128)(2,1)S(1)}, bf16[1408,128]{1,0:T(8,128)(2,1)S(1)}, u32[]{:S(2)}, u32[]{:S(2)}) collective-permute-start(bf16[1408,128]{1,0:T(8,128)(2,1)S(1)} %pad_maximum_fusion.here_ref.refs_5_), channel_id=1, source_target_pairs={{0,15},{1,0},{2,1},{3,2},{4,3},{5,4},{6,5},{7,6},{8,7},{9,8},{10,9... | collective-permute-start | bytes 1081352 | tf_op jit(solution)/shard_map/ppermute | solution.py:302
  14.8 1.3 %fusion.10.key_ref = s32[8,128]{1,0:T(8,128)} fusion(s32[1,128,8]{1,2,0:T(8,128)} %param.13, s32[128]{0:T(128)S(1)} %get-tuple-element.56, s32[128]{0:T(128)S(1)} %get-tuple-element.57, s32[]{:T(128)S(6)} %axis_index.12, s32[128]{0:T(128)} %bitcast.39), kind=kLoop, calls=%fused_computation.15 | loop fusion | flops 18432 | bytes 9732 | tf_op jit(solution)/shard_map/or | solution.py:140
  16.1 5.1 %shard_map.104 = (s32[9248]{0:T(1024)}, s32[18]{0:T(128)}) custom-call(s32[8,128]{1,0:T(8,128)} %fusion.10.key_ref), custom_call_target="tpu_custom_call" | custom-call | flops 1000000 | bytes 10000000 | tf_op jit(solution)/shard_map/pallas_call | solution.py:106
  21.1 0.0 collective-permute-done.refs_3_
  21.2 0.0 copy-start.7
  21.2 0.0 copy-start.6
  21.2 1.9 %collective-permute-start.1 = (bf16[1408,128]{1,0:T(8,128)(2,1)S(1)}, bf16[1408,128]{1,0:T(8,128)(2,1)S(1)}, u32[]{:S(2)}, u32[]{:S(2)}) collective-permute-start(bf16[1408,128]{1,0:T(8,128)(2,1)S(1)} %collective-permute-done.refs_3_), channel_id=1, source_target_pairs={{0,1},{1,2},{2,3},{3,4},{4,5},{5,6},{6,7},{7,8},{8,9},{9,10},{10,1... | collective-permute-start | bytes 1081352 | tf_op jit(solution)/shard_map/ppermute | solution.py:302
  23.1 0.0 collective-permute-done.3.refs_4_
  23.1 4.6 %collective-permute-start.5 = (bf16[1408,128]{1,0:T(8,128)(2,1)S(1)}, bf16[1408,128]{1,0:T(8,128)(2,1)S(1)}, u32[]{:S(2)}, u32[]{:S(2)}) collective-permute-start(bf16[1408,128]{1,0:T(8,128)(2,1)S(1)} %collective-permute-done.3.refs_4_), channel_id=1, source_target_pairs={{0,15},{1,0},{2,1},{3,2},{4,3},{5,4},{6,5},{7,6},{8,7},{9,8},{10,9... | collective-permute-start | bytes 1081352 | tf_op jit(solution)/shard_map/ppermute | solution.py:302
  27.7 3.7 %shard_map.105.refs_2_ = bf16[128,128,32]{2,1,0:T(8,128)(2,1)S(1)} custom-call(bf16[1408,128]{1,0:T(8,128)(2,1)S(1)} %pad_maximum_fusion.here_ref.refs_5_), custom_call_target="tpu_custom_call" | custom-call | flops 1000000 | bytes 10000000 | tf_op jit(solution)/shard_map/pallas_call | solution.py:120
  31.4 0.0 copy-start.1
  31.5 1.6 %collective-permute-done.1.refs_3_ = bf16[1408,128]{1,0:T(8,128)(2,1)S(1)} collective-permute-done((bf16[1408,128]{1,0:T(8,128)(2,1)S(1)}, bf16[1408,128]{1,0:T(8,128)(2,1)S(1)}, u32[]{:S(2)}, u32[]{:S(2)}) %collective-permute-start.1) | collective-permute-done | bytes 360480 | tf_op jit(solution)/shard_map/ppermute | solution.py:302
  33.1 1.9 %collective-permute-start.2 = (bf16[1408,128]{1,0:T(8,128)(2,1)S(1)}, bf16[1408,128]{1,0:T(8,128)(2,1)S(1)}, u32[]{:S(2)}, u32[]{:S(2)}) collective-permute-start(bf16[1408,128]{1,0:T(8,128)(2,1)S(1)} %collective-permute-done.1.refs_3_), channel_id=1, source_target_pairs={{0,1},{1,2},{2,3},{3,4},{4,5},{5,6},{6,7},{7,8},{8,9},{9,10},{10,1... | collective-permute-start | bytes 1081352 | tf_op jit(solution)/shard_map/ppermute | solution.py:302
  35.0 0.0 copy-done.7
  35.0 0.0 collective-permute-done.5.refs_4_
  35.0 4.6 %collective-permute-start.7 = (bf16[1408,128]{1,0:T(8,128)(2,1)S(1)}, bf16[1408,128]{1,0:T(8,128)(2,1)S(1)}, u32[]{:S(2)}, u32[]{:S(2)}) collective-permute-start(bf16[1408,128]{1,0:T(8,128)(2,1)S(1)} %collective-permute-done.5.refs_4_), channel_id=1, source_target_pairs={{0,15},{1,0},{2,1},{3,2},{4,3},{5,4},{6,5},{7,6},{8,7},{9,8},{10,9... | collective-permute-start | bytes 1081352 | tf_op jit(solution)/shard_map/ppermute | solution.py:302
  39.6 0.0 copy-done.6
  39.6 3.3 %shard_map.106.refs_6_ = f32[2064,128]{1,0:T(8,128)S(1)} custom-call(s32[18]{0:T(128)S(1)} %copy-done.6, s32[1056]{0:T(1024)S(1)} %get-tuple-element.52.refs_1_, bf16[128,128,32]{2,1,0:T(8,128)(2,1)S(1)} %shard_map.105.refs_2_, bf16[1408,128]{1,0:T(8,128)(2,1)S(1)} %collective-permute-done.refs_3_, bf16[1408,128]{1,0:T(8,128)(2,1)S(1)} %collective-permute-done.3.refs_4_, ...), custom_call_target="tpu_custom_call" | custom-call | flops 671088640 | bytes 8388608 | tf_op jit(solution)/shard_map/pallas_call | solution.py:287
  42.9 1.1 collective-permute-done.2.refs_3_
  44.0 1.9 %collective-permute-start.4 = (bf16[1408,128]{1,0:T(8,128)(2,1)S(1)}, bf16[1408,128]{1,0:T(8,128)(2,1)S(1)}, u32[]{:S(2)}, u32[]{:S(2)}) collective-permute-start(bf16[1408,128]{1,0:T(8,128)(2,1)S(1)} %collective-permute-done.2.refs_3_), channel_id=1, source_target_pairs={{0,1},{1,2},{2,3},{3,4},{4,5},{5,6},{6,7},{7,8},{8,9},{9,10},{10,1... | collective-permute-start | bytes 1081352 | tf_op jit(solution)/shard_map/ppermute | solution.py:302
  45.9 0.0 collective-permute-done.7.refs_4_
  45.9 4.6 %collective-permute-start.9 = (bf16[1408,128]{1,0:T(8,128)(2,1)S(1)}, bf16[1408,128]{1,0:T(8,128)(2,1)S(1)}, u32[]{:S(2)}, u32[]{:S(2)}) collective-permute-start(bf16[1408,128]{1,0:T(8,128)(2,1)S(1)} %collective-permute-done.7.refs_4_), channel_id=1, source_target_pairs={{0,15},{1,0},{2,1},{3,2},{4,3},{5,4},{6,5},{7,6},{8,7},{9,8},{10,9... | collective-permute-start | bytes 1081352 | tf_op jit(solution)/shard_map/ppermute | solution.py:302
  50.5 3.3 %shard_map.107.refs_6_ = f32[2064,128]{1,0:T(8,128)S(1)} custom-call(s32[18]{0:T(128)S(1)} %copy-done.6, s32[1056]{0:T(1024)S(1)} %get-tuple-element.51.refs_1_, bf16[128,128,32]{2,1,0:T(8,128)(2,1)S(1)} %shard_map.105.refs_2_, bf16[1408,128]{1,0:T(8,128)(2,1)S(1)} %collective-permute-done.1.refs_3_, bf16[1408,128]{1,0:T(8,128)(2,1)S(1)} %collective-permute-done.5.refs_4_, ...), custom_call_target="tpu_custom_call" | custom-call | flops 671088640 | bytes 8388608 | tf_op jit(solution)/shard_map/pallas_call | solution.py:287
  53.8 0.2 collective-permute-done.4.refs_3_
  54.0 1.9 %collective-permute-start.6 = (bf16[1408,128]{1,0:T(8,128)(2,1)S(1)}, bf16[1408,128]{1,0:T(8,128)(2,1)S(1)}, u32[]{:S(2)}, u32[]{:S(2)}) collective-permute-start(bf16[1408,128]{1,0:T(8,128)(2,1)S(1)} %collective-permute-done.4.refs_3_), channel_id=1, source_target_pairs={{0,1},{1,2},{2,3},{3,4},{4,5},{5,6},{6,7},{7,8},{8,9},{9,10},{10,1... | collective-permute-start | bytes 1081352 | tf_op jit(solution)/shard_map/ppermute | solution.py:302
  56.0 0.0 collective-permute-done.9.refs_4_
  56.0 4.6 %collective-permute-start.11 = (bf16[1408,128]{1,0:T(8,128)(2,1)S(1)}, bf16[1408,128]{1,0:T(8,128)(2,1)S(1)}, u32[]{:S(2)}, u32[]{:S(2)}) collective-permute-start(bf16[1408,128]{1,0:T(8,128)(2,1)S(1)} %collective-permute-done.9.refs_4_), channel_id=1, source_target_pairs={{0,15},{1,0},{2,1},{3,2},{4,3},{5,4},{6,5},{7,6},{8,7},{9,8},{10,9... | collective-permute-start | bytes 1081352 | tf_op jit(solution)/shard_map/ppermute | solution.py:302
  60.5 4.0 %shard_map.108.refs_5_ = f32[2064,128]{1,0:T(8,128)S(1)} custom-call(s32[18]{0:T(128)S(1)} %copy-done.6, s32[1056]{0:T(1024)S(1)} %get-tuple-element.50.refs_1_, bf16[128,128,32]{2,1,0:T(8,128)(2,1)S(1)} %shard_map.105.refs_2_, bf16[1408,128]{1,0:T(8,128)(2,1)S(1)} %collective-permute-done.2.refs_3_, bf16[1408,128]{1,0:T(8,128)(2,1)S(1)} %collective-permute-done.7.refs_4_, ...), custom_call_target="tpu_custom_call" | custom-call | flops 671088640 | bytes 8388608 | tf_op jit(solution)/shard_map/pallas_call | solution.py:287
  64.6 0.0 collective-permute-done.6.refs_3_
  64.6 1.9 %collective-permute-start.8 = (bf16[1408,128]{1,0:T(8,128)(2,1)S(1)}, bf16[1408,128]{1,0:T(8,128)(2,1)S(1)}, u32[]{:S(2)}, u32[]{:S(2)}) collective-permute-start(bf16[1408,128]{1,0:T(8,128)(2,1)S(1)} %collective-permute-done.6.refs_3_), channel_id=1, source_target_pairs={{0,1},{1,2},{2,3},{3,4},{4,5},{5,6},{6,7},{7,8},{8,9},{9,10},{10,1... | collective-permute-start | bytes 1081352 | tf_op jit(solution)/shard_map/ppermute | solution.py:302
  66.5 0.0 collective-permute-done.11.refs_4_
  66.5 4.6 %collective-permute-start.13 = (bf16[1408,128]{1,0:T(8,128)(2,1)S(1)}, bf16[1408,128]{1,0:T(8,128)(2,1)S(1)}, u32[]{:S(2)}, u32[]{:S(2)}) collective-permute-start(bf16[1408,128]{1,0:T(8,128)(2,1)S(1)} %collective-permute-done.11.refs_4_), channel_id=1, source_target_pairs={{0,15},{1,0},{2,1},{3,2},{4,3},{5,4},{6,5},{7,6},{8,7},{9,8},{10,9... | collective-permute-start | bytes 1081352 | tf_op jit(solution)/shard_map/ppermute | solution.py:302
  71.1 2.4 %shard_map.109.refs_5_ = f32[2064,128]{1,0:T(8,128)S(1)} custom-call(s32[18]{0:T(128)S(1)} %copy-done.6, s32[1056]{0:T(1024)S(1)} %get-tuple-element.49.refs_1_, bf16[128,128,32]{2,1,0:T(8,128)(2,1)S(1)} %shard_map.105.refs_2_, bf16[1408,128]{1,0:T(8,128)(2,1)S(1)} %collective-permute-done.4.refs_3_, bf16[1408,128]{1,0:T(8,128)(2,1)S(1)} %collective-permute-done.9.refs_4_, ...), custom_call_target="tpu_custom_call" | custom-call | flops 671088640 | bytes 8388608 | tf_op jit(solution)/shard_map/pallas_call | solution.py:287
  73.5 0.4 collective-permute-done.8.refs_3_
  74.0 1.9 %collective-permute-start.10 = (bf16[1408,128]{1,0:T(8,128)(2,1)S(1)}, bf16[1408,128]{1,0:T(8,128)(2,1)S(1)}, u32[]{:S(2)}, u32[]{:S(2)}) collective-permute-start(bf16[1408,128]{1,0:T(8,128)(2,1)S(1)} %collective-permute-done.8.refs_3_), channel_id=1, source_target_pairs={{0,1},{1,2},{2,3},{3,4},{4,5},{5,6},{6,7},{7,8},{8,9},{9,10},{10,1... | collective-permute-start | bytes 1081352 | tf_op jit(solution)/shard_map/ppermute | solution.py:302
  75.9 0.0 collective-permute-done.13.refs_4_
  75.9 4.6 %collective-permute-start.14 = (bf16[1408,128]{1,0:T(8,128)(2,1)S(1)}, bf16[1408,128]{1,0:T(8,128)(2,1)S(1)}, u32[]{:S(2)}, u32[]{:S(2)}) collective-permute-start(bf16[1408,128]{1,0:T(8,128)(2,1)S(1)} %collective-permute-done.13.refs_4_), channel_id=1, source_target_pairs={{0,15},{1,0},{2,1},{3,2},{4,3},{5,4},{6,5},{7,6},{8,7},{9,8},{10,9... | collective-permute-start | bytes 1081352 | tf_op jit(solution)/shard_map/ppermute | solution.py:302
  80.5 0.0 copy-start.8
  80.5 2.4 %shard_map.110.refs_5_ = f32[2064,128]{1,0:T(8,128)S(1)} custom-call(s32[18]{0:T(128)S(1)} %copy-done.6, s32[1056]{0:T(1024)S(1)} %get-tuple-element.48.refs_1_, bf16[128,128,32]{2,1,0:T(8,128)(2,1)S(1)} %shard_map.105.refs_2_, bf16[1408,128]{1,0:T(8,128)(2,1)S(1)} %collective-permute-done.6.refs_3_, bf16[1408,128]{1,0:T(8,128)(2,1)S(1)} %collective-permute-done.11.refs_4_, ...), custom_call_target="tpu_custom_call" | custom-call | flops 671088640 | bytes 8388608 | tf_op jit(solution)/shard_map/pallas_call | solution.py:287
  82.9 0.4 collective-permute-done.10.refs_3_
  83.3 1.9 %collective-permute-start.12 = (bf16[1408,128]{1,0:T(8,128)(2,1)S(1)}, bf16[1408,128]{1,0:T(8,128)(2,1)S(1)}, u32[]{:S(2)}, u32[]{:S(2)}) collective-permute-start(bf16[1408,128]{1,0:T(8,128)(2,1)S(1)} %collective-permute-done.10.refs_3_), channel_id=1, source_target_pairs={{0,1},{1,2},{2,3},{3,4},{4,5},{5,6},{6,7},{7,8},{8,9},{9,10},{10,1... | collective-permute-start | bytes 1081352 | tf_op jit(solution)/shard_map/ppermute | solution.py:302
  85.3 0.0 copy-start.2
  85.3 2.2 %copy-done.2 = bf16[128,128,32]{2,1,0:T(8,128)(2,1)S(1)} copy-done((bf16[128,128,32]{2,1,0:T(8,128)(2,1)S(1)}, bf16[128,128,32]{2,1,0:T(8,128)(2,1)}, u32[]{:S(2)}) %copy-start.2) | copy-done | bytes 1048600
  87.5 2.4 %shard_map.111.refs_5_ = f32[2064,128]{1,0:T(8,128)S(1)} custom-call(s32[18]{0:T(128)S(1)} %copy-done.6, s32[1056]{0:T(1024)S(1)} %get-tuple-element.46.refs_1_, bf16[128,128,32]{2,1,0:T(8,128)(2,1)S(1)} %copy-done.2, bf16[1408,128]{1,0:T(8,128)(2,1)S(1)} %collective-permute-done.8.refs_3_, bf16[1408,128]{1,0:T(8,128)(2,1)S(1)} %collective-permute-done.13.refs_4_, ...), custom_call_target="tpu_custom_call" | custom-call | flops 671088640 | bytes 8388608 | tf_op jit(solution)/shard_map/pallas_call | solution.py:287
  89.9 0.0 collective-permute-done.14.refs_4_
  89.9 0.0 copy-start.3
  89.9 0.0 copy-start.4
  89.9 0.0 copy-start.5
  89.9 2.4 %shard_map.112.refs_4_ = f32[2064,128]{1,0:T(8,128)S(1)} custom-call(s32[18]{0:T(128)S(1)} %copy-done.6, s32[1056]{0:T(1024)S(1)} %get-tuple-element.47.refs_1_, bf16[128,128,32]{2,1,0:T(8,128)(2,1)S(1)} %copy-done.2, bf16[1408,128]{1,0:T(8,128)(2,1)S(1)} %collective-permute-done.10.refs_3_, bf16[1408,128]{1,0:T(8,128)(2,1)S(1)} %collective-permute-done.14.refs_4_, ...), custom_call_target="tpu_custom_call" | custom-call | flops 671088640 | bytes 8388608 | tf_op jit(solution)/shard_map/pallas_call | solution.py:287
  92.3 0.4 collective-permute-done.12.refs_3_
  92.7 0.0 copy-done.4
  92.7 2.3 %shard_map.113 = (f32[128,128]{1,0:T(8,128)}, f32[96,128]{1,0:T(8,128)S(1)}) custom-call(s32[18]{0:T(128)S(1)} %copy-done.6, s32[1056]{0:T(1024)S(1)} %get-tuple-element.53.refs_1_, bf16[128,128,32]{2,1,0:T(8,128)(2,1)S(1)} %copy-done.2, bf16[1408,128]{1,0:T(8,128)(2,1)S(1)} %collective-permute-done.12.refs_3_, f32[2064,128]{1,0:T(8,128)S(1)} %shard_map.112.refs_4_, ...), custom_call_target="tpu_custom_call" | custom-call | flops 671088640 | bytes 8388608 | tf_op jit(solution)/shard_map/pallas_call | solution.py:287
  95.0 1.3 %collective-permute-start.15 = (f32[32,128]{1,0:T(8,128)S(1)}, f32[32,128]{1,0:T(8,128)S(1)}, u32[]{:S(2)}, u32[]{:S(2)}) collective-permute-start(f32[32,128]{1,0:T(8,128)S(1)} %get-tuple-element.44), channel_id=1, source_target_pairs={{0,1},{1,2},{2,3},{3,4},{4,5},{5,6},{6,7},{7,8},{8,9},{9,10},{10,1... | collective-permute-start | bytes 49160 | tf_op jit(solution)/shard_map/ppermute | solution.py:308
  96.3 1.3 %collective-permute-start.16 = (f32[32,128]{1,0:T(8,128)S(1)}, f32[32,128]{1,0:T(8,128)S(1)}, u32[]{:S(2)}, u32[]{:S(2)}) collective-permute-start(f32[32,128]{1,0:T(8,128)S(1)} %get-tuple-element.45), channel_id=1, source_target_pairs={{1,0},{2,1},{3,2},{4,3},{5,4},{6,5},{7,6},{8,7},{9,8},{10,9},{11,1... | collective-permute-start | bytes 49160 | tf_op jit(solution)/shard_map/ppermute | solution.py:308
  97.6 0.0 collective-permute-done.15
  97.6 3.2 %collective-permute-done.16 = f32[32,128]{1,0:T(8,128)S(1)} collective-permute-done((f32[32,128]{1,0:T(8,128)S(1)}, f32[32,128]{1,0:T(8,128)S(1)}, u32[]{:S(2)}, u32[]{:S(2)}) %collective-permute-start.16) | collective-permute-done | bytes 16416 | tf_op jit(solution)/shard_map/ppermute | solution.py:308
  100.8 13.8 %collective-permute-start.17 = (f32[1,128]{1,0:T(1,128)S(1)}, f32[1,128]{1,0:T(1,128)S(1)}, u32[]{:S(2)}, u32[]{:S(2)}) collective-permute-start(f32[1,128]{1,0:T(1,128)S(1)} %get-tuple-element.54), channel_id=1, source_target_pairs={{0,16},{16,32},{32,48},{48,64},{64,80},{80,96},{96,112},{112,128},... | collective-permute-start | bytes 1544 | tf_op jit(solution)/shard_map/ppermute | solution.py:308
  114.5 1.9 %collective-permute-start.18 = (f32[1,128]{1,0:T(1,128)S(1)}, f32[1,128]{1,0:T(1,128)S(1)}, u32[]{:S(2)}, u32[]{:S(2)}) collective-permute-start(f32[1,128]{1,0:T(1,128)S(1)} %get-tuple-element.55), channel_id=1, source_target_pairs={{16,0},{32,16},{48,32},{64,48},{80,64},{96,80},{112,96},{128,112},... | collective-permute-start | bytes 1544 | tf_op jit(solution)/shard_map/ppermute | solution.py:308
  116.4 0.0 collective-permute-done.17
  116.5 5.0 %collective-permute-done.18 = f32[1,128]{1,0:T(1,128)S(1)} collective-permute-done((f32[1,128]{1,0:T(1,128)S(1)}, f32[1,128]{1,0:T(1,128)S(1)}, u32[]{:S(2)}, u32[]{:S(2)}) %collective-permute-start.18) | collective-permute-done | bytes 544 | tf_op jit(solution)/shard_map/ppermute | solution.py:308
  121.5 0.8 convolution_add_fusion
  (11 shorter events, 0.0 us)
Async XLA Ops:
  0.6 120.9 %copy-start = (f32[128,128]{1,0:T(8,128)S(1)}, f32[128,128]{1,0:T(8,128)}, u32[]{:S(2)}) copy-start(f32[128,128]{1,0:T(8,128)} %param.17) | copy-start | bytes 196612
  1.7 19.4 %collective-permute-start = (bf16[1408,128]{1,0:T(8,128)(2,1)S(1)}, bf16[1408,128]{1,0:T(8,128)(2,1)S(1)}, u32[]{:S(2)}, u32[]{:S(2)}) collective-permute-start(bf16[1408,128]{1,0:T(8,128)(2,1)S(1)} %pad_maximum_fusion.here_ref.refs_5_), channel_id=1, source_target_pairs={{0,1},{1,2},{2,3},{3,4},{4,5},{5,6},{6,7},{7,8},{8,9},{9,10},{10,1... | collective-permute-start | bytes 1081352 | tf_op jit(solution)/shard_map/ppermute | solution.py:302
  5.3 17.9 %collective-permute-start.3 = (bf16[1408,128]{1,0:T(8,128)(2,1)S(1)}, bf16[1408,128]{1,0:T(8,128)(2,1)S(1)}, u32[]{:S(2)}, u32[]{:S(2)}) collective-permute-start(bf16[1408,128]{1,0:T(8,128)(2,1)S(1)} %pad_maximum_fusion.here_ref.refs_5_), channel_id=1, source_target_pairs={{0,15},{1,0},{2,1},{3,2},{4,3},{5,4},{6,5},{7,6},{8,7},{9,8},{10,9... | collective-permute-start | bytes 1081352 | tf_op jit(solution)/shard_map/ppermute | solution.py:302
  21.2 13.8 %copy-start.7 = (s32[9248]{0:T(1024)S(1)}, s32[9248]{0:T(1024)}, u32[]{:S(2)}) copy-start(s32[9248]{0:T(1024)} %get-tuple-element.25) | copy-start | bytes 110980
  21.2 18.4 %copy-start.6 = (s32[18]{0:T(128)S(1)}, s32[18]{0:T(128)}, u32[]{:S(2)}) copy-start(s32[18]{0:T(128)} %get-tuple-element.24.refs_0_) | copy-start | bytes 220
  21.2 11.9 %collective-permute-start.1 = (bf16[1408,128]{1,0:T(8,128)(2,1)S(1)}, bf16[1408,128]{1,0:T(8,128)(2,1)S(1)}, u32[]{:S(2)}, u32[]{:S(2)}) collective-permute-start(bf16[1408,128]{1,0:T(8,128)(2,1)S(1)} %collective-permute-done.refs_3_), channel_id=1, source_target_pairs={{0,1},{1,2},{2,3},{3,4},{4,5},{5,6},{6,7},{7,8},{8,9},{9,10},{10,1... | collective-permute-start | bytes 1081352 | tf_op jit(solution)/shard_map/ppermute | solution.py:302
  23.1 11.9 %collective-permute-start.5 = (bf16[1408,128]{1,0:T(8,128)(2,1)S(1)}, bf16[1408,128]{1,0:T(8,128)(2,1)S(1)}, u32[]{:S(2)}, u32[]{:S(2)}) collective-permute-start(bf16[1408,128]{1,0:T(8,128)(2,1)S(1)} %collective-permute-done.3.refs_4_), channel_id=1, source_target_pairs={{0,15},{1,0},{2,1},{3,2},{4,3},{5,4},{6,5},{7,6},{8,7},{9,8},{10,9... | collective-permute-start | bytes 1081352 | tf_op jit(solution)/shard_map/ppermute | solution.py:302
  31.4 49.0 %copy-start.1 = (bf16[128,128,32]{2,1,0:T(8,128)(2,1)}, bf16[128,128,32]{2,1,0:T(8,128)(2,1)S(1)}, u32[]{:S(2)}) copy-start(bf16[128,128,32]{2,1,0:T(8,128)(2,1)S(1)} %shard_map.105.refs_2_) | copy-start | bytes 3145732
  33.1 10.9 %collective-permute-start.2 = (bf16[1408,128]{1,0:T(8,128)(2,1)S(1)}, bf16[1408,128]{1,0:T(8,128)(2,1)S(1)}, u32[]{:S(2)}, u32[]{:S(2)}) collective-permute-start(bf16[1408,128]{1,0:T(8,128)(2,1)S(1)} %collective-permute-done.1.refs_3_), channel_id=1, source_target_pairs={{0,1},{1,2},{2,3},{3,4},{4,5},{5,6},{6,7},{7,8},{8,9},{9,10},{10,1... | collective-permute-start | bytes 1081352 | tf_op jit(solution)/shard_map/ppermute | solution.py:302
  35.0 10.9 %collective-permute-start.7 = (bf16[1408,128]{1,0:T(8,128)(2,1)S(1)}, bf16[1408,128]{1,0:T(8,128)(2,1)S(1)}, u32[]{:S(2)}, u32[]{:S(2)}) collective-permute-start(bf16[1408,128]{1,0:T(8,128)(2,1)S(1)} %collective-permute-done.5.refs_4_), channel_id=1, source_target_pairs={{0,15},{1,0},{2,1},{3,2},{4,3},{5,4},{6,5},{7,6},{8,7},{9,8},{10,9... | collective-permute-start | bytes 1081352 | tf_op jit(solution)/shard_map/ppermute | solution.py:302
  44.0 10.0 %collective-permute-start.4 = (bf16[1408,128]{1,0:T(8,128)(2,1)S(1)}, bf16[1408,128]{1,0:T(8,128)(2,1)S(1)}, u32[]{:S(2)}, u32[]{:S(2)}) collective-permute-start(bf16[1408,128]{1,0:T(8,128)(2,1)S(1)} %collective-permute-done.2.refs_3_), channel_id=1, source_target_pairs={{0,1},{1,2},{2,3},{3,4},{4,5},{5,6},{6,7},{7,8},{8,9},{9,10},{10,1... | collective-permute-start | bytes 1081352 | tf_op jit(solution)/shard_map/ppermute | solution.py:302
  45.9 10.0 %collective-permute-start.9 = (bf16[1408,128]{1,0:T(8,128)(2,1)S(1)}, bf16[1408,128]{1,0:T(8,128)(2,1)S(1)}, u32[]{:S(2)}, u32[]{:S(2)}) collective-permute-start(bf16[1408,128]{1,0:T(8,128)(2,1)S(1)} %collective-permute-done.7.refs_4_), channel_id=1, source_target_pairs={{0,15},{1,0},{2,1},{3,2},{4,3},{5,4},{6,5},{7,6},{8,7},{9,8},{10,9... | collective-permute-start | bytes 1081352 | tf_op jit(solution)/shard_map/ppermute | solution.py:302
  54.0 10.5 %collective-permute-start.6 = (bf16[1408,128]{1,0:T(8,128)(2,1)S(1)}, bf16[1408,128]{1,0:T(8,128)(2,1)S(1)}, u32[]{:S(2)}, u32[]{:S(2)}) collective-permute-start(bf16[1408,128]{1,0:T(8,128)(2,1)S(1)} %collective-permute-done.4.refs_3_), channel_id=1, source_target_pairs={{0,1},{1,2},{2,3},{3,4},{4,5},{5,6},{6,7},{7,8},{8,9},{9,10},{10,1... | collective-permute-start | bytes 1081352 | tf_op jit(solution)/shard_map/ppermute | solution.py:302
  56.0 10.5 %collective-permute-start.11 = (bf16[1408,128]{1,0:T(8,128)(2,1)S(1)}, bf16[1408,128]{1,0:T(8,128)(2,1)S(1)}, u32[]{:S(2)}, u32[]{:S(2)}) collective-permute-start(bf16[1408,128]{1,0:T(8,128)(2,1)S(1)} %collective-permute-done.9.refs_4_), channel_id=1, source_target_pairs={{0,15},{1,0},{2,1},{3,2},{4,3},{5,4},{6,5},{7,6},{8,7},{9,8},{10,9... | collective-permute-start | bytes 1081352 | tf_op jit(solution)/shard_map/ppermute | solution.py:302
  64.6 9.4 %collective-permute-start.8 = (bf16[1408,128]{1,0:T(8,128)(2,1)S(1)}, bf16[1408,128]{1,0:T(8,128)(2,1)S(1)}, u32[]{:S(2)}, u32[]{:S(2)}) collective-permute-start(bf16[1408,128]{1,0:T(8,128)(2,1)S(1)} %collective-permute-done.6.refs_3_), channel_id=1, source_target_pairs={{0,1},{1,2},{2,3},{3,4},{4,5},{5,6},{6,7},{7,8},{8,9},{9,10},{10,1... | collective-permute-start | bytes 1081352 | tf_op jit(solution)/shard_map/ppermute | solution.py:302
  66.5 9.4 %collective-permute-start.13 = (bf16[1408,128]{1,0:T(8,128)(2,1)S(1)}, bf16[1408,128]{1,0:T(8,128)(2,1)S(1)}, u32[]{:S(2)}, u32[]{:S(2)}) collective-permute-start(bf16[1408,128]{1,0:T(8,128)(2,1)S(1)} %collective-permute-done.11.refs_4_), channel_id=1, source_target_pairs={{0,15},{1,0},{2,1},{3,2},{4,3},{5,4},{6,5},{7,6},{8,7},{9,8},{10,9... | collective-permute-start | bytes 1081352 | tf_op jit(solution)/shard_map/ppermute | solution.py:302
  74.0 9.4 %collective-permute-start.10 = (bf16[1408,128]{1,0:T(8,128)(2,1)S(1)}, bf16[1408,128]{1,0:T(8,128)(2,1)S(1)}, u32[]{:S(2)}, u32[]{:S(2)}) collective-permute-start(bf16[1408,128]{1,0:T(8,128)(2,1)S(1)} %collective-permute-done.8.refs_3_), channel_id=1, source_target_pairs={{0,1},{1,2},{2,3},{3,4},{4,5},{5,6},{6,7},{7,8},{8,9},{9,10},{10,1... | collective-permute-start | bytes 1081352 | tf_op jit(solution)/shard_map/ppermute | solution.py:302
  75.9 14.0 %collective-permute-start.14 = (bf16[1408,128]{1,0:T(8,128)(2,1)S(1)}, bf16[1408,128]{1,0:T(8,128)(2,1)S(1)}, u32[]{:S(2)}, u32[]{:S(2)}) collective-permute-start(bf16[1408,128]{1,0:T(8,128)(2,1)S(1)} %collective-permute-done.13.refs_4_), channel_id=1, source_target_pairs={{0,15},{1,0},{2,1},{3,2},{4,3},{5,4},{6,5},{7,6},{8,7},{9,8},{10,9... | collective-permute-start | bytes 1081352 | tf_op jit(solution)/shard_map/ppermute | solution.py:302
  80.5 4.8 %copy-start.8 = (s32[1,128]{1,0:T(1,128)S(1)}, s32[1,128]{1,0:T(1,128)}, u32[]{:S(2)}) copy-start(s32[1,128]{1,0:T(1,128)} %param.15) | copy-start | bytes 1540
  83.3 9.4 %collective-permute-start.12 = (bf16[1408,128]{1,0:T(8,128)(2,1)S(1)}, bf16[1408,128]{1,0:T(8,128)(2,1)S(1)}, u32[]{:S(2)}, u32[]{:S(2)}) collective-permute-start(bf16[1408,128]{1,0:T(8,128)(2,1)S(1)} %collective-permute-done.10.refs_3_), channel_id=1, source_target_pairs={{0,1},{1,2},{2,3},{3,4},{4,5},{5,6},{6,7},{7,8},{8,9},{9,10},{10,1... | collective-permute-start | bytes 1081352 | tf_op jit(solution)/shard_map/ppermute | solution.py:302
  85.3 2.2 %copy-start.2 = (bf16[128,128,32]{2,1,0:T(8,128)(2,1)S(1)}, bf16[128,128,32]{2,1,0:T(8,128)(2,1)}, u32[]{:S(2)}) copy-start(bf16[128,128,32]{2,1,0:T(8,128)(2,1)} %copy-done.1) | copy-start | bytes 3145732
  89.9 2.8 %copy-start.3 = (bf16[1024,128]{1,0:T(8,128)(2,1)S(1)}, bf16[1024,128]{1,0:T(8,128)(2,1)}, u32[]{:S(2)}) copy-start(bf16[1024,128]{1,0:T(8,128)(2,1)} %refs_7_.1) | copy-start | bytes 786436
  89.9 2.8 %copy-start.4 = (f32[1,128,128]{2,1,0:T(8,128)S(1)}, f32[1,128,128]{2,1,0:T(8,128)}, u32[]{:S(2)}) copy-start(f32[1,128,128]{2,1,0:T(8,128)} %param.11) | copy-start | bytes 196612
  89.9 2.8 %copy-start.5 = (f32[1,128,128]{2,1,0:T(8,128)S(1)}, f32[1,128,128]{2,1,0:T(8,128)}, u32[]{:S(2)}) copy-start(f32[1,128,128]{2,1,0:T(8,128)} %param.12) | copy-start | bytes 196612
  95.0 2.6 %collective-permute-start.15 = (f32[32,128]{1,0:T(8,128)S(1)}, f32[32,128]{1,0:T(8,128)S(1)}, u32[]{:S(2)}, u32[]{:S(2)}) collective-permute-start(f32[32,128]{1,0:T(8,128)S(1)} %get-tuple-element.44), channel_id=1, source_target_pairs={{0,1},{1,2},{2,3},{3,4},{4,5},{5,6},{6,7},{7,8},{8,9},{9,10},{10,1... | collective-permute-start | bytes 49160 | tf_op jit(solution)/shard_map/ppermute | solution.py:308
  96.3 4.5 %collective-permute-start.16 = (f32[32,128]{1,0:T(8,128)S(1)}, f32[32,128]{1,0:T(8,128)S(1)}, u32[]{:S(2)}, u32[]{:S(2)}) collective-permute-start(f32[32,128]{1,0:T(8,128)S(1)} %get-tuple-element.45), channel_id=1, source_target_pairs={{1,0},{2,1},{3,2},{4,3},{5,4},{6,5},{7,6},{8,7},{9,8},{10,9},{11,1... | collective-permute-start | bytes 49160 | tf_op jit(solution)/shard_map/ppermute | solution.py:308
  100.8 15.7 %collective-permute-start.17 = (f32[1,128]{1,0:T(1,128)S(1)}, f32[1,128]{1,0:T(1,128)S(1)}, u32[]{:S(2)}, u32[]{:S(2)}) collective-permute-start(f32[1,128]{1,0:T(1,128)S(1)} %get-tuple-element.54), channel_id=1, source_target_pairs={{0,16},{16,32},{32,48},{48,64},{64,80},{80,96},{96,112},{112,128},... | collective-permute-start | bytes 1544 | tf_op jit(solution)/shard_map/ppermute | solution.py:308
  114.5 7.0 %collective-permute-start.18 = (f32[1,128]{1,0:T(1,128)S(1)}, f32[1,128]{1,0:T(1,128)S(1)}, u32[]{:S(2)}, u32[]{:S(2)}) collective-permute-start(f32[1,128]{1,0:T(1,128)S(1)} %get-tuple-element.55), channel_id=1, source_target_pairs={{16,0},{32,16},{48,32},{64,48},{80,64},{96,80},{112,96},{128,112},... | collective-permute-start | bytes 1544 | tf_op jit(solution)/shard_map/ppermute | solution.py:308

commit v9 on v8

--- a/solution.py
+++ b/solution.py
@@ -23,7 +23,7 @@
 ROUNDS = N_TILE // 2 + 1
 REGION = CL * PAIRS
 KEY_SHIFT = 20
-OWN_ROUNDS = 3
+OWN_ROUNDS = 4
 YDIM = 8
 KDIM = 2 * YDIM
 HIST_ROWS = CL * COLS

time: 123 us -> 122 us (level)
  starting transfers between devices: 72.1 us -> 70.2 us
    ppermute x4, starting transfers between devices: 18.2 us -> 16.3 us  [shifted(): return lax.ppermute(block, axis, route)]
  transfers between devices with their start and end apart: 19 -> 19, of which waited for: 8 -> 7; matrix products, arithmetic and copies ran while one was open for 1% -> 1% of each run, Pallas kernels for 24% -> 24%
where the time goes in v9:
time: 122 us; the launch traced here: 120 us
  starting transfers between devices  70.2 us (58%)
  Pallas kernels  31.4 us (26%)
  waiting for transfers between devices  12.4 us (10%)
  other arithmetic  2.36 us (2%)
  local copies, waits for them, and re-layouts  2.25 us (2%)
    ppermute x15, starting transfers between devices, hop(): lax.ppermute(block, 'tile', [(i, (i + distance) % peers) for i in range(p...  53.9 us
    pallas_call x8, Pallas kernels, consume(): pl.pallas_call(functools.partial(ring_kernel, turn, shape, acc is not Non...  22.6 us
    ppermute x4, starting transfers between devices, shifted(): return lax.ppermute(block, axis, route)  16.3 us
    ppermute x4, waiting for transfers between devices, shifted(): return lax.ppermute(block, axis, route)  8.21 us
    pallas_call x1, Pallas kernels, make_lists(): pl.pallas_call(list_kernel, out_shape=[jax.ShapeDtypeStruct((ROUNDS * REG...  5.07 us
    ppermute x15, waiting for transfers between devices, hop(): lax.ppermute(block, 'tile', [(i, (i + distance) % peers) for i in range(p...  4.21 us
    pallas_call x1, Pallas kernels, turned_rows(): pl.pallas_call(turn_kernel, out_shape=jax.ShapeDtypeStruct((CL, PTS, 2 *...  3.74 us
  transfers between devices with their start and end apart: 19, of which 7 were waited for; matrix products, arithmetic and copies ran while one was open for 1% of the time, Pallas kernels for 24%

profile of v9, /device:TPU:7, one launch (start us, length us, event | category | flops | bytes accessed | tf_op | source)
XLA Modules:
  0.0 120.5 jit_solution(17869030419443787686)
XLA Ops:
  0.6 0.0 copy-start
  0.6 1.1 pad_maximum_fusion.here_ref.refs_5_
  1.7 3.5 %collective-permute-start = (bf16[1408,128]{1,0:T(8,128)(2,1)S(1)}, bf16[1408,128]{1,0:T(8,128)(2,1)S(1)}, u32[]{:S(2)}, u32[]{:S(2)}) collective-permute-start(bf16[1408,128]{1,0:T(8,128)(2,1)S(1)} %pad_maximum_fusion.here_ref.refs_5_), channel_id=1, source_target_pairs={{0,1},{1,2},{2,3},{3,4},{4,5},{5,6},{6,7},{7,8},{8,9},{9,10},{10,1... | collective-permute-start | bytes 1081352 | tf_op jit(solution)/shard_map/ppermute | solution.py:302
  5.3 9.5 %collective-permute-start.3 = (bf16[1408,128]{1,0:T(8,128)(2,1)S(1)}, bf16[1408,128]{1,0:T(8,128)(2,1)S(1)}, u32[]{:S(2)}, u32[]{:S(2)}) collective-permute-start(bf16[1408,128]{1,0:T(8,128)(2,1)S(1)} %pad_maximum_fusion.here_ref.refs_5_), channel_id=1, source_target_pairs={{0,15},{1,0},{2,1},{3,2},{4,3},{5,4},{6,5},{7,6},{8,7},{9,8},{10,9... | collective-permute-start | bytes 1081352 | tf_op jit(solution)/shard_map/ppermute | solution.py:302
  14.8 1.3 %fusion.10.key_ref = s32[8,128]{1,0:T(8,128)} fusion(s32[1,128,8]{1,2,0:T(8,128)} %param.13, s32[128]{0:T(128)S(1)} %get-tuple-element.56, s32[128]{0:T(128)S(1)} %get-tuple-element.57, s32[]{:T(128)S(6)} %axis_index.12, s32[128]{0:T(128)} %bitcast.39), kind=kLoop, calls=%fused_computation.15 | loop fusion | flops 18432 | bytes 9732 | tf_op jit(solution)/shard_map/or | solution.py:140
  16.1 5.1 %shard_map.104 = (s32[9248]{0:T(1024)}, s32[18]{0:T(128)}) custom-call(s32[8,128]{1,0:T(8,128)} %fusion.10.key_ref), custom_call_target="tpu_custom_call" | custom-call | flops 1000000 | bytes 10000000 | tf_op jit(solution)/shard_map/pallas_call | solution.py:106
  21.1 0.0 collective-permute-done.refs_3_
  21.2 0.0 copy-start.7
  21.2 0.0 copy-start.6
  21.2 1.9 %collective-permute-start.1 = (bf16[1408,128]{1,0:T(8,128)(2,1)S(1)}, bf16[1408,128]{1,0:T(8,128)(2,1)S(1)}, u32[]{:S(2)}, u32[]{:S(2)}) collective-permute-start(bf16[1408,128]{1,0:T(8,128)(2,1)S(1)} %collective-permute-done.refs_3_), channel_id=1, source_target_pairs={{0,1},{1,2},{2,3},{3,4},{4,5},{5,6},{6,7},{7,8},{8,9},{9,10},{10,1... | collective-permute-start | bytes 1081352 | tf_op jit(solution)/shard_map/ppermute | solution.py:302
  23.1 0.0 collective-permute-done.3.refs_4_
  23.1 4.6 %collective-permute-start.5 = (bf16[1408,128]{1,0:T(8,128)(2,1)S(1)}, bf16[1408,128]{1,0:T(8,128)(2,1)S(1)}, u32[]{:S(2)}, u32[]{:S(2)}) collective-permute-start(bf16[1408,128]{1,0:T(8,128)(2,1)S(1)} %collective-permute-done.3.refs_4_), channel_id=1, source_target_pairs={{0,15},{1,0},{2,1},{3,2},{4,3},{5,4},{6,5},{7,6},{8,7},{9,8},{10,9... | collective-permute-start | bytes 1081352 | tf_op jit(solution)/shard_map/ppermute | solution.py:302
  27.7 3.7 %shard_map.105.refs_2_ = bf16[128,128,32]{2,1,0:T(8,128)(2,1)S(1)} custom-call(bf16[1408,128]{1,0:T(8,128)(2,1)S(1)} %pad_maximum_fusion.here_ref.refs_5_), custom_call_target="tpu_custom_call" | custom-call | flops 1000000 | bytes 10000000 | tf_op jit(solution)/shard_map/pallas_call | solution.py:120
  31.4 0.0 copy-start.1
  31.5 1.6 %collective-permute-done.1.refs_3_ = bf16[1408,128]{1,0:T(8,128)(2,1)S(1)} collective-permute-done((bf16[1408,128]{1,0:T(8,128)(2,1)S(1)}, bf16[1408,128]{1,0:T(8,128)(2,1)S(1)}, u32[]{:S(2)}, u32[]{:S(2)}) %collective-permute-start.1) | collective-permute-done | bytes 360480 | tf_op jit(solution)/shard_map/ppermute | solution.py:302
  33.1 1.9 %collective-permute-start.2 = (bf16[1408,128]{1,0:T(8,128)(2,1)S(1)}, bf16[1408,128]{1,0:T(8,128)(2,1)S(1)}, u32[]{:S(2)}, u32[]{:S(2)}) collective-permute-start(bf16[1408,128]{1,0:T(8,128)(2,1)S(1)} %collective-permute-done.1.refs_3_), channel_id=1, source_target_pairs={{0,1},{1,2},{2,3},{3,4},{4,5},{5,6},{6,7},{7,8},{8,9},{9,10},{10,1... | collective-permute-start | bytes 1081352 | tf_op jit(solution)/shard_map/ppermute | solution.py:302
  35.0 0.0 copy-done.7
  35.0 0.0 collective-permute-done.5.refs_4_
  35.0 4.6 %collective-permute-start.7 = (bf16[1408,128]{1,0:T(8,128)(2,1)S(1)}, bf16[1408,128]{1,0:T(8,128)(2,1)S(1)}, u32[]{:S(2)}, u32[]{:S(2)}) collective-permute-start(bf16[1408,128]{1,0:T(8,128)(2,1)S(1)} %collective-permute-done.5.refs_4_), channel_id=1, source_target_pairs={{0,15},{1,0},{2,1},{3,2},{4,3},{5,4},{6,5},{7,6},{8,7},{9,8},{10,9... | collective-permute-start | bytes 1081352 | tf_op jit(solution)/shard_map/ppermute | solution.py:302
  39.6 0.0 copy-done.6
  39.6 3.3 %shard_map.106.refs_6_ = f32[2064,128]{1,0:T(8,128)S(1)} custom-call(s32[18]{0:T(128)S(1)} %copy-done.6, s32[1056]{0:T(1024)S(1)} %get-tuple-element.52.refs_1_, bf16[128,128,32]{2,1,0:T(8,128)(2,1)S(1)} %shard_map.105.refs_2_, bf16[1408,128]{1,0:T(8,128)(2,1)S(1)} %collective-permute-done.refs_3_, bf16[1408,128]{1,0:T(8,128)(2,1)S(1)} %collective-permute-done.3.refs_4_, ...), custom_call_target="tpu_custom_call" | custom-call | flops 671088640 | bytes 8388608 | tf_op jit(solution)/shard_map/pallas_call | solution.py:287
  42.9 1.1 collective-permute-done.2.refs_3_
  44.0 1.9 %collective-permute-start.4 = (bf16[1408,128]{1,0:T(8,128)(2,1)S(1)}, bf16[1408,128]{1,0:T(8,128)(2,1)S(1)}, u32[]{:S(2)}, u32[]{:S(2)}) collective-permute-start(bf16[1408,128]{1,0:T(8,128)(2,1)S(1)} %collective-permute-done.2.refs_3_), channel_id=1, source_target_pairs={{0,1},{1,2},{2,3},{3,4},{4,5},{5,6},{6,7},{7,8},{8,9},{9,10},{10,1... | collective-permute-start | bytes 1081352 | tf_op jit(solution)/shard_map/ppermute | solution.py:302
  45.9 0.0 collective-permute-done.7.refs_4_
  45.9 4.6 %collective-permute-start.9 = (bf16[1408,128]{1,0:T(8,128)(2,1)S(1)}, bf16[1408,128]{1,0:T(8,128)(2,1)S(1)}, u32[]{:S(2)}, u32[]{:S(2)}) collective-permute-start(bf16[1408,128]{1,0:T(8,128)(2,1)S(1)} %collective-permute-done.7.refs_4_), channel_id=1, source_target_pairs={{0,15},{1,0},{2,1},{3,2},{4,3},{5,4},{6,5},{7,6},{8,7},{9,8},{10,9... | collective-permute-start | bytes 1081352 | tf_op jit(solution)/shard_map/ppermute | solution.py:302
  50.5 3.3 %shard_map.107.refs_6_ = f32[2064,128]{1,0:T(8,128)S(1)} custom-call(s32[18]{0:T(128)S(1)} %copy-done.6, s32[1056]{0:T(1024)S(1)} %get-tuple-element.51.refs_1_, bf16[128,128,32]{2,1,0:T(8,128)(2,1)S(1)} %shard_map.105.refs_2_, bf16[1408,128]{1,0:T(8,128)(2,1)S(1)} %collective-permute-done.1.refs_3_, bf16[1408,128]{1,0:T(8,128)(2,1)S(1)} %collective-permute-done.5.refs_4_, ...), custom_call_target="tpu_custom_call" | custom-call | flops 671088640 | bytes 8388608 | tf_op jit(solution)/shard_map/pallas_call | solution.py:287
  53.8 0.2 collective-permute-done.4.refs_3_
  54.0 1.9 %collective-permute-start.6 = (bf16[1408,128]{1,0:T(8,128)(2,1)S(1)}, bf16[1408,128]{1,0:T(8,128)(2,1)S(1)}, u32[]{:S(2)}, u32[]{:S(2)}) collective-permute-start(bf16[1408,128]{1,0:T(8,128)(2,1)S(1)} %collective-permute-done.4.refs_3_), channel_id=1, source_target_pairs={{0,1},{1,2},{2,3},{3,4},{4,5},{5,6},{6,7},{7,8},{8,9},{9,10},{10,1... | collective-permute-start | bytes 1081352 | tf_op jit(solution)/shard_map/ppermute | solution.py:302
  56.0 0.0 collective-permute-done.9.refs_4_
  56.0 4.6 %collective-permute-start.11 = (bf16[1408,128]{1,0:T(8,128)(2,1)S(1)}, bf16[1408,128]{1,0:T(8,128)(2,1)S(1)}, u32[]{:S(2)}, u32[]{:S(2)}) collective-permute-start(bf16[1408,128]{1,0:T(8,128)(2,1)S(1)} %collective-permute-done.9.refs_4_), channel_id=1, source_target_pairs={{0,15},{1,0},{2,1},{3,2},{4,3},{5,4},{6,5},{7,6},{8,7},{9,8},{10,9... | collective-permute-start | bytes 1081352 | tf_op jit(solution)/shard_map/ppermute | solution.py:302
  60.5 3.3 %shard_map.108.refs_6_ = f32[2064,128]{1,0:T(8,128)S(1)} custom-call(s32[18]{0:T(128)S(1)} %copy-done.6, s32[1056]{0:T(1024)S(1)} %get-tuple-element.50.refs_1_, bf16[128,128,32]{2,1,0:T(8,128)(2,1)S(1)} %shard_map.105.refs_2_, bf16[1408,128]{1,0:T(8,128)(2,1)S(1)} %collective-permute-done.2.refs_3_, bf16[1408,128]{1,0:T(8,128)(2,1)S(1)} %collective-permute-done.7.refs_4_, ...), custom_call_target="tpu_custom_call" | custom-call | flops 671088640 | bytes 8388608 | tf_op jit(solution)/shard_map/pallas_call | solution.py:287
  63.8 0.0 collective-permute-done.6.refs_3_
  63.8 1.9 %collective-permute-start.8 = (bf16[1408,128]{1,0:T(8,128)(2,1)S(1)}, bf16[1408,128]{1,0:T(8,128)(2,1)S(1)}, u32[]{:S(2)}, u32[]{:S(2)}) collective-permute-start(bf16[1408,128]{1,0:T(8,128)(2,1)S(1)} %collective-permute-done.6.refs_3_), channel_id=1, source_target_pairs={{0,1},{1,2},{2,3},{3,4},{4,5},{5,6},{6,7},{7,8},{8,9},{9,10},{10,1... | collective-permute-start | bytes 1081352 | tf_op jit(solution)/shard_map/ppermute | solution.py:302
  65.8 0.0 collective-permute-done.11.refs_4_
  65.8 4.6 %collective-permute-start.13 = (bf16[1408,128]{1,0:T(8,128)(2,1)S(1)}, bf16[1408,128]{1,0:T(8,128)(2,1)S(1)}, u32[]{:S(2)}, u32[]{:S(2)}) collective-permute-start(bf16[1408,128]{1,0:T(8,128)(2,1)S(1)} %collective-permute-done.11.refs_4_), channel_id=1, source_target_pairs={{0,15},{1,0},{2,1},{3,2},{4,3},{5,4},{6,5},{7,6},{8,7},{9,8},{10,9... | collective-permute-start | bytes 1081352 | tf_op jit(solution)/shard_map/ppermute | solution.py:302
  70.4 3.3 %shard_map.109.refs_5_ = f32[2064,128]{1,0:T(8,128)S(1)} custom-call(s32[18]{0:T(128)S(1)} %copy-done.6, s32[1056]{0:T(1024)S(1)} %get-tuple-element.49.refs_1_, bf16[128,128,32]{2,1,0:T(8,128)(2,1)S(1)} %shard_map.105.refs_2_, bf16[1408,128]{1,0:T(8,128)(2,1)S(1)} %collective-permute-done.4.refs_3_, bf16[1408,128]{1,0:T(8,128)(2,1)S(1)} %collective-permute-done.9.refs_4_, ...), custom_call_target="tpu_custom_call" | custom-call | flops 671088640 | bytes 8388608 | tf_op jit(solution)/shard_map/pallas_call | solution.py:287
  73.6 0.0 collective-permute-done.8.refs_3_
  73.6 1.9 %collective-permute-start.10 = (bf16[1408,128]{1,0:T(8,128)(2,1)S(1)}, bf16[1408,128]{1,0:T(8,128)(2,1)S(1)}, u32[]{:S(2)}, u32[]{:S(2)}) collective-permute-start(bf16[1408,128]{1,0:T(8,128)(2,1)S(1)} %collective-permute-done.8.refs_3_), channel_id=1, source_target_pairs={{0,1},{1,2},{2,3},{3,4},{4,5},{5,6},{6,7},{7,8},{8,9},{9,10},{10,1... | collective-permute-start | bytes 1081352 | tf_op jit(solution)/shard_map/ppermute | solution.py:302
  75.6 0.0 collective-permute-done.13.refs_4_
  75.6 4.6 %collective-permute-start.14 = (bf16[1408,128]{1,0:T(8,128)(2,1)S(1)}, bf16[1408,128]{1,0:T(8,128)(2,1)S(1)}, u32[]{:S(2)}, u32[]{:S(2)}) collective-permute-start(bf16[1408,128]{1,0:T(8,128)(2,1)S(1)} %collective-permute-done.13.refs_4_), channel_id=1, source_target_pairs={{0,15},{1,0},{2,1},{3,2},{4,3},{5,4},{6,5},{7,6},{8,7},{9,8},{10,9... | collective-permute-start | bytes 1081352 | tf_op jit(solution)/shard_map/ppermute | solution.py:302
  80.2 0.0 copy-done.1
  80.2 0.0 copy-start.8
  80.2 2.4 %shard_map.110.refs_5_ = f32[2064,128]{1,0:T(8,128)S(1)} custom-call(s32[18]{0:T(128)S(1)} %copy-done.6, s32[1056]{0:T(1024)S(1)} %get-tuple-element.48.refs_1_, bf16[128,128,32]{2,1,0:T(8,128)(2,1)S(1)} %shard_map.105.refs_2_, bf16[1408,128]{1,0:T(8,128)(2,1)S(1)} %collective-permute-done.6.refs_3_, bf16[1408,128]{1,0:T(8,128)(2,1)S(1)} %collective-permute-done.11.refs_4_, ...), custom_call_target="tpu_custom_call" | custom-call | flops 671088640 | bytes 8388608 | tf_op jit(solution)/shard_map/pallas_call | solution.py:287
  82.6 0.4 collective-permute-done.10.refs_3_
  83.0 1.9 %collective-permute-start.12 = (bf16[1408,128]{1,0:T(8,128)(2,1)S(1)}, bf16[1408,128]{1,0:T(8,128)(2,1)S(1)}, u32[]{:S(2)}, u32[]{:S(2)}) collective-permute-start(bf16[1408,128]{1,0:T(8,128)(2,1)S(1)} %collective-permute-done.10.refs_3_), channel_id=1, source_target_pairs={{0,1},{1,2},{2,3},{3,4},{4,5},{5,6},{6,7},{7,8},{8,9},{9,10},{10,1... | collective-permute-start | bytes 1081352 | tf_op jit(solution)/shard_map/ppermute | solution.py:302
  85.0 2.2 %copy-done.2 = bf16[128,128,32]{2,1,0:T(8,128)(2,1)S(1)} copy-done((bf16[128,128,32]{2,1,0:T(8,128)(2,1)S(1)}, bf16[128,128,32]{2,1,0:T(8,128)(2,1)}, u32[]{:S(2)}) %copy-start.2) | copy-done | bytes 1048600
  87.2 2.4 %shard_map.111.refs_5_ = f32[2064,128]{1,0:T(8,128)S(1)} custom-call(s32[18]{0:T(128)S(1)} %copy-done.6, s32[1056]{0:T(1024)S(1)} %get-tuple-element.46.refs_1_, bf16[128,128,32]{2,1,0:T(8,128)(2,1)S(1)} %copy-done.2, bf16[1408,128]{1,0:T(8,128)(2,1)S(1)} %collective-permute-done.8.refs_3_, bf16[1408,128]{1,0:T(8,128)(2,1)S(1)} %collective-permute-done.13.refs_4_, ...), custom_call_target="tpu_custom_call" | custom-call | flops 671088640 | bytes 8388608 | tf_op jit(solution)/shard_map/pallas_call | solution.py:287
  89.6 0.0 collective-permute-done.14.refs_4_
  89.6 0.0 copy-start.3
  89.6 0.0 copy-start.4
  89.6 0.0 copy-start.5
  89.6 2.4 %shard_map.112.refs_4_ = f32[2064,128]{1,0:T(8,128)S(1)} custom-call(s32[18]{0:T(128)S(1)} %copy-done.6, s32[1056]{0:T(1024)S(1)} %get-tuple-element.47.refs_1_, bf16[128,128,32]{2,1,0:T(8,128)(2,1)S(1)} %copy-done.2, bf16[1408,128]{1,0:T(8,128)(2,1)S(1)} %collective-permute-done.10.refs_3_, bf16[1408,128]{1,0:T(8,128)(2,1)S(1)} %collective-permute-done.14.refs_4_, ...), custom_call_target="tpu_custom_call" | custom-call | flops 671088640 | bytes 8388608 | tf_op jit(solution)/shard_map/pallas_call | solution.py:287
  92.0 0.8 collective-permute-done.12.refs_3_
  92.8 2.3 %shard_map.113 = (f32[128,128]{1,0:T(8,128)}, f32[96,128]{1,0:T(8,128)S(1)}) custom-call(s32[18]{0:T(128)S(1)} %copy-done.6, s32[1056]{0:T(1024)S(1)} %get-tuple-element.53.refs_1_, bf16[128,128,32]{2,1,0:T(8,128)(2,1)S(1)} %copy-done.2, bf16[1408,128]{1,0:T(8,128)(2,1)S(1)} %collective-permute-done.12.refs_3_, f32[2064,128]{1,0:T(8,128)S(1)} %shard_map.112.refs_4_, ...), custom_call_target="tpu_custom_call" | custom-call | flops 671088640 | bytes 8388608 | tf_op jit(solution)/shard_map/pallas_call | solution.py:287
  95.1 1.3 %collective-permute-start.15 = (f32[32,128]{1,0:T(8,128)S(1)}, f32[32,128]{1,0:T(8,128)S(1)}, u32[]{:S(2)}, u32[]{:S(2)}) collective-permute-start(f32[32,128]{1,0:T(8,128)S(1)} %get-tuple-element.44), channel_id=1, source_target_pairs={{0,1},{1,2},{2,3},{3,4},{4,5},{5,6},{6,7},{7,8},{8,9},{9,10},{10,1... | collective-permute-start | bytes 49160 | tf_op jit(solution)/shard_map/ppermute | solution.py:308
  96.4 1.3 %collective-permute-start.16 = (f32[32,128]{1,0:T(8,128)S(1)}, f32[32,128]{1,0:T(8,128)S(1)}, u32[]{:S(2)}, u32[]{:S(2)}) collective-permute-start(f32[32,128]{1,0:T(8,128)S(1)} %get-tuple-element.45), channel_id=1, source_target_pairs={{1,0},{2,1},{3,2},{4,3},{5,4},{6,5},{7,6},{8,7},{9,8},{10,9},{11,1... | collective-permute-start | bytes 49160 | tf_op jit(solution)/shard_map/ppermute | solution.py:308
  97.7 0.0 collective-permute-done.15
  97.7 3.2 %collective-permute-done.16 = f32[32,128]{1,0:T(8,128)S(1)} collective-permute-done((f32[32,128]{1,0:T(8,128)S(1)}, f32[32,128]{1,0:T(8,128)S(1)}, u32[]{:S(2)}, u32[]{:S(2)}) %collective-permute-start.16) | collective-permute-done | bytes 16416 | tf_op jit(solution)/shard_map/ppermute | solution.py:308
  100.9 11.8 %collective-permute-start.17 = (f32[1,128]{1,0:T(1,128)S(1)}, f32[1,128]{1,0:T(1,128)S(1)}, u32[]{:S(2)}, u32[]{:S(2)}) collective-permute-start(f32[1,128]{1,0:T(1,128)S(1)} %get-tuple-element.54), channel_id=1, source_target_pairs={{0,16},{16,32},{32,48},{48,64},{64,80},{80,96},{96,112},{112,128},... | collective-permute-start | bytes 1544 | tf_op jit(solution)/shard_map/ppermute | solution.py:308
  112.7 1.9 %collective-permute-start.18 = (f32[1,128]{1,0:T(1,128)S(1)}, f32[1,128]{1,0:T(1,128)S(1)}, u32[]{:S(2)}, u32[]{:S(2)}) collective-permute-start(f32[1,128]{1,0:T(1,128)S(1)} %get-tuple-element.55), channel_id=1, source_target_pairs={{16,0},{32,16},{48,32},{64,48},{80,64},{96,80},{112,96},{128,112},... | collective-permute-start | bytes 1544 | tf_op jit(solution)/shard_map/ppermute | solution.py:308
  114.7 0.0 collective-permute-done.17
  114.7 5.0 %collective-permute-done.18 = f32[1,128]{1,0:T(1,128)S(1)} collective-permute-done((f32[1,128]{1,0:T(1,128)S(1)}, f32[1,128]{1,0:T(1,128)S(1)}, u32[]{:S(2)}, u32[]{:S(2)}) %collective-permute-start.18) | collective-permute-done | bytes 544 | tf_op jit(solution)/shard_map/ppermute | solution.py:308
  119.7 0.0 copy-done
  119.7 0.8 convolution_add_fusion
  (11 shorter events, 0.0 us)
Async XLA Ops:
  0.6 119.1 %copy-start = (f32[128,128]{1,0:T(8,128)S(1)}, f32[128,128]{1,0:T(8,128)}, u32[]{:S(2)}) copy-start(f32[128,128]{1,0:T(8,128)} %param.17) | copy-start | bytes 196612
  1.7 19.4 %collective-permute-start = (bf16[1408,128]{1,0:T(8,128)(2,1)S(1)}, bf16[1408,128]{1,0:T(8,128)(2,1)S(1)}, u32[]{:S(2)}, u32[]{:S(2)}) collective-permute-start(bf16[1408,128]{1,0:T(8,128)(2,1)S(1)} %pad_maximum_fusion.here_ref.refs_5_), channel_id=1, source_target_pairs={{0,1},{1,2},{2,3},{3,4},{4,5},{5,6},{6,7},{7,8},{8,9},{9,10},{10,1... | collective-permute-start | bytes 1081352 | tf_op jit(solution)/shard_map/ppermute | solution.py:302
  5.3 17.9 %collective-permute-start.3 = (bf16[1408,128]{1,0:T(8,128)(2,1)S(1)}, bf16[1408,128]{1,0:T(8,128)(2,1)S(1)}, u32[]{:S(2)}, u32[]{:S(2)}) collective-permute-start(bf16[1408,128]{1,0:T(8,128)(2,1)S(1)} %pad_maximum_fusion.here_ref.refs_5_), channel_id=1, source_target_pairs={{0,15},{1,0},{2,1},{3,2},{4,3},{5,4},{6,5},{7,6},{8,7},{9,8},{10,9... | collective-permute-start | bytes 1081352 | tf_op jit(solution)/shard_map/ppermute | solution.py:302
  21.2 13.8 %copy-start.7 = (s32[9248]{0:T(1024)S(1)}, s32[9248]{0:T(1024)}, u32[]{:S(2)}) copy-start(s32[9248]{0:T(1024)} %get-tuple-element.25) | copy-start | bytes 110980
  21.2 18.4 %copy-start.6 = (s32[18]{0:T(128)S(1)}, s32[18]{0:T(128)}, u32[]{:S(2)}) copy-start(s32[18]{0:T(128)} %get-tuple-element.24.refs_0_) | copy-start | bytes 220
  21.2 11.9 %collective-permute-start.1 = (bf16[1408,128]{1,0:T(8,128)(2,1)S(1)}, bf16[1408,128]{1,0:T(8,128)(2,1)S(1)}, u32[]{:S(2)}, u32[]{:S(2)}) collective-permute-start(bf16[1408,128]{1,0:T(8,128)(2,1)S(1)} %collective-permute-done.refs_3_), channel_id=1, source_target_pairs={{0,1},{1,2},{2,3},{3,4},{4,5},{5,6},{6,7},{7,8},{8,9},{9,10},{10,1... | collective-permute-start | bytes 1081352 | tf_op jit(solution)/shard_map/ppermute | solution.py:302
  23.1 11.9 %collective-permute-start.5 = (bf16[1408,128]{1,0:T(8,128)(2,1)S(1)}, bf16[1408,128]{1,0:T(8,128)(2,1)S(1)}, u32[]{:S(2)}, u32[]{:S(2)}) collective-permute-start(bf16[1408,128]{1,0:T(8,128)(2,1)S(1)} %collective-permute-done.3.refs_4_), channel_id=1, source_target_pairs={{0,15},{1,0},{2,1},{3,2},{4,3},{5,4},{6,5},{7,6},{8,7},{9,8},{10,9... | collective-permute-start | bytes 1081352 | tf_op jit(solution)/shard_map/ppermute | solution.py:302
  31.4 48.7 %copy-start.1 = (bf16[128,128,32]{2,1,0:T(8,128)(2,1)}, bf16[128,128,32]{2,1,0:T(8,128)(2,1)S(1)}, u32[]{:S(2)}) copy-start(bf16[128,128,32]{2,1,0:T(8,128)(2,1)S(1)} %shard_map.105.refs_2_) | copy-start | bytes 3145732
  33.1 10.9 %collective-permute-start.2 = (bf16[1408,128]{1,0:T(8,128)(2,1)S(1)}, bf16[1408,128]{1,0:T(8,128)(2,1)S(1)}, u32[]{:S(2)}, u32[]{:S(2)}) collective-permute-start(bf16[1408,128]{1,0:T(8,128)(2,1)S(1)} %collective-permute-done.1.refs_3_), channel_id=1, source_target_pairs={{0,1},{1,2},{2,3},{3,4},{4,5},{5,6},{6,7},{7,8},{8,9},{9,10},{10,1... | collective-permute-start | bytes 1081352 | tf_op jit(solution)/shard_map/ppermute | solution.py:302
  35.0 10.9 %collective-permute-start.7 = (bf16[1408,128]{1,0:T(8,128)(2,1)S(1)}, bf16[1408,128]{1,0:T(8,128)(2,1)S(1)}, u32[]{:S(2)}, u32[]{:S(2)}) collective-permute-start(bf16[1408,128]{1,0:T(8,128)(2,1)S(1)} %collective-permute-done.5.refs_4_), channel_id=1, source_target_pairs={{0,15},{1,0},{2,1},{3,2},{4,3},{5,4},{6,5},{7,6},{8,7},{9,8},{10,9... | collective-permute-start | bytes 1081352 | tf_op jit(solution)/shard_map/ppermute | solution.py:302
  44.0 10.0 %collective-permute-start.4 = (bf16[1408,128]{1,0:T(8,128)(2,1)S(1)}, bf16[1408,128]{1,0:T(8,128)(2,1)S(1)}, u32[]{:S(2)}, u32[]{:S(2)}) collective-permute-start(bf16[1408,128]{1,0:T(8,128)(2,1)S(1)} %collective-permute-done.2.refs_3_), channel_id=1, source_target_pairs={{0,1},{1,2},{2,3},{3,4},{4,5},{5,6},{6,7},{7,8},{8,9},{9,10},{10,1... | collective-permute-start | bytes 1081352 | tf_op jit(solution)/shard_map/ppermute | solution.py:302
  45.9 10.0 %collective-permute-start.9 = (bf16[1408,128]{1,0:T(8,128)(2,1)S(1)}, bf16[1408,128]{1,0:T(8,128)(2,1)S(1)}, u32[]{:S(2)}, u32[]{:S(2)}) collective-permute-start(bf16[1408,128]{1,0:T(8,128)(2,1)S(1)} %collective-permute-done.7.refs_4_), channel_id=1, source_target_pairs={{0,15},{1,0},{2,1},{3,2},{4,3},{5,4},{6,5},{7,6},{8,7},{9,8},{10,9... | collective-permute-start | bytes 1081352 | tf_op jit(solution)/shard_map/ppermute | solution.py:302
  54.0 9.8 %collective-permute-start.6 = (bf16[1408,128]{1,0:T(8,128)(2,1)S(1)}, bf16[1408,128]{1,0:T(8,128)(2,1)S(1)}, u32[]{:S(2)}, u32[]{:S(2)}) collective-permute-start(bf16[1408,128]{1,0:T(8,128)(2,1)S(1)} %collective-permute-done.4.refs_3_), channel_id=1, source_target_pairs={{0,1},{1,2},{2,3},{3,4},{4,5},{5,6},{6,7},{7,8},{8,9},{9,10},{10,1... | collective-permute-start | bytes 1081352 | tf_op jit(solution)/shard_map/ppermute | solution.py:302
  56.0 9.8 %collective-permute-start.11 = (bf16[1408,128]{1,0:T(8,128)(2,1)S(1)}, bf16[1408,128]{1,0:T(8,128)(2,1)S(1)}, u32[]{:S(2)}, u32[]{:S(2)}) collective-permute-start(bf16[1408,128]{1,0:T(8,128)(2,1)S(1)} %collective-permute-done.9.refs_4_), channel_id=1, source_target_pairs={{0,15},{1,0},{2,1},{3,2},{4,3},{5,4},{6,5},{7,6},{8,7},{9,8},{10,9... | collective-permute-start | bytes 1081352 | tf_op jit(solution)/shard_map/ppermute | solution.py:302
  63.8 9.8 %collective-permute-start.8 = (bf16[1408,128]{1,0:T(8,128)(2,1)S(1)}, bf16[1408,128]{1,0:T(8,128)(2,1)S(1)}, u32[]{:S(2)}, u32[]{:S(2)}) collective-permute-start(bf16[1408,128]{1,0:T(8,128)(2,1)S(1)} %collective-permute-done.6.refs_3_), channel_id=1, source_target_pairs={{0,1},{1,2},{2,3},{3,4},{4,5},{5,6},{6,7},{7,8},{8,9},{9,10},{10,1... | collective-permute-start | bytes 1081352 | tf_op jit(solution)/shard_map/ppermute | solution.py:302
  65.8 9.8 %collective-permute-start.13 = (bf16[1408,128]{1,0:T(8,128)(2,1)S(1)}, bf16[1408,128]{1,0:T(8,128)(2,1)S(1)}, u32[]{:S(2)}, u32[]{:S(2)}) collective-permute-start(bf16[1408,128]{1,0:T(8,128)(2,1)S(1)} %collective-permute-done.11.refs_4_), channel_id=1, source_target_pairs={{0,15},{1,0},{2,1},{3,2},{4,3},{5,4},{6,5},{7,6},{8,7},{9,8},{10,9... | collective-permute-start | bytes 1081352 | tf_op jit(solution)/shard_map/ppermute | solution.py:302
  73.6 9.4 %collective-permute-start.10 = (bf16[1408,128]{1,0:T(8,128)(2,1)S(1)}, bf16[1408,128]{1,0:T(8,128)(2,1)S(1)}, u32[]{:S(2)}, u32[]{:S(2)}) collective-permute-start(bf16[1408,128]{1,0:T(8,128)(2,1)S(1)} %collective-permute-done.8.refs_3_), channel_id=1, source_target_pairs={{0,1},{1,2},{2,3},{3,4},{4,5},{5,6},{6,7},{7,8},{8,9},{9,10},{10,1... | collective-permute-start | bytes 1081352 | tf_op jit(solution)/shard_map/ppermute | solution.py:302
  75.6 14.0 %collective-permute-start.14 = (bf16[1408,128]{1,0:T(8,128)(2,1)S(1)}, bf16[1408,128]{1,0:T(8,128)(2,1)S(1)}, u32[]{:S(2)}, u32[]{:S(2)}) collective-permute-start(bf16[1408,128]{1,0:T(8,128)(2,1)S(1)} %collective-permute-done.13.refs_4_), channel_id=1, source_target_pairs={{0,15},{1,0},{2,1},{3,2},{4,3},{5,4},{6,5},{7,6},{8,7},{9,8},{10,9... | collective-permute-start | bytes 1081352 | tf_op jit(solution)/shard_map/ppermute | solution.py:302
  80.2 4.8 %copy-start.8 = (s32[1,128]{1,0:T(1,128)S(1)}, s32[1,128]{1,0:T(1,128)}, u32[]{:S(2)}) copy-start(s32[1,128]{1,0:T(1,128)} %param.15) | copy-start | bytes 1540
  83.0 9.8 %collective-permute-start.12 = (bf16[1408,128]{1,0:T(8,128)(2,1)S(1)}, bf16[1408,128]{1,0:T(8,128)(2,1)S(1)}, u32[]{:S(2)}, u32[]{:S(2)}) collective-permute-start(bf16[1408,128]{1,0:T(8,128)(2,1)S(1)} %collective-permute-done.10.refs_3_), channel_id=1, source_target_pairs={{0,1},{1,2},{2,3},{3,4},{4,5},{5,6},{6,7},{7,8},{8,9},{9,10},{10,1... | collective-permute-start | bytes 1081352 | tf_op jit(solution)/shard_map/ppermute | solution.py:302
  85.0 2.2 %copy-start.2 = (bf16[128,128,32]{2,1,0:T(8,128)(2,1)S(1)}, bf16[128,128,32]{2,1,0:T(8,128)(2,1)}, u32[]{:S(2)}) copy-start(bf16[128,128,32]{2,1,0:T(8,128)(2,1)} %copy-done.1) | copy-start | bytes 3145732
  89.6 3.2 %copy-start.3 = (bf16[1024,128]{1,0:T(8,128)(2,1)S(1)}, bf16[1024,128]{1,0:T(8,128)(2,1)}, u32[]{:S(2)}) copy-start(bf16[1024,128]{1,0:T(8,128)(2,1)} %refs_7_.1) | copy-start | bytes 786436
  89.6 3.2 %copy-start.4 = (f32[1,128,128]{2,1,0:T(8,128)S(1)}, f32[1,128,128]{2,1,0:T(8,128)}, u32[]{:S(2)}) copy-start(f32[1,128,128]{2,1,0:T(8,128)} %param.11) | copy-start | bytes 196612
  89.6 3.2 %copy-start.5 = (f32[1,128,128]{2,1,0:T(8,128)S(1)}, f32[1,128,128]{2,1,0:T(8,128)}, u32[]{:S(2)}) copy-start(f32[1,128,128]{2,1,0:T(8,128)} %param.12) | copy-start | bytes 196612
  95.1 2.6 %collective-permute-start.15 = (f32[32,128]{1,0:T(8,128)S(1)}, f32[32,128]{1,0:T(8,128)S(1)}, u32[]{:S(2)}, u32[]{:S(2)}) collective-permute-start(f32[32,128]{1,0:T(8,128)S(1)} %get-tuple-element.44), channel_id=1, source_target_pairs={{0,1},{1,2},{2,3},{3,4},{4,5},{5,6},{6,7},{7,8},{8,9},{9,10},{10,1... | collective-permute-start | bytes 49160 | tf_op jit(solution)/shard_map/ppermute | solution.py:308
  96.4 4.5 %collective-permute-start.16 = (f32[32,128]{1,0:T(8,128)S(1)}, f32[32,128]{1,0:T(8,128)S(1)}, u32[]{:S(2)}, u32[]{:S(2)}) collective-permute-start(f32[32,128]{1,0:T(8,128)S(1)} %get-tuple-element.45), channel_id=1, source_target_pairs={{1,0},{2,1},{3,2},{4,3},{5,4},{6,5},{7,6},{8,7},{9,8},{10,9},{11,1... | collective-permute-start | bytes 49160 | tf_op jit(solution)/shard_map/ppermute | solution.py:308
  100.9 13.8 %collective-permute-start.17 = (f32[1,128]{1,0:T(1,128)S(1)}, f32[1,128]{1,0:T(1,128)S(1)}, u32[]{:S(2)}, u32[]{:S(2)}) collective-permute-start(f32[1,128]{1,0:T(1,128)S(1)} %get-tuple-element.54), channel_id=1, source_target_pairs={{0,16},{16,32},{32,48},{48,64},{64,80},{80,96},{96,112},{112,128},... | collective-permute-start | bytes 1544 | tf_op jit(solution)/shard_map/ppermute | solution.py:308
  112.7 7.0 %collective-permute-start.18 = (f32[1,128]{1,0:T(1,128)S(1)}, f32[1,128]{1,0:T(1,128)S(1)}, u32[]{:S(2)}, u32[]{:S(2)}) collective-permute-start(f32[1,128]{1,0:T(1,128)S(1)} %get-tuple-element.55), channel_id=1, source_target_pairs={{16,0},{32,16},{48,32},{64,48},{80,64},{96,80},{112,96},{128,112},... | collective-permute-start | bytes 1544 | tf_op jit(solution)/shard_map/ppermute | solution.py:308
